TPU v7x, 32 devices: a whole 2x2x4 slice. The times are simulated.
32 devices in a mesh: blk: 8 (over y, x, core), group: 4 (over z).
Axes of the slice: x: 2, y: 2, z: 4, core: 2. Of those that a mesh axis runs over, the one named last changes fastest.
Arguments:
- row_factors: float32 [16384, 256], P(('blk', 'group')), may hold values from -0.45 to 0.45
- col_factors: float32 [16384, 256], P(('blk', 'group')), may hold values from -0.45 to 0.45
- tile_values: bfloat16 [5, 256, 128, 128], P(None, ('blk', 'group')), may hold values from -4 to 4
- tile_coords: int32 [5, 256, 2], P(None, ('blk', 'group')), may hold values from 0 to 3, as said below
- tile_counts: int32 [5, 32], P(None, ('blk', 'group')), may hold values from 2 to 8, as said below
Outputs:
- rows_out: float32 [16384, 256], P(('blk', 'group'))
- cols_out: float32 [16384, 256], P(('blk', 'group'))
Inputs may be any that keep to these rules, and one draw needn't show every extreme that they name: `tile_coords`: the 8 entries of one device and stratum name distinct tiles; the row tile is below 4, the column tile below 4. `tile_counts`: in every stratum some device lists 8 live tiles.
All inputs are finite; a program needn't handle non-finite values.
Results may differ from a plain program's by a relative error of at most 0.005.
Values sent between devices are 32-bit elements; how exact they have to be, the bound alone decides.
No kernel may reach another device: no remote copies, remote signals or barrier semaphores. Data moves between devices by JAX's collectives and lax.ppermute only.
A program may use at most 64 MiB of HBM per device.

v0:
```python
import jax
import jax.numpy as jnp
from jax import lax
from jax.sharding import PartitionSpec as P

STRATA = 5


LEARN_RATE = 0.03
DECAY_RATE = 0.1


def shifted(block, axis, distance):
    devices = range(lax.axis_size(axis))
    route = [((i - distance) % len(devices), i) for i in devices]
    return lax.ppermute(block, axis, route)


def picker(positions, extent, live_mask):
    return (positions[:, None] == jnp.arange(extent)[None, :]).astype(jnp.float32) * live_mask[
        :, None
    ]


def padded_parts(row_block, col_block, values, tile_pos, live_mask):
    tile = values.shape[1]
    rank = row_block.shape[1]
    row_pick = picker(tile_pos[:, 0], row_block.shape[0] // tile, live_mask)
    col_pick = picker(tile_pos[:, 1], col_block.shape[0] // tile, live_mask)
    row_half = row_block.astype(jnp.bfloat16).reshape(-1, tile, rank)
    col_half = col_block.astype(jnp.bfloat16).reshape(-1, tile, rank)
    row_sel = jnp.einsum(
        "tk,kia->tia", row_pick.astype(jnp.bfloat16), row_half, preferred_element_type=jnp.float32
    ).astype(jnp.bfloat16)
    col_sel = jnp.einsum(
        "tk,kja->tja", col_pick.astype(jnp.bfloat16), col_half, preferred_element_type=jnp.float32
    ).astype(jnp.bfloat16)
    estimate = jnp.einsum("tia,tja->tij", row_sel, col_sel, preferred_element_type=jnp.float32)
    residue = (values.astype(jnp.float32) - estimate).astype(jnp.bfloat16)
    return (residue, row_sel, col_sel, row_pick, col_pick)


def padded_rows(parts):
    residue, row_sel, col_sel, row_pick, col_pick = parts
    terms = jnp.einsum("tij,tja->tia", residue, col_sel, preferred_element_type=jnp.float32)
    summed = jnp.einsum("tk,tia->kia", row_pick, terms, precision=lax.Precision.HIGHEST)
    return summed.reshape(-1, summed.shape[2])


def padded_cols(parts):
    residue, row_sel, col_sel, row_pick, col_pick = parts
    terms = jnp.einsum("tij,tia->tja", residue, row_sel, preferred_element_type=jnp.float32)
    summed = jnp.einsum("tk,tja->kja", col_pick, terms, precision=lax.Precision.HIGHEST)
    return summed.reshape(-1, summed.shape[2])


def rotate(col_block, stratum):
    if stratum == 2:
        return shifted(col_block, "group", 1)
    return shifted(col_block, "blk", 1)


def per_device(row_factors, col_factors, tile_values, tile_coords, tile_counts):
    row_block = row_factors
    col_block = col_factors
    for stratum in range(STRATA):
        values = tile_values[stratum]
        tile_pos = tile_coords[stratum]
        tile_count = tile_counts[stratum, 0]
        live_mask = (jnp.arange(values.shape[0]) < tile_count).astype(jnp.float32)
        parts = padded_parts(row_block, col_block, values, tile_pos, live_mask)
        grad_rows = padded_rows(parts)
        grad_cols = padded_cols(parts)
        row_block = row_block + LEARN_RATE * (grad_rows - DECAY_RATE * row_block)
        col_block = col_block + LEARN_RATE * (grad_cols - DECAY_RATE * col_block)
        if stratum + 1 < STRATA:
            col_block = rotate(col_block, stratum)
    return (row_block, col_block)


def solution(mesh):
    return jax.shard_map(
        per_device,
        mesh=mesh,
        in_specs=(
            P(("blk", "group"), None),
            P(("blk", "group"), None),
            P(None, ("blk", "group"), None, None),
            P(None, ("blk", "group"), None),
            P(None, ("blk", "group")),
        ),
        out_specs=(P(("blk", "group"), None), P(("blk", "group"), None)),
        check_vma=False,
    )
```

profile of v0, /device:TPU:0, one launch (start us, length us, event | category | flops | bytes accessed | tf_op | source)
XLA Modules:
  0.0 69.6 jit_solution(8988008222525137440)
XLA Ops:
  0.6 1.5 %fusion.190 = (s32[1,1]{0,1:T(1,128)}, s32[1,1]{0,1:T(1,128)}, s32[1,1]{0,1:T(1,128)}, s32[1,1]{0,1:T(1,128)}, s32[1,1]{0,1:T(1,128)}) fusion(s32[5,1]{0,1:T(1,128)} %param.9), kind=kLoop, calls=%fused_computation.254 | loop fusion | bytes 40 | tf_op jit(solution)/shard_map/slice | solution.py:69
  2.1 0.6 compare_convert_fusion.4
  2.7 0.8 %slice_bitcast_fusion = (s32[8,2]{0,1:T(2,128)S(1)}, s32[8,2]{0,1:T(2,128)S(1)}, s32[8,2]{0,1:T(2,128)S(1)}, s32[8,2]{0,1:T(2,128)S(1)}, s32[8,2]{0,1:T(2,128)S(1)}) fusion(s32[5,8,2]{1,2,0:T(2,128)} %param.8), kind=kLoop, calls=%fused_computation.165 | loop fusion | bytes 640 | tf_op jit(solution)/shard_map/squeeze | solution.py:68
  3.4 1.1 %convert_element_type.187 = bf16[512,256]{1,0:T(8,128)(2,1)S(1)} convert(f32[512,256]{1,0:T(8,128)} %param.6) | non-fusion elementwise | flops 131072 | bytes 786432 | tf_op jit(solution)/shard_map/convert_element_type | solution.py:31
  4.5 1.2 %convert_element_type.184 = bf16[512,256]{1,0:T(8,128)(2,1)S(1)} convert(f32[512,256]{1,0:T(8,128)} %param.5) | non-fusion elementwise | flops 131072 | bytes 786432 | tf_op jit(solution)/shard_map/convert_element_type | solution.py:30
  5.7 0.4 convolution_convert_fusion.8
  6.0 0.4 convolution_convert_fusion.9
  6.4 0.3 fusion
  6.7 0.3 fusion.72
  7.1 1.5 %fusion.21 = f32[4,128,256]{2,0,1:T(4,128)S(1)} fusion(f32[8,128,256]{2,1,0:T(8,128)S(1)} %fusion.72, s32[8]{0:T(128)S(1)} %get-tuple-element.18, f32[8]{0:T(128)S(1)} %compare_convert_fusion.4), kind=kOutput, calls=%fused_computation.36 | convolution fusion | flops 12582976 | bytes 1572928 | tf_op jit(solution)/shard_map/tk,tja->kja/dot_general | solution.py:53
  8.8 0.5 collective-permute-start
  9.6 0.7 compare_convert_fusion
  10.3 0.7 compare_convert_fusion.2
  10.9 0.6 compare_convert_fusion.3
  11.6 1.5 %fusion.23 = f32[4,128,256]{2,0,1:T(4,128)S(1)} fusion(f32[8,128,256]{2,1,0:T(8,128)S(1)} %fusion.69, f32[8]{0:T(128)S(1)} %compare_convert_fusion.4, s32[8]{0:T(128)S(1)} %get-tuple-element.17), kind=kOutput, calls=%fused_computation.38 | convolution fusion | flops 12582976 | bytes 1572928 | tf_op jit(solution)/shard_map/tk,tia->kia/dot_general | solution.py:46
  13.1 0.6 compare_convert_fusion.1
  14.0 0.4 convolution_convert_fusion.7
  14.3 4.8 %collective-permute-done = f32[512,256]{1,0:T(8,128)S(1)} collective-permute-done((f32[512,256]{1,0:T(8,128)S(1)}, f32[512,256]{1,0:T(8,128)S(1)}, u32[]{:S(2)}, u32[]{:S(2)}) %collective-permute-start) | collective-permute-done | bytes 524320 | tf_op jit(solution)/shard_map/ppermute | solution.py:16
  19.1 0.4 convolution_convert_fusion.6
  19.5 0.3 fusion.1
  19.8 0.3 fusion.66
  20.4 1.5 %fusion.17 = f32[4,128,256]{2,0,1:T(4,128)S(1)} fusion(f32[8,128,256]{2,1,0:T(8,128)S(1)} %fusion.66, s32[8]{0:T(128)S(1)} %get-tuple-element.26, f32[8]{0:T(128)S(1)} %compare_convert_fusion.3), kind=kOutput, calls=%fused_computation.32 | convolution fusion | flops 12582976 | bytes 1572928 | tf_op jit(solution)/shard_map/tk,tja->kja/dot_general | solution.py:53
  22.0 1.5 %fusion.19 = f32[4,128,256]{2,0,1:T(4,128)S(1)} fusion(f32[8,128,256]{2,1,0:T(8,128)S(1)} %fusion.63, f32[8]{0:T(128)S(1)} %compare_convert_fusion.3, s32[8]{0:T(128)S(1)} %get-tuple-element.27), kind=kOutput, calls=%fused_computation.34 | convolution fusion | flops 12582976 | bytes 1572928 | tf_op jit(solution)/shard_map/tk,tia->kia/dot_general | solution.py:46
  24.1 0.4 convolution_convert_fusion.5
  24.5 9.0 %collective-permute-done.1 = f32[512,256]{1,0:T(8,128)S(1)} collective-permute-done((f32[512,256]{1,0:T(8,128)S(1)}, f32[512,256]{1,0:T(8,128)S(1)}, u32[]{:S(2)}, u32[]{:S(2)}) %collective-permute-start.1) | collective-permute-done | bytes 524320 | tf_op jit(solution)/shard_map/ppermute | solution.py:16
  33.5 0.4 convolution_convert_fusion.4
  33.9 0.3 fusion.2
  34.2 0.3 fusion.60
  34.5 0.3 fusion.57
  34.8 1.5 %fusion.13 = f32[4,128,256]{2,0,1:T(4,128)S(1)} fusion(f32[8,128,256]{2,1,0:T(8,128)S(1)} %fusion.60, s32[8]{0:T(128)S(1)} %get-tuple-element.14, f32[8]{0:T(128)S(1)} %compare_convert_fusion.2), kind=kOutput, calls=%fused_computation.28 | convolution fusion | flops 12582976 | bytes 1572928 | tf_op jit(solution)/shard_map/tk,tja->kja/dot_general | solution.py:53
  36.5 2.4 %collective-permute-start.2 = (f32[512,256]{1,0:T(8,128)S(1)}, f32[512,256]{1,0:T(8,128)S(1)}, u32[]{:S(2)}, u32[]{:S(2)}) collective-permute-start(f32[512,256]{1,0:T(8,128)S(1)} %fusion.34), channel_id=1, source_target_pairs={{3,0},{0,1},{1,2},{2,3},{7,4},{4,5},{5,6},{6,7},{11,8},{8,9},{9,10... | collective-permute-start | bytes 1572872 | tf_op jit(solution)/shard_map/ppermute | solution.py:16
  38.9 1.5 %fusion.15 = f32[4,128,256]{2,0,1:T(4,128)S(1)} fusion(f32[8,128,256]{2,1,0:T(8,128)S(1)} %fusion.57, f32[8]{0:T(128)S(1)} %compare_convert_fusion.2, s32[8]{0:T(128)S(1)} %get-tuple-element.13), kind=kOutput, calls=%fused_computation.30 | convolution fusion | flops 12582976 | bytes 1572928 | tf_op jit(solution)/shard_map/tk,tia->kia/dot_general | solution.py:46
  40.6 0.4 convolution_convert_fusion.3
  40.9 9.4 %collective-permute-done.2 = f32[512,256]{1,0:T(8,128)S(1)} collective-permute-done((f32[512,256]{1,0:T(8,128)S(1)}, f32[512,256]{1,0:T(8,128)S(1)}, u32[]{:S(2)}, u32[]{:S(2)}) %collective-permute-start.2) | collective-permute-done | bytes 524320 | tf_op jit(solution)/shard_map/ppermute | solution.py:16
  50.4 0.4 convolution_convert_fusion.2
  50.7 0.3 fusion.3
  51.1 0.3 fusion.54
  51.7 1.5 %fusion.9 = f32[4,128,256]{2,0,1:T(4,128)S(1)} fusion(f32[8,128,256]{2,1,0:T(8,128)S(1)} %fusion.54, s32[8]{0:T(128)S(1)} %get-tuple-element.24, f32[8]{0:T(128)S(1)} %compare_convert_fusion.1), kind=kOutput, calls=%fused_computation.24 | convolution fusion | flops 12582976 | bytes 1572928 | tf_op jit(solution)/shard_map/tk,tja->kja/dot_general | solution.py:53
  53.7 1.5 %fusion.11 = f32[4,128,256]{2,0,1:T(4,128)S(1)} fusion(f32[8,128,256]{2,1,0:T(8,128)S(1)} %fusion.51, f32[8]{0:T(128)S(1)} %compare_convert_fusion.1, s32[8]{0:T(128)S(1)} %get-tuple-element.25), kind=kOutput, calls=%fused_computation.26 | convolution fusion | flops 12582976 | bytes 1572928 | tf_op jit(solution)/shard_map/tk,tia->kia/dot_general | solution.py:46
  55.4 0.4 convolution_convert_fusion.1
  55.8 7.4 %collective-permute-done.3 = f32[512,256]{1,0:T(8,128)S(1)} collective-permute-done((f32[512,256]{1,0:T(8,128)S(1)}, f32[512,256]{1,0:T(8,128)S(1)}, u32[]{:S(2)}, u32[]{:S(2)}) %collective-permute-start.3) | collective-permute-done | bytes 524320 | tf_op jit(solution)/shard_map/ppermute | solution.py:16
  63.2 0.4 convolution_convert_fusion
  63.6 0.3 fusion.4
  63.9 0.3 fusion.48
  64.5 1.5 %fusion.5 = f32[4,128,256]{2,0,1:T(4,128)S(1)} fusion(f32[8,128,256]{2,1,0:T(8,128)S(1)} %fusion.48, s32[8]{0:T(128)S(1)} %get-tuple-element.10, f32[8]{0:T(128)S(1)} %compare_convert_fusion), kind=kOutput, calls=%fused_computation.20 | convolution fusion | flops 12582976 | bytes 1572928 | tf_op jit(solution)/shard_map/tk,tja->kja/dot_general | solution.py:53
  66.1 1.5 %fusion.7 = f32[4,128,256]{2,0,1:T(4,128)S(1)} fusion(f32[8,128,256]{2,1,0:T(8,128)S(1)} %fusion.45, f32[8]{0:T(128)S(1)} %compare_convert_fusion, s32[8]{0:T(128)S(1)} %get-tuple-element.9), kind=kOutput, calls=%fused_computation.22 | convolution fusion | flops 12582976 | bytes 1572928 | tf_op jit(solution)/shard_map/tk,tia->kia/dot_general | solution.py:46
  67.7 1.0 %fusion.28 = f32[512,256]{1,0:T(8,128)} fusion(f32[4,128,256]{2,1,0:T(8,128)S(1)} %copy.51, f32[4,128,256]{2,1,0:T(8,128)S(1)} %copy.45, f32[512,256]{1,0:T(8,128)S(1)} %get-tuple-element.3, f32[4,128,256]{2,1,0:T(8,128)S(1)} %copy.39), kind=kLoop, calls=%fused_computation.45 | loop fusion | flops 1572864 | bytes 2621440 | tf_op jit(solution)/shard_map/add | solution.py:74
  68.7 0.9 %fusion.26 = f32[512,256]{1,0:T(8,128)} fusion(f32[512,256]{1,0:T(8,128)S(1)} %collective-permute-done.3, f32[4,128,256]{2,1,0:T(8,128)S(1)} %copy.52), kind=kLoop, calls=%fused_computation.42 | loop fusion | flops 524288 | bytes 1572864 | tf_op jit(solution)/shard_map/add | solution.py:75
  (37 shorter events, 3.7 us)
Async XLA Ops:
  4.5 1.9 %copy-start.2 = (bf16[5,8,128,128]{3,2,1,0:T(8,128)(2,1)S(1)}, bf16[5,8,128,128]{3,2,1,0:T(8,128)(2,1)}, u32[]{:S(2)}) copy-start(bf16[5,8,128,128]{3,2,1,0:T(8,128)(2,1)} %param.7) | copy-start | bytes 3932164
  7.1 1.6 %copy-start.1 = (f32[512,256]{1,0:T(8,128)S(1)}, f32[512,256]{1,0:T(8,128)}, u32[]{:S(2)}) copy-start(f32[512,256]{1,0:T(8,128)} %param.6) | copy-start | bytes 1572868
  8.8 10.3 %collective-permute-start = (f32[512,256]{1,0:T(8,128)S(1)}, f32[512,256]{1,0:T(8,128)S(1)}, u32[]{:S(2)}, u32[]{:S(2)}) collective-permute-start(f32[512,256]{1,0:T(8,128)S(1)} %fusion.42), channel_id=1, source_target_pairs={{28,0},{0,4},{4,8},{8,12},{12,16},{16,20},{20,24},{24,28},{29,1},{... | collective-permute-start | bytes 1572872 | tf_op jit(solution)/shard_map/ppermute | solution.py:16
  11.6 2.3 %copy-start = (f32[512,256]{1,0:T(8,128)S(1)}, f32[512,256]{1,0:T(8,128)}, u32[]{:S(2)}) copy-start(f32[512,256]{1,0:T(8,128)} %param.5) | copy-start | bytes 1572868
  23.7 9.7 %collective-permute-start.1 = (f32[512,256]{1,0:T(8,128)S(1)}, f32[512,256]{1,0:T(8,128)S(1)}, u32[]{:S(2)}, u32[]{:S(2)}) collective-permute-start(f32[512,256]{1,0:T(8,128)S(1)} %fusion.38), channel_id=1, source_target_pairs={{28,0},{0,4},{4,8},{8,12},{12,16},{16,20},{20,24},{24,28},{29,1},{... | collective-permute-start | bytes 1572872 | tf_op jit(solution)/shard_map/ppermute | solution.py:16
  36.5 13.8 %collective-permute-start.2 = (f32[512,256]{1,0:T(8,128)S(1)}, f32[512,256]{1,0:T(8,128)S(1)}, u32[]{:S(2)}, u32[]{:S(2)}) collective-permute-start(f32[512,256]{1,0:T(8,128)S(1)} %fusion.34), channel_id=1, source_target_pairs={{3,0},{0,1},{1,2},{2,3},{7,4},{4,5},{5,6},{6,7},{11,8},{8,9},{9,10... | collective-permute-start | bytes 1572872 | tf_op jit(solution)/shard_map/ppermute | solution.py:16
  53.4 9.8 %collective-permute-start.3 = (f32[512,256]{1,0:T(8,128)S(1)}, f32[512,256]{1,0:T(8,128)S(1)}, u32[]{:S(2)}, u32[]{:S(2)}) collective-permute-start(f32[512,256]{1,0:T(8,128)S(1)} %fusion.30), channel_id=1, source_target_pairs={{28,0},{0,4},{4,8},{8,12},{12,16},{16,20},{20,24},{24,28},{29,1},{... | collective-permute-start | bytes 1572872 | tf_op jit(solution)/shard_map/ppermute | solution.py:16
where the time goes:
time: 69.9 us; the launch traced here: 69.6 us
  waiting for transfers between devices  30.5 us (44%)
  matrix products  23.1 us (33%)
  other arithmetic  8.21 us (12%)
  starting transfers between devices  3.39 us (5%)
  local copies, waits for them, and re-layouts  3.29 us (5%)
  between operations  1.14 us (2%)
    ppermute x4, waiting for transfers between devices, shifted(): return lax.ppermute(block, axis, route)  30.5 us
    dot_general x5, matrix products, padded_rows(): jnp.einsum('tk,tia->kia', row_pick, terms, precision=lax.Precision.HIGHEST)  7.39 us
    dot_general x5, matrix products, padded_cols(): jnp.einsum('tk,tja->kja', col_pick, terms, precision=lax.Precision.HIGHEST)  7.39 us
    ppermute x4, starting transfers between devices, shifted(): return lax.ppermute(block, axis, route)  3.39 us
    convert_element_type x5, other arithmetic, per_device(): live_mask = (jnp.arange(values.shape[0]) < tile_count).astype(jnp.float32)  3.13 us
    dot_general x5, matrix products, padded_parts(): jnp.einsum('tk,kja->tja', col_pick.astype(jnp.bfloat16), col_half, prefer...  1.78 us
    dot_general x5, matrix products, padded_parts(): jnp.einsum('tk,kia->tia', row_pick.astype(jnp.bfloat16), row_half, prefer...  1.77 us
    dot_general x5, matrix products, padded_cols(): jnp.einsum('tij,tia->tja', residue, row_sel, preferred_element_type=jnp.f...  1.73 us
  transfers between devices with their start and end apart: 4, of which 4 were waited for; matrix products, arithmetic and copies ran while one was open for 14% of the time, Pallas kernels for 0%

commit v1 on v0

v1 whole, which is shorter than its diff:
```python
import functools

import jax
import jax.numpy as jnp
from jax import lax
from jax.experimental import pallas as pl
from jax.experimental.pallas import tpu as pltpu
from jax.sharding import PartitionSpec as P

STRATA = 5
LEARN_RATE = 0.03
DECAY_RATE = 0.1
CHUNKS = 2
SUBLANES = 8

VMEM = pl.BlockSpec(memory_space=pltpu.VMEM)
SMEM = pl.BlockSpec(memory_space=pltpu.SMEM)
ANY = pl.BlockSpec(memory_space=pl.ANY)


def params():
    return pltpu.CompilerParams(vmem_limit_bytes=24 * 1024 * 1024)


def cost(flops, moved):
    return pl.CostEstimate(flops=flops, bytes_accessed=moved, transcendentals=0)


def scatter(stratum, values, coords, counts, dense, live):
    listed, tile, _ = values.shape
    dense[...] = jnp.zeros_like(dense)
    live[...] = jnp.zeros_like(live)
    count = counts[stratum, 0]
    for t in range(listed):

        @pl.when(t < count)
        def _():
            r = coords[stratum, t, 0]
            c = pl.multiple_of(coords[stratum, t, 1] * tile, tile)
            dense[pl.ds(pl.multiple_of(r * tile, tile), tile), pl.ds(c, tile)] = values[t]
            named = lax.broadcasted_iota(jnp.int32, (SUBLANES, tile), 0) == r
            live[:, pl.ds(c, tile)] = jnp.where(named, 1.0, live[:, pl.ds(c, tile)])


def sgd(old, grad):
    return old + LEARN_RATE * (grad - DECAY_RATE * old)


def chunk_step(tile, rows, cols, dense, live):
    row_half = rows.astype(jnp.bfloat16)
    col_half = cols.astype(jnp.bfloat16)
    estimate = lax.dot_general(
        row_half, col_half, (((1,), (1,)), ((), ())), preferred_element_type=jnp.float32
    )
    parts = []
    for r in range(rows.shape[0] // tile):
        at = slice(r * tile, (r + 1) * tile)
        residue = dense[at].astype(jnp.float32) - estimate[at]
        parts.append(jnp.where(live[r : r + 1] > 0, residue, 0.0).astype(jnp.bfloat16))
    residue = jnp.concatenate(parts, axis=0)
    grad_rows = jnp.dot(residue, col_half, preferred_element_type=jnp.float32)
    grad_cols = lax.dot_general(
        residue, row_half, (((0,), (0,)), ((), ())), preferred_element_type=jnp.float32
    )
    return grad_rows, sgd(cols, grad_cols)


def first_kernel(u_ref, c_ref, x_ref, coords, counts, u_out, *rest):
    c_outs, (dense, live) = rest[:CHUNKS], rest[CHUNKS:]
    tile = x_ref.shape[2]
    scatter(0, x_ref.at[0], coords, counts, dense, live)
    rows = u_ref[...]
    width = c_ref.shape[0] // CHUNKS
    total = None
    for h in range(CHUNKS):
        at = slice(h * width, (h + 1) * width)
        grad, c_outs[h][...] = chunk_step(tile, rows, c_ref[at], dense[:, at], live[:, at])
        total = grad if total is None else total + grad
    u_out[...] = sgd(rows, total)


def first(u, c, values, coords, counts):
    rows, rank = u.shape
    cols = c.shape[0]
    _, listed, tile, _ = values.shape
    out = pl.pallas_call(
        first_kernel,
        grid=(1,),
        out_shape=[jax.ShapeDtypeStruct(u.shape, u.dtype)]
        + [jax.ShapeDtypeStruct((cols // CHUNKS, rank), c.dtype)] * CHUNKS,
        in_specs=[VMEM, VMEM, pl.BlockSpec((1, listed, tile, tile), lambda i: (0, 0, 0, 0)), SMEM, SMEM],
        out_specs=[VMEM] * (1 + CHUNKS),
        scratch_shapes=[
            pltpu.VMEM((rows, cols), jnp.bfloat16),
            pltpu.VMEM((SUBLANES, cols), jnp.float32),
        ],
        compiler_params=params(),
        cost_estimate=cost(6 * rows * cols * rank, 4 * rows * rank * 4),
        name="first_stratum",
    )(u, c, values, coords, counts)
    return out[0], out[1:]


def layout_kernel(x_ref, coords, counts, _, *outs):
    later = len(outs) // 2
    for s in range(later):
        scatter(s + 1, x_ref.at[s + 1], coords, counts, outs[s], outs[later + s])


def layout(values, coords, counts, rows, cols, after):
    strata = values.shape[0]
    out = pl.pallas_call(
        layout_kernel,
        out_shape=[jax.ShapeDtypeStruct((rows, cols), jnp.bfloat16)] * (strata - 1)
        + [jax.ShapeDtypeStruct((SUBLANES, cols), jnp.float32)] * (strata - 1),
        in_specs=[VMEM, SMEM, SMEM, ANY],
        out_specs=[VMEM] * (2 * (strata - 1)),
        compiler_params=params(),
        cost_estimate=cost(0, 8 * rows * cols),
        name="lay_out_tiles",
    )(values, coords, counts, after)
    return list(zip(out[: strata - 1], out[strata - 1 :]))


def chunk_kernel(h, parity, tile, u_ref, c_ref, dense, live, *rest):
    last = h == CHUNKS - 1
    acc_ref = rest[0] if h else None
    u_out, c_out = rest[-2:]
    width = c_ref.shape[0]

    def body():
        at = slice(h * width, (h + 1) * width)
        rows = u_ref[...]
        grad, c_out[...] = chunk_step(tile, rows, c_ref[...], dense[:, at], live[:, at])
        if h:
            grad = grad + acc_ref[...]
        u_out[...] = sgd(rows, grad) if last else grad

    if parity is None:
        body()
        return
    mine = lax.axis_index("blk") % 2 == parity
    pl.when(mine)(body)
    if last:

        @pl.when(jnp.logical_not(mine))
        def _():
            u_out[...] = u_ref[...]


def chunk(h, parity, tile, u, c, laid, acc):
    dense, live = laid
    operands = [u, c, dense, live] + ([acc] if h else [])
    return pl.pallas_call(
        functools.partial(chunk_kernel, h, parity, tile),
        out_shape=[jax.ShapeDtypeStruct(u.shape, u.dtype), jax.ShapeDtypeStruct(c.shape, c.dtype)],
        in_specs=[VMEM] * len(operands),
        out_specs=[VMEM] * 2,
        compiler_params=params(),
        cost_estimate=cost(6 * u.size * c.shape[0], 4 * u.size * 4),
        name="chunk_step",
    )(*operands)


def stratum_chunks(parity, tile, u, cs, laid):
    acc, outs = None, []
    for h in range(CHUNKS):
        acc, c = chunk(h, parity, tile, u, cs[h], laid, acc)
        outs.append(c)
    return acc, outs


def send(chunks, axis, senders):
    n = lax.axis_size(axis)
    return [lax.ppermute(c, axis, [(i, (i + 1) % n) for i in senders]) for c in chunks]


def send_group(chunks, parity):
    blk, group = lax.axis_size("blk"), lax.axis_size("group")
    route = [
        (b * group + g, b * group + (g + 1) % group)
        for b in range(parity, blk, 2)
        for g in range(group)
    ]
    return [lax.ppermute(c, ("blk", "group"), route) for c in chunks]


def per_device(row_factors, col_factors, tile_values, tile_coords, tile_counts):
    u, c = row_factors, col_factors
    tile = tile_values.shape[2]
    blk = lax.axis_size("blk")
    even, odd = range(0, blk, 2), range(1, blk, 2)

    u, c0 = first(u, c, tile_values, tile_coords, tile_counts)
    to_even = send(c0, "blk", odd)
    to_odd = send(c0, "blk", even)
    laid = layout(tile_values, tile_coords, tile_counts, u.shape[0], c.shape[0], c0[-1])
    u, odd1 = stratum_chunks(1, tile, u, to_odd, laid[0])
    u, even1 = stratum_chunks(0, tile, u, to_even, laid[0])
    to_even = send(odd1, "blk", odd)
    to_odd = send(even1, "blk", even)
    u, odd2 = stratum_chunks(1, tile, u, to_odd, laid[1])
    u, even2 = stratum_chunks(0, tile, u, to_even, laid[1])
    odd3 = send_group(odd2, 1)
    even3 = send_group(even2, 0)
    u, odd3 = stratum_chunks(1, tile, u, odd3, laid[2])
    u, even3 = stratum_chunks(0, tile, u, even3, laid[2])
    to_even = send(odd3, "blk", odd)
    to_odd = send(even3, "blk", even)
    cs = [a + b for a, b in zip(to_even, to_odd)]
    u, cs = stratum_chunks(None, tile, u, cs, laid[3])
    return u, jnp.concatenate(cs, axis=0)


def solution(mesh):
    return jax.shard_map(
        per_device,
        mesh=mesh,
        in_specs=(
            P(("blk", "group"), None),
            P(("blk", "group"), None),
            P(None, ("blk", "group"), None, None),
            P(None, ("blk", "group"), None),
            P(None, ("blk", "group")),
        ),
        out_specs=(P(("blk", "group"), None), P(("blk", "group"), None)),
        check_vma=False,
    )
```

time: 69.9 us -> 59.2 us (0.85)
  starting transfers between devices: 3.39 us -> 29.7 us
  matrix products: 23.1 us -> 0 us
  waiting for transfers between devices: 30.5 us -> 12.7 us
  Pallas kernels: 0 us -> 9.34 us
  other arithmetic: 8.21 us -> 0.9 us
  local copies, waits for them, and re-layouts: 3.29 us -> 4.93 us
    ppermute x4 -> x16, starting transfers between devices: 3.39 us -> 29.7 us  [the longest x12 20.6 us: send(): lax.ppermute(c, axis, [(i, (i + 1) % n) for i in senders])]
    dot_general x35 -> x0, matrix products: 23.1 us -> none  [the longest x5 7.39 us: padded_rows(): jnp.einsum('tk,tia->kia', row_pick, terms, precision=lax.Precision.HIGHEST)]
    ppermute x4 -> x16, waiting for transfers between devices: 30.5 us -> 12.7 us  [the longest x12 10.6 us: send(): lax.ppermute(c, axis, [(i, (i + 1) % n) for i in senders])]
    pallas_call x0 -> x16, Pallas kernels: none -> 9.34 us  [the longest x14 6.01 us: chunk(): pl.pallas_call(functools.partial(chunk_kernel, h, parity, tile), out_shap...]
    convert_element_type x15 -> x0, other arithmetic: 5.97 us -> none  [the longest x5 3.13 us: per_device(): live_mask = (jnp.arange(values.shape[0]) < tile_count).astype(jnp.float32)]
    unnamed x6 -> x10, local copies, waits for them, and re-layouts: 0.02 us -> 4.93 us
    add x6 -> x2, other arithmetic: 2.24 us -> 0.07 us  [per_device(): cs = [a + b for a, b in zip(to_even, to_odd)]]
    slice x1 -> x0, local copies, waits for them, and re-layouts: 1.47 us -> none  [per_device(): tile_count = tile_counts[stratum, 0]]
  transfers between devices with their start and end apart: 4 -> 16, of which waited for: 4 -> 5; matrix products, arithmetic and copies ran while one was open for 14% -> 0% of each run, Pallas kernels for 0% -> 10%
where the time goes in v1:
time: 59.2 us; the launch traced here: 58.6 us
  starting transfers between devices  29.7 us (50%)
  waiting for transfers between devices  12.7 us (21%)
  Pallas kernels  9.34 us (16%)
  local copies, waits for them, and re-layouts  4.93 us (8%)
  between operations  0.98 us (2%)
  other arithmetic  0.9 us (2%)
    ppermute x12, starting transfers between devices, send(): lax.ppermute(c, axis, [(i, (i + 1) % n) for i in senders])  20.6 us
    ppermute x12, waiting for transfers between devices, send(): lax.ppermute(c, axis, [(i, (i + 1) % n) for i in senders])  10.6 us
    ppermute x4, starting transfers between devices, send_group(): return [lax.ppermute(c, ('blk', 'group'), route) for c in chunks]  9.13 us
    pallas_call x14, Pallas kernels, chunk(): pl.pallas_call(functools.partial(chunk_kernel, h, parity, tile), out_shap...  6.01 us
    unnamed x10, local copies, waits for them, and re-layouts  4.93 us
    ppermute x4, waiting for transfers between devices, send_group(): return [lax.ppermute(c, ('blk', 'group'), route) for c in chunks]  2.09 us
    pallas_call x1, Pallas kernels, first(): pl.pallas_call(first_kernel, grid=(1,), out_shape=[jax.ShapeDtypeStruct(u...  1.97 us
    pallas_call x1, Pallas kernels, layout(): pl.pallas_call(layout_kernel, out_shape=[jax.ShapeDtypeStruct((rows, cols...  1.36 us
  transfers between devices with their start and end apart: 16, of which 5 were waited for; matrix products, arithmetic and copies ran while one was open for 0% of the time, Pallas kernels for 10%

profile of v1, /device:TPU:0, one launch (start us, length us, event | category | flops | bytes accessed | tf_op | source)
XLA Modules:
  0.0 58.6 jit_solution(5859054546428943494)
XLA Ops:
  0.6 0.7 %copy.8.counts = s32[5,1]{1,0:T(8,128)S(1)} copy(s32[5,1]{0,1:T(1,128)} %param.9) | data formatting | bytes 40 | tf_op args[4]
  1.4 0.8 %copy.7.coords = s32[5,8,2]{2,1,0:T(8,128)S(1)} copy(s32[5,8,2]{1,2,0:T(2,128)} %param.8) | data formatting | bytes 640 | tf_op args[3]
  2.2 1.3 %copy-done = bf16[5,8,128,128]{3,2,1,0:T(8,128)(2,1)S(1)} copy-done((bf16[5,8,128,128]{3,2,1,0:T(8,128)(2,1)S(1)}, bf16[5,8,128,128]{3,2,1,0:T(8,128)(2,1)}, u32[]{:S(2)}) %copy-start) | copy-done | bytes 1310744
  3.5 1.0 %copy-done.2 = f32[512,256]{1,0:T(8,128)S(1)} copy-done((f32[512,256]{1,0:T(8,128)S(1)}, f32[512,256]{1,0:T(8,128)}, u32[]{:S(2)}) %copy-start.2) | copy-done | bytes 524312
  4.5 1.0 %copy-done.3 = f32[512,256]{1,0:T(8,128)S(1)} copy-done((f32[512,256]{1,0:T(8,128)S(1)}, f32[512,256]{1,0:T(8,128)}, u32[]{:S(2)}) %copy-start.3) | copy-done | bytes 524312
  5.6 2.0 %first_stratum.1 = (f32[512,256]{1,0:T(8,128)S(1)}, f32[256,256]{1,0:T(8,128)S(1)}, f32[256,256]{1,0:T(8,128)S(1)}) custom-call(f32[512,256]{1,0:T(8,128)S(1)} %copy-done.2, f32[512,256]{1,0:T(8,128)S(1)} %copy-done.3, bf16[5,8,128,128]{3,2,1,0:T(8,128)(2,1)S(1)} %copy-done, s32[5,8,2]{2,1,0:T(8,128)S(1)} %copy.7.coords, s32[5,1]{1,0:T(8,128)S(1)} %copy.8.counts), custom_call_target="tpu_custom_call" | custom-call | flops 402653184 | bytes 2097152 | tf_op jit(solution)/shard_map/first_stratum/pallas_call | solution.py:86
  7.5 2.4 %collective-permute-start.1 = (f32[256,256]{1,0:T(8,128)S(1)}, f32[256,256]{1,0:T(8,128)S(1)}, u32[]{:S(2)}, u32[]{:S(2)}) collective-permute-start(f32[256,256]{1,0:T(8,128)S(1)} %get-tuple-element.45), channel_id=1, source_target_pairs={{0,4},{8,12},{16,20},{24,28},{1,5},{9,13},{17,21},{25,29},{2,6},{1... | collective-permute-start | bytes 786440 | tf_op jit(solution)/shard_map/ppermute | solution.py:175
  9.9 1.3 %collective-permute-start = (f32[256,256]{1,0:T(8,128)S(1)}, f32[256,256]{1,0:T(8,128)S(1)}, u32[]{:S(2)}, u32[]{:S(2)}) collective-permute-start(f32[256,256]{1,0:T(8,128)S(1)} %get-tuple-element.42._), channel_id=1, source_target_pairs={{0,4},{8,12},{16,20},{24,28},{1,5},{9,13},{17,21},{25,29},{2,6},{1... | collective-permute-start | bytes 786440 | tf_op jit(solution)/shard_map/ppermute | solution.py:175
  11.3 1.3 %collective-permute-start.3 = (f32[256,256]{1,0:T(8,128)S(1)}, f32[256,256]{1,0:T(8,128)S(1)}, u32[]{:S(2)}, u32[]{:S(2)}) collective-permute-start(f32[256,256]{1,0:T(8,128)S(1)} %get-tuple-element.45), channel_id=1, source_target_pairs={{4,8},{12,16},{20,24},{28,0},{5,9},{13,17},{21,25},{29,1},{6,10},{... | collective-permute-start | bytes 786440 | tf_op jit(solution)/shard_map/ppermute | solution.py:175
  12.6 1.3 %collective-permute-start.2 = (f32[256,256]{1,0:T(8,128)S(1)}, f32[256,256]{1,0:T(8,128)S(1)}, u32[]{:S(2)}, u32[]{:S(2)}) collective-permute-start(f32[256,256]{1,0:T(8,128)S(1)} %get-tuple-element.42._), channel_id=1, source_target_pairs={{4,8},{12,16},{20,24},{28,0},{5,9},{13,17},{21,25},{29,1},{6,10},{... | collective-permute-start | bytes 786440 | tf_op jit(solution)/shard_map/ppermute | solution.py:175
  13.9 1.4 %lay_out_tiles.1 = (bf16[512,512]{1,0:T(8,128)(2,1)S(1)}, bf16[512,512]{1,0:T(8,128)(2,1)S(1)}, bf16[512,512]{1,0:T(8,128)(2,1)S(1)}, bf16[512,512]{1,0:T(8,128)...) custom-call(bf16[5,8,128,128]{3,2,1,0:T(8,128)(2,1)S(1)} %copy-done.1, ...), custom_call_target="tpu_custom_call" | custom-call | bytes 2097152 | tf_op jit(solution)/shard_map/lay_out_tiles/pallas_call | solution.py:112
  15.2 0.0 collective-permute-done.1.c_ref
  15.3 0.0 collective-permute-done.c_ref
  15.3 0.1 chunk_step.15
  15.3 4.5 %collective-permute-done.3.c_ref = f32[256,256]{1,0:T(8,128)S(1)} collective-permute-done((f32[256,256]{1,0:T(8,128)S(1)}, f32[256,256]{1,0:T(8,128)S(1)}, u32[]{:S(2)}, u32[]{:S(2)}) %collective-permute-start.3) | collective-permute-done | bytes 262176 | tf_op jit(solution)/shard_map/ppermute | solution.py:175
  19.8 0.6 chunk_step.16
  20.4 1.3 %collective-permute-start.5 = (f32[256,256]{1,0:T(8,128)S(1)}, f32[256,256]{1,0:T(8,128)S(1)}, u32[]{:S(2)}, u32[]{:S(2)}) collective-permute-start(f32[256,256]{1,0:T(8,128)S(1)} %get-tuple-element.53), channel_id=1, source_target_pairs={{0,4},{8,12},{16,20},{24,28},{1,5},{9,13},{17,21},{25,29},{2,6},{1... | collective-permute-start | bytes 786440 | tf_op jit(solution)/shard_map/ppermute | solution.py:175
  21.7 0.9 %collective-permute-done.2.c_ref = f32[256,256]{1,0:T(8,128)S(1)} collective-permute-done((f32[256,256]{1,0:T(8,128)S(1)}, f32[256,256]{1,0:T(8,128)S(1)}, u32[]{:S(2)}, u32[]{:S(2)}) %collective-permute-start.2) | collective-permute-done | bytes 262176 | tf_op jit(solution)/shard_map/ppermute | solution.py:175
  22.7 0.7 %chunk_step.17 = (f32[512,256]{1,0:T(8,128)S(1)}, f32[256,256]{1,0:T(8,128)S(1)}) custom-call(f32[512,256]{1,0:T(8,128)S(1)} %get-tuple-element.47.u_ref, f32[256,256]{1,0:T(8,128)S(1)} %collective-permute-done.2.c_ref, bf16[512,512]{1,0:T(8,128)(2,1)S(1)} %get-tuple-element.43.dense, f32[8,512]{1,0:T(8,128)S(1)} %get-tuple-element.44.live, ...), custom_call_target="tpu_custom_call" | custom-call | flops 201326592 | bytes 2097152 | tf_op jit(solution)/shard_map/chunk_step/pallas_call | solution.py:154
  23.3 1.3 %collective-permute-start.4 = (f32[256,256]{1,0:T(8,128)S(1)}, f32[256,256]{1,0:T(8,128)S(1)}, u32[]{:S(2)}, u32[]{:S(2)}) collective-permute-start(f32[256,256]{1,0:T(8,128)S(1)} %get-tuple-element.50), channel_id=1, source_target_pairs={{0,4},{8,12},{16,20},{24,28},{1,5},{9,13},{17,21},{25,29},{2,6},{1... | collective-permute-start | bytes 786440 | tf_op jit(solution)/shard_map/ppermute | solution.py:175
  24.6 1.3 %collective-permute-start.7 = (f32[256,256]{1,0:T(8,128)S(1)}, f32[256,256]{1,0:T(8,128)S(1)}, u32[]{:S(2)}, u32[]{:S(2)}) collective-permute-start(f32[256,256]{1,0:T(8,128)S(1)} %get-tuple-element.57), channel_id=1, source_target_pairs={{4,8},{12,16},{20,24},{28,0},{5,9},{13,17},{21,25},{29,1},{6,10},{... | collective-permute-start | bytes 786440 | tf_op jit(solution)/shard_map/ppermute | solution.py:175
  25.9 1.3 %collective-permute-start.6 = (f32[256,256]{1,0:T(8,128)S(1)}, f32[256,256]{1,0:T(8,128)S(1)}, u32[]{:S(2)}, u32[]{:S(2)}) collective-permute-start(f32[256,256]{1,0:T(8,128)S(1)} %get-tuple-element.56), channel_id=1, source_target_pairs={{4,8},{12,16},{20,24},{28,0},{5,9},{13,17},{21,25},{29,1},{6,10},{... | collective-permute-start | bytes 786440 | tf_op jit(solution)/shard_map/ppermute | solution.py:175
  27.2 0.0 collective-permute-done.5.c_ref
  27.3 0.7 %collective-permute-start.9 = (f32[256,256]{1,0:T(8,128)S(1)}, f32[256,256]{1,0:T(8,128)S(1)}, u32[]{:S(2)}, u32[]{:S(2)}) collective-permute-start(f32[256,256]{1,0:T(8,128)S(1)} %get-tuple-element.63), channel_id=1, source_target_pairs={{4,5},{5,6},{6,7},{7,4},{12,13},{13,14},{14,15},{15,12},{20,21},{2... | collective-permute-start | bytes 786440 | tf_op jit(solution)/shard_map/ppermute | solution.py:185
  28.0 0.0 collective-permute-done.4.c_ref
  28.0 0.1 chunk_step.19
  28.0 0.7 %collective-permute-start.8 = (f32[256,256]{1,0:T(8,128)S(1)}, f32[256,256]{1,0:T(8,128)S(1)}, u32[]{:S(2)}, u32[]{:S(2)}) collective-permute-start(f32[256,256]{1,0:T(8,128)S(1)} %get-tuple-element.60), channel_id=1, source_target_pairs={{4,5},{5,6},{6,7},{7,4},{12,13},{13,14},{14,15},{15,12},{20,21},{2... | collective-permute-start | bytes 786440 | tf_op jit(solution)/shard_map/ppermute | solution.py:185
  28.7 4.5 %collective-permute-done.7.c_ref = f32[256,256]{1,0:T(8,128)S(1)} collective-permute-done((f32[256,256]{1,0:T(8,128)S(1)}, f32[256,256]{1,0:T(8,128)S(1)}, u32[]{:S(2)}, u32[]{:S(2)}) %collective-permute-start.7) | collective-permute-done | bytes 262176 | tf_op jit(solution)/shard_map/ppermute | solution.py:175
  33.2 0.6 chunk_step.20
  33.8 4.3 %collective-permute-start.11 = (f32[256,256]{1,0:T(8,128)S(1)}, f32[256,256]{1,0:T(8,128)S(1)}, u32[]{:S(2)}, u32[]{:S(2)}) collective-permute-start(f32[256,256]{1,0:T(8,128)S(1)} %get-tuple-element.67), channel_id=1, source_target_pairs={{0,1},{1,2},{2,3},{3,0},{8,9},{9,10},{10,11},{11,8},{16,17},{17,18... | collective-permute-start | bytes 786440 | tf_op jit(solution)/shard_map/ppermute | solution.py:185
  38.1 0.7 %chunk_step.21 = (f32[512,256]{1,0:T(8,128)S(1)}, f32[256,256]{1,0:T(8,128)S(1)}) custom-call(f32[512,256]{1,0:T(8,128)S(1)} %get-tuple-element.55.u_ref, f32[256,256]{1,0:T(8,128)S(1)} %collective-permute-done.6.c_ref, bf16[512,512]{1,0:T(8,128)(2,1)S(1)} %get-tuple-element.51.dense, f32[8,512]{1,0:T(8,128)S(1)} %get-tuple-element.52.live, ...), custom_call_target="tpu_custom_call" | custom-call | flops 201326592 | bytes 2097152 | tf_op jit(solution)/shard_map/chunk_step/pallas_call | solution.py:154
  38.8 3.5 %collective-permute-start.10 = (f32[256,256]{1,0:T(8,128)S(1)}, f32[256,256]{1,0:T(8,128)S(1)}, u32[]{:S(2)}, u32[]{:S(2)}) collective-permute-start(f32[256,256]{1,0:T(8,128)S(1)} %get-tuple-element.66), channel_id=1, source_target_pairs={{0,1},{1,2},{2,3},{3,0},{8,9},{9,10},{10,11},{11,8},{16,17},{17,18... | collective-permute-start | bytes 786440 | tf_op jit(solution)/shard_map/ppermute | solution.py:185
  42.4 1.3 %collective-permute-start.14 = (f32[256,256]{1,0:T(8,128)S(1)}, f32[256,256]{1,0:T(8,128)S(1)}, u32[]{:S(2)}, u32[]{:S(2)}) collective-permute-start(f32[256,256]{1,0:T(8,128)S(1)} %get-tuple-element.74), channel_id=1, source_target_pairs={{4,8},{12,16},{20,24},{28,0},{5,9},{13,17},{21,25},{29,1},{6,10},{... | collective-permute-start | bytes 786440 | tf_op jit(solution)/shard_map/ppermute | solution.py:175
  43.6 0.0 collective-permute-done.8.c_ref
  43.7 0.1 chunk_step.23
  43.7 2.1 %collective-permute-done.11.c_ref = f32[256,256]{1,0:T(8,128)S(1)} collective-permute-done((f32[256,256]{1,0:T(8,128)S(1)}, f32[256,256]{1,0:T(8,128)S(1)}, u32[]{:S(2)}, u32[]{:S(2)}) %collective-permute-start.11) | collective-permute-done | bytes 262176 | tf_op jit(solution)/shard_map/ppermute | solution.py:185
  45.8 0.6 chunk_step.24
  46.4 1.3 %collective-permute-start.15 = (f32[256,256]{1,0:T(8,128)S(1)}, f32[256,256]{1,0:T(8,128)S(1)}, u32[]{:S(2)}, u32[]{:S(2)}) collective-permute-start(f32[256,256]{1,0:T(8,128)S(1)} %get-tuple-element.75), channel_id=1, source_target_pairs={{0,4},{8,12},{16,20},{24,28},{1,5},{9,13},{17,21},{25,29},{2,6},{1... | collective-permute-start | bytes 786440 | tf_op jit(solution)/shard_map/ppermute | solution.py:175
  47.7 1.3 %collective-permute-start.12 = (f32[256,256]{1,0:T(8,128)S(1)}, f32[256,256]{1,0:T(8,128)S(1)}, u32[]{:S(2)}, u32[]{:S(2)}) collective-permute-start(f32[256,256]{1,0:T(8,128)S(1)} %get-tuple-element.70), channel_id=1, source_target_pairs={{4,8},{12,16},{20,24},{28,0},{5,9},{13,17},{21,25},{29,1},{6,10},{... | collective-permute-start | bytes 786440 | tf_op jit(solution)/shard_map/ppermute | solution.py:175
  49.0 0.0 collective-permute-done.10.c_ref
  49.0 0.7 %chunk_step.25 = (f32[512,256]{1,0:T(8,128)S(1)}, f32[256,256]{1,0:T(8,128)S(1)}) custom-call(f32[512,256]{1,0:T(8,128)S(1)} %get-tuple-element.65.u_ref, f32[256,256]{1,0:T(8,128)S(1)} %collective-permute-done.10.c_ref, bf16[512,512]{1,0:T(8,128)(2,1)S(1)} %get-tuple-element.61.dense, f32[8,512]{1,0:T(8,128)S(1)} %get-tuple-element.62.live, ...), custom_call_target="tpu_custom_call" | custom-call | flops 201326592 | bytes 2097152 | tf_op jit(solution)/shard_map/chunk_step/pallas_call | solution.py:154
  49.7 5.2 %collective-permute-start.13 = (f32[256,256]{1,0:T(8,128)S(1)}, f32[256,256]{1,0:T(8,128)S(1)}, u32[]{:S(2)}, u32[]{:S(2)}) collective-permute-start(f32[256,256]{1,0:T(8,128)S(1)} %get-tuple-element.71), channel_id=1, source_target_pairs={{0,4},{8,12},{16,20},{24,28},{1,5},{9,13},{17,21},{25,29},{2,6},{1... | collective-permute-start | bytes 786440 | tf_op jit(solution)/shard_map/ppermute | solution.py:175
  54.9 0.0 collective-permute-done.15
  55.0 0.6 chunk_step.26
  55.6 0.7 %collective-permute-done.12 = f32[256,256]{1,0:T(8,128)S(1)} collective-permute-done((f32[256,256]{1,0:T(8,128)S(1)}, f32[256,256]{1,0:T(8,128)S(1)}, u32[]{:S(2)}, u32[]{:S(2)}) %collective-permute-start.12) | collective-permute-done | bytes 262176 | tf_op jit(solution)/shard_map/ppermute | solution.py:175
  56.3 0.0 collective-permute-done.13
  56.3 1.4 %chunk_step.27 = (f32[512,256]{1,0:T(8,128)}, f32[256,256]{1,0:T(8,128)S(1)}) custom-call(f32[512,256]{1,0:T(8,128)S(1)} %get-tuple-element.69.u_ref, f32[256,256]{1,0:T(8,128)S(1)} %add.6.c_ref, bf16[512,512]{1,0:T(8,128)(2,1)S(1)} %get-tuple-element.72.dense, f32[8,512]{1,0:T(8,128)S(1)} %get-tuple-element.73.live, f32[512,256]{1,0:T(8,128)S(1)} %get-tuple-element.76.rest_0_), custom_call_target="tpu_custom_call" | custom-call | flops 201326592 | bytes 2097152 | tf_op jit(solution)/shard_map/chunk_step/pallas_call | solution.py:154
  57.8 0.8 %pad_maximum_fusion = f32[512,256]{1,0:T(8,128)} fusion(f32[256,256]{1,0:T(8,128)S(1)} %get-tuple-element.79, f32[256,256]{1,0:T(8,128)S(1)} %get-tuple-element.78), kind=kLoop, calls=%fused_computation | loop fusion | flops 131072 | bytes 1048576 | tf_op jit(solution)/shard_map/concatenate | solution.py:212
  (13 shorter events, 0.1 us)
Async XLA Ops:
  2.2 1.3 %copy-start = (bf16[5,8,128,128]{3,2,1,0:T(8,128)(2,1)S(1)}, bf16[5,8,128,128]{3,2,1,0:T(8,128)(2,1)}, u32[]{:S(2)}) copy-start(bf16[5,8,128,128]{3,2,1,0:T(8,128)(2,1)} %x_ref.3) | copy-start | bytes 3932164
  3.5 1.0 %copy-start.2 = (f32[512,256]{1,0:T(8,128)S(1)}, f32[512,256]{1,0:T(8,128)}, u32[]{:S(2)}) copy-start(f32[512,256]{1,0:T(8,128)} %u_ref.1) | copy-start | bytes 1572868
  4.5 1.0 %copy-start.3 = (f32[512,256]{1,0:T(8,128)S(1)}, f32[512,256]{1,0:T(8,128)}, u32[]{:S(2)}) copy-start(f32[512,256]{1,0:T(8,128)} %c_ref.1) | copy-start | bytes 1572868
  5.6 8.3 %copy-start.1 = (bf16[5,8,128,128]{3,2,1,0:T(8,128)(2,1)S(1)}, bf16[5,8,128,128]{3,2,1,0:T(8,128)(2,1)}, u32[]{:S(2)}) copy-start(bf16[5,8,128,128]{3,2,1,0:T(8,128)(2,1)} %x_ref.3) | copy-start | bytes 3932164
  7.5 7.7 %collective-permute-start.1 = (f32[256,256]{1,0:T(8,128)S(1)}, f32[256,256]{1,0:T(8,128)S(1)}, u32[]{:S(2)}, u32[]{:S(2)}) collective-permute-start(f32[256,256]{1,0:T(8,128)S(1)} %get-tuple-element.45), channel_id=1, source_target_pairs={{0,4},{8,12},{16,20},{24,28},{1,5},{9,13},{17,21},{25,29},{2,6},{1... | collective-permute-start | bytes 786440 | tf_op jit(solution)/shard_map/ppermute | solution.py:175
  9.9 5.3 %collective-permute-start = (f32[256,256]{1,0:T(8,128)S(1)}, f32[256,256]{1,0:T(8,128)S(1)}, u32[]{:S(2)}, u32[]{:S(2)}) collective-permute-start(f32[256,256]{1,0:T(8,128)S(1)} %get-tuple-element.42._), channel_id=1, source_target_pairs={{0,4},{8,12},{16,20},{24,28},{1,5},{9,13},{17,21},{25,29},{2,6},{1... | collective-permute-start | bytes 786440 | tf_op jit(solution)/shard_map/ppermute | solution.py:175
  11.3 8.6 %collective-permute-start.3 = (f32[256,256]{1,0:T(8,128)S(1)}, f32[256,256]{1,0:T(8,128)S(1)}, u32[]{:S(2)}, u32[]{:S(2)}) collective-permute-start(f32[256,256]{1,0:T(8,128)S(1)} %get-tuple-element.45), channel_id=1, source_target_pairs={{4,8},{12,16},{20,24},{28,0},{5,9},{13,17},{21,25},{29,1},{6,10},{... | collective-permute-start | bytes 786440 | tf_op jit(solution)/shard_map/ppermute | solution.py:175
  12.6 10.1 %collective-permute-start.2 = (f32[256,256]{1,0:T(8,128)S(1)}, f32[256,256]{1,0:T(8,128)S(1)}, u32[]{:S(2)}, u32[]{:S(2)}) collective-permute-start(f32[256,256]{1,0:T(8,128)S(1)} %get-tuple-element.42._), channel_id=1, source_target_pairs={{4,8},{12,16},{20,24},{28,0},{5,9},{13,17},{21,25},{29,1},{6,10},{... | collective-permute-start | bytes 786440 | tf_op jit(solution)/shard_map/ppermute | solution.py:175
  20.4 6.8 %collective-permute-start.5 = (f32[256,256]{1,0:T(8,128)S(1)}, f32[256,256]{1,0:T(8,128)S(1)}, u32[]{:S(2)}, u32[]{:S(2)}) collective-permute-start(f32[256,256]{1,0:T(8,128)S(1)} %get-tuple-element.53), channel_id=1, source_target_pairs={{0,4},{8,12},{16,20},{24,28},{1,5},{9,13},{17,21},{25,29},{2,6},{1... | collective-permute-start | bytes 786440 | tf_op jit(solution)/shard_map/ppermute | solution.py:175
  23.3 4.6 %collective-permute-start.4 = (f32[256,256]{1,0:T(8,128)S(1)}, f32[256,256]{1,0:T(8,128)S(1)}, u32[]{:S(2)}, u32[]{:S(2)}) collective-permute-start(f32[256,256]{1,0:T(8,128)S(1)} %get-tuple-element.50), channel_id=1, source_target_pairs={{0,4},{8,12},{16,20},{24,28},{1,5},{9,13},{17,21},{25,29},{2,6},{1... | collective-permute-start | bytes 786440 | tf_op jit(solution)/shard_map/ppermute | solution.py:175
  24.6 8.6 %collective-permute-start.7 = (f32[256,256]{1,0:T(8,128)S(1)}, f32[256,256]{1,0:T(8,128)S(1)}, u32[]{:S(2)}, u32[]{:S(2)}) collective-permute-start(f32[256,256]{1,0:T(8,128)S(1)} %get-tuple-element.57), channel_id=1, source_target_pairs={{4,8},{12,16},{20,24},{28,0},{5,9},{13,17},{21,25},{29,1},{6,10},{... | collective-permute-start | bytes 786440 | tf_op jit(solution)/shard_map/ppermute | solution.py:175
  25.9 12.2 %collective-permute-start.6 = (f32[256,256]{1,0:T(8,128)S(1)}, f32[256,256]{1,0:T(8,128)S(1)}, u32[]{:S(2)}, u32[]{:S(2)}) collective-permute-start(f32[256,256]{1,0:T(8,128)S(1)} %get-tuple-element.56), channel_id=1, source_target_pairs={{4,8},{12,16},{20,24},{28,0},{5,9},{13,17},{21,25},{29,1},{6,10},{... | collective-permute-start | bytes 786440 | tf_op jit(solution)/shard_map/ppermute | solution.py:175
  27.3 15.0 %collective-permute-start.9 = (f32[256,256]{1,0:T(8,128)S(1)}, f32[256,256]{1,0:T(8,128)S(1)}, u32[]{:S(2)}, u32[]{:S(2)}) collective-permute-start(f32[256,256]{1,0:T(8,128)S(1)} %get-tuple-element.63), channel_id=1, source_target_pairs={{4,5},{5,6},{6,7},{7,4},{12,13},{13,14},{14,15},{15,12},{20,21},{2... | collective-permute-start | bytes 786440 | tf_op jit(solution)/shard_map/ppermute | solution.py:185
  28.0 15.6 %collective-permute-start.8 = (f32[256,256]{1,0:T(8,128)S(1)}, f32[256,256]{1,0:T(8,128)S(1)}, u32[]{:S(2)}, u32[]{:S(2)}) collective-permute-start(f32[256,256]{1,0:T(8,128)S(1)} %get-tuple-element.60), channel_id=1, source_target_pairs={{4,5},{5,6},{6,7},{7,4},{12,13},{13,14},{14,15},{15,12},{20,21},{2... | collective-permute-start | bytes 786440 | tf_op jit(solution)/shard_map/ppermute | solution.py:185
  33.8 12.0 %collective-permute-start.11 = (f32[256,256]{1,0:T(8,128)S(1)}, f32[256,256]{1,0:T(8,128)S(1)}, u32[]{:S(2)}, u32[]{:S(2)}) collective-permute-start(f32[256,256]{1,0:T(8,128)S(1)} %get-tuple-element.67), channel_id=1, source_target_pairs={{0,1},{1,2},{2,3},{3,0},{8,9},{9,10},{10,11},{11,8},{16,17},{17,18... | collective-permute-start | bytes 786440 | tf_op jit(solution)/shard_map/ppermute | solution.py:185
  38.8 10.2 %collective-permute-start.10 = (f32[256,256]{1,0:T(8,128)S(1)}, f32[256,256]{1,0:T(8,128)S(1)}, u32[]{:S(2)}, u32[]{:S(2)}) collective-permute-start(f32[256,256]{1,0:T(8,128)S(1)} %get-tuple-element.66), channel_id=1, source_target_pairs={{0,1},{1,2},{2,3},{3,0},{8,9},{9,10},{10,11},{11,8},{16,17},{17,18... | collective-permute-start | bytes 786440 | tf_op jit(solution)/shard_map/ppermute | solution.py:185
  42.4 12.6 %collective-permute-start.14 = (f32[256,256]{1,0:T(8,128)S(1)}, f32[256,256]{1,0:T(8,128)S(1)}, u32[]{:S(2)}, u32[]{:S(2)}) collective-permute-start(f32[256,256]{1,0:T(8,128)S(1)} %get-tuple-element.74), channel_id=1, source_target_pairs={{4,8},{12,16},{20,24},{28,0},{5,9},{13,17},{21,25},{29,1},{6,10},{... | collective-permute-start | bytes 786440 | tf_op jit(solution)/shard_map/ppermute | solution.py:175
  46.4 8.6 %collective-permute-start.15 = (f32[256,256]{1,0:T(8,128)S(1)}, f32[256,256]{1,0:T(8,128)S(1)}, u32[]{:S(2)}, u32[]{:S(2)}) collective-permute-start(f32[256,256]{1,0:T(8,128)S(1)} %get-tuple-element.75), channel_id=1, source_target_pairs={{0,4},{8,12},{16,20},{24,28},{1,5},{9,13},{17,21},{25,29},{2,6},{1... | collective-permute-start | bytes 786440 | tf_op jit(solution)/shard_map/ppermute | solution.py:175
  47.7 8.6 %collective-permute-start.12 = (f32[256,256]{1,0:T(8,128)S(1)}, f32[256,256]{1,0:T(8,128)S(1)}, u32[]{:S(2)}, u32[]{:S(2)}) collective-permute-start(f32[256,256]{1,0:T(8,128)S(1)} %get-tuple-element.70), channel_id=1, source_target_pairs={{4,8},{12,16},{20,24},{28,0},{5,9},{13,17},{21,25},{29,1},{6,10},{... | collective-permute-start | bytes 786440 | tf_op jit(solution)/shard_map/ppermute | solution.py:175
  49.7 6.6 %collective-permute-start.13 = (f32[256,256]{1,0:T(8,128)S(1)}, f32[256,256]{1,0:T(8,128)S(1)}, u32[]{:S(2)}, u32[]{:S(2)}) collective-permute-start(f32[256,256]{1,0:T(8,128)S(1)} %get-tuple-element.71), channel_id=1, source_target_pairs={{0,4},{8,12},{16,20},{24,28},{1,5},{9,13},{17,21},{25,29},{2,6},{1... | collective-permute-start | bytes 786440 | tf_op jit(solution)/shard_map/ppermute | solution.py:175

commit v2 on v0

v2 whole, which is shorter than its diff:
```python
import functools

import jax
import jax.numpy as jnp
from jax import lax
from jax.experimental import pallas as pl
from jax.experimental.pallas import tpu as pltpu
from jax.sharding import PartitionSpec as P

LEARN_RATE = 0.03
DECAY_RATE = 0.1
CHUNKS = 4
SUBLANES = 8

VMEM = pl.BlockSpec(memory_space=pltpu.VMEM)
SMEM = pl.BlockSpec(memory_space=pltpu.SMEM)
HBM = pl.BlockSpec(memory_space=pltpu.HBM)
ANY = pl.BlockSpec(memory_space=pl.ANY)


def call(body, name, operands, in_specs, outs, out_specs, flops=0, moved=0, aliases=None, scratch=(), vmem=24):
    return pl.pallas_call(
        body,
        out_shape=outs,
        in_specs=in_specs,
        out_specs=out_specs,
        input_output_aliases=aliases or {},
        scratch_shapes=list(scratch),
        compiler_params=pltpu.CompilerParams(vmem_limit_bytes=vmem * 1024 * 1024),
        cost_estimate=pl.CostEstimate(flops=flops, bytes_accessed=moved, transcendentals=0),
        name=name,
    )(*operands)


def like(array, shape=None, dtype=None):
    return jax.ShapeDtypeStruct(shape or array.shape, dtype or array.dtype)


def scatter(stratum, values, coords, counts, dense, live):
    listed, tile, _ = values.shape
    dense[...] = jnp.zeros_like(dense)
    live[...] = jnp.zeros_like(live)
    for t in range(listed):

        @pl.when(t < counts[0, stratum])
        def _():
            r = coords[stratum, 0, t]
            c = pl.multiple_of(coords[stratum, 1, t] * tile, tile)
            dense[pl.ds(pl.multiple_of(r * tile, tile), tile), pl.ds(c, tile)] = values[t]
            named = lax.broadcasted_iota(jnp.int32, (SUBLANES, tile), 0) == r
            live[:, pl.ds(c, tile)] = jnp.where(named, 1.0, live[:, pl.ds(c, tile)])


def sgd(old, grad):
    return old + LEARN_RATE * (grad - DECAY_RATE * old)


def chunk_step(tile, rows, cols, dense, live):
    row_half = rows.astype(jnp.bfloat16)
    col_half = cols.astype(jnp.bfloat16)
    estimate = lax.dot_general(
        row_half, col_half, (((1,), (1,)), ((), ())), preferred_element_type=jnp.float32
    )
    parts = []
    for r in range(rows.shape[0] // tile):
        at = slice(r * tile, (r + 1) * tile)
        residue = dense[at].astype(jnp.float32) - estimate[at]
        parts.append(jnp.where(live[r : r + 1] > 0, residue, 0.0).astype(jnp.bfloat16))
    residue = jnp.concatenate(parts, axis=0)
    grad_cols = lax.dot_general(
        residue, row_half, (((0,), (0,)), ((), ())), preferred_element_type=jnp.float32
    )
    grad_rows = jnp.dot(residue, col_half, preferred_element_type=jnp.float32)
    return grad_rows, sgd(cols, grad_cols)


def span(h, width):
    return slice(h * width, (h + 1) * width)


def first_kernel(u_hbm, c_hbm, x_hbm, coords_hbm, counts_hbm, *refs):
    u_ref, acc, dense, live, c_out = refs[:5]
    c_rest = refs[5 : 4 + CHUNKS]
    x_ref, c_ref, coords, counts, sems = refs[4 + CHUNKS :]
    width, tile = c_ref.shape[0], x_ref.shape[1]
    pairs = [(coords_hbm, coords), (counts_hbm, counts), (x_hbm.at[0], x_ref), (u_hbm, u_ref)]
    pairs += [(c_hbm.at[pl.ds(0, width)], c_ref)]
    pairs += [(c_hbm.at[pl.ds((i + 1) * width, width)], c) for i, c in enumerate(c_rest)]
    copies = [pltpu.make_async_copy(s, d, sems.at[i]) for i, (s, d) in enumerate(pairs)]
    for copy in copies:
        copy.start()
    for copy in copies[:3]:
        copy.wait()
    scatter(0, x_ref, coords, counts, dense, live)
    for copy in copies[3:5]:
        copy.wait()
    at = span(0, width)
    acc[...], c_out[...] = chunk_step(tile, u_ref[...], c_ref[...], dense[:, at], live[:, at])
    for copy in copies[5:]:
        copy.wait()


def first(u, c, values, coords, counts):
    rows, cols = u.shape[0], c.shape[0]
    part = (cols // CHUNKS, c.shape[1])
    outs = [like(u), like(u), like(u, (rows, cols), jnp.bfloat16), like(u, (SUBLANES, cols))]
    outs += [like(c, part)] * CHUNKS
    operands = [pltpu.with_memory_space_constraint(x, pltpu.HBM) for x in (u, c, values, coords, counts)]
    u, acc, dense, live, done, *rest = call(
        first_kernel,
        "first_chunk",
        operands,
        [HBM] * 5,
        outs,
        [VMEM] * len(outs),
        flops=6 * u.size * part[0],
        moved=8 * u.size,
        scratch=[
            pltpu.VMEM(values.shape[1:], values.dtype),
            pltpu.VMEM(part, c.dtype),
            pltpu.SMEM(coords.shape, coords.dtype),
            pltpu.SMEM(counts.shape, counts.dtype),
            pltpu.SemaphoreType.DMA((4 + CHUNKS,)),
        ],
    )
    return u, acc, (dense, live), done, rest


def layout_kernel(x_ref, coords, counts, _, *outs):
    later = len(outs) // 2
    for s in range(later):
        scatter(s + 1, x_ref.at[s + 1], coords, counts, outs[s], outs[later + s])


def layout(values, coords, counts, rows, cols, after):
    later = values.shape[0] - 1
    outs = [like(values, (rows, cols))] * later
    outs += [like(values, (SUBLANES, cols), jnp.float32)] * later
    out = call(
        layout_kernel,
        "lay_out_tiles",
        (values, coords, counts, after),
        [VMEM, SMEM, SMEM, ANY],
        outs,
        [VMEM] * len(outs),
        moved=8 * rows * cols,
    )
    return list(zip(out[:later], out[later:]))


def chunk_kernel(h, tile, u_ref, c_ref, dense, live, *rest):
    u_out, c_out = rest[-2:]
    last = h == CHUNKS - 1
    at = span(h, c_ref.shape[0])
    rows = u_out[...] if last else u_ref[...]
    grad, c_out[...] = chunk_step(tile, rows, c_ref[...], dense[:, at], live[:, at])
    if h:
        grad = grad + rest[0][...]
    u_out[...] = sgd(rows, grad) if last else grad


def chunk(h, tile, u, c, laid, acc):
    operands = [u, c, *laid] + ([acc] if h else [])
    return call(
        functools.partial(chunk_kernel, h, tile),
        "chunk_step",
        operands,
        [VMEM] * len(operands),
        [like(u), like(c)],
        [VMEM] * 2,
        flops=6 * u.size * c.shape[0],
        moved=16 * u.size,
        aliases={0: 0} if h == CHUNKS - 1 else None,
    )


def final_kernel(h, tile, u_ref, c_in, dense, live, *rest):
    width = c_in.shape[0]
    at, place = span(h, width), pl.ds(h * width, width)
    last = h == CHUNKS - 1
    acc_in, rest = (rest[0], rest[2:]) if h else (None, rest)
    first_out, c_hbm, *scratch = rest
    c_new, sems = scratch[-2:]
    rows = u_ref[...]
    grad, c_new[...] = chunk_step(tile, rows, c_in[...], dense[:, at], live[:, at])
    copies = [pltpu.make_async_copy(c_new, c_hbm.at[place], sems.at[0])]
    copies[0].start()
    for r in range(rows.shape[0] // tile):
        part = span(r, tile)
        total = grad[part] if acc_in is None else grad[part] + acc_in[part]
        if last:
            u_new = scratch[0]
            u_new[part] = sgd(rows[part], total)
            rows_at = pl.ds(r * tile, tile)
            copies.append(pltpu.make_async_copy(u_new.at[rows_at], first_out.at[rows_at], sems.at[r + 1]))
            copies[-1].start()
        else:
            first_out[part] = total
    for copy in copies:
        copy.wait()


def final(tile, u, cs, laid):
    part = cs[0]
    whole = like(part, (part.shape[0] * CHUNKS, part.shape[1]))
    carried = []
    for h in range(CHUNKS):
        last = h == CHUNKS - 1
        operands = (u, cs[h], *laid, *carried)
        carried = call(
            functools.partial(final_kernel, h, tile),
            "final_chunk",
            operands,
            [VMEM] * 4 + ([VMEM, HBM] if h else []),
            [like(u), whole],
            [HBM if last else VMEM, HBM],
            flops=6 * u.size * part.shape[0],
            moved=16 * u.size,
            aliases={5: 1} if h else None,
            scratch=([pltpu.VMEM(u.shape, u.dtype)] if last else [])
            + [
                pltpu.VMEM(part.shape, part.dtype),
                pltpu.SemaphoreType.DMA((1 + u.shape[0] // tile,)),
            ],
        )
    return carried


def shifted(chunk, axis):
    n = lax.axis_size(axis)
    return lax.ppermute(chunk, axis, [(i, (i + 1) % n) for i in range(n)])


def per_device(row_factors, col_factors, tile_values, tile_coords, tile_counts):
    tile = tile_values.shape[2]
    strata = tile_values.shape[0]
    coords, counts = tile_coords.transpose(0, 2, 1), tile_counts.transpose(1, 0)
    u, acc, laid0, done, rest = first(row_factors, col_factors, tile_values, coords, counts)
    cs = [shifted(done, "blk")]
    for h in range(1, CHUNKS):
        acc, done = chunk(h, tile, u, rest[h - 1], laid0, acc)
        cs.append(shifted(done, "blk"))
    u = acc
    laid = layout(tile_values, coords, counts, u.shape[0], col_factors.shape[0], done)
    for stratum in range(1, strata - 1):
        axis = "group" if stratum == 2 else "blk"
        acc, arrived, cs = None, cs, []
        for h in range(CHUNKS):
            acc, done = chunk(h, tile, u, arrived[h], laid[stratum - 1], acc)
            cs.append(shifted(done, axis))
        u = acc
    return final(tile, u, cs, laid[-1])


def solution(mesh):
    return jax.shard_map(
        per_device,
        mesh=mesh,
        in_specs=(
            P(("blk", "group"), None),
            P(("blk", "group"), None),
            P(None, ("blk", "group"), None, None),
            P(None, ("blk", "group"), None),
            P(None, ("blk", "group")),
        ),
        out_specs=(P(("blk", "group"), None), P(("blk", "group"), None)),
        check_vma=False,
    )
```

time: 69.9 us -> 39.9 us (0.57)
  matrix products: 23.1 us -> 0 us
  waiting for transfers between devices: 30.5 us -> 8.41 us
  Pallas kernels: 0 us -> 17.2 us
  starting transfers between devices: 3.39 us -> 13.2 us
  other arithmetic: 8.21 us -> 0 us
  local copies, waits for them, and re-layouts: 3.29 us -> 0.01 us
    dot_general x35 -> x0, matrix products: 23.1 us -> none  [the longest x5 7.39 us: padded_rows(): jnp.einsum('tk,tia->kia', row_pick, terms, precision=lax.Precision.HIGHEST)]
    ppermute x4 -> x16, waiting for transfers between devices: 30.5 us -> 8.41 us  [shifted(): return lax.ppermute(chunk, axis, [(i, (i + 1) % n) for i in range(n)])]
    pallas_call x0 -> x21, Pallas kernels: none -> 17.2 us  [call(): pl.pallas_call(body, out_shape=outs, in_specs=in_specs, out_specs=out_spe...]
    ppermute x4 -> x16, starting transfers between devices: 3.39 us -> 13.2 us  [shifted(): return lax.ppermute(chunk, axis, [(i, (i + 1) % n) for i in range(n)])]
    convert_element_type x15 -> x0, other arithmetic: 5.97 us -> none  [the longest x5 3.13 us: per_device(): live_mask = (jnp.arange(values.shape[0]) < tile_count).astype(jnp.float32)]
    add x6 -> x0, other arithmetic: 2.24 us -> none  [the longest x5 1.24 us: per_device(): col_block = col_block + LEARN_RATE * (grad_cols - DECAY_RATE * col_block)]
    slice x1 -> x0, local copies, waits for them, and re-layouts: 1.47 us -> none  [per_device(): tile_count = tile_counts[stratum, 0]]
    dot_general x10 -> x0, local copies, waits for them, and re-layouts: 1.03 us -> none  [the longest x5 0.52 us: padded_cols(): jnp.einsum('tk,tja->kja', col_pick, terms, precision=lax.Precision.HIGHEST)]
  transfers between devices with their start and end apart: 4 -> 16, of which waited for: 4 -> 7; matrix products, arithmetic and copies ran while one was open for 14% -> 0% of each run, Pallas kernels for 0% -> 35%
where the time goes in v2:
time: 39.9 us; the launch traced here: 39.7 us
  Pallas kernels  17.2 us (43%)
  starting transfers between devices  13.2 us (33%)
  waiting for transfers between devices  8.41 us (21%)
  between operations  0.82 us (2%)
    pallas_call x21, Pallas kernels, call(): pl.pallas_call(body, out_shape=outs, in_specs=in_specs, out_specs=out_spe...  17.2 us
    ppermute x16, starting transfers between devices, shifted(): return lax.ppermute(chunk, axis, [(i, (i + 1) % n) for i in range(n)])  13.2 us
    ppermute x16, waiting for transfers between devices, shifted(): return lax.ppermute(chunk, axis, [(i, (i + 1) % n) for i in range(n)])  8.41 us
  transfers between devices with their start and end apart: 16, of which 7 were waited for; matrix products, arithmetic and copies ran while one was open for 0% of the time, Pallas kernels for 35%

profile of v2, /device:TPU:0, one launch (start us, length us, event | category | flops | bytes accessed | tf_op | source)
XLA Modules:
  0.0 39.7 jit_solution(4721363409432827530)
XLA Ops:
  0.6 1.8 %first_chunk.1 = (f32[512,256]{1,0:T(8,128)S(1)}, f32[512,256]{1,0:T(8,128)S(1)}, bf16[512,512]{1,0:T(8,128)(2,1)S(1)}, f32[8,512]{1,0:T(8,128)S(1)}, f32[128,25...) custom-call(f32[512,256]{1,0:T(8,128)} %u_hbm.1, f32[512,256]{1,0:T(8,128)} %c_hbm.1, ...), custom_call_target="tpu_custom_call" | custom-call | flops 100663296 | bytes 1048576 | tf_op jit(solution)/shard_map/first_chunk/pallas_call | solution.py:22
  2.5 0.5 %collective-permute-start.3 = (f32[128,256]{1,0:T(8,128)S(1)}, f32[128,256]{1,0:T(8,128)S(1)}, u32[]{:S(2)}, u32[]{:S(2)}) collective-permute-start(f32[128,256]{1,0:T(8,128)S(1)} %get-tuple-element.69), channel_id=1, source_target_pairs={{0,4},{4,8},{8,12},{12,16},{16,20},{20,24},{24,28},{28,0},{1,5},{5... | collective-permute-start | bytes 393224 | tf_op jit(solution)/shard_map/ppermute | solution.py:231
  3.0 0.6 %chunk_step.15 = (f32[512,256]{1,0:T(8,128)S(1)}, f32[128,256]{1,0:T(8,128)S(1)}) custom-call(f32[512,256]{1,0:T(8,128)S(1)} %get-tuple-element.54.u_ref, f32[128,256]{1,0:T(8,128)S(1)} %get-tuple-element.59.c_ref, bf16[512,512]{1,0:T(8,128)(2,1)S(1)} %get-tuple-element.56.dense, f32[8,512]{1,0:T(8,128)S(1)} %get-tuple-element.57.live, ...), custom_call_target="tpu_custom_call" | custom-call | flops 100663296 | bytes 2097152 | tf_op jit(solution)/shard_map/chunk_step/pallas_call | solution.py:22
  3.6 2.7 %collective-permute-start.2 = (f32[128,256]{1,0:T(8,128)S(1)}, f32[128,256]{1,0:T(8,128)S(1)}, u32[]{:S(2)}, u32[]{:S(2)}) collective-permute-start(f32[128,256]{1,0:T(8,128)S(1)} %get-tuple-element.68), channel_id=1, source_target_pairs={{0,4},{4,8},{8,12},{12,16},{16,20},{20,24},{24,28},{28,0},{1,5},{5... | collective-permute-start | bytes 393224 | tf_op jit(solution)/shard_map/ppermute | solution.py:231
  6.3 0.6 %chunk_step.16 = (f32[512,256]{1,0:T(8,128)S(1)}, f32[128,256]{1,0:T(8,128)S(1)}) custom-call(f32[512,256]{1,0:T(8,128)S(1)} %get-tuple-element.54.u_ref, f32[128,256]{1,0:T(8,128)S(1)} %get-tuple-element.58.c_ref, bf16[512,512]{1,0:T(8,128)(2,1)S(1)} %get-tuple-element.56.dense, f32[8,512]{1,0:T(8,128)S(1)} %get-tuple-element.57.live, ...), custom_call_target="tpu_custom_call" | custom-call | flops 100663296 | bytes 2097152 | tf_op jit(solution)/shard_map/chunk_step/pallas_call | solution.py:22
  6.9 0.1 collective-permute-start.1
  7.0 0.6 %chunk_step.17 = (f32[512,256]{1,0:T(8,128)S(1)}, f32[128,256]{1,0:T(8,128)S(1)}) custom-call(f32[512,256]{1,0:T(8,128)S(1)} %get-tuple-element.54.u_ref, f32[128,256]{1,0:T(8,128)S(1)} %get-tuple-element.55.c_ref, bf16[512,512]{1,0:T(8,128)(2,1)S(1)} %get-tuple-element.56.dense, ...), custom_call_target="tpu_custom_call", output_to_operand_aliasing={{0}: (0, {})} | custom-call | flops 100663296 | bytes 2097152 | tf_op jit(solution)/shard_map/chunk_step/pallas_call | solution.py:22
  7.6 1.6 %collective-permute-start = (f32[128,256]{1,0:T(8,128)S(1)}, f32[128,256]{1,0:T(8,128)S(1)}, u32[]{:S(2)}, u32[]{:S(2)}) collective-permute-start(f32[128,256]{1,0:T(8,128)S(1)} %get-tuple-element.64._), channel_id=1, source_target_pairs={{0,4},{4,8},{8,12},{12,16},{16,20},{20,24},{24,28},{28,0},{1,5},{5... | collective-permute-start | bytes 393224 | tf_op jit(solution)/shard_map/ppermute | solution.py:231
  9.2 1.1 %lay_out_tiles.1 = (bf16[512,512]{1,0:T(8,128)(2,1)S(1)}, bf16[512,512]{1,0:T(8,128)(2,1)S(1)}, bf16[512,512]{1,0:T(8,128)(2,1)S(1)}, bf16[512,512]{1,0:T(8,128)...) custom-call(bf16[5,8,128,128]{3,2,1,0:T(8,128)(2,1)S(1)} %copy-done, ...), custom_call_target="tpu_custom_call" | custom-call | bytes 2097152 | tf_op jit(solution)/shard_map/lay_out_tiles/pallas_call | solution.py:22
  10.3 0.6 %chunk_step.18 = (f32[512,256]{1,0:T(8,128)S(1)}, f32[128,256]{1,0:T(8,128)S(1)}) custom-call(f32[512,256]{1,0:T(8,128)S(1)} %get-tuple-element.63.u_ref, f32[128,256]{1,0:T(8,128)S(1)} %collective-permute-done.3.c_ref, bf16[512,512]{1,0:T(8,128)(2,1)S(1)} %get-tuple-element.65.dense, f32[8,512]{1,0:T(8,128)S(1)} %get-tuple-element.66.live), custom_call_target="tpu_custom_call" | custom-call | flops 100663296 | bytes 2097152 | tf_op jit(solution)/shard_map/chunk_step/pallas_call | solution.py:22
  11.0 0.2 collective-permute-start.7
  11.1 0.0 collective-permute-done.2.c_ref
  11.1 0.6 %chunk_step.19 = (f32[512,256]{1,0:T(8,128)S(1)}, f32[128,256]{1,0:T(8,128)S(1)}) custom-call(f32[512,256]{1,0:T(8,128)S(1)} %get-tuple-element.63.u_ref, f32[128,256]{1,0:T(8,128)S(1)} %collective-permute-done.2.c_ref, bf16[512,512]{1,0:T(8,128)(2,1)S(1)} %get-tuple-element.65.dense, f32[8,512]{1,0:T(8,128)S(1)} %get-tuple-element.66.live, ...), custom_call_target="tpu_custom_call" | custom-call | flops 100663296 | bytes 2097152 | tf_op jit(solution)/shard_map/chunk_step/pallas_call | solution.py:22
  11.8 1.6 %collective-permute-start.6 = (f32[128,256]{1,0:T(8,128)S(1)}, f32[128,256]{1,0:T(8,128)S(1)}, u32[]{:S(2)}, u32[]{:S(2)}) collective-permute-start(f32[128,256]{1,0:T(8,128)S(1)} %get-tuple-element.78), channel_id=1, source_target_pairs={{0,4},{4,8},{8,12},{12,16},{16,20},{20,24},{24,28},{28,0},{1,5},{5... | collective-permute-start | bytes 393224 | tf_op jit(solution)/shard_map/ppermute | solution.py:231
  13.4 0.0 collective-permute-done.1.c_ref
  13.4 0.6 %chunk_step.20 = (f32[512,256]{1,0:T(8,128)S(1)}, f32[128,256]{1,0:T(8,128)S(1)}) custom-call(f32[512,256]{1,0:T(8,128)S(1)} %get-tuple-element.63.u_ref, f32[128,256]{1,0:T(8,128)S(1)} %collective-permute-done.1.c_ref, bf16[512,512]{1,0:T(8,128)(2,1)S(1)} %get-tuple-element.65.dense, f32[8,512]{1,0:T(8,128)S(1)} %get-tuple-element.66.live, ...), custom_call_target="tpu_custom_call" | custom-call | flops 100663296 | bytes 2097152 | tf_op jit(solution)/shard_map/chunk_step/pallas_call | solution.py:22
  14.0 0.1 collective-permute-start.5
  14.1 0.6 %chunk_step.21 = (f32[512,256]{1,0:T(8,128)S(1)}, f32[128,256]{1,0:T(8,128)S(1)}) custom-call(f32[512,256]{1,0:T(8,128)S(1)} %get-tuple-element.63.u_ref, f32[128,256]{1,0:T(8,128)S(1)} %collective-permute-done.c_ref, bf16[512,512]{1,0:T(8,128)(2,1)S(1)} %get-tuple-element.65.dense, ...), custom_call_target="tpu_custom_call", output_to_operand_aliasing={{0}: (0, {})} | custom-call | flops 100663296 | bytes 2097152 | tf_op jit(solution)/shard_map/chunk_step/pallas_call | solution.py:22
  14.7 0.5 %collective-permute-start.4 = (f32[128,256]{1,0:T(8,128)S(1)}, f32[128,256]{1,0:T(8,128)S(1)}, u32[]{:S(2)}, u32[]{:S(2)}) collective-permute-start(f32[128,256]{1,0:T(8,128)S(1)} %get-tuple-element.74), channel_id=1, source_target_pairs={{0,4},{4,8},{8,12},{12,16},{16,20},{20,24},{24,28},{28,0},{1,5},{5... | collective-permute-start | bytes 393224 | tf_op jit(solution)/shard_map/ppermute | solution.py:231
  15.2 1.1 %collective-permute-done.7.c_ref = f32[128,256]{1,0:T(8,128)S(1)} collective-permute-done((f32[128,256]{1,0:T(8,128)S(1)}, f32[128,256]{1,0:T(8,128)S(1)}, u32[]{:S(2)}, u32[]{:S(2)}) %collective-permute-start.7) | collective-permute-done | bytes 131104 | tf_op jit(solution)/shard_map/ppermute | solution.py:231
  16.3 0.6 %chunk_step.22 = (f32[512,256]{1,0:T(8,128)S(1)}, f32[128,256]{1,0:T(8,128)S(1)}) custom-call(f32[512,256]{1,0:T(8,128)S(1)} %get-tuple-element.73.u_ref, f32[128,256]{1,0:T(8,128)S(1)} %collective-permute-done.7.c_ref, bf16[512,512]{1,0:T(8,128)(2,1)S(1)} %get-tuple-element.75.dense, f32[8,512]{1,0:T(8,128)S(1)} %get-tuple-element.76.live), custom_call_target="tpu_custom_call" | custom-call | flops 100663296 | bytes 2097152 | tf_op jit(solution)/shard_map/chunk_step/pallas_call | solution.py:22
  16.9 1.7 %collective-permute-start.11 = (f32[128,256]{1,0:T(8,128)S(1)}, f32[128,256]{1,0:T(8,128)S(1)}, u32[]{:S(2)}, u32[]{:S(2)}) collective-permute-start(f32[128,256]{1,0:T(8,128)S(1)} %get-tuple-element.89), channel_id=1, source_target_pairs={{0,1},{1,2},{2,3},{3,0},{4,5},{5,6},{6,7},{7,4},{8,9},{9,10},{10,1... | collective-permute-start | bytes 393224 | tf_op jit(solution)/shard_map/ppermute | solution.py:231
  18.6 0.0 collective-permute-done.6.c_ref
  18.6 0.6 %chunk_step.23 = (f32[512,256]{1,0:T(8,128)S(1)}, f32[128,256]{1,0:T(8,128)S(1)}) custom-call(f32[512,256]{1,0:T(8,128)S(1)} %get-tuple-element.73.u_ref, f32[128,256]{1,0:T(8,128)S(1)} %collective-permute-done.6.c_ref, bf16[512,512]{1,0:T(8,128)(2,1)S(1)} %get-tuple-element.75.dense, f32[8,512]{1,0:T(8,128)S(1)} %get-tuple-element.76.live, ...), custom_call_target="tpu_custom_call" | custom-call | flops 100663296 | bytes 2097152 | tf_op jit(solution)/shard_map/chunk_step/pallas_call | solution.py:22
  19.2 1.6 %collective-permute-start.10 = (f32[128,256]{1,0:T(8,128)S(1)}, f32[128,256]{1,0:T(8,128)S(1)}, u32[]{:S(2)}, u32[]{:S(2)}) collective-permute-start(f32[128,256]{1,0:T(8,128)S(1)} %get-tuple-element.88), channel_id=1, source_target_pairs={{0,1},{1,2},{2,3},{3,0},{4,5},{5,6},{6,7},{7,4},{8,9},{9,10},{10,1... | collective-permute-start | bytes 393224 | tf_op jit(solution)/shard_map/ppermute | solution.py:231
  20.9 0.0 collective-permute-done.5.c_ref
  20.9 0.6 %chunk_step.24 = (f32[512,256]{1,0:T(8,128)S(1)}, f32[128,256]{1,0:T(8,128)S(1)}) custom-call(f32[512,256]{1,0:T(8,128)S(1)} %get-tuple-element.73.u_ref, f32[128,256]{1,0:T(8,128)S(1)} %collective-permute-done.5.c_ref, bf16[512,512]{1,0:T(8,128)(2,1)S(1)} %get-tuple-element.75.dense, f32[8,512]{1,0:T(8,128)S(1)} %get-tuple-element.76.live, ...), custom_call_target="tpu_custom_call" | custom-call | flops 100663296 | bytes 2097152 | tf_op jit(solution)/shard_map/chunk_step/pallas_call | solution.py:22
  21.5 1.6 %collective-permute-start.9 = (f32[128,256]{1,0:T(8,128)S(1)}, f32[128,256]{1,0:T(8,128)S(1)}, u32[]{:S(2)}, u32[]{:S(2)}) collective-permute-start(f32[128,256]{1,0:T(8,128)S(1)} %get-tuple-element.87), channel_id=1, source_target_pairs={{0,1},{1,2},{2,3},{3,0},{4,5},{5,6},{6,7},{7,4},{8,9},{9,10},{10,1... | collective-permute-start | bytes 393224 | tf_op jit(solution)/shard_map/ppermute | solution.py:231
  23.1 0.6 %chunk_step.25 = (f32[512,256]{1,0:T(8,128)S(1)}, f32[128,256]{1,0:T(8,128)S(1)}) custom-call(f32[512,256]{1,0:T(8,128)S(1)} %get-tuple-element.73.u_ref, f32[128,256]{1,0:T(8,128)S(1)} %collective-permute-done.4.c_ref, bf16[512,512]{1,0:T(8,128)(2,1)S(1)} %get-tuple-element.75.dense, ...), custom_call_target="tpu_custom_call", output_to_operand_aliasing={{0}: (0, {})} | custom-call | flops 100663296 | bytes 2097152 | tf_op jit(solution)/shard_map/chunk_step/pallas_call | solution.py:22
  23.8 0.8 %collective-permute-start.8 = (f32[128,256]{1,0:T(8,128)S(1)}, f32[128,256]{1,0:T(8,128)S(1)}, u32[]{:S(2)}, u32[]{:S(2)}) collective-permute-start(f32[128,256]{1,0:T(8,128)S(1)} %get-tuple-element.84), channel_id=1, source_target_pairs={{0,1},{1,2},{2,3},{3,0},{4,5},{5,6},{6,7},{7,4},{8,9},{9,10},{10,1... | collective-permute-start | bytes 393224 | tf_op jit(solution)/shard_map/ppermute | solution.py:231
  24.6 0.3 collective-permute-done.11.c_ref
  24.8 0.6 %chunk_step.26 = (f32[512,256]{1,0:T(8,128)S(1)}, f32[128,256]{1,0:T(8,128)S(1)}) custom-call(f32[512,256]{1,0:T(8,128)S(1)} %get-tuple-element.83.u_ref, f32[128,256]{1,0:T(8,128)S(1)} %collective-permute-done.11.c_ref, bf16[512,512]{1,0:T(8,128)(2,1)S(1)} %get-tuple-element.85.dense, f32[8,512]{1,0:T(8,128)S(1)} %get-tuple-element.86.live), custom_call_target="tpu_custom_call" | custom-call | flops 100663296 | bytes 2097152 | tf_op jit(solution)/shard_map/chunk_step/pallas_call | solution.py:22
  25.4 0.1 collective-permute-start.15
  25.5 2.1 %collective-permute-done.10.c_ref = f32[128,256]{1,0:T(8,128)S(1)} collective-permute-done((f32[128,256]{1,0:T(8,128)S(1)}, f32[128,256]{1,0:T(8,128)S(1)}, u32[]{:S(2)}, u32[]{:S(2)}) %collective-permute-start.10) | collective-permute-done | bytes 131104 | tf_op jit(solution)/shard_map/ppermute | solution.py:231
  27.6 0.6 %chunk_step.27 = (f32[512,256]{1,0:T(8,128)S(1)}, f32[128,256]{1,0:T(8,128)S(1)}) custom-call(f32[512,256]{1,0:T(8,128)S(1)} %get-tuple-element.83.u_ref, f32[128,256]{1,0:T(8,128)S(1)} %collective-permute-done.10.c_ref, bf16[512,512]{1,0:T(8,128)(2,1)S(1)} %get-tuple-element.85.dense, f32[8,512]{1,0:T(8,128)S(1)} %get-tuple-element.86.live, ...), custom_call_target="tpu_custom_call" | custom-call | flops 100663296 | bytes 2097152 | tf_op jit(solution)/shard_map/chunk_step/pallas_call | solution.py:22
  28.3 0.1 collective-permute-start.14
  28.3 2.1 %collective-permute-done.9.c_ref = f32[128,256]{1,0:T(8,128)S(1)} collective-permute-done((f32[128,256]{1,0:T(8,128)S(1)}, f32[128,256]{1,0:T(8,128)S(1)}, u32[]{:S(2)}, u32[]{:S(2)}) %collective-permute-start.9) | collective-permute-done | bytes 131104 | tf_op jit(solution)/shard_map/ppermute | solution.py:231
  30.4 0.6 %chunk_step.28 = (f32[512,256]{1,0:T(8,128)S(1)}, f32[128,256]{1,0:T(8,128)S(1)}) custom-call(f32[512,256]{1,0:T(8,128)S(1)} %get-tuple-element.83.u_ref, f32[128,256]{1,0:T(8,128)S(1)} %collective-permute-done.9.c_ref, bf16[512,512]{1,0:T(8,128)(2,1)S(1)} %get-tuple-element.85.dense, f32[8,512]{1,0:T(8,128)S(1)} %get-tuple-element.86.live, ...), custom_call_target="tpu_custom_call" | custom-call | flops 100663296 | bytes 2097152 | tf_op jit(solution)/shard_map/chunk_step/pallas_call | solution.py:22
  31.1 0.1 collective-permute-start.13
  31.1 1.2 %collective-permute-done.8.c_ref = f32[128,256]{1,0:T(8,128)S(1)} collective-permute-done((f32[128,256]{1,0:T(8,128)S(1)}, f32[128,256]{1,0:T(8,128)S(1)}, u32[]{:S(2)}, u32[]{:S(2)}) %collective-permute-start.8) | collective-permute-done | bytes 131104 | tf_op jit(solution)/shard_map/ppermute | solution.py:231
  32.3 0.6 %chunk_step.29 = (f32[512,256]{1,0:T(8,128)S(1)}, f32[128,256]{1,0:T(8,128)S(1)}) custom-call(f32[512,256]{1,0:T(8,128)S(1)} %get-tuple-element.83.u_ref, f32[128,256]{1,0:T(8,128)S(1)} %collective-permute-done.8.c_ref, bf16[512,512]{1,0:T(8,128)(2,1)S(1)} %get-tuple-element.85.dense, ...), custom_call_target="tpu_custom_call", output_to_operand_aliasing={{0}: (0, {})} | custom-call | flops 100663296 | bytes 2097152 | tf_op jit(solution)/shard_map/chunk_step/pallas_call | solution.py:22
  32.9 0.1 collective-permute-start.12
  33.0 1.2 %final_chunk.4 = (f32[512,256]{1,0:T(8,128)S(1)}, f32[512,256]{1,0:T(8,128)}) custom-call(f32[512,256]{1,0:T(8,128)S(1)} %get-tuple-element.93.u_ref, f32[128,256]{1,0:T(8,128)S(1)} %collective-permute-done.15.c_in, bf16[512,512]{1,0:T(8,128)(2,1)S(1)} %get-tuple-element.95.dense, f32[8,512]{1,0:T(8,128)S(1)} %get-tuple-element.96.live), custom_call_target="tpu_custom_call" | custom-call | flops 100663296 | bytes 2097152 | tf_op jit(solution)/shard_map/final_chunk/pallas_call | solution.py:22
  34.2 1.2 %final_chunk.5 = (f32[512,256]{1,0:T(8,128)S(1)}, f32[512,256]{1,0:T(8,128)}) custom-call(f32[512,256]{1,0:T(8,128)S(1)} %get-tuple-element.93.u_ref, f32[128,256]{1,0:T(8,128)S(1)} %collective-permute-done.14.c_in, bf16[512,512]{1,0:T(8,128)(2,1)S(1)} %get-tuple-element.95.dense, ...), custom_call_target="tpu_custom_call", output_to_operand_aliasing={{1}: (5, {})} | custom-call | flops 100663296 | bytes 2097152 | tf_op jit(solution)/shard_map/final_chunk/pallas_call | solution.py:22
  35.5 0.9 %collective-permute-done.13.c_in = f32[128,256]{1,0:T(8,128)S(1)} collective-permute-done((f32[128,256]{1,0:T(8,128)S(1)}, f32[128,256]{1,0:T(8,128)S(1)}, u32[]{:S(2)}, u32[]{:S(2)}) %collective-permute-start.13) | collective-permute-done | bytes 131104 | tf_op jit(solution)/shard_map/ppermute | solution.py:231
  36.4 1.2 %final_chunk.6 = (f32[512,256]{1,0:T(8,128)S(1)}, f32[512,256]{1,0:T(8,128)}) custom-call(f32[512,256]{1,0:T(8,128)S(1)} %get-tuple-element.93.u_ref, f32[128,256]{1,0:T(8,128)S(1)} %collective-permute-done.13.c_in, bf16[512,512]{1,0:T(8,128)(2,1)S(1)} %get-tuple-element.95.dense, ...), custom_call_target="tpu_custom_call", output_to_operand_aliasing={{1}: (5, {})} | custom-call | flops 100663296 | bytes 2097152 | tf_op jit(solution)/shard_map/final_chunk/pallas_call | solution.py:22
  37.6 0.7 %collective-permute-done.12.c_in = f32[128,256]{1,0:T(8,128)S(1)} collective-permute-done((f32[128,256]{1,0:T(8,128)S(1)}, f32[128,256]{1,0:T(8,128)S(1)}, u32[]{:S(2)}, u32[]{:S(2)}) %collective-permute-start.12) | collective-permute-done | bytes 131104 | tf_op jit(solution)/shard_map/ppermute | solution.py:231
  38.3 1.4 %final_chunk.7 = (f32[512,256]{1,0:T(8,128)}, f32[512,256]{1,0:T(8,128)}) custom-call(f32[512,256]{1,0:T(8,128)S(1)} %get-tuple-element.93.u_ref, f32[128,256]{1,0:T(8,128)S(1)} %collective-permute-done.12.c_in, bf16[512,512]{1,0:T(8,128)(2,1)S(1)} %get-tuple-element.95.dense, f32[8,512]{1,0:T(8,128)S(1)} %get-tuple-element.96.live, ...), custom_call_target="tpu_custom_call", output_to_operand_aliasing={{1}: (5, {})} | custom-call | flops 100663296 | bytes 2097152 | tf_op jit(solution)/shard_map/final_chunk/pallas_call | solution.py:22
  (11 shorter events, 0.0 us)
Async XLA Ops:
  2.5 7.9 %collective-permute-start.3 = (f32[128,256]{1,0:T(8,128)S(1)}, f32[128,256]{1,0:T(8,128)S(1)}, u32[]{:S(2)}, u32[]{:S(2)}) collective-permute-start(f32[128,256]{1,0:T(8,128)S(1)} %get-tuple-element.69), channel_id=1, source_target_pairs={{0,4},{4,8},{8,12},{12,16},{16,20},{20,24},{24,28},{28,0},{1,5},{5... | collective-permute-start | bytes 393224 | tf_op jit(solution)/shard_map/ppermute | solution.py:231
  3.6 7.5 %collective-permute-start.2 = (f32[128,256]{1,0:T(8,128)S(1)}, f32[128,256]{1,0:T(8,128)S(1)}, u32[]{:S(2)}, u32[]{:S(2)}) collective-permute-start(f32[128,256]{1,0:T(8,128)S(1)} %get-tuple-element.68), channel_id=1, source_target_pairs={{0,4},{4,8},{8,12},{12,16},{16,20},{20,24},{24,28},{28,0},{1,5},{5... | collective-permute-start | bytes 393224 | tf_op jit(solution)/shard_map/ppermute | solution.py:231
  6.3 3.0 %copy-start = (bf16[5,8,128,128]{3,2,1,0:T(8,128)(2,1)S(1)}, bf16[5,8,128,128]{3,2,1,0:T(8,128)(2,1)}, u32[]{:S(2)}) copy-start(bf16[5,8,128,128]{3,2,1,0:T(8,128)(2,1)} %x_ref.1) | copy-start | bytes 3932164
  6.3 3.0 %copy-start.1 = (s32[5,8,2]{1,2,0:T(2,128)S(1)}, s32[5,8,2]{1,2,0:T(2,128)}, u32[]{:S(2)}) copy-start(s32[5,8,2]{1,2,0:T(2,128)} %param.8) | copy-start | bytes 964
  6.3 3.0 %copy-start.2 = (s32[5,1]{0,1:T(1,128)S(1)}, s32[5,1]{0,1:T(1,128)}, u32[]{:S(2)}) copy-start(s32[5,1]{0,1:T(1,128)} %param.9) | copy-start | bytes 64
  6.9 6.5 %collective-permute-start.1 = (f32[128,256]{1,0:T(8,128)S(1)}, f32[128,256]{1,0:T(8,128)S(1)}, u32[]{:S(2)}, u32[]{:S(2)}) collective-permute-start(f32[128,256]{1,0:T(8,128)S(1)} %get-tuple-element.67), channel_id=1, source_target_pairs={{0,4},{4,8},{8,12},{12,16},{16,20},{20,24},{24,28},{28,0},{1,5},{5... | collective-permute-start | bytes 393224 | tf_op jit(solution)/shard_map/ppermute | solution.py:231
  7.6 6.5 %collective-permute-start = (f32[128,256]{1,0:T(8,128)S(1)}, f32[128,256]{1,0:T(8,128)S(1)}, u32[]{:S(2)}, u32[]{:S(2)}) collective-permute-start(f32[128,256]{1,0:T(8,128)S(1)} %get-tuple-element.64._), channel_id=1, source_target_pairs={{0,4},{4,8},{8,12},{12,16},{16,20},{20,24},{24,28},{28,0},{1,5},{5... | collective-permute-start | bytes 393224 | tf_op jit(solution)/shard_map/ppermute | solution.py:231
  11.0 5.3 %collective-permute-start.7 = (f32[128,256]{1,0:T(8,128)S(1)}, f32[128,256]{1,0:T(8,128)S(1)}, u32[]{:S(2)}, u32[]{:S(2)}) collective-permute-start(f32[128,256]{1,0:T(8,128)S(1)} %get-tuple-element.79), channel_id=1, source_target_pairs={{0,4},{4,8},{8,12},{12,16},{16,20},{20,24},{24,28},{28,0},{1,5},{5... | collective-permute-start | bytes 393224 | tf_op jit(solution)/shard_map/ppermute | solution.py:231
  11.8 6.9 %collective-permute-start.6 = (f32[128,256]{1,0:T(8,128)S(1)}, f32[128,256]{1,0:T(8,128)S(1)}, u32[]{:S(2)}, u32[]{:S(2)}) collective-permute-start(f32[128,256]{1,0:T(8,128)S(1)} %get-tuple-element.78), channel_id=1, source_target_pairs={{0,4},{4,8},{8,12},{12,16},{16,20},{20,24},{24,28},{28,0},{1,5},{5... | collective-permute-start | bytes 393224 | tf_op jit(solution)/shard_map/ppermute | solution.py:231
  14.0 6.9 %collective-permute-start.5 = (f32[128,256]{1,0:T(8,128)S(1)}, f32[128,256]{1,0:T(8,128)S(1)}, u32[]{:S(2)}, u32[]{:S(2)}) collective-permute-start(f32[128,256]{1,0:T(8,128)S(1)} %get-tuple-element.77), channel_id=1, source_target_pairs={{0,4},{4,8},{8,12},{12,16},{16,20},{20,24},{24,28},{28,0},{1,5},{5... | collective-permute-start | bytes 393224 | tf_op jit(solution)/shard_map/ppermute | solution.py:231
  14.7 8.4 %collective-permute-start.4 = (f32[128,256]{1,0:T(8,128)S(1)}, f32[128,256]{1,0:T(8,128)S(1)}, u32[]{:S(2)}, u32[]{:S(2)}) collective-permute-start(f32[128,256]{1,0:T(8,128)S(1)} %get-tuple-element.74), channel_id=1, source_target_pairs={{0,4},{4,8},{8,12},{12,16},{16,20},{20,24},{24,28},{28,0},{1,5},{5... | collective-permute-start | bytes 393224 | tf_op jit(solution)/shard_map/ppermute | solution.py:231
  16.9 7.9 %collective-permute-start.11 = (f32[128,256]{1,0:T(8,128)S(1)}, f32[128,256]{1,0:T(8,128)S(1)}, u32[]{:S(2)}, u32[]{:S(2)}) collective-permute-start(f32[128,256]{1,0:T(8,128)S(1)} %get-tuple-element.89), channel_id=1, source_target_pairs={{0,1},{1,2},{2,3},{3,0},{4,5},{5,6},{6,7},{7,4},{8,9},{9,10},{10,1... | collective-permute-start | bytes 393224 | tf_op jit(solution)/shard_map/ppermute | solution.py:231
  19.2 8.4 %collective-permute-start.10 = (f32[128,256]{1,0:T(8,128)S(1)}, f32[128,256]{1,0:T(8,128)S(1)}, u32[]{:S(2)}, u32[]{:S(2)}) collective-permute-start(f32[128,256]{1,0:T(8,128)S(1)} %get-tuple-element.88), channel_id=1, source_target_pairs={{0,1},{1,2},{2,3},{3,0},{4,5},{5,6},{6,7},{7,4},{8,9},{9,10},{10,1... | collective-permute-start | bytes 393224 | tf_op jit(solution)/shard_map/ppermute | solution.py:231
  21.5 8.9 %collective-permute-start.9 = (f32[128,256]{1,0:T(8,128)S(1)}, f32[128,256]{1,0:T(8,128)S(1)}, u32[]{:S(2)}, u32[]{:S(2)}) collective-permute-start(f32[128,256]{1,0:T(8,128)S(1)} %get-tuple-element.87), channel_id=1, source_target_pairs={{0,1},{1,2},{2,3},{3,0},{4,5},{5,6},{6,7},{7,4},{8,9},{9,10},{10,1... | collective-permute-start | bytes 393224 | tf_op jit(solution)/shard_map/ppermute | solution.py:231
  23.8 8.5 %collective-permute-start.8 = (f32[128,256]{1,0:T(8,128)S(1)}, f32[128,256]{1,0:T(8,128)S(1)}, u32[]{:S(2)}, u32[]{:S(2)}) collective-permute-start(f32[128,256]{1,0:T(8,128)S(1)} %get-tuple-element.84), channel_id=1, source_target_pairs={{0,1},{1,2},{2,3},{3,0},{4,5},{5,6},{6,7},{7,4},{8,9},{9,10},{10,1... | collective-permute-start | bytes 393224 | tf_op jit(solution)/shard_map/ppermute | solution.py:231
  25.4 7.6 %collective-permute-start.15 = (f32[128,256]{1,0:T(8,128)S(1)}, f32[128,256]{1,0:T(8,128)S(1)}, u32[]{:S(2)}, u32[]{:S(2)}) collective-permute-start(f32[128,256]{1,0:T(8,128)S(1)} %get-tuple-element.99), channel_id=1, source_target_pairs={{0,4},{4,8},{8,12},{12,16},{16,20},{20,24},{24,28},{28,0},{1,5},{5... | collective-permute-start | bytes 393224 | tf_op jit(solution)/shard_map/ppermute | solution.py:231
  28.3 6.0 %collective-permute-start.14 = (f32[128,256]{1,0:T(8,128)S(1)}, f32[128,256]{1,0:T(8,128)S(1)}, u32[]{:S(2)}, u32[]{:S(2)}) collective-permute-start(f32[128,256]{1,0:T(8,128)S(1)} %get-tuple-element.98), channel_id=1, source_target_pairs={{0,4},{4,8},{8,12},{12,16},{16,20},{20,24},{24,28},{28,0},{1,5},{5... | collective-permute-start | bytes 393224 | tf_op jit(solution)/shard_map/ppermute | solution.py:231
  31.1 5.3 %collective-permute-start.13 = (f32[128,256]{1,0:T(8,128)S(1)}, f32[128,256]{1,0:T(8,128)S(1)}, u32[]{:S(2)}, u32[]{:S(2)}) collective-permute-start(f32[128,256]{1,0:T(8,128)S(1)} %get-tuple-element.97), channel_id=1, source_target_pairs={{0,4},{4,8},{8,12},{12,16},{16,20},{20,24},{24,28},{28,0},{1,5},{5... | collective-permute-start | bytes 393224 | tf_op jit(solution)/shard_map/ppermute | solution.py:231
  32.9 5.3 %collective-permute-start.12 = (f32[128,256]{1,0:T(8,128)S(1)}, f32[128,256]{1,0:T(8,128)S(1)}, u32[]{:S(2)}, u32[]{:S(2)}) collective-permute-start(f32[128,256]{1,0:T(8,128)S(1)} %get-tuple-element.94), channel_id=1, source_target_pairs={{0,4},{4,8},{8,12},{12,16},{16,20},{20,24},{24,28},{28,0},{1,5},{5... | collective-permute-start | bytes 393224 | tf_op jit(solution)/shard_map/ppermute | solution.py:231

commit v3 on v0

v3 whole, which is shorter than its diff:
```python
import functools

import jax
import jax.numpy as jnp
from jax import lax
from jax.experimental import pallas as pl
from jax.experimental.pallas import tpu as pltpu
from jax.sharding import PartitionSpec as P

LEARN_RATE = 0.03
DECAY_RATE = 0.1
CHUNKS = 4
SUBLANES = 8

VMEM = pl.BlockSpec(memory_space=pltpu.VMEM)
SMEM = pl.BlockSpec(memory_space=pltpu.SMEM)
HBM = pl.BlockSpec(memory_space=pltpu.HBM)
ANY = pl.BlockSpec(memory_space=pl.ANY)


def call(body, name, operands, in_specs, outs, out_specs, flops=0, moved=0, aliases=None, scratch=()):
    return pl.pallas_call(
        body,
        out_shape=outs,
        in_specs=in_specs,
        out_specs=out_specs,
        input_output_aliases=aliases or {},
        scratch_shapes=list(scratch),
        compiler_params=pltpu.CompilerParams(vmem_limit_bytes=24 * 1024 * 1024),
        cost_estimate=pl.CostEstimate(flops=flops, bytes_accessed=moved, transcendentals=0),
        name=name,
    )(*operands)


def like(array, shape=None, dtype=None):
    return jax.ShapeDtypeStruct(shape or array.shape, dtype or array.dtype)


def span(h, width):
    return slice(h * width, (h + 1) * width)


def scatter(stratum, values, coords, counts, dense, live):
    listed, tile, _ = values.shape
    dense[...] = jnp.zeros_like(dense)
    live[...] = jnp.zeros_like(live)
    for t in range(listed):

        @pl.when(t < counts[0, stratum])
        def _():
            r = pl.multiple_of(coords[stratum, 0, t] * tile, tile)
            c = coords[stratum, 1, t]
            dense[pl.ds(pl.multiple_of(c * tile, tile), tile), pl.ds(r, tile)] = values[t].T
            named = lax.broadcasted_iota(jnp.int32, (SUBLANES, tile), 0) == c
            live[:, pl.ds(r, tile)] = jnp.where(named, 1.0, live[:, pl.ds(r, tile)])


def sgd(old, grad):
    return old + LEARN_RATE * (grad - DECAY_RATE * old)


def dot(a, b, contract):
    return lax.dot_general(a, b, (contract, ((), ())), preferred_element_type=jnp.float32)


def columns_step(first_tile, tile, row_half, cols, dense, live):
    estimate = dot(cols.astype(jnp.bfloat16), row_half, ((1,), (1,)))
    parts = []
    for i in range(cols.shape[0] // tile):
        at = span(i, tile)
        residue = dense[at].astype(jnp.float32) - estimate[at]
        named = live[first_tile + i : first_tile + i + 1] > 0
        parts.append(jnp.where(named, residue, 0.0).astype(jnp.bfloat16))
    residue = parts[0] if len(parts) == 1 else jnp.concatenate(parts, axis=0)
    return residue, sgd(cols, dot(residue, row_half, ((1,), (0,))))


def rows_gradient(residues, cols):
    return sum(
        dot(e[...], c[...].astype(jnp.bfloat16), ((0,), (0,))) for e, c in zip(residues, cols)
    )


def first_kernel(u_hbm, c_hbm, x_hbm, coords_hbm, counts_hbm, *refs):
    u_ref, c_ref, residue = refs[:3]
    c_outs = refs[3 : 3 + CHUNKS]
    dense, live, x_ref, coords, counts, sems = refs[3 + CHUNKS :]
    tile = x_ref.shape[1]
    pairs = [(coords_hbm, coords), (counts_hbm, counts), (x_hbm.at[0], x_ref)]
    pairs += [(u_hbm, u_ref), (c_hbm, c_ref)]
    copies = [pltpu.make_async_copy(s, d, sems.at[i]) for i, (s, d) in enumerate(pairs)]
    for copy in copies:
        copy.start()
    for copy in copies[:3]:
        copy.wait()
    scatter(0, x_ref, coords, counts, dense, live)
    for copy in copies[3:]:
        copy.wait()
    row_half = u_ref[...].astype(jnp.bfloat16)
    for h in range(CHUNKS):
        at = span(h, c_ref.shape[0] // CHUNKS)
        first_tile = at.start // tile
        residue[at], c_outs[h][...] = columns_step(
            first_tile, tile, row_half, c_ref[at], dense[at], live
        )


def first(u, c, values, coords, counts):
    rows, cols = u.shape[0], c.shape[0]
    part = (cols // CHUNKS, c.shape[1])
    outs = [like(u), like(c), like(u, (cols, rows), jnp.bfloat16)] + [like(c, part)] * CHUNKS
    operands = (u, c, values, coords, counts)
    u, c, residue, *cs = call(
        first_kernel,
        "first_columns",
        [pltpu.with_memory_space_constraint(x, pltpu.HBM) for x in operands],
        [HBM] * 5,
        outs,
        [VMEM] * len(outs),
        flops=4 * u.size * cols,
        moved=8 * u.size,
        scratch=[
            pltpu.VMEM((cols, rows), jnp.bfloat16),
            pltpu.VMEM((SUBLANES, rows), jnp.float32),
            pltpu.VMEM(values.shape[1:], values.dtype),
            pltpu.SMEM(coords.shape, coords.dtype),
            pltpu.SMEM(counts.shape, counts.dtype),
            pltpu.SemaphoreType.DMA((5,)),
        ],
    )
    return u, c, residue, cs


def layout_kernel(stratum, x_ref, coords, counts, _, dense, live):
    scatter(stratum, x_ref.at[stratum], coords, counts, dense, live)


def layout(stratum, values, coords, counts, rows, cols, after):
    return call(
        functools.partial(layout_kernel, stratum),
        "lay_out_tiles",
        (values, coords, counts, after),
        [VMEM, SMEM, SMEM, ANY],
        [like(values, (cols, rows)), like(values, (SUBLANES, rows), jnp.float32)],
        [VMEM] * 2,
        moved=4 * rows * cols,
    )


def columns_kernel(h, tile, row_half, c_ref, dense, live, c_out, residue):
    width = c_ref.shape[0]
    residue[...], c_out[...] = columns_step(
        h * width // tile, tile, row_half[...], c_ref[...], dense[span(h, width)], live
    )


def columns(h, tile, row_half, c, laid):
    return call(
        functools.partial(columns_kernel, h, tile),
        "columns_step",
        (row_half, c, *laid),
        [VMEM] * 4,
        [like(c), like(row_half, (c.shape[0], row_half.shape[0]))],
        [VMEM] * 2,
        flops=4 * row_half.size * c.shape[0],
        moved=2 * row_half.size + 8 * c.size,
    )


def rows_kernel(*refs):
    *refs, u_out, half_out = refs
    u_ref, pairs = refs[0], refs[1:]
    n = len(pairs) // 2
    u_new = sgd(u_ref[...], rows_gradient(pairs[:n], pairs[n:]))
    u_out[...] = u_new
    half_out[...] = u_new.astype(jnp.bfloat16)


def rows(u, residues, cols):
    operands = (u, *residues, *cols)
    return call(
        rows_kernel,
        "rows_step",
        operands,
        [VMEM] * len(operands),
        [like(u), like(u, dtype=jnp.bfloat16)],
        [VMEM] * 2,
        flops=2 * u.size * sum(c.shape[0] for c in cols),
        moved=10 * u.size,
    )


def before_last_kernel(*refs):
    n = CHUNKS - 1
    residues, cols, done = refs[:n], refs[n : 2 * n], refs[2 * n : 3 * n]
    acc, c_hbm, sems = refs[3 * n :]
    width = done[0].shape[0]
    copies = [
        pltpu.make_async_copy(c, c_hbm.at[pl.ds(h * width, width)], sems.at[h])
        for h, c in enumerate(done)
    ]
    for copy in copies:
        copy.start()
    acc[...] = rows_gradient(residues, cols)
    for copy in copies:
        copy.wait()


def last_kernel(tile, u_ref, row_half, c_ref, dense, live, acc, _, u_hbm, c_hbm, u_new, c_new, sems):
    h, width = CHUNKS - 1, c_ref.shape[0]
    cols = c_ref[...]
    residue, c_new[...] = columns_step(
        h * width // tile, tile, row_half[...], cols, dense[span(h, width)], live
    )
    copies = [pltpu.make_async_copy(c_new, c_hbm.at[pl.ds(h * width, width)], sems.at[0])]
    copies[0].start()
    col_half = cols.astype(jnp.bfloat16)
    for r in range(u_ref.shape[0] // tile):
        part, place = span(r, tile), pl.ds(r * tile, tile)
        grad = dot(residue[:, part], col_half, ((0,), (0,)))
        u_new[part] = sgd(u_ref[part], acc[part] + grad)
        copies.append(pltpu.make_async_copy(u_new.at[place], u_hbm.at[place], sems.at[r + 1]))
        copies[-1].start()
    for copy in copies:
        copy.wait()


def final(tile, u, row_half, cs, laid):
    n = CHUNKS - 1
    width, rank = cs[0].shape
    whole = like(cs[0], (CHUNKS * width, rank))
    done, residues = [], []
    for h in range(n):
        c, residue = columns(h, tile, row_half, cs[h], laid)
        done.append(c)
        residues.append(residue)
    acc, out = call(
        before_last_kernel,
        "rows_before_last",
        (*residues, *cs[:n], *done),
        [VMEM] * (3 * n),
        [like(u), whole],
        [VMEM, HBM],
        flops=2 * u.size * n * width,
        moved=8 * u.size,
        scratch=[pltpu.SemaphoreType.DMA((n,))],
    )
    return call(
        functools.partial(last_kernel, tile),
        "last_columns_and_rows",
        (u, row_half, cs[n], *laid, acc, out),
        [VMEM] * 6 + [HBM],
        [like(u), whole],
        [HBM, HBM],
        flops=6 * u.size * width,
        moved=8 * u.size,
        aliases={6: 1},
        scratch=[
            pltpu.VMEM(u.shape, u.dtype),
            pltpu.VMEM((width, rank), u.dtype),
            pltpu.SemaphoreType.DMA((1 + u.shape[0] // tile,)),
        ],
    )


def shifted(chunk, axis):
    n = lax.axis_size(axis)
    return lax.ppermute(chunk, axis, [(i, (i + 1) % n) for i in range(n)])


def per_device(row_factors, col_factors, tile_values, tile_coords, tile_counts):
    tile = tile_values.shape[2]
    strata = tile_values.shape[0]
    coords, counts = tile_coords.transpose(0, 2, 1), tile_counts.transpose(1, 0)
    sizes = row_factors.shape[0], col_factors.shape[0]
    u, c, residue, done = first(row_factors, col_factors, tile_values, coords, counts)
    cs = [shifted(d, "blk") for d in done]
    u, row_half = rows(u, [residue], [c])
    for stratum in range(1, strata):
        laid = layout(stratum, tile_values, coords, counts, *sizes, done[-1])
        if stratum == strata - 1:
            return final(tile, u, row_half, cs, laid)
        axis = "group" if stratum == 2 else "blk"
        arrived, cs, done, residues = cs, [], [], []
        for h in range(CHUNKS):
            d, residue = columns(h, tile, row_half, arrived[h], laid)
            done.append(d)
            residues.append(residue)
            cs.append(shifted(d, axis))
        u, row_half = rows(u, residues, arrived)


def solution(mesh):
    return jax.shard_map(
        per_device,
        mesh=mesh,
        in_specs=(
            P(("blk", "group"), None),
            P(("blk", "group"), None),
            P(None, ("blk", "group"), None, None),
            P(None, ("blk", "group"), None),
            P(None, ("blk", "group")),
        ),
        out_specs=(P(("blk", "group"), None), P(("blk", "group"), None)),
        check_vma=False,
    )
```

time: 69.9 us -> 40.1 us (0.57)
  matrix products: 23.1 us -> 0 us
  waiting for transfers between devices: 30.5 us -> 9.2 us
  Pallas kernels: 0 us -> 15.6 us
  starting transfers between devices: 3.39 us -> 14.4 us
  other arithmetic: 8.21 us -> 0 us
  local copies, waits for them, and re-layouts: 3.29 us -> 0.01 us
    dot_general x35 -> x0, matrix products: 23.1 us -> none  [the longest x5 7.39 us: padded_rows(): jnp.einsum('tk,tia->kia', row_pick, terms, precision=lax.Precision.HIGHEST)]
    ppermute x4 -> x16, waiting for transfers between devices: 30.5 us -> 9.2 us  [shifted(): return lax.ppermute(chunk, axis, [(i, (i + 1) % n) for i in range(n)])]
    pallas_call x0 -> x26, Pallas kernels: none -> 15.6 us  [call(): pl.pallas_call(body, out_shape=outs, in_specs=in_specs, out_specs=out_spe...]
    ppermute x4 -> x16, starting transfers between devices: 3.39 us -> 14.4 us  [shifted(): return lax.ppermute(chunk, axis, [(i, (i + 1) % n) for i in range(n)])]
    convert_element_type x15 -> x0, other arithmetic: 5.97 us -> none  [the longest x5 3.13 us: per_device(): live_mask = (jnp.arange(values.shape[0]) < tile_count).astype(jnp.float32)]
    add x6 -> x0, other arithmetic: 2.24 us -> none  [the longest x5 1.24 us: per_device(): col_block = col_block + LEARN_RATE * (grad_cols - DECAY_RATE * col_block)]
    slice x1 -> x0, local copies, waits for them, and re-layouts: 1.47 us -> none  [per_device(): tile_count = tile_counts[stratum, 0]]
    dot_general x10 -> x0, local copies, waits for them, and re-layouts: 1.03 us -> none  [the longest x5 0.52 us: padded_cols(): jnp.einsum('tk,tja->kja', col_pick, terms, precision=lax.Precision.HIGHEST)]
  transfers between devices with their start and end apart: 4 -> 16, of which waited for: 4 -> 9; matrix products, arithmetic and copies ran while one was open for 14% -> 0% of each run, Pallas kernels for 0% -> 30%
where the time goes in v3:
time: 40.1 us
  Pallas kernels  15.6 us (39%)
  starting transfers between devices  14.4 us (36%)
  waiting for transfers between devices  9.2 us (23%)
  between operations  0.91 us (2%)
    pallas_call x26, Pallas kernels, call(): pl.pallas_call(body, out_shape=outs, in_specs=in_specs, out_specs=out_spe...  15.6 us
    ppermute x16, starting transfers between devices, shifted(): return lax.ppermute(chunk, axis, [(i, (i + 1) % n) for i in range(n)])  14.4 us
    ppermute x16, waiting for transfers between devices, shifted(): return lax.ppermute(chunk, axis, [(i, (i + 1) % n) for i in range(n)])  9.2 us
  transfers between devices with their start and end apart: 16, of which 9 were waited for; matrix products, arithmetic and copies ran while one was open for 0% of the time, Pallas kernels for 30%

profile of v3, /device:TPU:0, one launch (start us, length us, event | category | flops | bytes accessed | tf_op | source)
XLA Modules:
  0.0 40.1 jit_solution(14778114394638139736)
XLA Ops:
  0.7 2.4 %first_columns.1 = (f32[512,256]{1,0:T(8,128)S(1)}, f32[512,256]{1,0:T(8,128)S(1)}, bf16[512,512]{1,0:T(8,128)(2,1)S(1)}, f32[128,256]{1,0:T(8,128)S(1)}, f32[12...) custom-call(f32[512,256]{1,0:T(8,128)} %u_hbm.1, f32[512,256]{1,0:T(8,128)} %c_hbm.1, ...), custom_call_target="tpu_custom_call" | custom-call | flops 268435456 | bytes 1048576 | tf_op jit(solution)/shard_map/first_columns/pallas_call | solution.py:22
  3.1 0.5 %collective-permute-start.2 = (f32[128,256]{1,0:T(8,128)S(1)}, f32[128,256]{1,0:T(8,128)S(1)}, u32[]{:S(2)}, u32[]{:S(2)}) collective-permute-start(f32[128,256]{1,0:T(8,128)S(1)} %get-tuple-element.69), channel_id=1, source_target_pairs={{0,4},{4,8},{8,12},{12,16},{16,20},{20,24},{24,28},{28,0},{1,5},{5... | collective-permute-start | bytes 393224 | tf_op jit(solution)/shard_map/ppermute | solution.py:268
  3.6 2.6 %collective-permute-start.1 = (f32[128,256]{1,0:T(8,128)S(1)}, f32[128,256]{1,0:T(8,128)S(1)}, u32[]{:S(2)}, u32[]{:S(2)}) collective-permute-start(f32[128,256]{1,0:T(8,128)S(1)} %get-tuple-element.67), channel_id=1, source_target_pairs={{0,4},{4,8},{8,12},{12,16},{16,20},{20,24},{24,28},{28,0},{1,5},{5... | collective-permute-start | bytes 393224 | tf_op jit(solution)/shard_map/ppermute | solution.py:268
  6.3 1.5 %collective-permute-start.3 = (f32[128,256]{1,0:T(8,128)S(1)}, f32[128,256]{1,0:T(8,128)S(1)}, u32[]{:S(2)}, u32[]{:S(2)}) collective-permute-start(f32[128,256]{1,0:T(8,128)S(1)} %get-tuple-element.63._), channel_id=1, source_target_pairs={{0,4},{4,8},{8,12},{12,16},{16,20},{20,24},{24,28},{28,0},{1,5},{5... | collective-permute-start | bytes 393224 | tf_op jit(solution)/shard_map/ppermute | solution.py:268
  7.8 1.1 %lay_out_tiles.4 = (bf16[512,512]{1,0:T(8,128)(2,1)S(1)}, f32[8,512]{1,0:T(8,128)S(1)}) custom-call(bf16[5,8,128,128]{3,2,1,0:T(8,128)(2,1)S(1)} %copy-done, s32[5,2,8]{2,1,0:T(2,128)S(1)} %bitcast.3, s32[1,5]{1,0:T(1,128)S(1)} %bitcast.8, f32[128,256]{1,0:T(8,128)S(1)} %get-tuple-element.63._), custom_call_target="tpu_custom_call" | custom-call | bytes 1048576 | tf_op jit(solution)/shard_map/lay_out_tiles/pallas_call | solution.py:22
  8.9 0.4 rows_step.4
  9.2 0.4 columns_step.17
  9.7 0.9 %collective-permute-done.1.c_ref.refs_6_ = f32[128,256]{1,0:T(8,128)S(1)} collective-permute-done((f32[128,256]{1,0:T(8,128)S(1)}, f32[128,256]{1,0:T(8,128)S(1)}, u32[]{:S(2)}, u32[]{:S(2)}) %collective-permute-start.1) | collective-permute-done | bytes 131104 | tf_op jit(solution)/shard_map/ppermute | solution.py:268
  10.5 0.4 columns_step.16
  10.9 0.9 %collective-permute-start.5 = (f32[128,256]{1,0:T(8,128)S(1)}, f32[128,256]{1,0:T(8,128)S(1)}, u32[]{:S(2)}, u32[]{:S(2)}) collective-permute-start(f32[128,256]{1,0:T(8,128)S(1)} %get-tuple-element.79), channel_id=1, source_target_pairs={{0,4},{4,8},{8,12},{12,16},{16,20},{20,24},{24,28},{28,0},{1,5},{5... | collective-permute-start | bytes 393224 | tf_op jit(solution)/shard_map/ppermute | solution.py:268
  11.8 0.1 collective-permute-done.c_ref.refs_5_
  11.9 0.4 columns_step.15
  12.3 0.6 %collective-permute-start.4 = (f32[128,256]{1,0:T(8,128)S(1)}, f32[128,256]{1,0:T(8,128)S(1)}, u32[]{:S(2)}, u32[]{:S(2)}) collective-permute-start(f32[128,256]{1,0:T(8,128)S(1)} %get-tuple-element.74), channel_id=1, source_target_pairs={{0,4},{4,8},{8,12},{12,16},{16,20},{20,24},{24,28},{28,0},{1,5},{5... | collective-permute-start | bytes 393224 | tf_op jit(solution)/shard_map/ppermute | solution.py:268
  12.9 0.5 %collective-permute-done.3.c_ref.refs_8_ = f32[128,256]{1,0:T(8,128)S(1)} collective-permute-done((f32[128,256]{1,0:T(8,128)S(1)}, f32[128,256]{1,0:T(8,128)S(1)}, u32[]{:S(2)}, u32[]{:S(2)}) %collective-permute-start.3) | collective-permute-done | bytes 131104 | tf_op jit(solution)/shard_map/ppermute | solution.py:268
  13.3 0.4 columns_step.18
  13.7 1.1 %collective-permute-start.7 = (f32[128,256]{1,0:T(8,128)S(1)}, f32[128,256]{1,0:T(8,128)S(1)}, u32[]{:S(2)}, u32[]{:S(2)}) collective-permute-start(f32[128,256]{1,0:T(8,128)S(1)} %get-tuple-element.75._), channel_id=1, source_target_pairs={{0,4},{4,8},{8,12},{12,16},{16,20},{20,24},{24,28},{28,0},{1,5},{5... | collective-permute-start | bytes 393224 | tf_op jit(solution)/shard_map/ppermute | solution.py:268
  14.8 1.1 %lay_out_tiles.5 = (bf16[512,512]{1,0:T(8,128)(2,1)S(1)}, f32[8,512]{1,0:T(8,128)S(1)}) custom-call(bf16[5,8,128,128]{3,2,1,0:T(8,128)(2,1)S(1)} %copy-done, s32[5,2,8]{2,1,0:T(2,128)S(1)} %bitcast.4, s32[1,5]{1,0:T(1,128)S(1)} %bitcast.9, f32[128,256]{1,0:T(8,128)S(1)} %get-tuple-element.75._), custom_call_target="tpu_custom_call" | custom-call | bytes 1048576 | tf_op jit(solution)/shard_map/lay_out_tiles/pallas_call | solution.py:22
  15.8 0.5 %rows_step.5 = (f32[512,256]{1,0:T(8,128)S(1)}, bf16[512,256]{1,0:T(8,128)(2,1)S(1)}) custom-call(f32[512,256]{1,0:T(8,128)S(1)} %get-tuple-element.60.refs_0_, bf16[128,512]{1,0:T(8,128)(2,1)S(1)} %get-tuple-element.66.refs_1_, bf16[128,512]{1,0:T(8,128)(2,1)S(1)} %get-tuple-element.68.refs_2_, bf16[128,512]{1,0:T(8,128)(2,1)S(1)} %get-tuple-element.70.refs_3_, ...), custom_call_target="tpu_custom_call" | custom-call | flops 134217728 | bytes 1310720 | tf_op jit(solution)/shard_map/rows_step/pallas_call | solution.py:22
  16.3 0.4 columns_step.21
  16.7 1.5 %collective-permute-start.10 = (f32[128,256]{1,0:T(8,128)S(1)}, f32[128,256]{1,0:T(8,128)S(1)}, u32[]{:S(2)}, u32[]{:S(2)}) collective-permute-start(f32[128,256]{1,0:T(8,128)S(1)} %get-tuple-element.93), channel_id=1, source_target_pairs={{0,1},{1,2},{2,3},{3,0},{4,5},{5,6},{6,7},{7,4},{8,9},{9,10},{10,1... | collective-permute-start | bytes 393224 | tf_op jit(solution)/shard_map/ppermute | solution.py:268
  18.2 0.4 columns_step.20
  18.6 1.9 %collective-permute-start.9 = (f32[128,256]{1,0:T(8,128)S(1)}, f32[128,256]{1,0:T(8,128)S(1)}, u32[]{:S(2)}, u32[]{:S(2)}) collective-permute-start(f32[128,256]{1,0:T(8,128)S(1)} %get-tuple-element.91), channel_id=1, source_target_pairs={{0,1},{1,2},{2,3},{3,0},{4,5},{5,6},{6,7},{7,4},{8,9},{9,10},{10,1... | collective-permute-start | bytes 393224 | tf_op jit(solution)/shard_map/ppermute | solution.py:268
  20.5 0.4 columns_step.19
  20.9 1.4 %collective-permute-start.8 = (f32[128,256]{1,0:T(8,128)S(1)}, f32[128,256]{1,0:T(8,128)S(1)}, u32[]{:S(2)}, u32[]{:S(2)}) collective-permute-start(f32[128,256]{1,0:T(8,128)S(1)} %get-tuple-element.86), channel_id=1, source_target_pairs={{0,1},{1,2},{2,3},{3,0},{4,5},{5,6},{6,7},{7,4},{8,9},{9,10},{10,1... | collective-permute-start | bytes 393224 | tf_op jit(solution)/shard_map/ppermute | solution.py:268
  22.3 0.4 columns_step.22
  22.6 0.4 collective-permute-start.11
  23.0 0.8 %lay_out_tiles.6 = (bf16[512,512]{1,0:T(8,128)(2,1)S(1)}, f32[8,512]{1,0:T(8,128)S(1)}) custom-call(bf16[5,8,128,128]{3,2,1,0:T(8,128)(2,1)S(1)} %copy-done, s32[5,2,8]{2,1,0:T(2,128)S(1)} %bitcast.5, s32[1,5]{1,0:T(1,128)S(1)} %bitcast.10, f32[128,256]{1,0:T(8,128)S(1)} %get-tuple-element.87._), custom_call_target="tpu_custom_call" | custom-call | bytes 1048576 | tf_op jit(solution)/shard_map/lay_out_tiles/pallas_call | solution.py:22
  23.8 0.5 %rows_step.6 = (f32[512,256]{1,0:T(8,128)S(1)}, bf16[512,256]{1,0:T(8,128)(2,1)S(1)}) custom-call(f32[512,256]{1,0:T(8,128)S(1)} %get-tuple-element.72.refs_0_, bf16[128,512]{1,0:T(8,128)(2,1)S(1)} %get-tuple-element.78.refs_1_, bf16[128,512]{1,0:T(8,128)(2,1)S(1)} %get-tuple-element.80.refs_2_, bf16[128,512]{1,0:T(8,128)(2,1)S(1)} %get-tuple-element.82.refs_3_, ...), custom_call_target="tpu_custom_call" | custom-call | flops 134217728 | bytes 1310720 | tf_op jit(solution)/shard_map/rows_step/pallas_call | solution.py:22
  24.3 0.4 %collective-permute-done.10.c_ref.refs_7_ = f32[128,256]{1,0:T(8,128)S(1)} collective-permute-done((f32[128,256]{1,0:T(8,128)S(1)}, f32[128,256]{1,0:T(8,128)S(1)}, u32[]{:S(2)}, u32[]{:S(2)}) %collective-permute-start.10) | collective-permute-done | bytes 131104 | tf_op jit(solution)/shard_map/ppermute | solution.py:268
  24.7 0.4 columns_step.25
  25.1 0.6 %collective-permute-start.15 = (f32[128,256]{1,0:T(8,128)S(1)}, f32[128,256]{1,0:T(8,128)S(1)}, u32[]{:S(2)}, u32[]{:S(2)}) collective-permute-start(f32[128,256]{1,0:T(8,128)S(1)} %get-tuple-element.105), channel_id=1, source_target_pairs={{0,4},{4,8},{8,12},{12,16},{16,20},{20,24},{24,28},{28,0},{1,5},{5... | collective-permute-start | bytes 393224 | tf_op jit(solution)/shard_map/ppermute | solution.py:268
  25.7 1.9 %collective-permute-done.9.c_ref.refs_6_ = f32[128,256]{1,0:T(8,128)S(1)} collective-permute-done((f32[128,256]{1,0:T(8,128)S(1)}, f32[128,256]{1,0:T(8,128)S(1)}, u32[]{:S(2)}, u32[]{:S(2)}) %collective-permute-start.9) | collective-permute-done | bytes 131104 | tf_op jit(solution)/shard_map/ppermute | solution.py:268
  27.5 0.4 columns_step.24
  27.9 0.6 %collective-permute-start.14 = (f32[128,256]{1,0:T(8,128)S(1)}, f32[128,256]{1,0:T(8,128)S(1)}, u32[]{:S(2)}, u32[]{:S(2)}) collective-permute-start(f32[128,256]{1,0:T(8,128)S(1)} %get-tuple-element.103), channel_id=1, source_target_pairs={{0,4},{4,8},{8,12},{12,16},{16,20},{20,24},{24,28},{28,0},{1,5},{5... | collective-permute-start | bytes 393224 | tf_op jit(solution)/shard_map/ppermute | solution.py:268
  28.5 1.9 %collective-permute-done.8.c_ref.refs_5_ = f32[128,256]{1,0:T(8,128)S(1)} collective-permute-done((f32[128,256]{1,0:T(8,128)S(1)}, f32[128,256]{1,0:T(8,128)S(1)}, u32[]{:S(2)}, u32[]{:S(2)}) %collective-permute-start.8) | collective-permute-done | bytes 131104 | tf_op jit(solution)/shard_map/ppermute | solution.py:268
  30.3 0.4 columns_step.23
  30.7 0.6 %collective-permute-start.13 = (f32[128,256]{1,0:T(8,128)S(1)}, f32[128,256]{1,0:T(8,128)S(1)}, u32[]{:S(2)}, u32[]{:S(2)}) collective-permute-start(f32[128,256]{1,0:T(8,128)S(1)} %get-tuple-element.101), channel_id=1, source_target_pairs={{0,4},{4,8},{8,12},{12,16},{16,20},{20,24},{24,28},{28,0},{1,5},{5... | collective-permute-start | bytes 393224 | tf_op jit(solution)/shard_map/ppermute | solution.py:268
  31.3 1.9 %collective-permute-done.11.c_ref.refs_8_ = f32[128,256]{1,0:T(8,128)S(1)} collective-permute-done((f32[128,256]{1,0:T(8,128)S(1)}, f32[128,256]{1,0:T(8,128)S(1)}, u32[]{:S(2)}, u32[]{:S(2)}) %collective-permute-start.11) | collective-permute-done | bytes 131104 | tf_op jit(solution)/shard_map/ppermute | solution.py:268
  33.1 0.4 columns_step.26
  33.5 0.2 collective-permute-start.12
  33.7 1.1 %lay_out_tiles.7 = (bf16[512,512]{1,0:T(8,128)(2,1)S(1)}, f32[8,512]{1,0:T(8,128)S(1)}) custom-call(bf16[5,8,128,128]{3,2,1,0:T(8,128)(2,1)S(1)} %copy-done, s32[5,2,8]{2,1,0:T(2,128)S(1)} %bitcast.6, s32[1,5]{1,0:T(1,128)S(1)} %bitcast.11, f32[128,256]{1,0:T(8,128)S(1)} %get-tuple-element.98._), custom_call_target="tpu_custom_call" | custom-call | bytes 1048576 | tf_op jit(solution)/shard_map/lay_out_tiles/pallas_call | solution.py:22
  34.7 0.5 %rows_step.7 = (f32[512,256]{1,0:T(8,128)S(1)}, bf16[512,256]{1,0:T(8,128)(2,1)S(1)}) custom-call(f32[512,256]{1,0:T(8,128)S(1)} %get-tuple-element.84.refs_0_, bf16[128,512]{1,0:T(8,128)(2,1)S(1)} %get-tuple-element.90.refs_1_, bf16[128,512]{1,0:T(8,128)(2,1)S(1)} %get-tuple-element.92.refs_2_, bf16[128,512]{1,0:T(8,128)(2,1)S(1)} %get-tuple-element.94.refs_3_, ...), custom_call_target="tpu_custom_call" | custom-call | flops 134217728 | bytes 1310720 | tf_op jit(solution)/shard_map/rows_step/pallas_call | solution.py:22
  35.2 0.4 columns_step.29
  35.6 0.4 columns_step.28
  36.0 0.4 columns_step.27
  36.4 0.8 %rows_before_last.1 = (f32[512,256]{1,0:T(8,128)S(1)}, f32[512,256]{1,0:T(8,128)}) custom-call(bf16[128,512]{1,0:T(8,128)(2,1)S(1)} %get-tuple-element.102.refs_0_, bf16[128,512]{1,0:T(8,128)(2,1)S(1)} %get-tuple-element.104.refs_1_, bf16[128,512]{1,0:T(8,128)(2,1)S(1)} %get-tuple-element.106.refs_2_, f32[128,256]{1,0:T(8,128)S(1)} %collective-permute-done.13.c_ref.refs_3_, ...), custom_call_target="tpu_custom_call" | custom-call | flops 100663296 | bytes 1048576 | tf_op jit(solution)/shard_map/rows_before_last/pallas_call | solution.py:22
  37.2 1.7 %collective-permute-done.12.c_ref = f32[128,256]{1,0:T(8,128)S(1)} collective-permute-done((f32[128,256]{1,0:T(8,128)S(1)}, f32[128,256]{1,0:T(8,128)S(1)}, u32[]{:S(2)}, u32[]{:S(2)}) %collective-permute-start.12) | collective-permute-done | bytes 131104 | tf_op jit(solution)/shard_map/ppermute | solution.py:268
  38.8 1.3 %last_columns_and_rows.1 = (f32[512,256]{1,0:T(8,128)}, f32[512,256]{1,0:T(8,128)}) custom-call(f32[512,256]{1,0:T(8,128)S(1)} %get-tuple-element.96.u_ref, bf16[512,256]{1,0:T(8,128)(2,1)S(1)} %get-tuple-element.97.row_half, f32[128,256]{1,0:T(8,128)S(1)} %collective-permute-done.12.c_ref, ...), custom_call_target="tpu_custom_call", output_to_operand_aliasing={{1}: (6, {})} | custom-call | flops 100663296 | bytes 1048576 | tf_op jit(solution)/shard_map/last_columns_and_rows/pallas_call | solution.py:22
  (16 shorter events, 0.2 us)
Async XLA Ops:
  0.6 7.2 %copy-start = (bf16[5,8,128,128]{3,2,1,0:T(8,128)(2,1)S(1)}, bf16[5,8,128,128]{3,2,1,0:T(8,128)(2,1)}, u32[]{:S(2)}) copy-start(bf16[5,8,128,128]{3,2,1,0:T(8,128)(2,1)} %x_ref.7) | copy-start | bytes 3932164
  0.6 7.2 %copy-start.2 = (s32[5,1]{0,1:T(1,128)S(1)}, s32[5,1]{0,1:T(1,128)}, u32[]{:S(2)}) copy-start(s32[5,1]{0,1:T(1,128)} %param.9) | copy-start | bytes 64
  0.7 7.2 %copy-start.1 = (s32[5,8,2]{1,2,0:T(2,128)S(1)}, s32[5,8,2]{1,2,0:T(2,128)}, u32[]{:S(2)}) copy-start(s32[5,8,2]{1,2,0:T(2,128)} %param.8) | copy-start | bytes 964
  3.1 6.1 %collective-permute-start.2 = (f32[128,256]{1,0:T(8,128)S(1)}, f32[128,256]{1,0:T(8,128)S(1)}, u32[]{:S(2)}, u32[]{:S(2)}) collective-permute-start(f32[128,256]{1,0:T(8,128)S(1)} %get-tuple-element.69), channel_id=1, source_target_pairs={{0,4},{4,8},{8,12},{12,16},{16,20},{20,24},{24,28},{28,0},{1,5},{5... | collective-permute-start | bytes 393224 | tf_op jit(solution)/shard_map/ppermute | solution.py:268
  3.6 6.9 %collective-permute-start.1 = (f32[128,256]{1,0:T(8,128)S(1)}, f32[128,256]{1,0:T(8,128)S(1)}, u32[]{:S(2)}, u32[]{:S(2)}) collective-permute-start(f32[128,256]{1,0:T(8,128)S(1)} %get-tuple-element.67), channel_id=1, source_target_pairs={{0,4},{4,8},{8,12},{12,16},{16,20},{20,24},{24,28},{28,0},{1,5},{5... | collective-permute-start | bytes 393224 | tf_op jit(solution)/shard_map/ppermute | solution.py:268
  6.2 5.7 %collective-permute-start = (f32[128,256]{1,0:T(8,128)S(1)}, f32[128,256]{1,0:T(8,128)S(1)}, u32[]{:S(2)}, u32[]{:S(2)}) collective-permute-start(f32[128,256]{1,0:T(8,128)S(1)} %get-tuple-element.62), channel_id=1, source_target_pairs={{0,4},{4,8},{8,12},{12,16},{16,20},{20,24},{24,28},{28,0},{1,5},{5... | collective-permute-start | bytes 393224 | tf_op jit(solution)/shard_map/ppermute | solution.py:268
  6.3 7.0 %collective-permute-start.3 = (f32[128,256]{1,0:T(8,128)S(1)}, f32[128,256]{1,0:T(8,128)S(1)}, u32[]{:S(2)}, u32[]{:S(2)}) collective-permute-start(f32[128,256]{1,0:T(8,128)S(1)} %get-tuple-element.63._), channel_id=1, source_target_pairs={{0,4},{4,8},{8,12},{12,16},{16,20},{20,24},{24,28},{28,0},{1,5},{5... | collective-permute-start | bytes 393224 | tf_op jit(solution)/shard_map/ppermute | solution.py:268
  9.6 6.7 %collective-permute-start.6 = (f32[128,256]{1,0:T(8,128)S(1)}, f32[128,256]{1,0:T(8,128)S(1)}, u32[]{:S(2)}, u32[]{:S(2)}) collective-permute-start(f32[128,256]{1,0:T(8,128)S(1)} %get-tuple-element.81), channel_id=1, source_target_pairs={{0,4},{4,8},{8,12},{12,16},{16,20},{20,24},{24,28},{28,0},{1,5},{5... | collective-permute-start | bytes 393224 | tf_op jit(solution)/shard_map/ppermute | solution.py:268
  10.9 7.3 %collective-permute-start.5 = (f32[128,256]{1,0:T(8,128)S(1)}, f32[128,256]{1,0:T(8,128)S(1)}, u32[]{:S(2)}, u32[]{:S(2)}) collective-permute-start(f32[128,256]{1,0:T(8,128)S(1)} %get-tuple-element.79), channel_id=1, source_target_pairs={{0,4},{4,8},{8,12},{12,16},{16,20},{20,24},{24,28},{28,0},{1,5},{5... | collective-permute-start | bytes 393224 | tf_op jit(solution)/shard_map/ppermute | solution.py:268
  12.3 8.2 %collective-permute-start.4 = (f32[128,256]{1,0:T(8,128)S(1)}, f32[128,256]{1,0:T(8,128)S(1)}, u32[]{:S(2)}, u32[]{:S(2)}) collective-permute-start(f32[128,256]{1,0:T(8,128)S(1)} %get-tuple-element.74), channel_id=1, source_target_pairs={{0,4},{4,8},{8,12},{12,16},{16,20},{20,24},{24,28},{28,0},{1,5},{5... | collective-permute-start | bytes 393224 | tf_op jit(solution)/shard_map/ppermute | solution.py:268
  13.7 8.6 %collective-permute-start.7 = (f32[128,256]{1,0:T(8,128)S(1)}, f32[128,256]{1,0:T(8,128)S(1)}, u32[]{:S(2)}, u32[]{:S(2)}) collective-permute-start(f32[128,256]{1,0:T(8,128)S(1)} %get-tuple-element.75._), channel_id=1, source_target_pairs={{0,4},{4,8},{8,12},{12,16},{16,20},{20,24},{24,28},{28,0},{1,5},{5... | collective-permute-start | bytes 393224 | tf_op jit(solution)/shard_map/ppermute | solution.py:268
  16.7 8.0 %collective-permute-start.10 = (f32[128,256]{1,0:T(8,128)S(1)}, f32[128,256]{1,0:T(8,128)S(1)}, u32[]{:S(2)}, u32[]{:S(2)}) collective-permute-start(f32[128,256]{1,0:T(8,128)S(1)} %get-tuple-element.93), channel_id=1, source_target_pairs={{0,1},{1,2},{2,3},{3,0},{4,5},{5,6},{6,7},{7,4},{8,9},{9,10},{10,1... | collective-permute-start | bytes 393224 | tf_op jit(solution)/shard_map/ppermute | solution.py:268
  18.6 8.9 %collective-permute-start.9 = (f32[128,256]{1,0:T(8,128)S(1)}, f32[128,256]{1,0:T(8,128)S(1)}, u32[]{:S(2)}, u32[]{:S(2)}) collective-permute-start(f32[128,256]{1,0:T(8,128)S(1)} %get-tuple-element.91), channel_id=1, source_target_pairs={{0,1},{1,2},{2,3},{3,0},{4,5},{5,6},{6,7},{7,4},{8,9},{9,10},{10,1... | collective-permute-start | bytes 393224 | tf_op jit(solution)/shard_map/ppermute | solution.py:268
  20.9 9.5 %collective-permute-start.8 = (f32[128,256]{1,0:T(8,128)S(1)}, f32[128,256]{1,0:T(8,128)S(1)}, u32[]{:S(2)}, u32[]{:S(2)}) collective-permute-start(f32[128,256]{1,0:T(8,128)S(1)} %get-tuple-element.86), channel_id=1, source_target_pairs={{0,1},{1,2},{2,3},{3,0},{4,5},{5,6},{6,7},{7,4},{8,9},{9,10},{10,1... | collective-permute-start | bytes 393224 | tf_op jit(solution)/shard_map/ppermute | solution.py:268
  22.6 10.5 %collective-permute-start.11 = (f32[128,256]{1,0:T(8,128)S(1)}, f32[128,256]{1,0:T(8,128)S(1)}, u32[]{:S(2)}, u32[]{:S(2)}) collective-permute-start(f32[128,256]{1,0:T(8,128)S(1)} %get-tuple-element.87._), channel_id=1, source_target_pairs={{0,1},{1,2},{2,3},{3,0},{4,5},{5,6},{6,7},{7,4},{8,9},{9,10},{10,1... | collective-permute-start | bytes 393224 | tf_op jit(solution)/shard_map/ppermute | solution.py:268
  25.1 10.1 %collective-permute-start.15 = (f32[128,256]{1,0:T(8,128)S(1)}, f32[128,256]{1,0:T(8,128)S(1)}, u32[]{:S(2)}, u32[]{:S(2)}) collective-permute-start(f32[128,256]{1,0:T(8,128)S(1)} %get-tuple-element.105), channel_id=1, source_target_pairs={{0,4},{4,8},{8,12},{12,16},{16,20},{20,24},{24,28},{28,0},{1,5},{5... | collective-permute-start | bytes 393224 | tf_op jit(solution)/shard_map/ppermute | solution.py:268
  27.9 7.7 %collective-permute-start.14 = (f32[128,256]{1,0:T(8,128)S(1)}, f32[128,256]{1,0:T(8,128)S(1)}, u32[]{:S(2)}, u32[]{:S(2)}) collective-permute-start(f32[128,256]{1,0:T(8,128)S(1)} %get-tuple-element.103), channel_id=1, source_target_pairs={{0,4},{4,8},{8,12},{12,16},{16,20},{20,24},{24,28},{28,0},{1,5},{5... | collective-permute-start | bytes 393224 | tf_op jit(solution)/shard_map/ppermute | solution.py:268
  30.7 5.3 %collective-permute-start.13 = (f32[128,256]{1,0:T(8,128)S(1)}, f32[128,256]{1,0:T(8,128)S(1)}, u32[]{:S(2)}, u32[]{:S(2)}) collective-permute-start(f32[128,256]{1,0:T(8,128)S(1)} %get-tuple-element.101), channel_id=1, source_target_pairs={{0,4},{4,8},{8,12},{12,16},{16,20},{20,24},{24,28},{28,0},{1,5},{5... | collective-permute-start | bytes 393224 | tf_op jit(solution)/shard_map/ppermute | solution.py:268
  33.5 5.3 %collective-permute-start.12 = (f32[128,256]{1,0:T(8,128)S(1)}, f32[128,256]{1,0:T(8,128)S(1)}, u32[]{:S(2)}, u32[]{:S(2)}) collective-permute-start(f32[128,256]{1,0:T(8,128)S(1)} %get-tuple-element.98._), channel_id=1, source_target_pairs={{0,4},{4,8},{8,12},{12,16},{16,20},{20,24},{24,28},{28,0},{1,5},{5... | collective-permute-start | bytes 393224 | tf_op jit(solution)/shard_map/ppermute | solution.py:268

commit v4 on v3

--- a/solution.py
+++ b/solution.py
@@ -42,17 +42,16 @@
 
 def scatter(stratum, values, coords, counts, dense, live):
     listed, tile, _ = values.shape
-    dense[...] = jnp.zeros_like(dense)
-    live[...] = jnp.zeros_like(live)
+    col = lax.broadcasted_iota(jnp.int32, live.shape, 0)
+    row = lax.broadcasted_iota(jnp.int32, live.shape, 1)
+    named = jnp.zeros(live.shape, jnp.float32)
     for t in range(listed):
-
-        @pl.when(t < counts[0, stratum])
-        def _():
-            r = pl.multiple_of(coords[stratum, 0, t] * tile, tile)
-            c = coords[stratum, 1, t]
-            dense[pl.ds(pl.multiple_of(c * tile, tile), tile), pl.ds(r, tile)] = values[t].T
-            named = lax.broadcasted_iota(jnp.int32, (SUBLANES, tile), 0) == c
-            live[:, pl.ds(r, tile)] = jnp.where(named, 1.0, live[:, pl.ds(r, tile)])
+        r = pl.multiple_of(coords[stratum, 0, t] * tile, tile)
+        c = coords[stratum, 1, t]
+        dense[pl.ds(pl.multiple_of(c * tile, tile), tile), pl.ds(r, tile)] = values[t].T
+        alive_c = jnp.where(t < counts[0, stratum], c, -1)
+        named = jnp.where((col == alive_c) & (row >= r) & (row < r + tile), 1.0, named)
+    live[...] = named
 
 
 def sgd(old, grad):
@@ -209,18 +208,20 @@
 def last_kernel(tile, u_ref, row_half, c_ref, dense, live, acc, _, u_hbm, c_hbm, u_new, c_new, sems):
     h, width = CHUNKS - 1, c_ref.shape[0]
     cols = c_ref[...]
-    residue, c_new[...] = columns_step(
+    residue, new_cols = columns_step(
         h * width // tile, tile, row_half[...], cols, dense[span(h, width)], live
     )
-    copies = [pltpu.make_async_copy(c_new, c_hbm.at[pl.ds(h * width, width)], sems.at[0])]
-    copies[0].start()
+    copies = []
     col_half = cols.astype(jnp.bfloat16)
     for r in range(u_ref.shape[0] // tile):
         part, place = span(r, tile), pl.ds(r * tile, tile)
         grad = dot(residue[:, part], col_half, ((0,), (0,)))
         u_new[part] = sgd(u_ref[part], acc[part] + grad)
-        copies.append(pltpu.make_async_copy(u_new.at[place], u_hbm.at[place], sems.at[r + 1]))
+        copies.append(pltpu.make_async_copy(u_new.at[place], u_hbm.at[place], sems.at[r]))
         copies[-1].start()
+    c_new[...] = new_cols
+    copies.append(pltpu.make_async_copy(c_new, c_hbm.at[pl.ds(h * width, width)], sems.at[len(copies)]))
+    copies[-1].start()
     for copy in copies:
         copy.wait()
 

time: 40.1 us -> 40.1 us (level)
  waiting for transfers between devices: 9.2 us -> 10.9 us
  Pallas kernels: 15.6 us -> 14.6 us
  starting transfers between devices: 14.4 us -> 13.5 us
    ppermute x16, waiting for transfers between devices: 9.2 us -> 10.9 us  [shifted(): return lax.ppermute(chunk, axis, [(i, (i + 1) % n) for i in range(n)])]
    pallas_call x26, Pallas kernels: 15.6 us -> 14.6 us  [call(): pl.pallas_call(body, out_shape=outs, in_specs=in_specs, out_specs=out_spe...]
    ppermute x16, starting transfers between devices: 14.4 us -> 13.5 us  [shifted(): return lax.ppermute(chunk, axis, [(i, (i + 1) % n) for i in range(n)])]
  transfers between devices with their start and end apart: 16 -> 16, of which waited for: 9 -> 10; matrix products, arithmetic and copies ran while one was open for 0% -> 0% of each run, Pallas kernels for 30% -> 27%
where the time goes in v4:
time: 40.1 us; the launch traced here: 40 us
  Pallas kernels  14.6 us (36%)
  starting transfers between devices  13.5 us (34%)
  waiting for transfers between devices  10.9 us (27%)
  between operations  0.9 us (2%)
    pallas_call x26, Pallas kernels, call(): pl.pallas_call(body, out_shape=outs, in_specs=in_specs, out_specs=out_spe...  14.6 us
    ppermute x16, starting transfers between devices, shifted(): return lax.ppermute(chunk, axis, [(i, (i + 1) % n) for i in range(n)])  13.5 us
    ppermute x16, waiting for transfers between devices, shifted(): return lax.ppermute(chunk, axis, [(i, (i + 1) % n) for i in range(n)])  10.9 us
  transfers between devices with their start and end apart: 16, of which 10 were waited for; matrix products, arithmetic and copies ran while one was open for 0% of the time, Pallas kernels for 27%

profile of v4, /device:TPU:0, one launch (start us, length us, event | category | flops | bytes accessed | tf_op | source)
XLA Modules:
  0.0 40.0 jit_solution(16040697124965424612)
XLA Ops:
  0.7 2.4 %first_columns.1 = (f32[512,256]{1,0:T(8,128)S(1)}, f32[512,256]{1,0:T(8,128)S(1)}, bf16[512,512]{1,0:T(8,128)(2,1)S(1)}, f32[128,256]{1,0:T(8,128)S(1)}, f32[12...) custom-call(f32[512,256]{1,0:T(8,128)} %u_hbm.1, f32[512,256]{1,0:T(8,128)} %c_hbm.1, ...), custom_call_target="tpu_custom_call" | custom-call | flops 268435456 | bytes 1048576 | tf_op jit(solution)/shard_map/first_columns/pallas_call | solution.py:22
  3.1 0.5 %collective-permute-start.2 = (f32[128,256]{1,0:T(8,128)S(1)}, f32[128,256]{1,0:T(8,128)S(1)}, u32[]{:S(2)}, u32[]{:S(2)}) collective-permute-start(f32[128,256]{1,0:T(8,128)S(1)} %get-tuple-element.69), channel_id=1, source_target_pairs={{0,4},{4,8},{8,12},{12,16},{16,20},{20,24},{24,28},{28,0},{1,5},{5... | collective-permute-start | bytes 393224 | tf_op jit(solution)/shard_map/ppermute | solution.py:269
  3.6 2.6 %collective-permute-start.1 = (f32[128,256]{1,0:T(8,128)S(1)}, f32[128,256]{1,0:T(8,128)S(1)}, u32[]{:S(2)}, u32[]{:S(2)}) collective-permute-start(f32[128,256]{1,0:T(8,128)S(1)} %get-tuple-element.67), channel_id=1, source_target_pairs={{0,4},{4,8},{8,12},{12,16},{16,20},{20,24},{24,28},{28,0},{1,5},{5... | collective-permute-start | bytes 393224 | tf_op jit(solution)/shard_map/ppermute | solution.py:269
  6.3 1.5 %collective-permute-start.3 = (f32[128,256]{1,0:T(8,128)S(1)}, f32[128,256]{1,0:T(8,128)S(1)}, u32[]{:S(2)}, u32[]{:S(2)}) collective-permute-start(f32[128,256]{1,0:T(8,128)S(1)} %get-tuple-element.63._), channel_id=1, source_target_pairs={{0,4},{4,8},{8,12},{12,16},{16,20},{20,24},{24,28},{28,0},{1,5},{5... | collective-permute-start | bytes 393224 | tf_op jit(solution)/shard_map/ppermute | solution.py:269
  7.8 0.8 %lay_out_tiles.4 = (bf16[512,512]{1,0:T(8,128)(2,1)S(1)}, f32[8,512]{1,0:T(8,128)S(1)}) custom-call(bf16[5,8,128,128]{3,2,1,0:T(8,128)(2,1)S(1)} %copy-done, s32[5,2,8]{2,1,0:T(2,128)S(1)} %bitcast.3, s32[1,5]{1,0:T(1,128)S(1)} %bitcast.8, f32[128,256]{1,0:T(8,128)S(1)} %get-tuple-element.63._), custom_call_target="tpu_custom_call" | custom-call | bytes 1048576 | tf_op jit(solution)/shard_map/lay_out_tiles/pallas_call | solution.py:22
  8.6 0.4 rows_step.4
  9.1 0.4 columns_step.17
  9.6 1.0 %collective-permute-done.1.c_ref.refs_6_ = f32[128,256]{1,0:T(8,128)S(1)} collective-permute-done((f32[128,256]{1,0:T(8,128)S(1)}, f32[128,256]{1,0:T(8,128)S(1)}, u32[]{:S(2)}, u32[]{:S(2)}) %collective-permute-start.1) | collective-permute-done | bytes 131104 | tf_op jit(solution)/shard_map/ppermute | solution.py:269
  10.5 0.4 columns_step.16
  10.9 0.5 %collective-permute-start.5 = (f32[128,256]{1,0:T(8,128)S(1)}, f32[128,256]{1,0:T(8,128)S(1)}, u32[]{:S(2)}, u32[]{:S(2)}) collective-permute-start(f32[128,256]{1,0:T(8,128)S(1)} %get-tuple-element.79), channel_id=1, source_target_pairs={{0,4},{4,8},{8,12},{12,16},{16,20},{20,24},{24,28},{28,0},{1,5},{5... | collective-permute-start | bytes 393224 | tf_op jit(solution)/shard_map/ppermute | solution.py:269
  11.4 0.5 %collective-permute-done.c_ref.refs_5_ = f32[128,256]{1,0:T(8,128)S(1)} collective-permute-done((f32[128,256]{1,0:T(8,128)S(1)}, f32[128,256]{1,0:T(8,128)S(1)}, u32[]{:S(2)}, u32[]{:S(2)}) %collective-permute-start) | collective-permute-done | bytes 131104 | tf_op jit(solution)/shard_map/ppermute | solution.py:269
  11.9 0.4 columns_step.15
  12.3 0.5 %collective-permute-start.4 = (f32[128,256]{1,0:T(8,128)S(1)}, f32[128,256]{1,0:T(8,128)S(1)}, u32[]{:S(2)}, u32[]{:S(2)}) collective-permute-start(f32[128,256]{1,0:T(8,128)S(1)} %get-tuple-element.74), channel_id=1, source_target_pairs={{0,4},{4,8},{8,12},{12,16},{16,20},{20,24},{24,28},{28,0},{1,5},{5... | collective-permute-start | bytes 393224 | tf_op jit(solution)/shard_map/ppermute | solution.py:269
  12.8 0.5 %collective-permute-done.3.c_ref.refs_8_ = f32[128,256]{1,0:T(8,128)S(1)} collective-permute-done((f32[128,256]{1,0:T(8,128)S(1)}, f32[128,256]{1,0:T(8,128)S(1)}, u32[]{:S(2)}, u32[]{:S(2)}) %collective-permute-start.3) | collective-permute-done | bytes 131104 | tf_op jit(solution)/shard_map/ppermute | solution.py:269
  13.3 0.4 columns_step.18
  13.7 1.1 %collective-permute-start.7 = (f32[128,256]{1,0:T(8,128)S(1)}, f32[128,256]{1,0:T(8,128)S(1)}, u32[]{:S(2)}, u32[]{:S(2)}) collective-permute-start(f32[128,256]{1,0:T(8,128)S(1)} %get-tuple-element.75._), channel_id=1, source_target_pairs={{0,4},{4,8},{8,12},{12,16},{16,20},{20,24},{24,28},{28,0},{1,5},{5... | collective-permute-start | bytes 393224 | tf_op jit(solution)/shard_map/ppermute | solution.py:269
  14.8 0.7 %lay_out_tiles.5 = (bf16[512,512]{1,0:T(8,128)(2,1)S(1)}, f32[8,512]{1,0:T(8,128)S(1)}) custom-call(bf16[5,8,128,128]{3,2,1,0:T(8,128)(2,1)S(1)} %copy-done, s32[5,2,8]{2,1,0:T(2,128)S(1)} %bitcast.4, s32[1,5]{1,0:T(1,128)S(1)} %bitcast.9, f32[128,256]{1,0:T(8,128)S(1)} %get-tuple-element.75._), custom_call_target="tpu_custom_call" | custom-call | bytes 1048576 | tf_op jit(solution)/shard_map/lay_out_tiles/pallas_call | solution.py:22
  15.5 0.5 %rows_step.5 = (f32[512,256]{1,0:T(8,128)S(1)}, bf16[512,256]{1,0:T(8,128)(2,1)S(1)}) custom-call(f32[512,256]{1,0:T(8,128)S(1)} %get-tuple-element.60.refs_0_, bf16[128,512]{1,0:T(8,128)(2,1)S(1)} %get-tuple-element.66.refs_1_, bf16[128,512]{1,0:T(8,128)(2,1)S(1)} %get-tuple-element.68.refs_2_, bf16[128,512]{1,0:T(8,128)(2,1)S(1)} %get-tuple-element.70.refs_3_, ...), custom_call_target="tpu_custom_call" | custom-call | flops 134217728 | bytes 1310720 | tf_op jit(solution)/shard_map/rows_step/pallas_call | solution.py:22
  16.0 0.4 columns_step.21
  16.4 1.6 %collective-permute-start.10 = (f32[128,256]{1,0:T(8,128)S(1)}, f32[128,256]{1,0:T(8,128)S(1)}, u32[]{:S(2)}, u32[]{:S(2)}) collective-permute-start(f32[128,256]{1,0:T(8,128)S(1)} %get-tuple-element.93), channel_id=1, source_target_pairs={{0,1},{1,2},{2,3},{3,0},{4,5},{5,6},{6,7},{7,4},{8,9},{9,10},{10,1... | collective-permute-start | bytes 393224 | tf_op jit(solution)/shard_map/ppermute | solution.py:269
  18.0 0.4 columns_step.20
  18.4 1.6 %collective-permute-start.9 = (f32[128,256]{1,0:T(8,128)S(1)}, f32[128,256]{1,0:T(8,128)S(1)}, u32[]{:S(2)}, u32[]{:S(2)}) collective-permute-start(f32[128,256]{1,0:T(8,128)S(1)} %get-tuple-element.91), channel_id=1, source_target_pairs={{0,1},{1,2},{2,3},{3,0},{4,5},{5,6},{6,7},{7,4},{8,9},{9,10},{10,1... | collective-permute-start | bytes 393224 | tf_op jit(solution)/shard_map/ppermute | solution.py:269
  20.0 0.4 columns_step.19
  20.4 1.6 %collective-permute-start.8 = (f32[128,256]{1,0:T(8,128)S(1)}, f32[128,256]{1,0:T(8,128)S(1)}, u32[]{:S(2)}, u32[]{:S(2)}) collective-permute-start(f32[128,256]{1,0:T(8,128)S(1)} %get-tuple-element.86), channel_id=1, source_target_pairs={{0,1},{1,2},{2,3},{3,0},{4,5},{5,6},{6,7},{7,4},{8,9},{9,10},{10,1... | collective-permute-start | bytes 393224 | tf_op jit(solution)/shard_map/ppermute | solution.py:269
  22.0 0.4 columns_step.22
  22.4 0.6 %collective-permute-start.11 = (f32[128,256]{1,0:T(8,128)S(1)}, f32[128,256]{1,0:T(8,128)S(1)}, u32[]{:S(2)}, u32[]{:S(2)}) collective-permute-start(f32[128,256]{1,0:T(8,128)S(1)} %get-tuple-element.87._), channel_id=1, source_target_pairs={{0,1},{1,2},{2,3},{3,0},{4,5},{5,6},{6,7},{7,4},{8,9},{9,10},{10,1... | collective-permute-start | bytes 393224 | tf_op jit(solution)/shard_map/ppermute | solution.py:269
  23.0 0.7 %lay_out_tiles.6 = (bf16[512,512]{1,0:T(8,128)(2,1)S(1)}, f32[8,512]{1,0:T(8,128)S(1)}) custom-call(bf16[5,8,128,128]{3,2,1,0:T(8,128)(2,1)S(1)} %copy-done, s32[5,2,8]{2,1,0:T(2,128)S(1)} %bitcast.5, s32[1,5]{1,0:T(1,128)S(1)} %bitcast.10, f32[128,256]{1,0:T(8,128)S(1)} %get-tuple-element.87._), custom_call_target="tpu_custom_call" | custom-call | bytes 1048576 | tf_op jit(solution)/shard_map/lay_out_tiles/pallas_call | solution.py:22
  23.7 0.5 %rows_step.6 = (f32[512,256]{1,0:T(8,128)S(1)}, bf16[512,256]{1,0:T(8,128)(2,1)S(1)}) custom-call(f32[512,256]{1,0:T(8,128)S(1)} %get-tuple-element.72.refs_0_, bf16[128,512]{1,0:T(8,128)(2,1)S(1)} %get-tuple-element.78.refs_1_, bf16[128,512]{1,0:T(8,128)(2,1)S(1)} %get-tuple-element.80.refs_2_, bf16[128,512]{1,0:T(8,128)(2,1)S(1)} %get-tuple-element.82.refs_3_, ...), custom_call_target="tpu_custom_call" | custom-call | flops 134217728 | bytes 1310720 | tf_op jit(solution)/shard_map/rows_step/pallas_call | solution.py:22
  24.2 0.3 collective-permute-done.10.c_ref.refs_7_
  24.5 0.4 columns_step.25
  24.9 0.3 collective-permute-start.15
  25.2 2.1 %collective-permute-done.9.c_ref.refs_6_ = f32[128,256]{1,0:T(8,128)S(1)} collective-permute-done((f32[128,256]{1,0:T(8,128)S(1)}, f32[128,256]{1,0:T(8,128)S(1)}, u32[]{:S(2)}, u32[]{:S(2)}) %collective-permute-start.9) | collective-permute-done | bytes 131104 | tf_op jit(solution)/shard_map/ppermute | solution.py:269
  27.3 0.4 columns_step.24
  27.7 0.3 collective-permute-start.14
  28.0 2.1 %collective-permute-done.8.c_ref.refs_5_ = f32[128,256]{1,0:T(8,128)S(1)} collective-permute-done((f32[128,256]{1,0:T(8,128)S(1)}, f32[128,256]{1,0:T(8,128)S(1)}, u32[]{:S(2)}, u32[]{:S(2)}) %collective-permute-start.8) | collective-permute-done | bytes 131104 | tf_op jit(solution)/shard_map/ppermute | solution.py:269
  30.1 0.4 columns_step.23
  30.5 0.3 collective-permute-start.13
  30.8 2.1 %collective-permute-done.11.c_ref.refs_8_ = f32[128,256]{1,0:T(8,128)S(1)} collective-permute-done((f32[128,256]{1,0:T(8,128)S(1)}, f32[128,256]{1,0:T(8,128)S(1)}, u32[]{:S(2)}, u32[]{:S(2)}) %collective-permute-start.11) | collective-permute-done | bytes 131104 | tf_op jit(solution)/shard_map/ppermute | solution.py:269
  33.0 0.4 columns_step.26
  33.5 0.7 %lay_out_tiles.7 = (bf16[512,512]{1,0:T(8,128)(2,1)S(1)}, f32[8,512]{1,0:T(8,128)S(1)}) custom-call(bf16[5,8,128,128]{3,2,1,0:T(8,128)(2,1)S(1)} %copy-done, s32[5,2,8]{2,1,0:T(2,128)S(1)} %bitcast.6, s32[1,5]{1,0:T(1,128)S(1)} %bitcast.11, f32[128,256]{1,0:T(8,128)S(1)} %get-tuple-element.98._), custom_call_target="tpu_custom_call" | custom-call | bytes 1048576 | tf_op jit(solution)/shard_map/lay_out_tiles/pallas_call | solution.py:22
  34.2 0.5 %rows_step.7 = (f32[512,256]{1,0:T(8,128)S(1)}, bf16[512,256]{1,0:T(8,128)(2,1)S(1)}) custom-call(f32[512,256]{1,0:T(8,128)S(1)} %get-tuple-element.84.refs_0_, bf16[128,512]{1,0:T(8,128)(2,1)S(1)} %get-tuple-element.90.refs_1_, bf16[128,512]{1,0:T(8,128)(2,1)S(1)} %get-tuple-element.92.refs_2_, bf16[128,512]{1,0:T(8,128)(2,1)S(1)} %get-tuple-element.94.refs_3_, ...), custom_call_target="tpu_custom_call" | custom-call | flops 134217728 | bytes 1310720 | tf_op jit(solution)/shard_map/rows_step/pallas_call | solution.py:22
  34.7 0.4 columns_step.29
  35.1 0.4 columns_step.28
  35.5 0.4 collective-permute-done.13.c_ref.refs_3_
  35.9 0.4 columns_step.27
  36.2 0.8 %rows_before_last.1 = (f32[512,256]{1,0:T(8,128)S(1)}, f32[512,256]{1,0:T(8,128)}) custom-call(bf16[128,512]{1,0:T(8,128)(2,1)S(1)} %get-tuple-element.102.refs_0_, bf16[128,512]{1,0:T(8,128)(2,1)S(1)} %get-tuple-element.104.refs_1_, bf16[128,512]{1,0:T(8,128)(2,1)S(1)} %get-tuple-element.106.refs_2_, f32[128,256]{1,0:T(8,128)S(1)} %collective-permute-done.13.c_ref.refs_3_, ...), custom_call_target="tpu_custom_call" | custom-call | flops 100663296 | bytes 1048576 | tf_op jit(solution)/shard_map/rows_before_last/pallas_call | solution.py:22
  37.0 1.7 %collective-permute-done.12.c_ref = f32[128,256]{1,0:T(8,128)S(1)} collective-permute-done((f32[128,256]{1,0:T(8,128)S(1)}, f32[128,256]{1,0:T(8,128)S(1)}, u32[]{:S(2)}, u32[]{:S(2)}) %collective-permute-start.12) | collective-permute-done | bytes 131104 | tf_op jit(solution)/shard_map/ppermute | solution.py:269
  38.7 1.3 %last_columns_and_rows.1 = (f32[512,256]{1,0:T(8,128)}, f32[512,256]{1,0:T(8,128)}) custom-call(f32[512,256]{1,0:T(8,128)S(1)} %get-tuple-element.96.u_ref, bf16[512,256]{1,0:T(8,128)(2,1)S(1)} %get-tuple-element.97.row_half, f32[128,256]{1,0:T(8,128)S(1)} %collective-permute-done.12.c_ref, ...), custom_call_target="tpu_custom_call", output_to_operand_aliasing={{1}: (6, {})} | custom-call | flops 100663296 | bytes 1048576 | tf_op jit(solution)/shard_map/last_columns_and_rows/pallas_call | solution.py:22
  (16 shorter events, 0.5 us)
Async XLA Ops:
  0.6 7.2 %copy-start = (bf16[5,8,128,128]{3,2,1,0:T(8,128)(2,1)S(1)}, bf16[5,8,128,128]{3,2,1,0:T(8,128)(2,1)}, u32[]{:S(2)}) copy-start(bf16[5,8,128,128]{3,2,1,0:T(8,128)(2,1)} %x_ref.7) | copy-start | bytes 3932164
  0.6 7.2 %copy-start.2 = (s32[5,1]{0,1:T(1,128)S(1)}, s32[5,1]{0,1:T(1,128)}, u32[]{:S(2)}) copy-start(s32[5,1]{0,1:T(1,128)} %param.9) | copy-start | bytes 64
  0.7 7.2 %copy-start.1 = (s32[5,8,2]{1,2,0:T(2,128)S(1)}, s32[5,8,2]{1,2,0:T(2,128)}, u32[]{:S(2)}) copy-start(s32[5,8,2]{1,2,0:T(2,128)} %param.8) | copy-start | bytes 964
  3.1 6.0 %collective-permute-start.2 = (f32[128,256]{1,0:T(8,128)S(1)}, f32[128,256]{1,0:T(8,128)S(1)}, u32[]{:S(2)}, u32[]{:S(2)}) collective-permute-start(f32[128,256]{1,0:T(8,128)S(1)} %get-tuple-element.69), channel_id=1, source_target_pairs={{0,4},{4,8},{8,12},{12,16},{16,20},{20,24},{24,28},{28,0},{1,5},{5... | collective-permute-start | bytes 393224 | tf_op jit(solution)/shard_map/ppermute | solution.py:269
  3.6 6.9 %collective-permute-start.1 = (f32[128,256]{1,0:T(8,128)S(1)}, f32[128,256]{1,0:T(8,128)S(1)}, u32[]{:S(2)}, u32[]{:S(2)}) collective-permute-start(f32[128,256]{1,0:T(8,128)S(1)} %get-tuple-element.67), channel_id=1, source_target_pairs={{0,4},{4,8},{8,12},{12,16},{16,20},{20,24},{24,28},{28,0},{1,5},{5... | collective-permute-start | bytes 393224 | tf_op jit(solution)/shard_map/ppermute | solution.py:269
  6.2 5.7 %collective-permute-start = (f32[128,256]{1,0:T(8,128)S(1)}, f32[128,256]{1,0:T(8,128)S(1)}, u32[]{:S(2)}, u32[]{:S(2)}) collective-permute-start(f32[128,256]{1,0:T(8,128)S(1)} %get-tuple-element.62), channel_id=1, source_target_pairs={{0,4},{4,8},{8,12},{12,16},{16,20},{20,24},{24,28},{28,0},{1,5},{5... | collective-permute-start | bytes 393224 | tf_op jit(solution)/shard_map/ppermute | solution.py:269
  6.3 7.1 %collective-permute-start.3 = (f32[128,256]{1,0:T(8,128)S(1)}, f32[128,256]{1,0:T(8,128)S(1)}, u32[]{:S(2)}, u32[]{:S(2)}) collective-permute-start(f32[128,256]{1,0:T(8,128)S(1)} %get-tuple-element.63._), channel_id=1, source_target_pairs={{0,4},{4,8},{8,12},{12,16},{16,20},{20,24},{24,28},{28,0},{1,5},{5... | collective-permute-start | bytes 393224 | tf_op jit(solution)/shard_map/ppermute | solution.py:269
  9.5 6.5 %collective-permute-start.6 = (f32[128,256]{1,0:T(8,128)S(1)}, f32[128,256]{1,0:T(8,128)S(1)}, u32[]{:S(2)}, u32[]{:S(2)}) collective-permute-start(f32[128,256]{1,0:T(8,128)S(1)} %get-tuple-element.81), channel_id=1, source_target_pairs={{0,4},{4,8},{8,12},{12,16},{16,20},{20,24},{24,28},{28,0},{1,5},{5... | collective-permute-start | bytes 393224 | tf_op jit(solution)/shard_map/ppermute | solution.py:269
  10.9 7.1 %collective-permute-start.5 = (f32[128,256]{1,0:T(8,128)S(1)}, f32[128,256]{1,0:T(8,128)S(1)}, u32[]{:S(2)}, u32[]{:S(2)}) collective-permute-start(f32[128,256]{1,0:T(8,128)S(1)} %get-tuple-element.79), channel_id=1, source_target_pairs={{0,4},{4,8},{8,12},{12,16},{16,20},{20,24},{24,28},{28,0},{1,5},{5... | collective-permute-start | bytes 393224 | tf_op jit(solution)/shard_map/ppermute | solution.py:269
  12.3 7.7 %collective-permute-start.4 = (f32[128,256]{1,0:T(8,128)S(1)}, f32[128,256]{1,0:T(8,128)S(1)}, u32[]{:S(2)}, u32[]{:S(2)}) collective-permute-start(f32[128,256]{1,0:T(8,128)S(1)} %get-tuple-element.74), channel_id=1, source_target_pairs={{0,4},{4,8},{8,12},{12,16},{16,20},{20,24},{24,28},{28,0},{1,5},{5... | collective-permute-start | bytes 393224 | tf_op jit(solution)/shard_map/ppermute | solution.py:269
  13.7 8.3 %collective-permute-start.7 = (f32[128,256]{1,0:T(8,128)S(1)}, f32[128,256]{1,0:T(8,128)S(1)}, u32[]{:S(2)}, u32[]{:S(2)}) collective-permute-start(f32[128,256]{1,0:T(8,128)S(1)} %get-tuple-element.75._), channel_id=1, source_target_pairs={{0,4},{4,8},{8,12},{12,16},{16,20},{20,24},{24,28},{28,0},{1,5},{5... | collective-permute-start | bytes 393224 | tf_op jit(solution)/shard_map/ppermute | solution.py:269
  16.4 8.1 %collective-permute-start.10 = (f32[128,256]{1,0:T(8,128)S(1)}, f32[128,256]{1,0:T(8,128)S(1)}, u32[]{:S(2)}, u32[]{:S(2)}) collective-permute-start(f32[128,256]{1,0:T(8,128)S(1)} %get-tuple-element.93), channel_id=1, source_target_pairs={{0,1},{1,2},{2,3},{3,0},{4,5},{5,6},{6,7},{7,4},{8,9},{9,10},{10,1... | collective-permute-start | bytes 393224 | tf_op jit(solution)/shard_map/ppermute | solution.py:269
  18.4 9.0 %collective-permute-start.9 = (f32[128,256]{1,0:T(8,128)S(1)}, f32[128,256]{1,0:T(8,128)S(1)}, u32[]{:S(2)}, u32[]{:S(2)}) collective-permute-start(f32[128,256]{1,0:T(8,128)S(1)} %get-tuple-element.91), channel_id=1, source_target_pairs={{0,1},{1,2},{2,3},{3,0},{4,5},{5,6},{6,7},{7,4},{8,9},{9,10},{10,1... | collective-permute-start | bytes 393224 | tf_op jit(solution)/shard_map/ppermute | solution.py:269
  20.4 9.8 %collective-permute-start.8 = (f32[128,256]{1,0:T(8,128)S(1)}, f32[128,256]{1,0:T(8,128)S(1)}, u32[]{:S(2)}, u32[]{:S(2)}) collective-permute-start(f32[128,256]{1,0:T(8,128)S(1)} %get-tuple-element.86), channel_id=1, source_target_pairs={{0,1},{1,2},{2,3},{3,0},{4,5},{5,6},{6,7},{7,4},{8,9},{9,10},{10,1... | collective-permute-start | bytes 393224 | tf_op jit(solution)/shard_map/ppermute | solution.py:269
  22.4 10.6 %collective-permute-start.11 = (f32[128,256]{1,0:T(8,128)S(1)}, f32[128,256]{1,0:T(8,128)S(1)}, u32[]{:S(2)}, u32[]{:S(2)}) collective-permute-start(f32[128,256]{1,0:T(8,128)S(1)} %get-tuple-element.87._), channel_id=1, source_target_pairs={{0,1},{1,2},{2,3},{3,0},{4,5},{5,6},{6,7},{7,4},{8,9},{9,10},{10,1... | collective-permute-start | bytes 393224 | tf_op jit(solution)/shard_map/ppermute | solution.py:269
  24.9 9.8 %collective-permute-start.15 = (f32[128,256]{1,0:T(8,128)S(1)}, f32[128,256]{1,0:T(8,128)S(1)}, u32[]{:S(2)}, u32[]{:S(2)}) collective-permute-start(f32[128,256]{1,0:T(8,128)S(1)} %get-tuple-element.105), channel_id=1, source_target_pairs={{0,4},{4,8},{8,12},{12,16},{16,20},{20,24},{24,28},{28,0},{1,5},{5... | collective-permute-start | bytes 393224 | tf_op jit(solution)/shard_map/ppermute | solution.py:269
  27.7 7.4 %collective-permute-start.14 = (f32[128,256]{1,0:T(8,128)S(1)}, f32[128,256]{1,0:T(8,128)S(1)}, u32[]{:S(2)}, u32[]{:S(2)}) collective-permute-start(f32[128,256]{1,0:T(8,128)S(1)} %get-tuple-element.103), channel_id=1, source_target_pairs={{0,4},{4,8},{8,12},{12,16},{16,20},{20,24},{24,28},{28,0},{1,5},{5... | collective-permute-start | bytes 393224 | tf_op jit(solution)/shard_map/ppermute | solution.py:269
  30.5 5.3 %collective-permute-start.13 = (f32[128,256]{1,0:T(8,128)S(1)}, f32[128,256]{1,0:T(8,128)S(1)}, u32[]{:S(2)}, u32[]{:S(2)}) collective-permute-start(f32[128,256]{1,0:T(8,128)S(1)} %get-tuple-element.101), channel_id=1, source_target_pairs={{0,4},{4,8},{8,12},{12,16},{16,20},{20,24},{24,28},{28,0},{1,5},{5... | collective-permute-start | bytes 393224 | tf_op jit(solution)/shard_map/ppermute | solution.py:269
  33.3 5.3 %collective-permute-start.12 = (f32[128,256]{1,0:T(8,128)S(1)}, f32[128,256]{1,0:T(8,128)S(1)}, u32[]{:S(2)}, u32[]{:S(2)}) collective-permute-start(f32[128,256]{1,0:T(8,128)S(1)} %get-tuple-element.98._), channel_id=1, source_target_pairs={{0,4},{4,8},{8,12},{12,16},{16,20},{20,24},{24,28},{28,0},{1,5},{5... | collective-permute-start | bytes 393224 | tf_op jit(solution)/shard_map/ppermute | solution.py:269

commit v5 on v4

v5 whole, which is shorter than its diff:
```python
import functools

import jax
import jax.numpy as jnp
from jax import lax
from jax.experimental import pallas as pl
from jax.experimental.pallas import tpu as pltpu
from jax.sharding import PartitionSpec as P

LEARN_RATE = 0.03
DECAY_RATE = 0.1
CHUNKS = 2
SUBLANES = 8
EVEN, ODD = 0, 1

VMEM = pl.BlockSpec(memory_space=pltpu.VMEM)
SMEM = pl.BlockSpec(memory_space=pltpu.SMEM)
HBM = pl.BlockSpec(memory_space=pltpu.HBM)
ANY = pl.BlockSpec(memory_space=pl.ANY)


def call(body, name, operands, in_specs, outs, out_specs, flops=0, moved=0, aliases=None, scratch=()):
    return pl.pallas_call(
        body,
        out_shape=outs,
        in_specs=in_specs,
        out_specs=out_specs,
        input_output_aliases=aliases or {},
        scratch_shapes=list(scratch),
        compiler_params=pltpu.CompilerParams(vmem_limit_bytes=24 * 1024 * 1024),
        cost_estimate=pl.CostEstimate(flops=flops, bytes_accessed=moved, transcendentals=0),
        name=name,
    )(*operands)


class Line:
    def __init__(self, turn):
        self.turn = turn

    def call(self, body, name, operands, outs, flops=0, moved=0, aliases=None, held=()):
        through = (self.turn, *held)
        n_in, n_out, n_through = len(operands), len(outs), len(through)
        aliases = dict(aliases or {})
        for i in range(n_through):
            aliases[n_in + i] = n_out + i

        def inner(*refs):
            body(*refs[:n_in], *refs[n_in + n_through : n_in + n_through + n_out])

        out = call(
            inner,
            name,
            (*operands, *through),
            [VMEM] * (n_in + n_through),
            [*outs, *map(like, through)],
            [VMEM] * (n_out + n_through),
            flops,
            moved,
            aliases,
        )
        self.turn = out[n_out]
        return tuple(out[:n_out]) + tuple(out[n_out + 1 :])


def like(array, shape=None, dtype=None):
    return jax.ShapeDtypeStruct(shape or array.shape, dtype or array.dtype)


def span(h, width):
    return slice(h * width, (h + 1) * width)


def scatter(stratum, values, coords, counts, dense, live):
    listed, tile, _ = values.shape
    col = lax.broadcasted_iota(jnp.int32, live.shape, 0)
    row = lax.broadcasted_iota(jnp.int32, live.shape, 1)
    named = jnp.zeros(live.shape, jnp.float32)
    for t in range(listed):
        r = pl.multiple_of(coords[stratum, 0, t] * tile, tile)
        c = coords[stratum, 1, t]
        dense[pl.ds(pl.multiple_of(c * tile, tile), tile), pl.ds(r, tile)] = values[t].T
        alive_c = jnp.where(t < counts[0, stratum], c, -1)
        named = jnp.where((col == alive_c) & (row >= r) & (row < r + tile), 1.0, named)
    live[...] = named


def sgd(old, grad):
    return old + LEARN_RATE * (grad - DECAY_RATE * old)


def dot(a, b, contract):
    return lax.dot_general(a, b, (contract, ((), ())), preferred_element_type=jnp.float32)


def columns_step(first_tile, tile, row_half, cols, dense, live):
    col_half = cols.astype(jnp.bfloat16)
    estimate = dot(col_half, row_half, ((1,), (1,)))
    parts = []
    for i in range(cols.shape[0] // tile):
        at = span(i, tile)
        residue = dense[at].astype(jnp.float32) - estimate[at]
        named = live[first_tile + i : first_tile + i + 1] > 0
        parts.append(jnp.where(named, residue, 0.0).astype(jnp.bfloat16))
    residue = parts[0] if len(parts) == 1 else jnp.concatenate(parts, axis=0)
    return residue, col_half, sgd(cols, dot(residue, row_half, ((1,), (0,))))


def rows_gradient(residues, halves):
    return sum(dot(e[...], c[...], ((0,), (0,))) for e, c in zip(residues, halves))


def odd_device():
    return lax.axis_index("blk") % 2 == ODD


def when_parity(parity, body):
    if parity is None:
        body()
    else:
        pl.when(odd_device() == (parity == ODD))(body)


def first_kernel(u_hbm, c_hbm, x_hbm, coords_hbm, counts_hbm, *refs):
    u_ref, half_ref, col_half, residue, turn, whole = refs[:6]
    c_outs = refs[6 : 6 + CHUNKS]
    dense, live, c_ref, x_ref, coords, counts, sems = refs[6 + CHUNKS :]
    turn[...] = jnp.zeros_like(turn)
    tile = x_ref.shape[1]
    pairs = [(coords_hbm, coords), (counts_hbm, counts), (x_hbm.at[0], x_ref)]
    pairs += [(u_hbm, u_ref), (c_hbm, c_ref)]
    copies = [pltpu.make_async_copy(s, d, sems.at[i]) for i, (s, d) in enumerate(pairs)]
    for copy in copies:
        copy.start()
    for copy in copies[:3]:
        copy.wait()
    scatter(0, x_ref, coords, counts, dense, live)
    for copy in copies[3:]:
        copy.wait()
    row_half = u_ref[...].astype(jnp.bfloat16)
    half_ref[...] = row_half
    for h in range(CHUNKS):
        at = span(h, c_ref.shape[0] // CHUNKS)
        first_tile = at.start // tile
        residue[at], col_half[at], new = columns_step(
            first_tile, tile, row_half, c_ref[at], dense[at], live
        )
        c_outs[h][...] = new
        whole[at] = new


def first(u, c, values, coords, counts):
    rows, cols = u.shape[0], c.shape[0]
    part = (cols // CHUNKS, c.shape[1])
    halves = [like(u, dtype=jnp.bfloat16), like(c, dtype=jnp.bfloat16)]
    outs = [like(u), *halves, like(u, (cols, rows), jnp.bfloat16)]
    outs += [like(u, (SUBLANES, 128)), like(c)] + [like(c, part)] * CHUNKS
    operands = (u, c, values, coords, counts)
    return call(
        first_kernel,
        "first_columns",
        [pltpu.with_memory_space_constraint(x, pltpu.HBM) for x in operands],
        [HBM] * 5,
        outs,
        [VMEM] * len(outs),
        flops=4 * u.size * cols,
        moved=8 * u.size,
        scratch=[
            pltpu.VMEM((cols, rows), jnp.bfloat16),
            pltpu.VMEM((SUBLANES, rows), jnp.float32),
            pltpu.VMEM(c.shape, c.dtype),
            pltpu.VMEM(values.shape[1:], values.dtype),
            pltpu.SMEM(coords.shape, coords.dtype),
            pltpu.SMEM(counts.shape, counts.dtype),
            pltpu.SemaphoreType.DMA((5,)),
        ],
    )


def layout_kernel(x_ref, coords, counts, *refs):
    outs = refs[4:]
    later = len(outs) // 2
    for s in range(later):
        scatter(s + 1, x_ref.at[s + 1], coords, counts, outs[s], outs[later + s])


def layout(line, values, coords, counts, rows, cols, held):
    later = values.shape[0] - 1
    outs = [like(values, (cols, rows))] * later
    outs += [like(values, (SUBLANES, rows), jnp.float32)] * later
    line.turn, held, *out = call(
        layout_kernel,
        "lay_out_tiles",
        (values, coords, counts, line.turn, held),
        [VMEM, SMEM, SMEM, VMEM, VMEM],
        [like(line.turn), like(held), *outs],
        [VMEM] * (2 + len(outs)),
        moved=4 * later * rows * cols,
        aliases={3: 0, 4: 1},
    )
    return list(zip(out[:later], out[later:])), held


def choose(cs):
    return jnp.where(odd_device(), cs[ODD][...], cs[EVEN][...]) if len(cs) > 1 else cs[0][...]


def columns_kernel(h, tile, parity, row_half, dense, live, *refs):
    *cs, c_out, residue, col_half = refs

    def body():
        cols = choose(cs)
        at = span(h, cols.shape[0])
        residue[...], col_half[...], c_out[...] = columns_step(
            at.start // tile, tile, row_half[...], cols, dense[at], live
        )

    when_parity(parity, body)


def columns(line, h, tile, row_half, cs, laid, parity=None, held=()):
    c = cs[0]
    return line.call(
        functools.partial(columns_kernel, h, tile, parity),
        "columns_step",
        (row_half, *laid, *cs),
        [like(c), like(row_half, (c.shape[0], row_half.shape[0])), like(c, dtype=jnp.bfloat16)],
        flops=4 * row_half.size * c.shape[0],
        moved=2 * row_half.size + 8 * c.size,
        held=held,
    )


def rows_kernel(parity, _, __, *refs):
    *pairs, u_out, half_out = refs
    n = len(pairs) // 2

    def body():
        u_new = sgd(u_out[...], rows_gradient(pairs[:n], pairs[n:]))
        u_out[...] = u_new
        half_out[...] = u_new.astype(jnp.bfloat16)

    when_parity(parity, body)


def rows(line, u, row_half, residues, halves, parity=None, held=()):
    return line.call(
        functools.partial(rows_kernel, parity),
        "rows_step",
        (u, row_half, *residues, *halves),
        [like(u), like(row_half)],
        flops=2 * u.size * sum(c.shape[0] for c in halves),
        moved=10 * u.size,
        aliases={0: 0, 1: 1},
        held=held,
    )


def whole_kernel(tile, parity, _, __, dense, live, c_ref, u_out, half_out, *c_outs):
    def body():
        row_half = half_out[...]
        cols = c_ref[...]
        residue, col_half, new = columns_step(0, tile, row_half, cols, dense[...], live)
        for h, c_out in enumerate(c_outs):
            c_out[...] = new[span(h, c_out.shape[0])]
        u_new = sgd(u_out[...], dot(residue, col_half, ((0,), (0,))))
        u_out[...] = u_new
        half_out[...] = u_new.astype(jnp.bfloat16)

    when_parity(parity, body)


def whole_stratum(line, tile, u, row_half, c, laid, parity):
    u, row_half, *cs = line.call(
        functools.partial(whole_kernel, tile, parity),
        "whole_stratum",
        (u, row_half, *laid, c),
        [like(u), like(row_half)] + [like(c, (c.shape[0] // CHUNKS, c.shape[1]))] * CHUNKS,
        flops=6 * u.size * c.shape[0],
        moved=16 * u.size,
        aliases={0: 0, 1: 1},
    )
    return u, row_half, cs


def last_kernel(tile, u_ref, row_half, dense, live, even_c, odd_c, done, residue, half, _, u_hbm, c_hbm, u_new, c_new, sems):
    width = even_c.shape[0]
    h = c_hbm.shape[0] // width - 1
    copies = []

    def copy(source, target, at):
        place = pl.ds(at, source.shape[0])
        copies.append(pltpu.make_async_copy(source, target.at[place], sems.at[len(copies)]))
        copies[-1].start()

    copy(done, c_hbm, 0)
    last_residue, last_half, new_cols = columns_step(
        h * width // tile, tile, row_half[...], choose((even_c, odd_c)), dense[span(h, width)], live
    )
    for r in range(u_ref.shape[0] // tile):
        part = span(r, tile)
        grad = dot(residue[:, part], half[...], ((0,), (0,)))
        grad = grad + dot(last_residue[:, part], last_half, ((0,), (0,)))
        u_new[part] = sgd(u_ref[part], grad)
        copy(u_new.at[pl.ds(r * tile, tile)], u_hbm, r * tile)
    c_new[...] = new_cols
    copy(c_new, c_hbm, h * width)
    for started in copies:
        started.wait()


def final(line, tile, u, row_half, cs, laid):
    width, rank = cs[0][0].shape
    done, residue, half, held = columns(line, 0, tile, row_half, cs[0], laid, held=(cs[1][0],))
    return call(
        functools.partial(last_kernel, tile),
        "last_columns_and_rows",
        (u, row_half, *laid, held, cs[1][1], done, residue, half, line.turn),
        [VMEM] * 10,
        [like(u), like(u, (CHUNKS * width, rank))],
        [HBM, HBM],
        flops=6 * u.size * width,
        moved=8 * u.size,
        scratch=[
            pltpu.VMEM(u.shape, u.dtype),
            pltpu.VMEM((width, rank), u.dtype),
            pltpu.SemaphoreType.DMA((CHUNKS + u.shape[0] // tile,)),
        ],
    )


def ring(chunk):
    n = lax.axis_size("blk")
    return lax.ppermute(chunk, "blk", [(i, (i + 1) % n) for i in range(n)])


def swap(chunk):
    return lax.ppermute(chunk, "blk", [(i, i ^ 1) for i in range(lax.axis_size("blk"))])


def along_group(chunk, parity):
    blk, groups = lax.axis_size("blk"), lax.axis_size("group")
    route = []
    for b in range(blk):
        for g in range(groups):
            to = (g + 1) % groups if b % 2 == parity else g
            route.append((b * groups + g, b * groups + to))
    return lax.ppermute(chunk, ("blk", "group"), route)


def per_device(row_factors, col_factors, tile_values, tile_coords, tile_counts):
    tile = tile_values.shape[2]
    coords, counts = tile_coords.transpose(0, 2, 1), tile_counts.transpose(1, 0)
    sizes = row_factors.shape[0], col_factors.shape[0]
    u, row_half, half, residue, turn, whole, *done = first(
        row_factors, col_factors, tile_values, coords, counts
    )
    line = Line(turn)
    b1 = [ring(d) for d in done]
    laid, whole = layout(line, tile_values, coords, counts, *sizes, whole)
    a1 = swap(whole)
    step = functools.partial(columns, line)
    u, row_half = rows(line, u, row_half, [residue], [half])

    e1_0 = step(0, tile, row_half, b1[:1], laid[0], EVEN)
    a2_0 = swap(e1_0[0])
    u, row_half, o1 = whole_stratum(line, tile, u, row_half, a1, laid[0], ODD)
    b2 = [ring(d) for d in o1]
    e1_1 = step(1, tile, row_half, b1[1:], laid[0], EVEN)
    a2_1 = swap(e1_1[0])
    o2_0 = step(0, tile, row_half, (a2_0,), laid[1], ODD)
    zo_0 = along_group(o2_0[0], ODD)
    u, row_half = rows(line, u, row_half, (e1_0[1], e1_1[1]), (e1_0[2], e1_1[2]), EVEN)

    e2_0 = step(0, tile, row_half, b2[:1], laid[1], EVEN)
    ze_0 = along_group(e2_0[0], EVEN)
    o2_1 = step(1, tile, row_half, (a2_1,), laid[1], ODD)
    zo_1 = along_group(o2_1[0], ODD)
    u, row_half = rows(line, u, row_half, (o2_0[1], o2_1[1]), (o2_0[2], o2_1[2]), ODD)

    e2_1 = step(1, tile, row_half, b2[1:], laid[1], EVEN)
    ze_1 = along_group(e2_1[0], EVEN)
    o3_0 = step(0, tile, row_half, (zo_0,), laid[2], ODD)
    b4_0 = ring(o3_0[0])
    u, row_half = rows(line, u, row_half, (e2_0[1], e2_1[1]), (e2_0[2], e2_1[2]), EVEN)

    o3_1 = step(1, tile, row_half, (zo_1,), laid[2], ODD)
    b4_1 = ring(o3_1[0])
    u, row_half = rows(line, u, row_half, (o3_0[1], o3_1[1]), (o3_0[2], o3_1[2]), ODD)
    e3_0 = step(0, tile, row_half, (ze_0,), laid[2], EVEN)
    a4_0 = swap(e3_0[0])
    e3_1 = step(1, tile, row_half, (ze_1,), laid[2], EVEN)
    a4_1 = swap(e3_1[0])
    u, row_half = rows(line, u, row_half, (e3_0[1], e3_1[1]), (e3_0[2], e3_1[2]), EVEN)
    return final(line, tile, u, row_half, ((b4_0, a4_0), (b4_1, a4_1)), laid[3])


def solution(mesh):
    return jax.shard_map(
        per_device,
        mesh=mesh,
        in_specs=(
            P(("blk", "group"), None),
            P(("blk", "group"), None),
            P(None, ("blk", "group"), None, None),
            P(None, ("blk", "group"), None),
            P(None, ("blk", "group")),
        ),
        out_specs=(P(("blk", "group"), None), P(("blk", "group"), None)),
        check_vma=False,
    )
```

time: 40.1 us -> 40.9 us (1.020)
  Pallas kernels: 14.6 us -> 9.13 us
  starting transfers between devices: 13.5 us -> 17 us
  waiting for transfers between devices: 10.9 us -> 13.6 us
    pallas_call x26 -> x21, Pallas kernels: 14.6 us -> 9.13 us  [call(): pl.pallas_call(body, out_shape=outs, in_specs=in_specs, out_specs=out_spe...]
    ppermute x16 -> x15, starting transfers between devices: 13.5 us -> 17 us  [the longest x4 8.46 us: along_group(): return lax.ppermute(chunk, ('blk', 'group'), route)]
    ppermute x16 -> x15, waiting for transfers between devices: 10.9 us -> 13.6 us  [the longest x6 10.9 us: ring(): return lax.ppermute(chunk, 'blk', [(i, (i + 1) % n) for i in range(n)])]
  transfers between devices with their start and end apart: 16 -> 15, of which waited for: 10 -> 6; matrix products, arithmetic and copies ran while one was open for 0% -> 0% of each run, Pallas kernels for 27% -> 12%
where the time goes in v5:
time: 40.9 us; the launch traced here: 40.7 us
  starting transfers between devices  17 us (42%)
  waiting for transfers between devices  13.6 us (33%)
  Pallas kernels  9.13 us (22%)
  between operations  0.95 us (2%)
    ppermute x6, waiting for transfers between devices, ring(): return lax.ppermute(chunk, 'blk', [(i, (i + 1) % n) for i in range(n)])  10.9 us
    pallas_call x21, Pallas kernels, call(): pl.pallas_call(body, out_shape=outs, in_specs=in_specs, out_specs=out_spe...  9.13 us
    ppermute x4, starting transfers between devices, along_group(): return lax.ppermute(chunk, ('blk', 'group'), route)  8.46 us
    ppermute x6, starting transfers between devices, ring(): return lax.ppermute(chunk, 'blk', [(i, (i + 1) % n) for i in range(n)])  7.75 us
    ppermute x4, waiting for transfers between devices, along_group(): return lax.ppermute(chunk, ('blk', 'group'), route)  2.67 us
  transfers between devices with their start and end apart: 15, of which 6 were waited for; matrix products, arithmetic and copies ran while one was open for 0% of the time, Pallas kernels for 12%

profile of v5, /device:TPU:0, one launch (start us, length us, event | category | flops | bytes accessed | tf_op | source)
XLA Modules:
  0.0 40.7 jit_solution(10454112694820336179)
XLA Ops:
  0.6 0.0 copy-start
  0.6 0.0 copy-start.2
  0.7 0.0 copy-start.1
  0.7 2.0 %first_columns.1 = (f32[512,256]{1,0:T(8,128)S(1)}, bf16[512,256]{1,0:T(8,128)(2,1)S(1)}, bf16[512,256]{1,0:T(8,128)(2,1)S(1)}, bf16[512,512]{1,0:T(8,128)(2,1)S...) custom-call(f32[512,256]{1,0:T(8,128)} %u_hbm.1, ...), custom_call_target="tpu_custom_call" | custom-call | flops 268435456 | bytes 1048576 | tf_op jit(solution)/shard_map/first_columns/pallas_call | solution.py:23
  2.7 0.0 copy-done
  2.7 1.0 %lay_out_tiles.1 = (f32[8,128]{1,0:T(8,128)S(1)}, f32[512,256]{1,0:T(8,128)S(1)}, bf16[512,512]{1,0:T(8,128)(2,1)S(1)}, bf16[512,512]{1,0:T(8,128)(2,1)S(1)}, bf...) custom-call(bf16[5,8,128,128]{3,2,1,0:T(8,128)(2,1)S(1)} %copy-done,, ...), custom_call_target="tpu_custom_call", output_to_operand_aliasing={{0}: (3, {}), {1}: (4, {})} | custom-call | bytes 4194304 | tf_op jit(solution)/shard_map/lay_out_tiles/pallas_call | solution.py:23
  3.7 0.5 %collective-permute-start = (f32[512,256]{1,0:T(8,128)S(1)}, f32[512,256]{1,0:T(8,128)S(1)}, u32[]{:S(2)}, u32[]{:S(2)}) collective-permute-start(f32[512,256]{1,0:T(8,128)S(1)} %get-tuple-element.99), channel_id=1, source_target_pairs={{0,4},{4,0},{8,12},{12,8},{16,20},{20,16},{24,28},{28,24},{1,5},{5... | collective-permute-start | bytes 1572872 | tf_op jit(solution)/shard_map/ppermute | solution.py:337
  4.2 0.1 collective-permute-start.1
  4.3 2.6 %collective-permute-start.2 = (f32[256,256]{1,0:T(8,128)S(1)}, f32[256,256]{1,0:T(8,128)S(1)}, u32[]{:S(2)}, u32[]{:S(2)}) collective-permute-start(f32[256,256]{1,0:T(8,128)S(1)} %get-tuple-element.106), channel_id=1, source_target_pairs={{0,4},{4,8},{8,12},{12,16},{16,20},{20,24},{24,28},{28,0},{1,5},{5... | collective-permute-start | bytes 786440 | tf_op jit(solution)/shard_map/ppermute | solution.py:333
  6.9 0.3 rows_step.6
  7.2 4.6 %collective-permute-done.1.refs_3_ = f32[256,256]{1,0:T(8,128)S(1)} collective-permute-done((f32[256,256]{1,0:T(8,128)S(1)}, f32[256,256]{1,0:T(8,128)S(1)}, u32[]{:S(2)}, u32[]{:S(2)}) %collective-permute-start.1) | collective-permute-done | bytes 262176 | tf_op jit(solution)/shard_map/ppermute | solution.py:333
  11.8 0.4 %columns_step.11 = (f32[256,256]{1,0:T(8,128)S(1)}, bf16[256,512]{1,0:T(8,128)(2,1)S(1)}, bf16[256,256]{1,0:T(8,128)(2,1)S(1)}, f32[8,128]{1,0:T(8,128)S(1)}) custom-call(bf16[512,256]{1,0:T(8,128)(2,1)S(1)} %get-tuple-element.96.refs_0_.refs_1_, bf16[512,512]{1,0:T(8,128)(2,1)S(1)} %get-tuple-element.97.refs_1_.refs_2_, ...), custom_call_target="tpu_custom_call", output_to_operand_aliasing={{3}: (4, {})} | custom-call | flops 134217728 | bytes 786432 | tf_op jit(solution)/shard_map/columns_step/pallas_call | solution.py:23
  12.3 0.1 collective-permute-start.3
  12.3 0.0 collective-permute-done.refs_4_
  12.4 1.2 %collective-permute-start.5 = (f32[256,256]{1,0:T(8,128)S(1)}, f32[256,256]{1,0:T(8,128)S(1)}, u32[]{:S(2)}, u32[]{:S(2)}) collective-permute-start(f32[256,256]{1,0:T(8,128)S(1)} %get-tuple-element.120), channel_id=1, source_target_pairs={{0,4},{4,8},{8,12},{12,16},{16,20},{20,24},{24,28},{28,0},{1,5},{5... | collective-permute-start | bytes 786440 | tf_op jit(solution)/shard_map/ppermute | solution.py:333
  13.6 1.0 %collective-permute-done.2.refs_3_ = f32[256,256]{1,0:T(8,128)S(1)} collective-permute-done((f32[256,256]{1,0:T(8,128)S(1)}, f32[256,256]{1,0:T(8,128)S(1)}, u32[]{:S(2)}, u32[]{:S(2)}) %collective-permute-start.2) | collective-permute-done | bytes 262176 | tf_op jit(solution)/shard_map/ppermute | solution.py:333
  14.6 0.4 %columns_step.12 = (f32[256,256]{1,0:T(8,128)S(1)}, bf16[256,512]{1,0:T(8,128)(2,1)S(1)}, bf16[256,256]{1,0:T(8,128)(2,1)S(1)}, f32[8,128]{1,0:T(8,128)S(1)}) custom-call(bf16[512,256]{1,0:T(8,128)(2,1)S(1)} %get-tuple-element.104.refs_0_.refs_1_, bf16[512,512]{1,0:T(8,128)(2,1)S(1)} %get-tuple-element.97.refs_1_.refs_2_, ...), custom_call_target="tpu_custom_call", output_to_operand_aliasing={{3}: (4, {})} | custom-call | flops 134217728 | bytes 786432 | tf_op jit(solution)/shard_map/columns_step/pallas_call | solution.py:23
  15.1 0.1 collective-permute-start.4
  15.1 0.5 %collective-permute-start.6 = (f32[256,256]{1,0:T(8,128)S(1)}, f32[256,256]{1,0:T(8,128)S(1)}, u32[]{:S(2)}, u32[]{:S(2)}) collective-permute-start(f32[256,256]{1,0:T(8,128)S(1)} %get-tuple-element.130), channel_id=1, source_target_pairs={{0,4},{4,8},{8,12},{12,16},{16,20},{20,24},{24,28},{28,0},{1,5},{5... | collective-permute-start | bytes 786440 | tf_op jit(solution)/shard_map/ppermute | solution.py:333
  15.6 0.0 collective-permute-done.3.refs_3_
  15.6 0.7 %collective-permute-start.7 = (f32[256,256]{1,0:T(8,128)S(1)}, f32[256,256]{1,0:T(8,128)S(1)}, u32[]{:S(2)}, u32[]{:S(2)}) collective-permute-start(f32[256,256]{1,0:T(8,128)S(1)} %get-tuple-element.137), channel_id=1, source_target_pairs={{0,0},{1,1},{2,2},{3,3},{4,5},{5,6},{6,7},{7,4},{8,8},{9,9},{10,10... | collective-permute-start | bytes 786440 | tf_op jit(solution)/shard_map/ppermute | solution.py:347
  16.3 0.4 rows_step.7
  16.7 2.4 %collective-permute-done.5.refs_3_ = f32[256,256]{1,0:T(8,128)S(1)} collective-permute-done((f32[256,256]{1,0:T(8,128)S(1)}, f32[256,256]{1,0:T(8,128)S(1)}, u32[]{:S(2)}, u32[]{:S(2)}) %collective-permute-start.5) | collective-permute-done | bytes 262176 | tf_op jit(solution)/shard_map/ppermute | solution.py:333
  19.1 0.4 %columns_step.14 = (f32[256,256]{1,0:T(8,128)S(1)}, bf16[256,512]{1,0:T(8,128)(2,1)S(1)}, bf16[256,256]{1,0:T(8,128)(2,1)S(1)}, f32[8,128]{1,0:T(8,128)S(1)}) custom-call(bf16[512,256]{1,0:T(8,128)(2,1)S(1)} %get-tuple-element.117.refs_0_.refs_1_, bf16[512,512]{1,0:T(8,128)(2,1)S(1)} %get-tuple-element.111.refs_1_, ...), custom_call_target="tpu_custom_call", output_to_operand_aliasing={{3}: (4, {})} | custom-call | flops 134217728 | bytes 786432 | tf_op jit(solution)/shard_map/columns_step/pallas_call | solution.py:23
  19.6 0.0 collective-permute-done.4.refs_3_
  19.6 0.7 %collective-permute-start.8 = (f32[256,256]{1,0:T(8,128)S(1)}, f32[256,256]{1,0:T(8,128)S(1)}, u32[]{:S(2)}, u32[]{:S(2)}) collective-permute-start(f32[256,256]{1,0:T(8,128)S(1)} %get-tuple-element.143), channel_id=1, source_target_pairs={{0,0},{1,1},{2,2},{3,3},{4,5},{5,6},{6,7},{7,4},{8,8},{9,9},{10,10... | collective-permute-start | bytes 786440 | tf_op jit(solution)/shard_map/ppermute | solution.py:347
  20.3 3.6 %collective-permute-start.9 = (f32[256,256]{1,0:T(8,128)S(1)}, f32[256,256]{1,0:T(8,128)S(1)}, u32[]{:S(2)}, u32[]{:S(2)}) collective-permute-start(f32[256,256]{1,0:T(8,128)S(1)} %get-tuple-element.151), channel_id=1, source_target_pairs={{0,1},{1,2},{2,3},{3,0},{4,4},{5,5},{6,6},{7,7},{8,9},{9,10},{10,1... | collective-permute-start | bytes 786440 | tf_op jit(solution)/shard_map/ppermute | solution.py:347
  24.0 0.0 collective-permute-done.6.refs_3_
  24.0 0.5 %columns_step.16 = (f32[256,256]{1,0:T(8,128)S(1)}, bf16[256,512]{1,0:T(8,128)(2,1)S(1)}, bf16[256,256]{1,0:T(8,128)(2,1)S(1)}, f32[8,128]{1,0:T(8,128)S(1)}) custom-call(bf16[512,256]{1,0:T(8,128)(2,1)S(1)} %get-tuple-element.128.refs_0_.refs_1_, bf16[512,512]{1,0:T(8,128)(2,1)S(1)} %get-tuple-element.111.refs_1_, ...), custom_call_target="tpu_custom_call", output_to_operand_aliasing={{3}: (4, {})} | custom-call | flops 134217728 | bytes 786432 | tf_op jit(solution)/shard_map/columns_step/pallas_call | solution.py:23
  24.5 3.5 %collective-permute-start.10 = (f32[256,256]{1,0:T(8,128)S(1)}, f32[256,256]{1,0:T(8,128)S(1)}, u32[]{:S(2)}, u32[]{:S(2)}) collective-permute-start(f32[256,256]{1,0:T(8,128)S(1)} %get-tuple-element.154), channel_id=1, source_target_pairs={{0,1},{1,2},{2,3},{3,0},{4,4},{5,5},{6,6},{7,7},{8,9},{9,10},{10,1... | collective-permute-start | bytes 786440 | tf_op jit(solution)/shard_map/ppermute | solution.py:347
  28.0 0.0 collective-permute-done.7.refs_3_
  28.0 0.1 collective-permute-start.11
  28.1 0.4 rows_step.9
  28.4 0.0 collective-permute-done.8.refs_3_
  28.5 3.3 %collective-permute-start.13 = (f32[256,256]{1,0:T(8,128)S(1)}, f32[256,256]{1,0:T(8,128)S(1)}, u32[]{:S(2)}, u32[]{:S(2)}) collective-permute-start(f32[256,256]{1,0:T(8,128)S(1)} %get-tuple-element.167), channel_id=1, source_target_pairs={{0,4},{4,8},{8,12},{12,16},{16,20},{20,24},{24,28},{28,0},{1,5},{5... | collective-permute-start | bytes 786440 | tf_op jit(solution)/shard_map/ppermute | solution.py:333
  31.8 0.4 collective-permute-done.9.refs_3_
  32.2 0.4 %columns_step.19 = (f32[256,256]{1,0:T(8,128)S(1)}, bf16[256,512]{1,0:T(8,128)(2,1)S(1)}, bf16[256,256]{1,0:T(8,128)(2,1)S(1)}, f32[8,128]{1,0:T(8,128)S(1)}) custom-call(bf16[512,256]{1,0:T(8,128)(2,1)S(1)} %get-tuple-element.150.refs_0_.refs_1_, bf16[512,512]{1,0:T(8,128)(2,1)S(1)} %get-tuple-element.135.refs_1_, ...), custom_call_target="tpu_custom_call", output_to_operand_aliasing={{3}: (4, {})} | custom-call | flops 134217728 | bytes 786432 | tf_op jit(solution)/shard_map/columns_step/pallas_call | solution.py:23
  32.6 0.1 collective-permute-start.12
  32.7 2.3 %collective-permute-done.10.refs_3_ = f32[256,256]{1,0:T(8,128)S(1)} collective-permute-done((f32[256,256]{1,0:T(8,128)S(1)}, f32[256,256]{1,0:T(8,128)S(1)}, u32[]{:S(2)}, u32[]{:S(2)}) %collective-permute-start.10) | collective-permute-done | bytes 262176 | tf_op jit(solution)/shard_map/ppermute | solution.py:347
  35.0 0.4 %columns_step.20 = (f32[256,256]{1,0:T(8,128)S(1)}, bf16[256,512]{1,0:T(8,128)(2,1)S(1)}, bf16[256,256]{1,0:T(8,128)(2,1)S(1)}, f32[8,128]{1,0:T(8,128)S(1)}) custom-call(bf16[512,256]{1,0:T(8,128)(2,1)S(1)} %get-tuple-element.150.refs_0_.refs_1_, bf16[512,512]{1,0:T(8,128)(2,1)S(1)} %get-tuple-element.135.refs_1_, ...), custom_call_target="tpu_custom_call", output_to_operand_aliasing={{3}: (4, {})} | custom-call | flops 134217728 | bytes 786432 | tf_op jit(solution)/shard_map/columns_step/pallas_call | solution.py:23
  35.4 0.1 collective-permute-start.14
  35.5 0.4 rows_step.11
  35.9 0.0 collective-permute-done.11.refs_3_
  35.9 2.9 %collective-permute-done.13.refs_6_ = f32[256,256]{1,0:T(8,128)S(1)} collective-permute-done((f32[256,256]{1,0:T(8,128)S(1)}, f32[256,256]{1,0:T(8,128)S(1)}, u32[]{:S(2)}, u32[]{:S(2)}) %collective-permute-start.13) | collective-permute-done | bytes 262176 | tf_op jit(solution)/shard_map/ppermute | solution.py:333
  38.8 0.0 collective-permute-done.12.refs_4_
  38.8 0.4 %columns_step.21 = (f32[256,256]{1,0:T(8,128)S(1)}, bf16[256,512]{1,0:T(8,128)(2,1)S(1)}, bf16[256,256]{1,0:T(8,128)(2,1)S(1)}, f32[8,128]{1,0:T(8,128)S(1)}, f32[256,256]{1,0:T(8,128)S(1)}) custom-call(bf16[512,256]{1,0:T(8,128)(2,1)S(1)} %get-tuple-element.161.refs_0_.row_half, ...), custom_call_target="tpu_custom_call", output_to_operand_aliasing={{3}: (5, {}), {4}: (6, {})} | custom-call | flops 134217728 | bytes 786432 | tf_op jit(solution)/shard_map/columns_step/pallas_call | solution.py:23
  39.2 0.0 collective-permute-done.14.odd_c
  39.2 1.5 %last_columns_and_rows.1 = (f32[512,256]{1,0:T(8,128)}, f32[512,256]{1,0:T(8,128)}) custom-call(f32[512,256]{1,0:T(8,128)S(1)} %get-tuple-element.160.u_ref, bf16[512,256]{1,0:T(8,128)(2,1)S(1)} %get-tuple-element.161.refs_0_.row_half, bf16[512,512]{1,0:T(8,128)(2,1)S(1)} %get-tuple-element.162.refs_1_.dense, f32[8,512]{1,0:T(8,128)S(1)} %get-tuple-element.163.refs_2_.live, ...), custom_call_target="tpu_custom_call" | custom-call | flops 201326592 | bytes 1048576 | tf_op jit(solution)/shard_map/last_columns_and_rows/pallas_call | solution.py:23
  (9 shorter events, 0.1 us)
Async XLA Ops:
  0.6 2.0 %copy-start = (bf16[5,8,128,128]{3,2,1,0:T(8,128)(2,1)S(1)}, bf16[5,8,128,128]{3,2,1,0:T(8,128)(2,1)}, u32[]{:S(2)}) copy-start(bf16[5,8,128,128]{3,2,1,0:T(8,128)(2,1)} %x_ref.1) | copy-start | bytes 3932164
  0.6 2.0 %copy-start.2 = (s32[5,1]{0,1:T(1,128)S(1)}, s32[5,1]{0,1:T(1,128)}, u32[]{:S(2)}) copy-start(s32[5,1]{0,1:T(1,128)} %param.9) | copy-start | bytes 64
  0.7 2.0 %copy-start.1 = (s32[5,8,2]{1,2,0:T(2,128)S(1)}, s32[5,8,2]{1,2,0:T(2,128)}, u32[]{:S(2)}) copy-start(s32[5,8,2]{1,2,0:T(2,128)} %param.8) | copy-start | bytes 964
  3.7 8.7 %collective-permute-start = (f32[512,256]{1,0:T(8,128)S(1)}, f32[512,256]{1,0:T(8,128)S(1)}, u32[]{:S(2)}, u32[]{:S(2)}) collective-permute-start(f32[512,256]{1,0:T(8,128)S(1)} %get-tuple-element.99), channel_id=1, source_target_pairs={{0,4},{4,0},{8,12},{12,8},{16,20},{20,16},{24,28},{28,24},{1,5},{5... | collective-permute-start | bytes 1572872 | tf_op jit(solution)/shard_map/ppermute | solution.py:337
  4.2 7.6 %collective-permute-start.1 = (f32[256,256]{1,0:T(8,128)S(1)}, f32[256,256]{1,0:T(8,128)S(1)}, u32[]{:S(2)}, u32[]{:S(2)}) collective-permute-start(f32[256,256]{1,0:T(8,128)S(1)} %get-tuple-element.100), channel_id=1, source_target_pairs={{0,4},{4,8},{8,12},{12,16},{16,20},{20,24},{24,28},{28,0},{1,5},{5... | collective-permute-start | bytes 786440 | tf_op jit(solution)/shard_map/ppermute | solution.py:333
  4.3 10.4 %collective-permute-start.2 = (f32[256,256]{1,0:T(8,128)S(1)}, f32[256,256]{1,0:T(8,128)S(1)}, u32[]{:S(2)}, u32[]{:S(2)}) collective-permute-start(f32[256,256]{1,0:T(8,128)S(1)} %get-tuple-element.106), channel_id=1, source_target_pairs={{0,4},{4,8},{8,12},{12,16},{16,20},{20,24},{24,28},{28,0},{1,5},{5... | collective-permute-start | bytes 786440 | tf_op jit(solution)/shard_map/ppermute | solution.py:333
  12.3 3.4 %collective-permute-start.3 = (f32[256,256]{1,0:T(8,128)S(1)}, f32[256,256]{1,0:T(8,128)S(1)}, u32[]{:S(2)}, u32[]{:S(2)}) collective-permute-start(f32[256,256]{1,0:T(8,128)S(1)} %get-tuple-element.113), channel_id=1, source_target_pairs={{0,4},{4,0},{8,12},{12,8},{16,20},{20,16},{24,28},{28,24},{1,5},{5... | collective-permute-start | bytes 786440 | tf_op jit(solution)/shard_map/ppermute | solution.py:337
  12.4 6.7 %collective-permute-start.5 = (f32[256,256]{1,0:T(8,128)S(1)}, f32[256,256]{1,0:T(8,128)S(1)}, u32[]{:S(2)}, u32[]{:S(2)}) collective-permute-start(f32[256,256]{1,0:T(8,128)S(1)} %get-tuple-element.120), channel_id=1, source_target_pairs={{0,4},{4,8},{8,12},{12,16},{16,20},{20,24},{24,28},{28,0},{1,5},{5... | collective-permute-start | bytes 786440 | tf_op jit(solution)/shard_map/ppermute | solution.py:333
  15.1 4.5 %collective-permute-start.4 = (f32[256,256]{1,0:T(8,128)S(1)}, f32[256,256]{1,0:T(8,128)S(1)}, u32[]{:S(2)}, u32[]{:S(2)}) collective-permute-start(f32[256,256]{1,0:T(8,128)S(1)} %get-tuple-element.119), channel_id=1, source_target_pairs={{0,4},{4,0},{8,12},{12,8},{16,20},{20,16},{24,28},{28,24},{1,5},{5... | collective-permute-start | bytes 786440 | tf_op jit(solution)/shard_map/ppermute | solution.py:337
  15.1 8.8 %collective-permute-start.6 = (f32[256,256]{1,0:T(8,128)S(1)}, f32[256,256]{1,0:T(8,128)S(1)}, u32[]{:S(2)}, u32[]{:S(2)}) collective-permute-start(f32[256,256]{1,0:T(8,128)S(1)} %get-tuple-element.130), channel_id=1, source_target_pairs={{0,4},{4,8},{8,12},{12,16},{16,20},{20,24},{24,28},{28,0},{1,5},{5... | collective-permute-start | bytes 786440 | tf_op jit(solution)/shard_map/ppermute | solution.py:333
  15.6 12.3 %collective-permute-start.7 = (f32[256,256]{1,0:T(8,128)S(1)}, f32[256,256]{1,0:T(8,128)S(1)}, u32[]{:S(2)}, u32[]{:S(2)}) collective-permute-start(f32[256,256]{1,0:T(8,128)S(1)} %get-tuple-element.137), channel_id=1, source_target_pairs={{0,0},{1,1},{2,2},{3,3},{4,5},{5,6},{6,7},{7,4},{8,8},{9,9},{10,10... | collective-permute-start | bytes 786440 | tf_op jit(solution)/shard_map/ppermute | solution.py:347
  19.6 8.8 %collective-permute-start.8 = (f32[256,256]{1,0:T(8,128)S(1)}, f32[256,256]{1,0:T(8,128)S(1)}, u32[]{:S(2)}, u32[]{:S(2)}) collective-permute-start(f32[256,256]{1,0:T(8,128)S(1)} %get-tuple-element.143), channel_id=1, source_target_pairs={{0,0},{1,1},{2,2},{3,3},{4,5},{5,6},{6,7},{7,4},{8,8},{9,9},{10,10... | collective-permute-start | bytes 786440 | tf_op jit(solution)/shard_map/ppermute | solution.py:347
  20.3 11.9 %collective-permute-start.9 = (f32[256,256]{1,0:T(8,128)S(1)}, f32[256,256]{1,0:T(8,128)S(1)}, u32[]{:S(2)}, u32[]{:S(2)}) collective-permute-start(f32[256,256]{1,0:T(8,128)S(1)} %get-tuple-element.151), channel_id=1, source_target_pairs={{0,1},{1,2},{2,3},{3,0},{4,4},{5,5},{6,6},{7,7},{8,9},{9,10},{10,1... | collective-permute-start | bytes 786440 | tf_op jit(solution)/shard_map/ppermute | solution.py:347
  24.5 10.5 %collective-permute-start.10 = (f32[256,256]{1,0:T(8,128)S(1)}, f32[256,256]{1,0:T(8,128)S(1)}, u32[]{:S(2)}, u32[]{:S(2)}) collective-permute-start(f32[256,256]{1,0:T(8,128)S(1)} %get-tuple-element.154), channel_id=1, source_target_pairs={{0,1},{1,2},{2,3},{3,0},{4,4},{5,5},{6,6},{7,7},{8,9},{9,10},{10,1... | collective-permute-start | bytes 786440 | tf_op jit(solution)/shard_map/ppermute | solution.py:347
  28.0 7.9 %collective-permute-start.11 = (f32[256,256]{1,0:T(8,128)S(1)}, f32[256,256]{1,0:T(8,128)S(1)}, u32[]{:S(2)}, u32[]{:S(2)}) collective-permute-start(f32[256,256]{1,0:T(8,128)S(1)} %get-tuple-element.164), channel_id=1, source_target_pairs={{0,4},{4,8},{8,12},{12,16},{16,20},{20,24},{24,28},{28,0},{1,5},{5... | collective-permute-start | bytes 786440 | tf_op jit(solution)/shard_map/ppermute | solution.py:333
  28.5 10.3 %collective-permute-start.13 = (f32[256,256]{1,0:T(8,128)S(1)}, f32[256,256]{1,0:T(8,128)S(1)}, u32[]{:S(2)}, u32[]{:S(2)}) collective-permute-start(f32[256,256]{1,0:T(8,128)S(1)} %get-tuple-element.167), channel_id=1, source_target_pairs={{0,4},{4,8},{8,12},{12,16},{16,20},{20,24},{24,28},{28,0},{1,5},{5... | collective-permute-start | bytes 786440 | tf_op jit(solution)/shard_map/ppermute | solution.py:333
  32.6 6.2 %collective-permute-start.12 = (f32[256,256]{1,0:T(8,128)S(1)}, f32[256,256]{1,0:T(8,128)S(1)}, u32[]{:S(2)}, u32[]{:S(2)}) collective-permute-start(f32[256,256]{1,0:T(8,128)S(1)} %get-tuple-element.165), channel_id=1, source_target_pairs={{0,4},{4,0},{8,12},{12,8},{16,20},{20,16},{24,28},{28,24},{1,5},{5... | collective-permute-start | bytes 786440 | tf_op jit(solution)/shard_map/ppermute | solution.py:337
  35.4 3.8 %collective-permute-start.14 = (f32[256,256]{1,0:T(8,128)S(1)}, f32[256,256]{1,0:T(8,128)S(1)}, u32[]{:S(2)}, u32[]{:S(2)}) collective-permute-start(f32[256,256]{1,0:T(8,128)S(1)} %get-tuple-element.169), channel_id=1, source_target_pairs={{0,4},{4,0},{8,12},{12,8},{16,20},{20,16},{24,28},{28,24},{1,5},{5... | collective-permute-start | bytes 786440 | tf_op jit(solution)/shard_map/ppermute | solution.py:337

commit v6 on v5

v6 whole, which is shorter than its diff:
```python
import functools

import jax
import jax.numpy as jnp
from jax import lax
from jax.experimental import pallas as pl
from jax.experimental.pallas import tpu as pltpu
from jax.sharding import PartitionSpec as P

LEARN_RATE = 0.03
DECAY_RATE = 0.1
CHUNKS = 4
SUBLANES = 8

VMEM = pl.BlockSpec(memory_space=pltpu.VMEM)
SMEM = pl.BlockSpec(memory_space=pltpu.SMEM)
HBM = pl.BlockSpec(memory_space=pltpu.HBM)
ANY = pl.BlockSpec(memory_space=pl.ANY)


def call(body, name, operands, in_specs, outs, out_specs, flops=0, moved=0, aliases=None, scratch=()):
    return pl.pallas_call(
        body,
        out_shape=outs,
        in_specs=in_specs,
        out_specs=out_specs,
        input_output_aliases=aliases or {},
        scratch_shapes=list(scratch),
        compiler_params=pltpu.CompilerParams(vmem_limit_bytes=24 * 1024 * 1024),
        cost_estimate=pl.CostEstimate(flops=flops, bytes_accessed=moved, transcendentals=0),
        name=name,
    )(*operands)


class Line:
    def __init__(self, turn):
        self.turn = turn

    def call(self, body, name, operands, outs, flops=0, moved=0, aliases=None, held=()):
        through = (self.turn, *held)
        n_in, n_out, n_through = len(operands), len(outs), len(through)
        aliases = dict(aliases or {})
        for i in range(n_through):
            aliases[n_in + i] = n_out + i

        def inner(*refs):
            body(*refs[:n_in], *refs[n_in + n_through : n_in + n_through + n_out])

        out = call(
            inner,
            name,
            (*operands, *through),
            [VMEM] * (n_in + n_through),
            [*outs, *map(like, through)],
            [VMEM] * (n_out + n_through),
            flops,
            moved,
            aliases,
        )
        self.turn = out[n_out]
        return tuple(out[:n_out]) + tuple(out[n_out + 1 :])


def like(array, shape=None, dtype=None):
    return jax.ShapeDtypeStruct(shape or array.shape, dtype or array.dtype)


def span(h, width):
    return slice(h * width, (h + 1) * width)


def scatter(stratum, values, coords, counts, dense, live):
    listed, tile, _ = values.shape
    col = lax.broadcasted_iota(jnp.int32, live.shape, 0)
    row = lax.broadcasted_iota(jnp.int32, live.shape, 1)
    named = jnp.zeros(live.shape, jnp.float32)
    for t in range(listed):
        r = pl.multiple_of(coords[stratum, 0, t] * tile, tile)
        c = coords[stratum, 1, t]
        dense[pl.ds(pl.multiple_of(c * tile, tile), tile), pl.ds(r, tile)] = values[t].T
        alive_c = jnp.where(t < counts[0, stratum], c, -1)
        named = jnp.where((col == alive_c) & (row >= r) & (row < r + tile), 1.0, named)
    live[...] = named


def sgd(old, grad):
    return old + LEARN_RATE * (grad - DECAY_RATE * old)


def dot(a, b, contract):
    return lax.dot_general(a, b, (contract, ((), ())), preferred_element_type=jnp.float32)


def columns_step(first_tile, tile, row_half, cols, dense, live):
    col_half = cols.astype(jnp.bfloat16)
    estimate = dot(col_half, row_half, ((1,), (1,)))
    parts = []
    for i in range(cols.shape[0] // tile):
        at = span(i, tile)
        residue = dense[at].astype(jnp.float32) - estimate[at]
        named = live[first_tile + i : first_tile + i + 1] > 0
        parts.append(jnp.where(named, residue, 0.0).astype(jnp.bfloat16))
    residue = parts[0] if len(parts) == 1 else jnp.concatenate(parts, axis=0)
    return residue, col_half, sgd(cols, dot(residue, row_half, ((1,), (0,))))


def rows_gradient(residues, halves):
    return sum(dot(e[...], c[...], ((0,), (0,))) for e, c in zip(residues, halves))


def first_kernel(u_hbm, c_hbm, x_hbm, coords_hbm, counts_hbm, *refs):
    u_ref, c_ref, half_ref, dense, live, turn, c_out, residue, col_half = refs[:9]
    x_ref, coords, counts, sems = refs[9:]
    width, tile = c_out.shape[0], x_ref.shape[1]
    cols = c_ref.shape[0]
    head, tail = pl.ds(0, width), pl.ds(width, cols - width)
    pairs = [(coords_hbm, coords), (counts_hbm, counts), (x_hbm.at[0], x_ref), (u_hbm, u_ref)]
    pairs += [(c_hbm.at[at], c_ref.at[at]) for at in (head, tail)]
    copies = [pltpu.make_async_copy(s, d, sems.at[i]) for i, (s, d) in enumerate(pairs)]
    for copy in copies:
        copy.start()
    turn[...] = jnp.zeros_like(turn)
    for copy in copies[:3]:
        copy.wait()
    scatter(0, x_ref, coords, counts, dense, live)
    copies[3].wait()
    row_half = u_ref[...].astype(jnp.bfloat16)
    half_ref[...] = row_half
    copies[4].wait()
    residue[...], col_half[...], c_out[...] = columns_step(
        0, tile, row_half, c_ref[:width], dense[:width], live
    )
    copies[5].wait()


def first(u, c, values, coords, counts):
    rows, cols = u.shape[0], c.shape[0]
    part = (cols // CHUNKS, c.shape[1])
    bf16 = jnp.bfloat16
    outs = [like(u), like(c), like(u, dtype=bf16), like(u, (cols, rows), bf16)]
    outs += [like(u, (SUBLANES, rows)), like(u, (SUBLANES, 128))]
    outs += [like(c, part), like(u, (part[0], rows), bf16), like(c, part, bf16)]
    operands = (u, c, values, coords, counts)
    return call(
        first_kernel,
        "first_chunk",
        [pltpu.with_memory_space_constraint(x, pltpu.HBM) for x in operands],
        [HBM] * 5,
        outs,
        [VMEM] * len(outs),
        flops=4 * u.size * part[0],
        moved=8 * u.size,
        scratch=[
            pltpu.VMEM(values.shape[1:], values.dtype),
            pltpu.SMEM(coords.shape, coords.dtype),
            pltpu.SMEM(counts.shape, counts.dtype),
            pltpu.SemaphoreType.DMA((6,)),
        ],
    )


def other_kernel(tile, row_half, c_ref, dense, live, residue, col_half, *c_outs):
    width = c_outs[0].shape[0]
    rest = slice(width, c_ref.shape[0])
    residue[...], col_half[...], new = columns_step(
        width // tile, tile, row_half[...], c_ref[rest], dense[rest], live
    )
    for h, c_out in enumerate(c_outs):
        c_out[...] = new[span(h, width)]


def others(line, tile, row_half, c, laid):
    cols, rank = c.shape
    width = cols // CHUNKS
    outs = [like(row_half, (cols - width, row_half.shape[0])), like(row_half, (cols - width, rank))]
    return line.call(
        functools.partial(other_kernel, tile),
        "other_chunks",
        (row_half, c, *laid),
        outs + [like(c, (width, rank))] * (CHUNKS - 1),
        flops=4 * row_half.size * (cols - width),
        moved=8 * c.size,
    )


def layout_kernel(x_ref, coords, counts, *refs):
    outs = refs[2:]
    later = len(outs) // 2
    for s in range(later):
        scatter(s + 1, x_ref.at[s + 1], coords, counts, outs[s], outs[later + s])


def layout(line, values, coords, counts, rows, cols):
    later = values.shape[0] - 1
    outs = [like(values, (cols, rows))] * later
    outs += [like(values, (SUBLANES, rows), jnp.float32)] * later
    line.turn, *out = call(
        layout_kernel,
        "lay_out_tiles",
        (values, coords, counts, line.turn),
        [VMEM, SMEM, SMEM, VMEM],
        [like(line.turn), *outs],
        [VMEM] * (1 + len(outs)),
        moved=4 * later * rows * cols,
        aliases={3: 0},
    )
    return list(zip(out[:later], out[later:]))


def columns_kernel(h, tile, row_half, c_ref, dense, live, c_out, residue, col_half):
    at = span(h, c_ref.shape[0])
    residue[...], col_half[...], c_out[...] = columns_step(
        at.start // tile, tile, row_half[...], c_ref[...], dense[at], live
    )


def columns(line, h, tile, row_half, c, laid, held=()):
    return line.call(
        functools.partial(columns_kernel, h, tile),
        "columns_step",
        (row_half, c, *laid),
        [like(c), like(row_half, (c.shape[0], row_half.shape[0])), like(c, dtype=jnp.bfloat16)],
        flops=4 * row_half.size * c.shape[0],
        moved=2 * row_half.size + 8 * c.size,
        held=held,
    )


def rows_kernel(_, __, *refs):
    *pairs, u_out, half_out = refs
    n = len(pairs) // 2
    u_new = sgd(u_out[...], rows_gradient(pairs[:n], pairs[n:]))
    u_out[...] = u_new
    half_out[...] = u_new.astype(jnp.bfloat16)


def rows(line, u, row_half, residues, halves):
    return line.call(
        rows_kernel,
        "rows_step",
        (u, row_half, *residues, *halves),
        [like(u), like(row_half)],
        flops=2 * u.size * sum(c.shape[0] for c in halves),
        moved=10 * u.size,
        aliases={0: 0, 1: 1},
    )


def gradient_kernel(*refs):
    *pairs, acc = refs
    n = len(pairs) // 2
    acc[...] = rows_gradient(pairs[:n], pairs[n:])


def last_kernel(tile, u_ref, row_half, dense, live, c_ref, acc, _, *refs):
    n = CHUNKS - 1
    done, (u_hbm, c_hbm, u_new, c_new, sems) = refs[:n], refs[n:]
    width = c_ref.shape[0]
    copies = []

    def copy(source, target, at):
        place = pl.ds(at, source.shape[0])
        copies.append(pltpu.make_async_copy(source, target.at[place], sems.at[len(copies)]))
        copies[-1].start()

    for h, c in enumerate(done):
        copy(c, c_hbm, h * width)
    residue, col_half, new_cols = columns_step(
        n * width // tile, tile, row_half[...], c_ref[...], dense[span(n, width)], live
    )
    for r in range(u_ref.shape[0] // tile):
        part = span(r, tile)
        grad = acc[part] + dot(residue[:, part], col_half, ((0,), (0,)))
        u_new[part] = sgd(u_ref[part], grad)
        copy(u_new.at[pl.ds(r * tile, tile)], u_hbm, r * tile)
    c_new[...] = new_cols
    copy(c_new, c_hbm, n * width)
    for started in copies:
        started.wait()


def final(line, tile, u, row_half, cs, laid):
    n = CHUNKS - 1
    width, rank = cs[0].shape
    steps = [columns(line, h, tile, row_half, cs[h], laid) for h in range(n)]
    done, residues, halves = zip(*steps)
    (acc,) = line.call(
        gradient_kernel,
        "rows_gradient",
        (*residues, *halves),
        [like(u)],
        flops=2 * u.size * n * width,
        moved=4 * u.size,
    )
    return call(
        functools.partial(last_kernel, tile),
        "last_columns_and_rows",
        (u, row_half, *laid, cs[n], acc, line.turn, *done),
        [VMEM] * (7 + n),
        [like(u), like(u, (CHUNKS * width, rank))],
        [HBM, HBM],
        flops=6 * u.size * width,
        moved=8 * u.size,
        scratch=[
            pltpu.VMEM(u.shape, u.dtype),
            pltpu.VMEM((width, rank), u.dtype),
            pltpu.SemaphoreType.DMA((CHUNKS + u.shape[0] // tile,)),
        ],
    )


def shifted(chunk, axis):
    n = lax.axis_size(axis)
    return lax.ppermute(chunk, axis, [(i, (i + 1) % n) for i in range(n)])


def per_device(row_factors, col_factors, tile_values, tile_coords, tile_counts):
    tile = tile_values.shape[2]
    strata = tile_values.shape[0]
    coords, counts = tile_coords.transpose(0, 2, 1), tile_counts.transpose(1, 0)
    sizes = row_factors.shape[0], col_factors.shape[0]
    u, c, row_half, *laid0, turn, done, residue, half = first(
        row_factors, col_factors, tile_values, coords, counts
    )
    line = Line(turn)
    cs = [shifted(done, "blk")]
    residues, halves, *done = others(line, tile, row_half, c, laid0)
    cs += [shifted(d, "blk") for d in done]
    laid = layout(line, tile_values, coords, counts, *sizes)
    u, row_half = rows(line, u, row_half, (residue, residues), (half, halves))

    waiting = []
    for stratum in range(1, strata - 1):
        axis = "group" if stratum == 2 else "blk"
        arrived, cs, residues, halves = cs, [], [], []
        for h in range(CHUNKS):
            held = tuple(waiting) if h == 1 else ()
            done, residue, half, *held = columns(
                line, h, tile, row_half, arrived[h], laid[stratum - 1], held
            )
            residues.append(residue)
            halves.append(half)
            cs.append(shifted(done, axis) if stratum != 1 or h + 1 < CHUNKS else done)
            for d in held:
                arrived[CHUNKS - 1] = shifted(d, "blk")
        waiting = cs[-1:] if stratum == 1 else []
        u, row_half = rows(line, u, row_half, residues, halves)
    return final(line, tile, u, row_half, cs, laid[-1])


def solution(mesh):
    return jax.shard_map(
        per_device,
        mesh=mesh,
        in_specs=(
            P(("blk", "group"), None),
            P(("blk", "group"), None),
            P(None, ("blk", "group"), None, None),
            P(None, ("blk", "group"), None),
            P(None, ("blk", "group")),
        ),
        out_specs=(P(("blk", "group"), None), P(("blk", "group"), None)),
        check_vma=False,
    )
```

time: 40.9 us -> 40.2 us (0.983)
  starting transfers between devices: 17 us -> 13.4 us
  Pallas kernels: 9.13 us -> 12.1 us
    ppermute x15 -> x16, starting transfers between devices: 17 us -> 13.4 us  [shifted(): return lax.ppermute(chunk, axis, [(i, (i + 1) % n) for i in range(n)])]
    pallas_call x21 -> x24, Pallas kernels: 9.13 us -> 12.1 us  [call(): pl.pallas_call(body, out_shape=outs, in_specs=in_specs, out_specs=out_spe...]
    ppermute x15 -> x16, waiting for transfers between devices: 13.6 us -> 13.6 us  [shifted(): return lax.ppermute(chunk, axis, [(i, (i + 1) % n) for i in range(n)])]
  transfers between devices with their start and end apart: 15 -> 16, of which waited for: 6 -> 10; matrix products, arithmetic and copies ran while one was open for 0% -> 0% of each run, Pallas kernels for 12% -> 23%
where the time goes in v6:
time: 40.2 us; the launch traced here: 40 us
  waiting for transfers between devices  13.6 us (34%)
  starting transfers between devices  13.4 us (33%)
  Pallas kernels  12.1 us (30%)
  between operations  0.91 us (2%)
    ppermute x16, waiting for transfers between devices, shifted(): return lax.ppermute(chunk, axis, [(i, (i + 1) % n) for i in range(n)])  13.6 us
    ppermute x16, starting transfers between devices, shifted(): return lax.ppermute(chunk, axis, [(i, (i + 1) % n) for i in range(n)])  13.4 us
    pallas_call x24, Pallas kernels, call(): pl.pallas_call(body, out_shape=outs, in_specs=in_specs, out_specs=out_spe...  12.1 us
  transfers between devices with their start and end apart: 16, of which 10 were waited for; matrix products, arithmetic and copies ran while one was open for 0% of the time, Pallas kernels for 23%

profile of v6, /device:TPU:0, one launch (start us, length us, event | category | flops | bytes accessed | tf_op | source)
XLA Modules:
  0.0 40.0 jit_solution(5332849084140757850)
XLA Ops:
  0.7 1.7 %first_chunk.1 = (f32[512,256]{1,0:T(8,128)S(1)}, f32[512,256]{1,0:T(8,128)S(1)}, bf16[512,256]{1,0:T(8,128)(2,1)S(1)}, bf16[512,512]{1,0:T(8,128)(2,1)S(1)}, f3...) custom-call(f32[512,256]{1,0:T(8,128)} %u_hbm.1, ...), custom_call_target="tpu_custom_call" | custom-call | flops 67108864 | bytes 1048576 | tf_op jit(solution)/shard_map/first_chunk/pallas_call | solution.py:22
  2.3 0.5 %collective-permute-start = (f32[128,256]{1,0:T(8,128)S(1)}, f32[128,256]{1,0:T(8,128)S(1)}, u32[]{:S(2)}, u32[]{:S(2)}) collective-permute-start(f32[128,256]{1,0:T(8,128)S(1)} %get-tuple-element.115), channel_id=1, source_target_pairs={{0,4},{4,8},{8,12},{12,16},{16,20},{20,24},{24,28},{28,0},{1,5},{5... | collective-permute-start | bytes 393224 | tf_op jit(solution)/shard_map/ppermute | solution.py:314
  2.8 0.5 %other_chunks.1 = (bf16[384,512]{1,0:T(8,128)(2,1)S(1)}, bf16[384,256]{1,0:T(8,128)(2,1)S(1)}, f32[128,256]{1,0:T(8,128)S(1)}, f32[128,256]{1,0:T(8,128)S(1)}, f...) custom-call(bf16[512,256]{1,0:T(8,128)(2,1)S(1)} %get-tuple-element.102.refs_0_.refs_1_, ...), custom_call_target="tpu_custom_call", output_to_operand_aliasing={{5}: (4, {})} | custom-call | flops 201326592 | bytes 1048576 | tf_op jit(solution)/shard_map/other_chunks/pallas_call | solution.py:22
  3.4 2.7 %collective-permute-start.1 = (f32[128,256]{1,0:T(8,128)S(1)}, f32[128,256]{1,0:T(8,128)S(1)}, u32[]{:S(2)}, u32[]{:S(2)}) collective-permute-start(f32[128,256]{1,0:T(8,128)S(1)} %get-tuple-element.120), channel_id=1, source_target_pairs={{0,4},{4,8},{8,12},{12,16},{16,20},{20,24},{24,28},{28,0},{1,5},{5... | collective-permute-start | bytes 393224 | tf_op jit(solution)/shard_map/ppermute | solution.py:314
  6.0 0.1 collective-permute-start.2
  6.1 1.5 %collective-permute-start.3 = (f32[128,256]{1,0:T(8,128)S(1)}, f32[128,256]{1,0:T(8,128)S(1)}, u32[]{:S(2)}, u32[]{:S(2)}) collective-permute-start(f32[128,256]{1,0:T(8,128)S(1)} %get-tuple-element.126), channel_id=1, source_target_pairs={{0,4},{4,8},{8,12},{12,16},{16,20},{20,24},{24,28},{28,0},{1,5},{5... | collective-permute-start | bytes 393224 | tf_op jit(solution)/shard_map/ppermute | solution.py:314
  7.6 1.0 %lay_out_tiles.1 = (f32[8,128]{1,0:T(8,128)S(1)}, bf16[512,512]{1,0:T(8,128)(2,1)S(1)}, bf16[512,512]{1,0:T(8,128)(2,1)S(1)}, bf16[512,512]{1,0:T(8,128)(2,1)S(1...) custom-call(bf16[5,8,128,128]{3,2,1,0:T(8,128)(2,1)S(1)} %copy-done,, ...), custom_call_target="tpu_custom_call", output_to_operand_aliasing={{0}: (3, {})} | custom-call | bytes 4194304 | tf_op jit(solution)/shard_map/lay_out_tiles/pallas_call | solution.py:22
  8.6 0.4 %rows_step.4 = (f32[512,256]{1,0:T(8,128)S(1)}, bf16[512,256]{1,0:T(8,128)(2,1)S(1)}, f32[8,128]{1,0:T(8,128)S(1)}) custom-call(f32[512,256]{1,0:T(8,128)S(1)} %get-tuple-element.101.refs_0_, bf16[512,256]{1,0:T(8,128)(2,1)S(1)} %get-tuple-element.102.refs_0_.refs_1_, ...), custom_call_target="tpu_custom_call", output_to_operand_aliasing={{0}: (0, {}), {1}: (1, {}), {2}: (6, {})} | custom-call | flops 134217728 | bytes 1310720 | tf_op jit(solution)/shard_map/rows_step/pallas_call | solution.py:22
  9.0 0.4 columns_step.15
  9.4 0.1 collective-permute-start.4
  9.5 0.3 collective-permute-done.1.refs_1_
  9.8 0.4 columns_step.16
  10.1 1.3 %collective-permute-start.5 = (f32[128,256]{1,0:T(8,128)S(1)}, f32[128,256]{1,0:T(8,128)S(1)}, u32[]{:S(2)}, u32[]{:S(2)}) collective-permute-start(f32[128,256]{1,0:T(8,128)S(1)} %get-tuple-element.141), channel_id=1, source_target_pairs={{0,4},{4,8},{8,12},{12,16},{16,20},{20,24},{24,28},{28,0},{1,5},{5... | collective-permute-start | bytes 393224 | tf_op jit(solution)/shard_map/ppermute | solution.py:314
  11.5 0.4 columns_step.17
  11.8 0.2 collective-permute-start.6
  12.1 0.6 %collective-permute-done.3.refs_1_ = f32[128,256]{1,0:T(8,128)S(1)} collective-permute-done((f32[128,256]{1,0:T(8,128)S(1)}, f32[128,256]{1,0:T(8,128)S(1)}, u32[]{:S(2)}, u32[]{:S(2)}) %collective-permute-start.3) | collective-permute-done | bytes 131104 | tf_op jit(solution)/shard_map/ppermute | solution.py:314
  12.7 0.4 columns_step.18
  13.1 0.5 %rows_step.5 = (f32[512,256]{1,0:T(8,128)S(1)}, bf16[512,256]{1,0:T(8,128)(2,1)S(1)}, f32[8,128]{1,0:T(8,128)S(1)}) custom-call(f32[512,256]{1,0:T(8,128)S(1)} %get-tuple-element.113.refs_0_, bf16[512,256]{1,0:T(8,128)(2,1)S(1)} %get-tuple-element.114.refs_0_.refs_1_, ...), custom_call_target="tpu_custom_call", output_to_operand_aliasing={{0}: (0, {}), {1}: (1, {}), {2}: (10, {})} | custom-call | flops 134217728 | bytes 1310720 | tf_op jit(solution)/shard_map/rows_step/pallas_call | solution.py:22
  13.6 1.2 %collective-permute-done.4.refs_1_ = f32[128,256]{1,0:T(8,128)S(1)} collective-permute-done((f32[128,256]{1,0:T(8,128)S(1)}, f32[128,256]{1,0:T(8,128)S(1)}, u32[]{:S(2)}, u32[]{:S(2)}) %collective-permute-start.4) | collective-permute-done | bytes 131104 | tf_op jit(solution)/shard_map/ppermute | solution.py:314
  14.7 0.4 columns_step.19
  15.1 1.0 %collective-permute-done.5.refs_1_ = f32[128,256]{1,0:T(8,128)S(1)} collective-permute-done((f32[128,256]{1,0:T(8,128)S(1)}, f32[128,256]{1,0:T(8,128)S(1)}, u32[]{:S(2)}, u32[]{:S(2)}) %collective-permute-start.5) | collective-permute-done | bytes 131104 | tf_op jit(solution)/shard_map/ppermute | solution.py:314
  16.1 0.4 columns_step.20
  16.6 1.7 %collective-permute-start.8 = (f32[128,256]{1,0:T(8,128)S(1)}, f32[128,256]{1,0:T(8,128)S(1)}, u32[]{:S(2)}, u32[]{:S(2)}) collective-permute-start(f32[128,256]{1,0:T(8,128)S(1)} %get-tuple-element.158), channel_id=1, source_target_pairs={{0,1},{1,2},{2,3},{3,0},{4,5},{5,6},{6,7},{7,4},{8,9},{9,10},{10,1... | collective-permute-start | bytes 393224 | tf_op jit(solution)/shard_map/ppermute | solution.py:314
  18.3 1.6 %collective-permute-start.9 = (f32[128,256]{1,0:T(8,128)S(1)}, f32[128,256]{1,0:T(8,128)S(1)}, u32[]{:S(2)}, u32[]{:S(2)}) collective-permute-start(f32[128,256]{1,0:T(8,128)S(1)} %get-tuple-element.163), channel_id=1, source_target_pairs={{0,1},{1,2},{2,3},{3,0},{4,5},{5,6},{6,7},{7,4},{8,9},{9,10},{10,1... | collective-permute-start | bytes 393224 | tf_op jit(solution)/shard_map/ppermute | solution.py:314
  19.9 0.4 columns_step.21
  20.3 1.6 %collective-permute-start.10 = (f32[128,256]{1,0:T(8,128)S(1)}, f32[128,256]{1,0:T(8,128)S(1)}, u32[]{:S(2)}, u32[]{:S(2)}) collective-permute-start(f32[128,256]{1,0:T(8,128)S(1)} %get-tuple-element.166), channel_id=1, source_target_pairs={{0,1},{1,2},{2,3},{3,0},{4,5},{5,6},{6,7},{7,4},{8,9},{9,10},{10,1... | collective-permute-start | bytes 393224 | tf_op jit(solution)/shard_map/ppermute | solution.py:314
  21.9 0.4 columns_step.22
  22.3 1.7 %collective-permute-start.11 = (f32[128,256]{1,0:T(8,128)S(1)}, f32[128,256]{1,0:T(8,128)S(1)}, u32[]{:S(2)}, u32[]{:S(2)}) collective-permute-start(f32[128,256]{1,0:T(8,128)S(1)} %get-tuple-element.169), channel_id=1, source_target_pairs={{0,1},{1,2},{2,3},{3,0},{4,5},{5,6},{6,7},{7,4},{8,9},{9,10},{10,1... | collective-permute-start | bytes 393224 | tf_op jit(solution)/shard_map/ppermute | solution.py:314
  24.0 0.5 %rows_step.6 = (f32[512,256]{1,0:T(8,128)S(1)}, bf16[512,256]{1,0:T(8,128)(2,1)S(1)}, f32[8,128]{1,0:T(8,128)S(1)}) custom-call(f32[512,256]{1,0:T(8,128)S(1)} %get-tuple-element.134.refs_0_, bf16[512,256]{1,0:T(8,128)(2,1)S(1)} %get-tuple-element.135.refs_0_.refs_1_, ...), custom_call_target="tpu_custom_call", output_to_operand_aliasing={{0}: (0, {}), {1}: (1, {}), {2}: (10, {})} | custom-call | flops 134217728 | bytes 1310720 | tf_op jit(solution)/shard_map/rows_step/pallas_call | solution.py:22
  24.4 0.4 collective-permute-done.8.refs_1_
  24.8 0.4 columns_step.23
  25.2 0.1 collective-permute-start.13
  25.2 2.4 %collective-permute-done.9.refs_1_ = f32[128,256]{1,0:T(8,128)S(1)} collective-permute-done((f32[128,256]{1,0:T(8,128)S(1)}, f32[128,256]{1,0:T(8,128)S(1)}, u32[]{:S(2)}, u32[]{:S(2)}) %collective-permute-start.9) | collective-permute-done | bytes 131104 | tf_op jit(solution)/shard_map/ppermute | solution.py:314
  27.6 0.4 columns_step.24
  28.0 0.1 collective-permute-start.14
  28.0 2.4 %collective-permute-done.10.refs_1_ = f32[128,256]{1,0:T(8,128)S(1)} collective-permute-done((f32[128,256]{1,0:T(8,128)S(1)}, f32[128,256]{1,0:T(8,128)S(1)}, u32[]{:S(2)}, u32[]{:S(2)}) %collective-permute-start.10) | collective-permute-done | bytes 131104 | tf_op jit(solution)/shard_map/ppermute | solution.py:314
  30.4 0.4 columns_step.25
  30.8 2.1 %collective-permute-done.11.refs_1_ = f32[128,256]{1,0:T(8,128)S(1)} collective-permute-done((f32[128,256]{1,0:T(8,128)S(1)}, f32[128,256]{1,0:T(8,128)S(1)}, u32[]{:S(2)}, u32[]{:S(2)}) %collective-permute-start.11) | collective-permute-done | bytes 131104 | tf_op jit(solution)/shard_map/ppermute | solution.py:314
  33.0 0.4 columns_step.26
  33.3 0.1 collective-permute-start.12
  33.4 0.5 %rows_step.7 = (f32[512,256]{1,0:T(8,128)S(1)}, bf16[512,256]{1,0:T(8,128)(2,1)S(1)}, f32[8,128]{1,0:T(8,128)S(1)}) custom-call(f32[512,256]{1,0:T(8,128)S(1)} %get-tuple-element.156.refs_0_, bf16[512,256]{1,0:T(8,128)(2,1)S(1)} %get-tuple-element.157.refs_0_.refs_1_, ...), custom_call_target="tpu_custom_call", output_to_operand_aliasing={{0}: (0, {}), {1}: (1, {}), {2}: (10, {})} | custom-call | flops 134217728 | bytes 1310720 | tf_op jit(solution)/shard_map/rows_step/pallas_call | solution.py:22
  33.9 0.4 columns_step.27
  34.3 0.4 columns_step.28
  34.6 1.5 %collective-permute-done.15.refs_1_ = f32[128,256]{1,0:T(8,128)S(1)} collective-permute-done((f32[128,256]{1,0:T(8,128)S(1)}, f32[128,256]{1,0:T(8,128)S(1)}, u32[]{:S(2)}, u32[]{:S(2)}) %collective-permute-start.15) | collective-permute-done | bytes 131104 | tf_op jit(solution)/shard_map/ppermute | solution.py:314
  36.1 0.4 columns_step.29
  36.5 0.4 rows_gradient.1
  36.9 1.8 %collective-permute-done.12.c_ref = f32[128,256]{1,0:T(8,128)S(1)} collective-permute-done((f32[128,256]{1,0:T(8,128)S(1)}, f32[128,256]{1,0:T(8,128)S(1)}, u32[]{:S(2)}, u32[]{:S(2)}) %collective-permute-start.12) | collective-permute-done | bytes 131104 | tf_op jit(solution)/shard_map/ppermute | solution.py:314
  38.7 1.3 %last_columns_and_rows.1 = (f32[512,256]{1,0:T(8,128)}, f32[512,256]{1,0:T(8,128)}) custom-call(f32[512,256]{1,0:T(8,128)S(1)} %get-tuple-element.177.u_ref, bf16[512,256]{1,0:T(8,128)(2,1)S(1)} %get-tuple-element.178.refs_0_.row_half, bf16[512,512]{1,0:T(8,128)(2,1)S(1)} %get-tuple-element.179.refs_2_.dense, f32[8,512]{1,0:T(8,128)S(1)} %get-tuple-element.180.refs_3_.live, ...), custom_call_target="tpu_custom_call" | custom-call | flops 100663296 | bytes 1048576 | tf_op jit(solution)/shard_map/last_columns_and_rows/pallas_call | solution.py:22
  (14 shorter events, 0.1 us)
Async XLA Ops:
  0.6 7.0 %copy-start = (bf16[5,8,128,128]{3,2,1,0:T(8,128)(2,1)S(1)}, bf16[5,8,128,128]{3,2,1,0:T(8,128)(2,1)}, u32[]{:S(2)}) copy-start(bf16[5,8,128,128]{3,2,1,0:T(8,128)(2,1)} %x_ref.1) | copy-start | bytes 3932164
  0.6 7.0 %copy-start.1 = (s32[5,8,2]{1,2,0:T(2,128)S(1)}, s32[5,8,2]{1,2,0:T(2,128)}, u32[]{:S(2)}) copy-start(s32[5,8,2]{1,2,0:T(2,128)} %param.8) | copy-start | bytes 964
  0.7 7.0 %copy-start.2 = (s32[5,1]{0,1:T(1,128)S(1)}, s32[5,1]{0,1:T(1,128)}, u32[]{:S(2)}) copy-start(s32[5,1]{0,1:T(1,128)} %param.9) | copy-start | bytes 64
  2.3 6.7 %collective-permute-start = (f32[128,256]{1,0:T(8,128)S(1)}, f32[128,256]{1,0:T(8,128)S(1)}, u32[]{:S(2)}, u32[]{:S(2)}) collective-permute-start(f32[128,256]{1,0:T(8,128)S(1)} %get-tuple-element.115), channel_id=1, source_target_pairs={{0,4},{4,8},{8,12},{12,16},{16,20},{20,24},{24,28},{28,0},{1,5},{5... | collective-permute-start | bytes 393224 | tf_op jit(solution)/shard_map/ppermute | solution.py:314
  3.4 6.4 %collective-permute-start.1 = (f32[128,256]{1,0:T(8,128)S(1)}, f32[128,256]{1,0:T(8,128)S(1)}, u32[]{:S(2)}, u32[]{:S(2)}) collective-permute-start(f32[128,256]{1,0:T(8,128)S(1)} %get-tuple-element.120), channel_id=1, source_target_pairs={{0,4},{4,8},{8,12},{12,16},{16,20},{20,24},{24,28},{28,0},{1,5},{5... | collective-permute-start | bytes 393224 | tf_op jit(solution)/shard_map/ppermute | solution.py:314
  6.0 5.5 %collective-permute-start.2 = (f32[128,256]{1,0:T(8,128)S(1)}, f32[128,256]{1,0:T(8,128)S(1)}, u32[]{:S(2)}, u32[]{:S(2)}) collective-permute-start(f32[128,256]{1,0:T(8,128)S(1)} %get-tuple-element.123), channel_id=1, source_target_pairs={{0,4},{4,8},{8,12},{12,16},{16,20},{20,24},{24,28},{28,0},{1,5},{5... | collective-permute-start | bytes 393224 | tf_op jit(solution)/shard_map/ppermute | solution.py:314
  6.1 6.6 %collective-permute-start.3 = (f32[128,256]{1,0:T(8,128)S(1)}, f32[128,256]{1,0:T(8,128)S(1)}, u32[]{:S(2)}, u32[]{:S(2)}) collective-permute-start(f32[128,256]{1,0:T(8,128)S(1)} %get-tuple-element.126), channel_id=1, source_target_pairs={{0,4},{4,8},{8,12},{12,16},{16,20},{20,24},{24,28},{28,0},{1,5},{5... | collective-permute-start | bytes 393224 | tf_op jit(solution)/shard_map/ppermute | solution.py:314
  9.4 5.3 %collective-permute-start.4 = (f32[128,256]{1,0:T(8,128)S(1)}, f32[128,256]{1,0:T(8,128)S(1)}, u32[]{:S(2)}, u32[]{:S(2)}) collective-permute-start(f32[128,256]{1,0:T(8,128)S(1)} %get-tuple-element.136), channel_id=1, source_target_pairs={{0,4},{4,8},{8,12},{12,16},{16,20},{20,24},{24,28},{28,0},{1,5},{5... | collective-permute-start | bytes 393224 | tf_op jit(solution)/shard_map/ppermute | solution.py:314
  10.1 6.0 %collective-permute-start.5 = (f32[128,256]{1,0:T(8,128)S(1)}, f32[128,256]{1,0:T(8,128)S(1)}, u32[]{:S(2)}, u32[]{:S(2)}) collective-permute-start(f32[128,256]{1,0:T(8,128)S(1)} %get-tuple-element.141), channel_id=1, source_target_pairs={{0,4},{4,8},{8,12},{12,16},{16,20},{20,24},{24,28},{28,0},{1,5},{5... | collective-permute-start | bytes 393224 | tf_op jit(solution)/shard_map/ppermute | solution.py:314
  11.8 8.0 %collective-permute-start.6 = (f32[128,256]{1,0:T(8,128)S(1)}, f32[128,256]{1,0:T(8,128)S(1)}, u32[]{:S(2)}, u32[]{:S(2)}) collective-permute-start(f32[128,256]{1,0:T(8,128)S(1)} %get-tuple-element.145), channel_id=1, source_target_pairs={{0,4},{4,8},{8,12},{12,16},{16,20},{20,24},{24,28},{28,0},{1,5},{5... | collective-permute-start | bytes 393224 | tf_op jit(solution)/shard_map/ppermute | solution.py:314
  16.5 5.4 %collective-permute-start.7 = (f32[128,256]{1,0:T(8,128)S(1)}, f32[128,256]{1,0:T(8,128)S(1)}, u32[]{:S(2)}, u32[]{:S(2)}) collective-permute-start(f32[128,256]{1,0:T(8,128)S(1)} %get-tuple-element.148), channel_id=1, source_target_pairs={{0,4},{4,8},{8,12},{12,16},{16,20},{20,24},{24,28},{28,0},{1,5},{5... | collective-permute-start | bytes 393224 | tf_op jit(solution)/shard_map/ppermute | solution.py:314
  16.6 8.2 %collective-permute-start.8 = (f32[128,256]{1,0:T(8,128)S(1)}, f32[128,256]{1,0:T(8,128)S(1)}, u32[]{:S(2)}, u32[]{:S(2)}) collective-permute-start(f32[128,256]{1,0:T(8,128)S(1)} %get-tuple-element.158), channel_id=1, source_target_pairs={{0,1},{1,2},{2,3},{3,0},{4,5},{5,6},{6,7},{7,4},{8,9},{9,10},{10,1... | collective-permute-start | bytes 393224 | tf_op jit(solution)/shard_map/ppermute | solution.py:314
  18.3 9.3 %collective-permute-start.9 = (f32[128,256]{1,0:T(8,128)S(1)}, f32[128,256]{1,0:T(8,128)S(1)}, u32[]{:S(2)}, u32[]{:S(2)}) collective-permute-start(f32[128,256]{1,0:T(8,128)S(1)} %get-tuple-element.163), channel_id=1, source_target_pairs={{0,1},{1,2},{2,3},{3,0},{4,5},{5,6},{6,7},{7,4},{8,9},{9,10},{10,1... | collective-permute-start | bytes 393224 | tf_op jit(solution)/shard_map/ppermute | solution.py:314
  20.3 10.2 %collective-permute-start.10 = (f32[128,256]{1,0:T(8,128)S(1)}, f32[128,256]{1,0:T(8,128)S(1)}, u32[]{:S(2)}, u32[]{:S(2)}) collective-permute-start(f32[128,256]{1,0:T(8,128)S(1)} %get-tuple-element.166), channel_id=1, source_target_pairs={{0,1},{1,2},{2,3},{3,0},{4,5},{5,6},{6,7},{7,4},{8,9},{9,10},{10,1... | collective-permute-start | bytes 393224 | tf_op jit(solution)/shard_map/ppermute | solution.py:314
  22.3 10.7 %collective-permute-start.11 = (f32[128,256]{1,0:T(8,128)S(1)}, f32[128,256]{1,0:T(8,128)S(1)}, u32[]{:S(2)}, u32[]{:S(2)}) collective-permute-start(f32[128,256]{1,0:T(8,128)S(1)} %get-tuple-element.169), channel_id=1, source_target_pairs={{0,1},{1,2},{2,3},{3,0},{4,5},{5,6},{6,7},{7,4},{8,9},{9,10},{10,1... | collective-permute-start | bytes 393224 | tf_op jit(solution)/shard_map/ppermute | solution.py:314
  25.2 8.7 %collective-permute-start.13 = (f32[128,256]{1,0:T(8,128)S(1)}, f32[128,256]{1,0:T(8,128)S(1)}, u32[]{:S(2)}, u32[]{:S(2)}) collective-permute-start(f32[128,256]{1,0:T(8,128)S(1)} %get-tuple-element.182), channel_id=1, source_target_pairs={{0,4},{4,8},{8,12},{12,16},{16,20},{20,24},{24,28},{28,0},{1,5},{5... | collective-permute-start | bytes 393224 | tf_op jit(solution)/shard_map/ppermute | solution.py:314
  28.0 6.3 %collective-permute-start.14 = (f32[128,256]{1,0:T(8,128)S(1)}, f32[128,256]{1,0:T(8,128)S(1)}, u32[]{:S(2)}, u32[]{:S(2)}) collective-permute-start(f32[128,256]{1,0:T(8,128)S(1)} %get-tuple-element.185), channel_id=1, source_target_pairs={{0,4},{4,8},{8,12},{12,16},{16,20},{20,24},{24,28},{28,0},{1,5},{5... | collective-permute-start | bytes 393224 | tf_op jit(solution)/shard_map/ppermute | solution.py:314
  30.8 5.3 %collective-permute-start.15 = (f32[128,256]{1,0:T(8,128)S(1)}, f32[128,256]{1,0:T(8,128)S(1)}, u32[]{:S(2)}, u32[]{:S(2)}) collective-permute-start(f32[128,256]{1,0:T(8,128)S(1)} %get-tuple-element.188), channel_id=1, source_target_pairs={{0,4},{4,8},{8,12},{12,16},{16,20},{20,24},{24,28},{28,0},{1,5},{5... | collective-permute-start | bytes 393224 | tf_op jit(solution)/shard_map/ppermute | solution.py:314
  33.3 5.3 %collective-permute-start.12 = (f32[128,256]{1,0:T(8,128)S(1)}, f32[128,256]{1,0:T(8,128)S(1)}, u32[]{:S(2)}, u32[]{:S(2)}) collective-permute-start(f32[128,256]{1,0:T(8,128)S(1)} %get-tuple-element.181), channel_id=1, source_target_pairs={{0,4},{4,8},{8,12},{12,16},{16,20},{20,24},{24,28},{28,0},{1,5},{5... | collective-permute-start | bytes 393224 | tf_op jit(solution)/shard_map/ppermute | solution.py:314

commit v7 on v6

--- a/solution.py
+++ b/solution.py
@@ -9,7 +9,9 @@
 
 LEARN_RATE = 0.03
 DECAY_RATE = 0.1
-CHUNKS = 4
+EDGES = (0, 3, 8, 13, 16)
+CHUNKS = len(EDGES) - 1
+WEIGHTS = (10**9, 10**7, 6 * 10**8, 2 * 10**9)
 SUBLANES = 8
 
 VMEM = pl.BlockSpec(memory_space=pltpu.VMEM)
@@ -18,7 +20,7 @@
 ANY = pl.BlockSpec(memory_space=pl.ANY)
 
 
-def call(body, name, operands, in_specs, outs, out_specs, flops=0, moved=0, aliases=None, scratch=()):
+def call(body, name, operands, in_specs, outs, out_specs, flops=10**7, aliases=None, scratch=()):
     return pl.pallas_call(
         body,
         out_shape=outs,
@@ -27,7 +29,7 @@
         input_output_aliases=aliases or {},
         scratch_shapes=list(scratch),
         compiler_params=pltpu.CompilerParams(vmem_limit_bytes=24 * 1024 * 1024),
-        cost_estimate=pl.CostEstimate(flops=flops, bytes_accessed=moved, transcendentals=0),
+        cost_estimate=pl.CostEstimate(flops=flops, bytes_accessed=1, transcendentals=0),
         name=name,
     )(*operands)
 
@@ -36,29 +38,23 @@
     def __init__(self, turn):
         self.turn = turn
 
-    def call(self, body, name, operands, outs, flops=0, moved=0, aliases=None, held=()):
-        through = (self.turn, *held)
-        n_in, n_out, n_through = len(operands), len(outs), len(through)
-        aliases = dict(aliases or {})
-        for i in range(n_through):
-            aliases[n_in + i] = n_out + i
+    def call(self, body, name, operands, outs, flops=10**7, aliases=None):
+        n_in = len(operands)
 
         def inner(*refs):
-            body(*refs[:n_in], *refs[n_in + n_through : n_in + n_through + n_out])
-
-        out = call(
+            body(*refs[:n_in], *refs[n_in + 2 :])
+
+        self.turn, *out = call(
             inner,
             name,
-            (*operands, *through),
-            [VMEM] * (n_in + n_through),
-            [*outs, *map(like, through)],
-            [VMEM] * (n_out + n_through),
+            (*operands, self.turn),
+            [VMEM] * (n_in + 1),
+            [like(self.turn), *outs],
+            [VMEM] * (1 + len(outs)),
             flops,
-            moved,
-            aliases,
+            {n_in: 0, **{i: o + 1 for i, o in (aliases or {}).items()}},
         )
-        self.turn = out[n_out]
-        return tuple(out[:n_out]) + tuple(out[n_out + 1 :])
+        return out
 
 
 def like(array, shape=None, dtype=None):
@@ -67,6 +63,15 @@
 
 def span(h, width):
     return slice(h * width, (h + 1) * width)
+
+
+def chunk_span(h, cols):
+    return slice(cols * EDGES[h] // 16, cols * EDGES[h + 1] // 16)
+
+
+def chunk_width(h, cols):
+    at = chunk_span(h, cols)
+    return at.stop - at.start
 
 
 def scatter(stratum, values, coords, counts, dense, live):
@@ -91,15 +96,17 @@
     return lax.dot_general(a, b, (contract, ((), ())), preferred_element_type=jnp.float32)
 
 
-def columns_step(first_tile, tile, row_half, cols, dense, live):
+def columns_step(start, tile, row_half, cols, dense, live):
     col_half = cols.astype(jnp.bfloat16)
     estimate = dot(col_half, row_half, ((1,), (1,)))
-    parts = []
-    for i in range(cols.shape[0] // tile):
-        at = span(i, tile)
-        residue = dense[at].astype(jnp.float32) - estimate[at]
-        named = live[first_tile + i : first_tile + i + 1] > 0
-        parts.append(jnp.where(named, residue, 0.0).astype(jnp.bfloat16))
+    parts, at, stop = [], start, start + cols.shape[0]
+    while at < stop:
+        c = at // tile
+        end = min((c + 1) * tile, stop)
+        here = slice(at - start, end - start)
+        residue = dense[here].astype(jnp.float32) - estimate[here]
+        parts.append(jnp.where(live[c : c + 1] > 0, residue, 0.0).astype(jnp.bfloat16))
+        at = end
     residue = parts[0] if len(parts) == 1 else jnp.concatenate(parts, axis=0)
     return residue, col_half, sgd(cols, dot(residue, row_half, ((1,), (0,))))
 
@@ -135,7 +142,7 @@
 
 def first(u, c, values, coords, counts):
     rows, cols = u.shape[0], c.shape[0]
-    part = (cols // CHUNKS, c.shape[1])
+    part = (chunk_width(0, cols), c.shape[1])
     bf16 = jnp.bfloat16
     outs = [like(u), like(c), like(u, dtype=bf16), like(u, (cols, rows), bf16)]
     outs += [like(u, (SUBLANES, rows)), like(u, (SUBLANES, 128))]
@@ -148,8 +155,6 @@
         [HBM] * 5,
         outs,
         [VMEM] * len(outs),
-        flops=4 * u.size * part[0],
-        moved=8 * u.size,
         scratch=[
             pltpu.VMEM(values.shape[1:], values.dtype),
             pltpu.SMEM(coords.shape, coords.dtype),
@@ -160,26 +165,25 @@
 
 
 def other_kernel(tile, row_half, c_ref, dense, live, residue, col_half, *c_outs):
-    width = c_outs[0].shape[0]
-    rest = slice(width, c_ref.shape[0])
+    start, cols = c_ref.shape[0] - residue.shape[0], c_ref.shape[0]
+    rest = slice(start, cols)
     residue[...], col_half[...], new = columns_step(
-        width // tile, tile, row_half[...], c_ref[rest], dense[rest], live
-    )
-    for h, c_out in enumerate(c_outs):
-        c_out[...] = new[span(h, width)]
+        start, tile, row_half[...], c_ref[rest], dense[rest], live
+    )
+    for h, c_out in enumerate(c_outs, 1):
+        at = chunk_span(h, cols)
+        c_out[...] = new[at.start - start : at.stop - start]
 
 
 def others(line, tile, row_half, c, laid):
     cols, rank = c.shape
-    width = cols // CHUNKS
-    outs = [like(row_half, (cols - width, row_half.shape[0])), like(row_half, (cols - width, rank))]
+    rest = cols - chunk_width(0, cols)
+    outs = [like(row_half, (rest, row_half.shape[0])), like(row_half, (rest, rank))]
     return line.call(
         functools.partial(other_kernel, tile),
         "other_chunks",
         (row_half, c, *laid),
-        outs + [like(c, (width, rank))] * (CHUNKS - 1),
-        flops=4 * row_half.size * (cols - width),
-        moved=8 * c.size,
+        outs + [like(c, (chunk_width(h, cols), rank)) for h in range(1, CHUNKS)],
     )
 
 
@@ -201,28 +205,25 @@
         [VMEM, SMEM, SMEM, VMEM],
         [like(line.turn), *outs],
         [VMEM] * (1 + len(outs)),
-        moved=4 * later * rows * cols,
         aliases={3: 0},
     )
     return list(zip(out[:later], out[later:]))
 
 
 def columns_kernel(h, tile, row_half, c_ref, dense, live, c_out, residue, col_half):
-    at = span(h, c_ref.shape[0])
+    at = chunk_span(h, dense.shape[0])
     residue[...], col_half[...], c_out[...] = columns_step(
-        at.start // tile, tile, row_half[...], c_ref[...], dense[at], live
-    )
-
-
-def columns(line, h, tile, row_half, c, laid, held=()):
+        at.start, tile, row_half[...], c_ref[...], dense[at], live
+    )
+
+
+def columns(line, h, tile, row_half, c, laid):
     return line.call(
         functools.partial(columns_kernel, h, tile),
         "columns_step",
         (row_half, c, *laid),
         [like(c), like(row_half, (c.shape[0], row_half.shape[0])), like(c, dtype=jnp.bfloat16)],
-        flops=4 * row_half.size * c.shape[0],
-        moved=2 * row_half.size + 8 * c.size,
-        held=held,
+        flops=WEIGHTS[h],
     )
 
 
@@ -240,8 +241,6 @@
         "rows_step",
         (u, row_half, *residues, *halves),
         [like(u), like(row_half)],
-        flops=2 * u.size * sum(c.shape[0] for c in halves),
-        moved=10 * u.size,
         aliases={0: 0, 1: 1},
     )
 
@@ -255,7 +254,7 @@
 def last_kernel(tile, u_ref, row_half, dense, live, c_ref, acc, _, *refs):
     n = CHUNKS - 1
     done, (u_hbm, c_hbm, u_new, c_new, sems) = refs[:n], refs[n:]
-    width = c_ref.shape[0]
+    cols = c_hbm.shape[0]
     copies = []
 
     def copy(source, target, at):
@@ -264,9 +263,10 @@
         copies[-1].start()
 
     for h, c in enumerate(done):
-        copy(c, c_hbm, h * width)
+        copy(c, c_hbm, chunk_span(h, cols).start)
+    at = chunk_span(n, cols)
     residue, col_half, new_cols = columns_step(
-        n * width // tile, tile, row_half[...], c_ref[...], dense[span(n, width)], live
+        at.start, tile, row_half[...], c_ref[...], dense[at], live
     )
     for r in range(u_ref.shape[0] // tile):
         part = span(r, tile)
@@ -274,14 +274,14 @@
         u_new[part] = sgd(u_ref[part], grad)
         copy(u_new.at[pl.ds(r * tile, tile)], u_hbm, r * tile)
     c_new[...] = new_cols
-    copy(c_new, c_hbm, n * width)
+    copy(c_new, c_hbm, at.start)
     for started in copies:
         started.wait()
 
 
 def final(line, tile, u, row_half, cs, laid):
     n = CHUNKS - 1
-    width, rank = cs[0].shape
+    cols, rank = laid[0].shape[0], u.shape[1]
     steps = [columns(line, h, tile, row_half, cs[h], laid) for h in range(n)]
     done, residues, halves = zip(*steps)
     (acc,) = line.call(
@@ -289,21 +289,17 @@
         "rows_gradient",
         (*residues, *halves),
         [like(u)],
-        flops=2 * u.size * n * width,
-        moved=4 * u.size,
     )
     return call(
         functools.partial(last_kernel, tile),
         "last_columns_and_rows",
         (u, row_half, *laid, cs[n], acc, line.turn, *done),
         [VMEM] * (7 + n),
-        [like(u), like(u, (CHUNKS * width, rank))],
+        [like(u), like(u, (cols, rank))],
         [HBM, HBM],
-        flops=6 * u.size * width,
-        moved=8 * u.size,
         scratch=[
             pltpu.VMEM(u.shape, u.dtype),
-            pltpu.VMEM((width, rank), u.dtype),
+            pltpu.VMEM(cs[n].shape, u.dtype),
             pltpu.SemaphoreType.DMA((CHUNKS + u.shape[0] // tile,)),
         ],
     )
@@ -329,21 +325,14 @@
     laid = layout(line, tile_values, coords, counts, *sizes)
     u, row_half = rows(line, u, row_half, (residue, residues), (half, halves))
 
-    waiting = []
     for stratum in range(1, strata - 1):
         axis = "group" if stratum == 2 else "blk"
         arrived, cs, residues, halves = cs, [], [], []
         for h in range(CHUNKS):
-            held = tuple(waiting) if h == 1 else ()
-            done, residue, half, *held = columns(
-                line, h, tile, row_half, arrived[h], laid[stratum - 1], held
-            )
+            done, residue, half = columns(line, h, tile, row_half, arrived[h], laid[stratum - 1])
+            cs.append(shifted(done, axis))
             residues.append(residue)
             halves.append(half)
-            cs.append(shifted(done, axis) if stratum != 1 or h + 1 < CHUNKS else done)
-            for d in held:
-                arrived[CHUNKS - 1] = shifted(d, "blk")
-        waiting = cs[-1:] if stratum == 1 else []
         u, row_half = rows(line, u, row_half, residues, halves)
     return final(line, tile, u, row_half, cs, laid[-1])
 

time: 40.2 us -> 38.2 us (0.950)
  waiting for transfers between devices: 13.6 us -> 9.93 us
  starting transfers between devices: 13.4 us -> 15.1 us
    ppermute x16, waiting for transfers between devices: 13.6 us -> 9.93 us  [shifted(): return lax.ppermute(chunk, axis, [(i, (i + 1) % n) for i in range(n)])]
    ppermute x16, starting transfers between devices: 13.4 us -> 15.1 us  [shifted(): return lax.ppermute(chunk, axis, [(i, (i + 1) % n) for i in range(n)])]
  transfers between devices with their start and end apart: 16 -> 16, of which waited for: 10 -> 9; matrix products, arithmetic and copies ran while one was open for 0% -> 0% of each run, Pallas kernels for 23% -> 24%
where the time goes in v7:
time: 38.2 us; the launch traced here: 38 us
  starting transfers between devices  15.1 us (40%)
  Pallas kernels  12 us (31%)
  waiting for transfers between devices  9.93 us (26%)
  between operations  0.9 us (2%)
    ppermute x16, starting transfers between devices, shifted(): return lax.ppermute(chunk, axis, [(i, (i + 1) % n) for i in range(n)])  15.1 us
    pallas_call x24, Pallas kernels, call(): pl.pallas_call(body, out_shape=outs, in_specs=in_specs, out_specs=out_spe...  12 us
    ppermute x16, waiting for transfers between devices, shifted(): return lax.ppermute(chunk, axis, [(i, (i + 1) % n) for i in range(n)])  9.93 us
  transfers between devices with their start and end apart: 16, of which 9 were waited for; matrix products, arithmetic and copies ran while one was open for 0% of the time, Pallas kernels for 24%

profile of v7, /device:TPU:0, one launch (start us, length us, event | category | flops | bytes accessed | tf_op | source)
XLA Modules:
  0.0 38.0 jit_solution(2495615757749022342)
XLA Ops:
  0.7 1.7 %first_chunk.1 = (f32[512,256]{1,0:T(8,128)S(1)}, f32[512,256]{1,0:T(8,128)S(1)}, bf16[512,256]{1,0:T(8,128)(2,1)S(1)}, bf16[512,512]{1,0:T(8,128)(2,1)S(1)}, f3...) custom-call(f32[512,256]{1,0:T(8,128)} %u_hbm.1, ...), custom_call_target="tpu_custom_call" | custom-call | flops 10000000 | bytes 1 | tf_op jit(solution)/shard_map/first_chunk/pallas_call | solution.py:24
  2.3 0.5 %collective-permute-start = (f32[96,256]{1,0:T(8,128)S(1)}, f32[96,256]{1,0:T(8,128)S(1)}, u32[]{:S(2)}, u32[]{:S(2)}) collective-permute-start(f32[96,256]{1,0:T(8,128)S(1)} %get-tuple-element.114), channel_id=1, source_target_pairs={{0,4},{4,8},{8,12},{12,16},{16,20},{20,24},{24,28},{28,0},{1,5},{5... | collective-permute-start | bytes 294920 | tf_op jit(solution)/shard_map/ppermute | solution.py:310
  2.8 0.5 %other_chunks.1 = (f32[8,128]{1,0:T(8,128)S(1)}, bf16[416,512]{1,0:T(8,128)(2,1)S(1)}, bf16[416,256]{1,0:T(8,128)(2,1)S(1)}, f32[160,256]{1,0:T(8,128)S(1)}, f32...) custom-call(bf16[512,256]{1,0:T(8,128)(2,1)S(1)} %get-tuple-element.101.refs_0_.refs_1_, ...), custom_call_target="tpu_custom_call", output_to_operand_aliasing={{0}: (4, {})} | custom-call | flops 10000000 | bytes 1 | tf_op jit(solution)/shard_map/other_chunks/pallas_call | solution.py:24
  3.4 2.7 %collective-permute-start.1 = (f32[160,256]{1,0:T(8,128)S(1)}, f32[160,256]{1,0:T(8,128)S(1)}, u32[]{:S(2)}, u32[]{:S(2)}) collective-permute-start(f32[160,256]{1,0:T(8,128)S(1)} %get-tuple-element.119), channel_id=1, source_target_pairs={{0,4},{4,8},{8,12},{12,16},{16,20},{20,24},{24,28},{28,0},{1,5},{5... | collective-permute-start | bytes 491528 | tf_op jit(solution)/shard_map/ppermute | solution.py:310
  6.0 0.1 collective-permute-start.2
  6.1 1.5 %collective-permute-start.3 = (f32[96,256]{1,0:T(8,128)S(1)}, f32[96,256]{1,0:T(8,128)S(1)}, u32[]{:S(2)}, u32[]{:S(2)}) collective-permute-start(f32[96,256]{1,0:T(8,128)S(1)} %get-tuple-element.125), channel_id=1, source_target_pairs={{0,4},{4,8},{8,12},{12,16},{16,20},{20,24},{24,28},{28,0},{1,5},{5... | collective-permute-start | bytes 294920 | tf_op jit(solution)/shard_map/ppermute | solution.py:310
  7.6 1.0 %lay_out_tiles.1 = (f32[8,128]{1,0:T(8,128)S(1)}, bf16[512,512]{1,0:T(8,128)(2,1)S(1)}, bf16[512,512]{1,0:T(8,128)(2,1)S(1)}, bf16[512,512]{1,0:T(8,128)(2,1)S(1...) custom-call(bf16[5,8,128,128]{3,2,1,0:T(8,128)(2,1)S(1)} %copy-done,, ...), custom_call_target="tpu_custom_call", output_to_operand_aliasing={{0}: (3, {})} | custom-call | flops 10000000 | bytes 1 | tf_op jit(solution)/shard_map/lay_out_tiles/pallas_call | solution.py:24
  8.6 0.4 %rows_step.4 = (f32[8,128]{1,0:T(8,128)S(1)}, f32[512,256]{1,0:T(8,128)S(1)}, bf16[512,256]{1,0:T(8,128)(2,1)S(1)}) custom-call(f32[512,256]{1,0:T(8,128)S(1)} %get-tuple-element.100.refs_0_, bf16[512,256]{1,0:T(8,128)(2,1)S(1)} %get-tuple-element.101.refs_0_.refs_1_, ...), custom_call_target="tpu_custom_call", output_to_operand_aliasing={{0}: (6, {}), {1}: (0, {}), {2}: (1, {})} | custom-call | flops 10000000 | bytes 1 | tf_op jit(solution)/shard_map/rows_step/pallas_call | solution.py:24
  9.0 0.3 columns_step.15
  9.4 0.1 collective-permute-start.4
  9.5 0.2 collective-permute-done.1.refs_1_
  9.8 0.4 columns_step.16
  10.1 1.4 %collective-permute-start.5 = (f32[160,256]{1,0:T(8,128)S(1)}, f32[160,256]{1,0:T(8,128)S(1)}, u32[]{:S(2)}, u32[]{:S(2)}) collective-permute-start(f32[160,256]{1,0:T(8,128)S(1)} %get-tuple-element.140), channel_id=1, source_target_pairs={{0,4},{4,8},{8,12},{12,16},{16,20},{20,24},{24,28},{28,0},{1,5},{5... | collective-permute-start | bytes 491528 | tf_op jit(solution)/shard_map/ppermute | solution.py:310
  11.5 0.2 collective-permute-done.2.refs_1_
  11.6 0.4 columns_step.17
  12.0 0.1 collective-permute-start.6
  12.1 0.6 %collective-permute-done.3.refs_1_ = f32[96,256]{1,0:T(8,128)S(1)} collective-permute-done((f32[96,256]{1,0:T(8,128)S(1)}, f32[96,256]{1,0:T(8,128)S(1)}, u32[]{:S(2)}, u32[]{:S(2)}) %collective-permute-start.3) | collective-permute-done | bytes 98336 | tf_op jit(solution)/shard_map/ppermute | solution.py:310
  12.7 0.3 columns_step.18
  13.0 0.8 %collective-permute-start.7 = (f32[96,256]{1,0:T(8,128)S(1)}, f32[96,256]{1,0:T(8,128)S(1)}, u32[]{:S(2)}, u32[]{:S(2)}) collective-permute-start(f32[96,256]{1,0:T(8,128)S(1)} %get-tuple-element.146), channel_id=1, source_target_pairs={{0,4},{4,8},{8,12},{12,16},{16,20},{20,24},{24,28},{28,0},{1,5},{5... | collective-permute-start | bytes 294920 | tf_op jit(solution)/shard_map/ppermute | solution.py:310
  13.8 0.5 %rows_step.5 = (f32[8,128]{1,0:T(8,128)S(1)}, f32[512,256]{1,0:T(8,128)S(1)}, bf16[512,256]{1,0:T(8,128)(2,1)S(1)}) custom-call(f32[512,256]{1,0:T(8,128)S(1)} %get-tuple-element.112.refs_0_, bf16[512,256]{1,0:T(8,128)(2,1)S(1)} %get-tuple-element.113.refs_0_.refs_1_, ...), custom_call_target="tpu_custom_call", output_to_operand_aliasing={{0}: (10, {}), {1}: (0, {}), {2}: (1, {})} | custom-call | flops 10000000 | bytes 1 | tf_op jit(solution)/shard_map/rows_step/pallas_call | solution.py:24
  14.3 0.1 collective-permute-done.4.refs_1_
  14.4 0.3 columns_step.19
  14.7 1.6 %collective-permute-start.8 = (f32[96,256]{1,0:T(8,128)S(1)}, f32[96,256]{1,0:T(8,128)S(1)}, u32[]{:S(2)}, u32[]{:S(2)}) collective-permute-start(f32[96,256]{1,0:T(8,128)S(1)} %get-tuple-element.156), channel_id=1, source_target_pairs={{0,1},{1,2},{2,3},{3,0},{4,5},{5,6},{6,7},{7,4},{8,9},{9,10},{10,1... | collective-permute-start | bytes 294920 | tf_op jit(solution)/shard_map/ppermute | solution.py:310
  16.4 0.4 columns_step.20
  16.7 1.8 %collective-permute-start.9 = (f32[160,256]{1,0:T(8,128)S(1)}, f32[160,256]{1,0:T(8,128)S(1)}, u32[]{:S(2)}, u32[]{:S(2)}) collective-permute-start(f32[160,256]{1,0:T(8,128)S(1)} %get-tuple-element.161), channel_id=1, source_target_pairs={{0,1},{1,2},{2,3},{3,0},{4,5},{5,6},{6,7},{7,4},{8,9},{9,10},{10,1... | collective-permute-start | bytes 491528 | tf_op jit(solution)/shard_map/ppermute | solution.py:310
  18.6 0.4 columns_step.21
  19.0 1.6 %collective-permute-start.10 = (f32[160,256]{1,0:T(8,128)S(1)}, f32[160,256]{1,0:T(8,128)S(1)}, u32[]{:S(2)}, u32[]{:S(2)}) collective-permute-start(f32[160,256]{1,0:T(8,128)S(1)} %get-tuple-element.164), channel_id=1, source_target_pairs={{0,1},{1,2},{2,3},{3,0},{4,5},{5,6},{6,7},{7,4},{8,9},{9,10},{10,1... | collective-permute-start | bytes 491528 | tf_op jit(solution)/shard_map/ppermute | solution.py:310
  20.6 0.3 columns_step.22
  21.0 1.6 %collective-permute-start.11 = (f32[96,256]{1,0:T(8,128)S(1)}, f32[96,256]{1,0:T(8,128)S(1)}, u32[]{:S(2)}, u32[]{:S(2)}) collective-permute-start(f32[96,256]{1,0:T(8,128)S(1)} %get-tuple-element.167), channel_id=1, source_target_pairs={{0,1},{1,2},{2,3},{3,0},{4,5},{5,6},{6,7},{7,4},{8,9},{9,10},{10,1... | collective-permute-start | bytes 294920 | tf_op jit(solution)/shard_map/ppermute | solution.py:310
  22.6 0.5 %rows_step.6 = (f32[8,128]{1,0:T(8,128)S(1)}, f32[512,256]{1,0:T(8,128)S(1)}, bf16[512,256]{1,0:T(8,128)(2,1)S(1)}) custom-call(f32[512,256]{1,0:T(8,128)S(1)} %get-tuple-element.133.refs_0_, bf16[512,256]{1,0:T(8,128)(2,1)S(1)} %get-tuple-element.134.refs_0_.refs_1_, ...), custom_call_target="tpu_custom_call", output_to_operand_aliasing={{0}: (10, {}), {1}: (0, {}), {2}: (1, {})} | custom-call | flops 10000000 | bytes 1 | tf_op jit(solution)/shard_map/rows_step/pallas_call | solution.py:24
  23.1 0.3 columns_step.23
  23.5 2.2 %collective-permute-done.9.refs_1_ = f32[160,256]{1,0:T(8,128)S(1)} collective-permute-done((f32[160,256]{1,0:T(8,128)S(1)}, f32[160,256]{1,0:T(8,128)S(1)}, u32[]{:S(2)}, u32[]{:S(2)}) %collective-permute-start.9) | collective-permute-done | bytes 163872 | tf_op jit(solution)/shard_map/ppermute | solution.py:310
  25.7 0.4 columns_step.24
  26.1 0.2 collective-permute-start.14
  26.3 2.9 %collective-permute-done.10.refs_1_ = f32[160,256]{1,0:T(8,128)S(1)} collective-permute-done((f32[160,256]{1,0:T(8,128)S(1)}, f32[160,256]{1,0:T(8,128)S(1)}, u32[]{:S(2)}, u32[]{:S(2)}) %collective-permute-start.10) | collective-permute-done | bytes 163872 | tf_op jit(solution)/shard_map/ppermute | solution.py:310
  29.2 0.4 columns_step.25
  29.6 0.2 collective-permute-start.15
  29.9 1.5 %collective-permute-done.11.refs_1_ = f32[96,256]{1,0:T(8,128)S(1)} collective-permute-done((f32[96,256]{1,0:T(8,128)S(1)}, f32[96,256]{1,0:T(8,128)S(1)}, u32[]{:S(2)}, u32[]{:S(2)}) %collective-permute-start.11) | collective-permute-done | bytes 98336 | tf_op jit(solution)/shard_map/ppermute | solution.py:310
  31.4 0.3 columns_step.26
  31.7 0.8 %collective-permute-start.12 = (f32[96,256]{1,0:T(8,128)S(1)}, f32[96,256]{1,0:T(8,128)S(1)}, u32[]{:S(2)}, u32[]{:S(2)}) collective-permute-start(f32[96,256]{1,0:T(8,128)S(1)} %get-tuple-element.179), channel_id=1, source_target_pairs={{0,4},{4,8},{8,12},{12,16},{16,20},{20,24},{24,28},{28,0},{1,5},{5... | collective-permute-start | bytes 294920 | tf_op jit(solution)/shard_map/ppermute | solution.py:310
  32.5 0.5 %rows_step.7 = (f32[8,128]{1,0:T(8,128)S(1)}, f32[512,256]{1,0:T(8,128)S(1)}, bf16[512,256]{1,0:T(8,128)(2,1)S(1)}) custom-call(f32[512,256]{1,0:T(8,128)S(1)} %get-tuple-element.154.refs_0_, bf16[512,256]{1,0:T(8,128)(2,1)S(1)} %get-tuple-element.155.refs_0_.refs_1_, ...), custom_call_target="tpu_custom_call", output_to_operand_aliasing={{0}: (10, {}), {1}: (0, {}), {2}: (1, {})} | custom-call | flops 10000000 | bytes 1 | tf_op jit(solution)/shard_map/rows_step/pallas_call | solution.py:24
  33.0 0.3 columns_step.27
  33.4 0.4 columns_step.28
  33.8 1.6 %collective-permute-done.15.refs_1_ = f32[160,256]{1,0:T(8,128)S(1)} collective-permute-done((f32[160,256]{1,0:T(8,128)S(1)}, f32[160,256]{1,0:T(8,128)S(1)}, u32[]{:S(2)}, u32[]{:S(2)}) %collective-permute-start.15) | collective-permute-done | bytes 163872 | tf_op jit(solution)/shard_map/ppermute | solution.py:310
  35.3 0.4 columns_step.29
  35.7 0.4 %rows_gradient.1 = (f32[8,128]{1,0:T(8,128)S(1)}, f32[512,256]{1,0:T(8,128)S(1)}) custom-call(bf16[96,512]{1,0:T(8,128)(2,1)S(1)} %get-tuple-element.182.refs_0_, bf16[160,512]{1,0:T(8,128)(2,1)S(1)} %get-tuple-element.185.refs_1_, bf16[160,512]{1,0:T(8,128)(2,1)S(1)} %get-tuple-element.188.refs_2_, ...), custom_call_target="tpu_custom_call", output_to_operand_aliasing={{0}: (6, {})} | custom-call | flops 10000000 | bytes 1 | tf_op jit(solution)/shard_map/rows_gradient/pallas_call | solution.py:24
  36.1 0.6 %collective-permute-done.12.c_ref = f32[96,256]{1,0:T(8,128)S(1)} collective-permute-done((f32[96,256]{1,0:T(8,128)S(1)}, f32[96,256]{1,0:T(8,128)S(1)}, u32[]{:S(2)}, u32[]{:S(2)}) %collective-permute-start.12) | collective-permute-done | bytes 98336 | tf_op jit(solution)/shard_map/ppermute | solution.py:310
  36.7 1.3 %last_columns_and_rows.1 = (f32[512,256]{1,0:T(8,128)}, f32[512,256]{1,0:T(8,128)}) custom-call(f32[512,256]{1,0:T(8,128)S(1)} %get-tuple-element.175.u_ref, bf16[512,256]{1,0:T(8,128)(2,1)S(1)} %get-tuple-element.176.refs_0_.row_half, bf16[512,512]{1,0:T(8,128)(2,1)S(1)} %get-tuple-element.177.refs_2_.dense, f32[8,512]{1,0:T(8,128)S(1)} %get-tuple-element.178.refs_3_.live, ...), custom_call_target="tpu_custom_call" | custom-call | flops 10000000 | bytes 1 | tf_op jit(solution)/shard_map/last_columns_and_rows/pallas_call | solution.py:24
  (14 shorter events, 0.1 us)
Async XLA Ops:
  0.6 7.0 %copy-start = (bf16[5,8,128,128]{3,2,1,0:T(8,128)(2,1)S(1)}, bf16[5,8,128,128]{3,2,1,0:T(8,128)(2,1)}, u32[]{:S(2)}) copy-start(bf16[5,8,128,128]{3,2,1,0:T(8,128)(2,1)} %x_ref.1) | copy-start | bytes 3932164
  0.6 7.0 %copy-start.1 = (s32[5,8,2]{1,2,0:T(2,128)S(1)}, s32[5,8,2]{1,2,0:T(2,128)}, u32[]{:S(2)}) copy-start(s32[5,8,2]{1,2,0:T(2,128)} %param.8) | copy-start | bytes 964
  0.7 7.0 %copy-start.2 = (s32[5,1]{0,1:T(1,128)S(1)}, s32[5,1]{0,1:T(1,128)}, u32[]{:S(2)}) copy-start(s32[5,1]{0,1:T(1,128)} %param.9) | copy-start | bytes 64
  2.3 6.7 %collective-permute-start = (f32[96,256]{1,0:T(8,128)S(1)}, f32[96,256]{1,0:T(8,128)S(1)}, u32[]{:S(2)}, u32[]{:S(2)}) collective-permute-start(f32[96,256]{1,0:T(8,128)S(1)} %get-tuple-element.114), channel_id=1, source_target_pairs={{0,4},{4,8},{8,12},{12,16},{16,20},{20,24},{24,28},{28,0},{1,5},{5... | collective-permute-start | bytes 294920 | tf_op jit(solution)/shard_map/ppermute | solution.py:310
  3.4 6.4 %collective-permute-start.1 = (f32[160,256]{1,0:T(8,128)S(1)}, f32[160,256]{1,0:T(8,128)S(1)}, u32[]{:S(2)}, u32[]{:S(2)}) collective-permute-start(f32[160,256]{1,0:T(8,128)S(1)} %get-tuple-element.119), channel_id=1, source_target_pairs={{0,4},{4,8},{8,12},{12,16},{16,20},{20,24},{24,28},{28,0},{1,5},{5... | collective-permute-start | bytes 491528 | tf_op jit(solution)/shard_map/ppermute | solution.py:310
  6.0 5.6 %collective-permute-start.2 = (f32[160,256]{1,0:T(8,128)S(1)}, f32[160,256]{1,0:T(8,128)S(1)}, u32[]{:S(2)}, u32[]{:S(2)}) collective-permute-start(f32[160,256]{1,0:T(8,128)S(1)} %get-tuple-element.122), channel_id=1, source_target_pairs={{0,4},{4,8},{8,12},{12,16},{16,20},{20,24},{24,28},{28,0},{1,5},{5... | collective-permute-start | bytes 491528 | tf_op jit(solution)/shard_map/ppermute | solution.py:310
  6.1 6.6 %collective-permute-start.3 = (f32[96,256]{1,0:T(8,128)S(1)}, f32[96,256]{1,0:T(8,128)S(1)}, u32[]{:S(2)}, u32[]{:S(2)}) collective-permute-start(f32[96,256]{1,0:T(8,128)S(1)} %get-tuple-element.125), channel_id=1, source_target_pairs={{0,4},{4,8},{8,12},{12,16},{16,20},{20,24},{24,28},{28,0},{1,5},{5... | collective-permute-start | bytes 294920 | tf_op jit(solution)/shard_map/ppermute | solution.py:310
  9.4 5.0 %collective-permute-start.4 = (f32[96,256]{1,0:T(8,128)S(1)}, f32[96,256]{1,0:T(8,128)S(1)}, u32[]{:S(2)}, u32[]{:S(2)}) collective-permute-start(f32[96,256]{1,0:T(8,128)S(1)} %get-tuple-element.135), channel_id=1, source_target_pairs={{0,4},{4,8},{8,12},{12,16},{16,20},{20,24},{24,28},{28,0},{1,5},{5... | collective-permute-start | bytes 294920 | tf_op jit(solution)/shard_map/ppermute | solution.py:310
  10.1 6.2 %collective-permute-start.5 = (f32[160,256]{1,0:T(8,128)S(1)}, f32[160,256]{1,0:T(8,128)S(1)}, u32[]{:S(2)}, u32[]{:S(2)}) collective-permute-start(f32[160,256]{1,0:T(8,128)S(1)} %get-tuple-element.140), channel_id=1, source_target_pairs={{0,4},{4,8},{8,12},{12,16},{16,20},{20,24},{24,28},{28,0},{1,5},{5... | collective-permute-start | bytes 491528 | tf_op jit(solution)/shard_map/ppermute | solution.py:310
  12.0 6.6 %collective-permute-start.6 = (f32[160,256]{1,0:T(8,128)S(1)}, f32[160,256]{1,0:T(8,128)S(1)}, u32[]{:S(2)}, u32[]{:S(2)}) collective-permute-start(f32[160,256]{1,0:T(8,128)S(1)} %get-tuple-element.143), channel_id=1, source_target_pairs={{0,4},{4,8},{8,12},{12,16},{16,20},{20,24},{24,28},{28,0},{1,5},{5... | collective-permute-start | bytes 491528 | tf_op jit(solution)/shard_map/ppermute | solution.py:310
  13.0 7.6 %collective-permute-start.7 = (f32[96,256]{1,0:T(8,128)S(1)}, f32[96,256]{1,0:T(8,128)S(1)}, u32[]{:S(2)}, u32[]{:S(2)}) collective-permute-start(f32[96,256]{1,0:T(8,128)S(1)} %get-tuple-element.146), channel_id=1, source_target_pairs={{0,4},{4,8},{8,12},{12,16},{16,20},{20,24},{24,28},{28,0},{1,5},{5... | collective-permute-start | bytes 294920 | tf_op jit(solution)/shard_map/ppermute | solution.py:310
  14.7 8.3 %collective-permute-start.8 = (f32[96,256]{1,0:T(8,128)S(1)}, f32[96,256]{1,0:T(8,128)S(1)}, u32[]{:S(2)}, u32[]{:S(2)}) collective-permute-start(f32[96,256]{1,0:T(8,128)S(1)} %get-tuple-element.156), channel_id=1, source_target_pairs={{0,1},{1,2},{2,3},{3,0},{4,5},{5,6},{6,7},{7,4},{8,9},{9,10},{10,1... | collective-permute-start | bytes 294920 | tf_op jit(solution)/shard_map/ppermute | solution.py:310
  16.7 9.0 %collective-permute-start.9 = (f32[160,256]{1,0:T(8,128)S(1)}, f32[160,256]{1,0:T(8,128)S(1)}, u32[]{:S(2)}, u32[]{:S(2)}) collective-permute-start(f32[160,256]{1,0:T(8,128)S(1)} %get-tuple-element.161), channel_id=1, source_target_pairs={{0,1},{1,2},{2,3},{3,0},{4,5},{5,6},{6,7},{7,4},{8,9},{9,10},{10,1... | collective-permute-start | bytes 491528 | tf_op jit(solution)/shard_map/ppermute | solution.py:310
  19.0 10.3 %collective-permute-start.10 = (f32[160,256]{1,0:T(8,128)S(1)}, f32[160,256]{1,0:T(8,128)S(1)}, u32[]{:S(2)}, u32[]{:S(2)}) collective-permute-start(f32[160,256]{1,0:T(8,128)S(1)} %get-tuple-element.164), channel_id=1, source_target_pairs={{0,1},{1,2},{2,3},{3,0},{4,5},{5,6},{6,7},{7,4},{8,9},{9,10},{10,1... | collective-permute-start | bytes 491528 | tf_op jit(solution)/shard_map/ppermute | solution.py:310
  21.0 10.4 %collective-permute-start.11 = (f32[96,256]{1,0:T(8,128)S(1)}, f32[96,256]{1,0:T(8,128)S(1)}, u32[]{:S(2)}, u32[]{:S(2)}) collective-permute-start(f32[96,256]{1,0:T(8,128)S(1)} %get-tuple-element.167), channel_id=1, source_target_pairs={{0,1},{1,2},{2,3},{3,0},{4,5},{5,6},{6,7},{7,4},{8,9},{9,10},{10,1... | collective-permute-start | bytes 294920 | tf_op jit(solution)/shard_map/ppermute | solution.py:310
  23.4 9.6 %collective-permute-start.13 = (f32[96,256]{1,0:T(8,128)S(1)}, f32[96,256]{1,0:T(8,128)S(1)}, u32[]{:S(2)}, u32[]{:S(2)}) collective-permute-start(f32[96,256]{1,0:T(8,128)S(1)} %get-tuple-element.180), channel_id=1, source_target_pairs={{0,4},{4,8},{8,12},{12,16},{16,20},{20,24},{24,28},{28,0},{1,5},{5... | collective-permute-start | bytes 294920 | tf_op jit(solution)/shard_map/ppermute | solution.py:310
  26.1 7.3 %collective-permute-start.14 = (f32[160,256]{1,0:T(8,128)S(1)}, f32[160,256]{1,0:T(8,128)S(1)}, u32[]{:S(2)}, u32[]{:S(2)}) collective-permute-start(f32[160,256]{1,0:T(8,128)S(1)} %get-tuple-element.183), channel_id=1, source_target_pairs={{0,4},{4,8},{8,12},{12,16},{16,20},{20,24},{24,28},{28,0},{1,5},{5... | collective-permute-start | bytes 491528 | tf_op jit(solution)/shard_map/ppermute | solution.py:310
  29.6 5.7 %collective-permute-start.15 = (f32[160,256]{1,0:T(8,128)S(1)}, f32[160,256]{1,0:T(8,128)S(1)}, u32[]{:S(2)}, u32[]{:S(2)}) collective-permute-start(f32[160,256]{1,0:T(8,128)S(1)} %get-tuple-element.186), channel_id=1, source_target_pairs={{0,4},{4,8},{8,12},{12,16},{16,20},{20,24},{24,28},{28,0},{1,5},{5... | collective-permute-start | bytes 491528 | tf_op jit(solution)/shard_map/ppermute | solution.py:310
  31.7 5.0 %collective-permute-start.12 = (f32[96,256]{1,0:T(8,128)S(1)}, f32[96,256]{1,0:T(8,128)S(1)}, u32[]{:S(2)}, u32[]{:S(2)}) collective-permute-start(f32[96,256]{1,0:T(8,128)S(1)} %get-tuple-element.179), channel_id=1, source_target_pairs={{0,4},{4,8},{8,12},{12,16},{16,20},{20,24},{24,28},{28,0},{1,5},{5... | collective-permute-start | bytes 294920 | tf_op jit(solution)/shard_map/ppermute | solution.py:310

commit v8 on v7

--- a/solution.py
+++ b/solution.py
@@ -96,10 +96,9 @@
     return lax.dot_general(a, b, (contract, ((), ())), preferred_element_type=jnp.float32)
 
 
-def columns_step(start, tile, row_half, cols, dense, live):
-    col_half = cols.astype(jnp.bfloat16)
+def residue_of(start, tile, row_half, col_half, dense, live):
     estimate = dot(col_half, row_half, ((1,), (1,)))
-    parts, at, stop = [], start, start + cols.shape[0]
+    parts, at, stop = [], start, start + col_half.shape[0]
     while at < stop:
         c = at // tile
         end = min((c + 1) * tile, stop)
@@ -107,7 +106,12 @@
         residue = dense[here].astype(jnp.float32) - estimate[here]
         parts.append(jnp.where(live[c : c + 1] > 0, residue, 0.0).astype(jnp.bfloat16))
         at = end
-    residue = parts[0] if len(parts) == 1 else jnp.concatenate(parts, axis=0)
+    return parts[0] if len(parts) == 1 else jnp.concatenate(parts, axis=0)
+
+
+def columns_step(start, tile, row_half, cols, dense, live):
+    col_half = cols.astype(jnp.bfloat16)
+    residue = residue_of(start, tile, row_half, col_half, dense, live)
     return residue, col_half, sgd(cols, dot(residue, row_half, ((1,), (0,))))
 
 
@@ -124,11 +128,12 @@
     pairs = [(coords_hbm, coords), (counts_hbm, counts), (x_hbm.at[0], x_ref), (u_hbm, u_ref)]
     pairs += [(c_hbm.at[at], c_ref.at[at]) for at in (head, tail)]
     copies = [pltpu.make_async_copy(s, d, sems.at[i]) for i, (s, d) in enumerate(pairs)]
-    for copy in copies:
+    for copy in copies[:5]:
         copy.start()
     turn[...] = jnp.zeros_like(turn)
     for copy in copies[:3]:
         copy.wait()
+    copies[5].start()
     scatter(0, x_ref, coords, counts, dense, live)
     copies[3].wait()
     row_half = u_ref[...].astype(jnp.bfloat16)
@@ -227,34 +232,42 @@
     )
 
 
-def rows_kernel(_, __, *refs):
-    *pairs, u_out, half_out = refs
-    n = len(pairs) // 2
-    u_new = sgd(u_out[...], rows_gradient(pairs[:n], pairs[n:]))
-    u_out[...] = u_new
-    half_out[...] = u_new.astype(jnp.bfloat16)
-
-
-def rows(line, u, row_half, residues, halves):
-    return line.call(
-        rows_kernel,
-        "rows_step",
-        (u, row_half, *residues, *halves),
-        [like(u), like(row_half)],
-        aliases={0: 0, 1: 1},
-    )
-
-
 def gradient_kernel(*refs):
     *pairs, acc = refs
     n = len(pairs) // 2
     acc[...] = rows_gradient(pairs[:n], pairs[n:])
 
 
+def gradient(line, u, residues, halves):
+    (acc,) = line.call(gradient_kernel, "rows_gradient", (*residues, *halves), [like(u)])
+    return acc
+
+
+def rows_kernel(part, _, __, *refs):
+    *pairs, u_out, half_out = refs
+    before, pairs = pairs[:part], pairs[part:]
+    n = len(pairs) // 2
+    grad = rows_gradient(pairs[:n], pairs[n:])
+    for acc in before:
+        grad = grad + acc[...]
+    u_new = sgd(u_out[...], grad)
+    u_out[...] = u_new
+    half_out[...] = u_new.astype(jnp.bfloat16)
+
+
+def rows(line, u, row_half, residues, halves, before=()):
+    return line.call(
+        functools.partial(rows_kernel, len(before)),
+        "rows_step",
+        (u, row_half, *before, *residues, *halves),
+        [like(u), like(row_half)],
+        aliases={0: 0, 1: 1},
+    )
+
+
 def last_kernel(tile, u_ref, row_half, dense, live, c_ref, acc, _, *refs):
     n = CHUNKS - 1
     done, (u_hbm, c_hbm, u_new, c_new, sems) = refs[:n], refs[n:]
-    cols = c_hbm.shape[0]
     copies = []
 
     def copy(source, target, at):
@@ -263,17 +276,21 @@
         copies[-1].start()
 
     for h, c in enumerate(done):
-        copy(c, c_hbm, chunk_span(h, cols).start)
-    at = chunk_span(n, cols)
-    residue, col_half, new_cols = columns_step(
-        at.start, tile, row_half[...], c_ref[...], dense[at], live
-    )
+        copy(c, c_hbm, chunk_span(h, c_hbm.shape[0]).start)
+    at = chunk_span(n, c_hbm.shape[0])
+    cols = c_ref[...]
+    col_half = cols.astype(jnp.bfloat16)
+    grad_cols = None
     for r in range(u_ref.shape[0] // tile):
         part = span(r, tile)
-        grad = acc[part] + dot(residue[:, part], col_half, ((0,), (0,)))
+        half = row_half[part]
+        residue = residue_of(at.start, tile, half, col_half, dense[at, part], live[:, part])
+        grad = acc[part] + dot(residue, col_half, ((0,), (0,)))
         u_new[part] = sgd(u_ref[part], grad)
         copy(u_new.at[pl.ds(r * tile, tile)], u_hbm, r * tile)
-    c_new[...] = new_cols
+        grad = dot(residue, half, ((1,), (0,)))
+        grad_cols = grad if grad_cols is None else grad_cols + grad
+    c_new[...] = sgd(cols, grad_cols)
     copy(c_new, c_hbm, at.start)
     for started in copies:
         started.wait()
@@ -284,12 +301,7 @@
     cols, rank = laid[0].shape[0], u.shape[1]
     steps = [columns(line, h, tile, row_half, cs[h], laid) for h in range(n)]
     done, residues, halves = zip(*steps)
-    (acc,) = line.call(
-        gradient_kernel,
-        "rows_gradient",
-        (*residues, *halves),
-        [like(u)],
-    )
+    acc = gradient(line, u, residues, halves)
     return call(
         functools.partial(last_kernel, tile),
         "last_columns_and_rows",
@@ -327,13 +339,16 @@
 
     for stratum in range(1, strata - 1):
         axis = "group" if stratum == 2 else "blk"
-        arrived, cs, residues, halves = cs, [], [], []
+        arrived, cs, residues, halves, before = cs, [], [], [], ()
         for h in range(CHUNKS):
             done, residue, half = columns(line, h, tile, row_half, arrived[h], laid[stratum - 1])
             cs.append(shifted(done, axis))
             residues.append(residue)
             halves.append(half)
-        u, row_half = rows(line, u, row_half, residues, halves)
+            if stratum == 1 and h == CHUNKS - 2:
+                before = (gradient(line, u, residues, halves),)
+                residues, halves = [], []
+        u, row_half = rows(line, u, row_half, residues, halves, before)
     return final(line, tile, u, row_half, cs, laid[-1])
 
 

time: 38.2 us -> 39.3 us (1.029)
  Pallas kernels: 12 us -> 13.3 us
  waiting for transfers between devices: 9.93 us -> 9.53 us
    pallas_call x24 -> x25, Pallas kernels: 12 us -> 13.3 us  [call(): pl.pallas_call(body, out_shape=outs, in_specs=in_specs, out_specs=out_spe...]
    ppermute x16, waiting for transfers between devices: 9.93 us -> 9.53 us  [shifted(): return lax.ppermute(chunk, axis, [(i, (i + 1) % n) for i in range(n)])]
  transfers between devices with their start and end apart: 16 -> 16, of which waited for: 9 -> 8; matrix products, arithmetic and copies ran while one was open for 0% -> 0% of each run, Pallas kernels for 24% -> 24%
where the time goes in v8:
time: 39.3 us; the launch traced here: 39.1 us
  starting transfers between devices  15.4 us (39%)
  Pallas kernels  13.3 us (34%)
  waiting for transfers between devices  9.53 us (24%)
  between operations  0.91 us (2%)
    ppermute x16, starting transfers between devices, shifted(): return lax.ppermute(chunk, axis, [(i, (i + 1) % n) for i in range(n)])  15.4 us
    pallas_call x25, Pallas kernels, call(): pl.pallas_call(body, out_shape=outs, in_specs=in_specs, out_specs=out_spe...  13.3 us
    ppermute x16, waiting for transfers between devices, shifted(): return lax.ppermute(chunk, axis, [(i, (i + 1) % n) for i in range(n)])  9.53 us
  transfers between devices with their start and end apart: 16, of which 8 were waited for; matrix products, arithmetic and copies ran while one was open for 0% of the time, Pallas kernels for 24%

profile of v8, /device:TPU:0, one launch (start us, length us, event | category | flops | bytes accessed | tf_op | source)
XLA Modules:
  0.0 39.1 jit_solution(2900562291884933048)
XLA Ops:
  0.7 2.2 %first_chunk.1 = (f32[512,256]{1,0:T(8,128)S(1)}, f32[512,256]{1,0:T(8,128)S(1)}, bf16[512,256]{1,0:T(8,128)(2,1)S(1)}, bf16[512,512]{1,0:T(8,128)(2,1)S(1)}, f3...) custom-call(f32[512,256]{1,0:T(8,128)} %u_hbm.1, ...), custom_call_target="tpu_custom_call" | custom-call | flops 10000000 | bytes 1 | tf_op jit(solution)/shard_map/first_chunk/pallas_call | solution.py:24
  2.9 0.5 %collective-permute-start = (f32[96,256]{1,0:T(8,128)S(1)}, f32[96,256]{1,0:T(8,128)S(1)}, u32[]{:S(2)}, u32[]{:S(2)}) collective-permute-start(f32[96,256]{1,0:T(8,128)S(1)} %get-tuple-element.116), channel_id=1, source_target_pairs={{0,4},{4,8},{8,12},{12,16},{16,20},{20,24},{24,28},{28,0},{1,5},{5... | collective-permute-start | bytes 294920 | tf_op jit(solution)/shard_map/ppermute | solution.py:322
  3.4 0.5 %other_chunks.1 = (f32[8,128]{1,0:T(8,128)S(1)}, bf16[416,512]{1,0:T(8,128)(2,1)S(1)}, bf16[416,256]{1,0:T(8,128)(2,1)S(1)}, f32[160,256]{1,0:T(8,128)S(1)}, f32...) custom-call(bf16[512,256]{1,0:T(8,128)(2,1)S(1)} %get-tuple-element.103.refs_0_.refs_1_, ...), custom_call_target="tpu_custom_call", output_to_operand_aliasing={{0}: (4, {})} | custom-call | flops 10000000 | bytes 1 | tf_op jit(solution)/shard_map/other_chunks/pallas_call | solution.py:24
  3.9 2.7 %collective-permute-start.1 = (f32[160,256]{1,0:T(8,128)S(1)}, f32[160,256]{1,0:T(8,128)S(1)}, u32[]{:S(2)}, u32[]{:S(2)}) collective-permute-start(f32[160,256]{1,0:T(8,128)S(1)} %get-tuple-element.121), channel_id=1, source_target_pairs={{0,4},{4,8},{8,12},{12,16},{16,20},{20,24},{24,28},{28,0},{1,5},{5... | collective-permute-start | bytes 491528 | tf_op jit(solution)/shard_map/ppermute | solution.py:322
  6.5 0.1 collective-permute-start.2
  6.6 1.5 %collective-permute-start.3 = (f32[96,256]{1,0:T(8,128)S(1)}, f32[96,256]{1,0:T(8,128)S(1)}, u32[]{:S(2)}, u32[]{:S(2)}) collective-permute-start(f32[96,256]{1,0:T(8,128)S(1)} %get-tuple-element.132), channel_id=1, source_target_pairs={{0,4},{4,8},{8,12},{12,16},{16,20},{20,24},{24,28},{28,0},{1,5},{5... | collective-permute-start | bytes 294920 | tf_op jit(solution)/shard_map/ppermute | solution.py:322
  8.2 1.0 %lay_out_tiles.1 = (f32[8,128]{1,0:T(8,128)S(1)}, bf16[512,512]{1,0:T(8,128)(2,1)S(1)}, bf16[512,512]{1,0:T(8,128)(2,1)S(1)}, bf16[512,512]{1,0:T(8,128)(2,1)S(1...) custom-call(bf16[5,8,128,128]{3,2,1,0:T(8,128)(2,1)S(1)} %copy-done,, ...), custom_call_target="tpu_custom_call", output_to_operand_aliasing={{0}: (3, {})} | custom-call | flops 10000000 | bytes 1 | tf_op jit(solution)/shard_map/lay_out_tiles/pallas_call | solution.py:24
  9.1 0.4 %rows_step.4 = (f32[8,128]{1,0:T(8,128)S(1)}, f32[512,256]{1,0:T(8,128)S(1)}, bf16[512,256]{1,0:T(8,128)(2,1)S(1)}) custom-call(f32[512,256]{1,0:T(8,128)S(1)} %get-tuple-element.102.refs_0_, bf16[512,256]{1,0:T(8,128)(2,1)S(1)} %get-tuple-element.103.refs_0_.refs_1_, ...), custom_call_target="tpu_custom_call", output_to_operand_aliasing={{0}: (6, {}), {1}: (0, {}), {2}: (1, {})} | custom-call | flops 10000000 | bytes 1 | tf_op jit(solution)/shard_map/rows_step/pallas_call | solution.py:24
  9.6 0.3 columns_step.15
  9.9 0.1 collective-permute-start.4
  10.1 0.2 collective-permute-done.1.refs_1_
  10.3 0.4 columns_step.16
  10.7 1.4 %collective-permute-start.5 = (f32[160,256]{1,0:T(8,128)S(1)}, f32[160,256]{1,0:T(8,128)S(1)}, u32[]{:S(2)}, u32[]{:S(2)}) collective-permute-start(f32[160,256]{1,0:T(8,128)S(1)} %get-tuple-element.144), channel_id=1, source_target_pairs={{0,4},{4,8},{8,12},{12,16},{16,20},{20,24},{24,28},{28,0},{1,5},{5... | collective-permute-start | bytes 491528 | tf_op jit(solution)/shard_map/ppermute | solution.py:322
  12.0 0.2 collective-permute-done.2.refs_1_
  12.2 0.4 columns_step.17
  12.6 0.4 %rows_gradient.2 = (f32[8,128]{1,0:T(8,128)S(1)}, f32[512,256]{1,0:T(8,128)S(1)}) custom-call(bf16[96,512]{1,0:T(8,128)(2,1)S(1)} %get-tuple-element.120.refs_0_, bf16[160,512]{1,0:T(8,128)(2,1)S(1)} %get-tuple-element.123.refs_1_, bf16[160,512]{1,0:T(8,128)(2,1)S(1)} %get-tuple-element.126.refs_2_, ...), custom_call_target="tpu_custom_call", output_to_operand_aliasing={{0}: (6, {})} | custom-call | flops 10000000 | bytes 1 | tf_op jit(solution)/shard_map/rows_gradient/pallas_call | solution.py:24
  13.0 0.2 collective-permute-done.3.refs_1_
  13.2 0.3 columns_step.18
  13.6 1.2 %collective-permute-start.7 = (f32[96,256]{1,0:T(8,128)S(1)}, f32[96,256]{1,0:T(8,128)S(1)}, u32[]{:S(2)}, u32[]{:S(2)}) collective-permute-start(f32[96,256]{1,0:T(8,128)S(1)} %get-tuple-element.150), channel_id=1, source_target_pairs={{0,4},{4,8},{8,12},{12,16},{16,20},{20,24},{24,28},{28,0},{1,5},{5... | collective-permute-start | bytes 294920 | tf_op jit(solution)/shard_map/ppermute | solution.py:322
  14.8 0.3 rows_step.5
  15.1 0.3 columns_step.19
  15.4 1.6 %collective-permute-start.8 = (f32[96,256]{1,0:T(8,128)S(1)}, f32[96,256]{1,0:T(8,128)S(1)}, u32[]{:S(2)}, u32[]{:S(2)}) collective-permute-start(f32[96,256]{1,0:T(8,128)S(1)} %get-tuple-element.160), channel_id=1, source_target_pairs={{0,1},{1,2},{2,3},{3,0},{4,5},{5,6},{6,7},{7,4},{8,9},{9,10},{10,1... | collective-permute-start | bytes 294920 | tf_op jit(solution)/shard_map/ppermute | solution.py:322
  17.0 0.4 columns_step.20
  17.4 1.7 %collective-permute-start.9 = (f32[160,256]{1,0:T(8,128)S(1)}, f32[160,256]{1,0:T(8,128)S(1)}, u32[]{:S(2)}, u32[]{:S(2)}) collective-permute-start(f32[160,256]{1,0:T(8,128)S(1)} %get-tuple-element.165), channel_id=1, source_target_pairs={{0,1},{1,2},{2,3},{3,0},{4,5},{5,6},{6,7},{7,4},{8,9},{9,10},{10,1... | collective-permute-start | bytes 491528 | tf_op jit(solution)/shard_map/ppermute | solution.py:322
  19.1 0.4 columns_step.21
  19.5 1.6 %collective-permute-start.10 = (f32[160,256]{1,0:T(8,128)S(1)}, f32[160,256]{1,0:T(8,128)S(1)}, u32[]{:S(2)}, u32[]{:S(2)}) collective-permute-start(f32[160,256]{1,0:T(8,128)S(1)} %get-tuple-element.168), channel_id=1, source_target_pairs={{0,1},{1,2},{2,3},{3,0},{4,5},{5,6},{6,7},{7,4},{8,9},{9,10},{10,1... | collective-permute-start | bytes 491528 | tf_op jit(solution)/shard_map/ppermute | solution.py:322
  21.1 0.3 columns_step.22
  21.5 1.6 %collective-permute-start.11 = (f32[96,256]{1,0:T(8,128)S(1)}, f32[96,256]{1,0:T(8,128)S(1)}, u32[]{:S(2)}, u32[]{:S(2)}) collective-permute-start(f32[96,256]{1,0:T(8,128)S(1)} %get-tuple-element.171), channel_id=1, source_target_pairs={{0,1},{1,2},{2,3},{3,0},{4,5},{5,6},{6,7},{7,4},{8,9},{9,10},{10,1... | collective-permute-start | bytes 294920 | tf_op jit(solution)/shard_map/ppermute | solution.py:322
  23.1 0.5 %rows_step.6 = (f32[8,128]{1,0:T(8,128)S(1)}, f32[512,256]{1,0:T(8,128)S(1)}, bf16[512,256]{1,0:T(8,128)(2,1)S(1)}) custom-call(f32[512,256]{1,0:T(8,128)S(1)} %get-tuple-element.137.refs_0_, bf16[512,256]{1,0:T(8,128)(2,1)S(1)} %get-tuple-element.138.refs_0_.refs_1_, ...), custom_call_target="tpu_custom_call", output_to_operand_aliasing={{0}: (10, {}), {1}: (0, {}), {2}: (1, {})} | custom-call | flops 10000000 | bytes 1 | tf_op jit(solution)/shard_map/rows_step/pallas_call | solution.py:24
  23.6 0.3 columns_step.23
  24.0 0.1 collective-permute-start.13
  24.0 2.4 %collective-permute-done.9.refs_1_ = f32[160,256]{1,0:T(8,128)S(1)} collective-permute-done((f32[160,256]{1,0:T(8,128)S(1)}, f32[160,256]{1,0:T(8,128)S(1)}, u32[]{:S(2)}, u32[]{:S(2)}) %collective-permute-start.9) | collective-permute-done | bytes 163872 | tf_op jit(solution)/shard_map/ppermute | solution.py:322
  26.4 0.4 columns_step.24
  26.8 0.2 collective-permute-start.14
  27.0 2.9 %collective-permute-done.10.refs_1_ = f32[160,256]{1,0:T(8,128)S(1)} collective-permute-done((f32[160,256]{1,0:T(8,128)S(1)}, f32[160,256]{1,0:T(8,128)S(1)}, u32[]{:S(2)}, u32[]{:S(2)}) %collective-permute-start.10) | collective-permute-done | bytes 163872 | tf_op jit(solution)/shard_map/ppermute | solution.py:322
  29.9 0.4 columns_step.25
  30.3 0.2 collective-permute-start.15
  30.5 1.5 %collective-permute-done.11.refs_1_ = f32[96,256]{1,0:T(8,128)S(1)} collective-permute-done((f32[96,256]{1,0:T(8,128)S(1)}, f32[96,256]{1,0:T(8,128)S(1)}, u32[]{:S(2)}, u32[]{:S(2)}) %collective-permute-start.11) | collective-permute-done | bytes 98336 | tf_op jit(solution)/shard_map/ppermute | solution.py:322
  32.0 0.3 columns_step.26
  32.4 0.8 %collective-permute-start.12 = (f32[96,256]{1,0:T(8,128)S(1)}, f32[96,256]{1,0:T(8,128)S(1)}, u32[]{:S(2)}, u32[]{:S(2)}) collective-permute-start(f32[96,256]{1,0:T(8,128)S(1)} %get-tuple-element.183), channel_id=1, source_target_pairs={{0,4},{4,8},{8,12},{12,16},{16,20},{20,24},{24,28},{28,0},{1,5},{5... | collective-permute-start | bytes 294920 | tf_op jit(solution)/shard_map/ppermute | solution.py:322
  33.2 0.5 %rows_step.7 = (f32[8,128]{1,0:T(8,128)S(1)}, f32[512,256]{1,0:T(8,128)S(1)}, bf16[512,256]{1,0:T(8,128)(2,1)S(1)}) custom-call(f32[512,256]{1,0:T(8,128)S(1)} %get-tuple-element.158.refs_0_, bf16[512,256]{1,0:T(8,128)(2,1)S(1)} %get-tuple-element.159.refs_0_.refs_1_, ...), custom_call_target="tpu_custom_call", output_to_operand_aliasing={{0}: (10, {}), {1}: (0, {}), {2}: (1, {})} | custom-call | flops 10000000 | bytes 1 | tf_op jit(solution)/shard_map/rows_step/pallas_call | solution.py:24
  33.7 0.3 columns_step.27
  34.1 0.4 columns_step.28
  34.4 1.6 %collective-permute-done.15.refs_1_ = f32[160,256]{1,0:T(8,128)S(1)} collective-permute-done((f32[160,256]{1,0:T(8,128)S(1)}, f32[160,256]{1,0:T(8,128)S(1)}, u32[]{:S(2)}, u32[]{:S(2)}) %collective-permute-start.15) | collective-permute-done | bytes 163872 | tf_op jit(solution)/shard_map/ppermute | solution.py:322
  36.0 0.4 columns_step.29
  36.4 0.4 %rows_gradient.3 = (f32[8,128]{1,0:T(8,128)S(1)}, f32[512,256]{1,0:T(8,128)S(1)}) custom-call(bf16[96,512]{1,0:T(8,128)(2,1)S(1)} %get-tuple-element.186.refs_0_, bf16[160,512]{1,0:T(8,128)(2,1)S(1)} %get-tuple-element.189.refs_1_, bf16[160,512]{1,0:T(8,128)(2,1)S(1)} %get-tuple-element.192.refs_2_, ...), custom_call_target="tpu_custom_call", output_to_operand_aliasing={{0}: (6, {})} | custom-call | flops 10000000 | bytes 1 | tf_op jit(solution)/shard_map/rows_gradient/pallas_call | solution.py:24
  36.8 0.6 %collective-permute-done.12.c_ref = f32[96,256]{1,0:T(8,128)S(1)} collective-permute-done((f32[96,256]{1,0:T(8,128)S(1)}, f32[96,256]{1,0:T(8,128)S(1)}, u32[]{:S(2)}, u32[]{:S(2)}) %collective-permute-start.12) | collective-permute-done | bytes 98336 | tf_op jit(solution)/shard_map/ppermute | solution.py:322
  37.4 1.8 %last_columns_and_rows.1 = (f32[512,256]{1,0:T(8,128)}, f32[512,256]{1,0:T(8,128)}) custom-call(f32[512,256]{1,0:T(8,128)S(1)} %get-tuple-element.179.u_ref, bf16[512,256]{1,0:T(8,128)(2,1)S(1)} %get-tuple-element.180.refs_0_.row_half, bf16[512,512]{1,0:T(8,128)(2,1)S(1)} %get-tuple-element.181.refs_2_.dense, f32[8,512]{1,0:T(8,128)S(1)} %get-tuple-element.182.refs_3_.live, ...), custom_call_target="tpu_custom_call" | custom-call | flops 10000000 | bytes 1 | tf_op jit(solution)/shard_map/last_columns_and_rows/pallas_call | solution.py:24
  (15 shorter events, 0.1 us)
Async XLA Ops:
  0.6 7.5 %copy-start = (bf16[5,8,128,128]{3,2,1,0:T(8,128)(2,1)S(1)}, bf16[5,8,128,128]{3,2,1,0:T(8,128)(2,1)}, u32[]{:S(2)}) copy-start(bf16[5,8,128,128]{3,2,1,0:T(8,128)(2,1)} %x_ref.1) | copy-start | bytes 3932164
  0.6 7.5 %copy-start.1 = (s32[5,8,2]{1,2,0:T(2,128)S(1)}, s32[5,8,2]{1,2,0:T(2,128)}, u32[]{:S(2)}) copy-start(s32[5,8,2]{1,2,0:T(2,128)} %param.8) | copy-start | bytes 964
  0.7 7.5 %copy-start.2 = (s32[5,1]{0,1:T(1,128)S(1)}, s32[5,1]{0,1:T(1,128)}, u32[]{:S(2)}) copy-start(s32[5,1]{0,1:T(1,128)} %param.9) | copy-start | bytes 64
  2.9 6.7 %collective-permute-start = (f32[96,256]{1,0:T(8,128)S(1)}, f32[96,256]{1,0:T(8,128)S(1)}, u32[]{:S(2)}, u32[]{:S(2)}) collective-permute-start(f32[96,256]{1,0:T(8,128)S(1)} %get-tuple-element.116), channel_id=1, source_target_pairs={{0,4},{4,8},{8,12},{12,16},{16,20},{20,24},{24,28},{28,0},{1,5},{5... | collective-permute-start | bytes 294920 | tf_op jit(solution)/shard_map/ppermute | solution.py:322
  3.9 6.4 %collective-permute-start.1 = (f32[160,256]{1,0:T(8,128)S(1)}, f32[160,256]{1,0:T(8,128)S(1)}, u32[]{:S(2)}, u32[]{:S(2)}) collective-permute-start(f32[160,256]{1,0:T(8,128)S(1)} %get-tuple-element.121), channel_id=1, source_target_pairs={{0,4},{4,8},{8,12},{12,16},{16,20},{20,24},{24,28},{28,0},{1,5},{5... | collective-permute-start | bytes 491528 | tf_op jit(solution)/shard_map/ppermute | solution.py:322
  6.5 5.6 %collective-permute-start.2 = (f32[160,256]{1,0:T(8,128)S(1)}, f32[160,256]{1,0:T(8,128)S(1)}, u32[]{:S(2)}, u32[]{:S(2)}) collective-permute-start(f32[160,256]{1,0:T(8,128)S(1)} %get-tuple-element.124), channel_id=1, source_target_pairs={{0,4},{4,8},{8,12},{12,16},{16,20},{20,24},{24,28},{28,0},{1,5},{5... | collective-permute-start | bytes 491528 | tf_op jit(solution)/shard_map/ppermute | solution.py:322
  6.6 6.6 %collective-permute-start.3 = (f32[96,256]{1,0:T(8,128)S(1)}, f32[96,256]{1,0:T(8,128)S(1)}, u32[]{:S(2)}, u32[]{:S(2)}) collective-permute-start(f32[96,256]{1,0:T(8,128)S(1)} %get-tuple-element.132), channel_id=1, source_target_pairs={{0,4},{4,8},{8,12},{12,16},{16,20},{20,24},{24,28},{28,0},{1,5},{5... | collective-permute-start | bytes 294920 | tf_op jit(solution)/shard_map/ppermute | solution.py:322
  9.9 5.1 %collective-permute-start.4 = (f32[96,256]{1,0:T(8,128)S(1)}, f32[96,256]{1,0:T(8,128)S(1)}, u32[]{:S(2)}, u32[]{:S(2)}) collective-permute-start(f32[96,256]{1,0:T(8,128)S(1)} %get-tuple-element.139), channel_id=1, source_target_pairs={{0,4},{4,8},{8,12},{12,16},{16,20},{20,24},{24,28},{28,0},{1,5},{5... | collective-permute-start | bytes 294920 | tf_op jit(solution)/shard_map/ppermute | solution.py:322
  10.7 6.4 %collective-permute-start.5 = (f32[160,256]{1,0:T(8,128)S(1)}, f32[160,256]{1,0:T(8,128)S(1)}, u32[]{:S(2)}, u32[]{:S(2)}) collective-permute-start(f32[160,256]{1,0:T(8,128)S(1)} %get-tuple-element.144), channel_id=1, source_target_pairs={{0,4},{4,8},{8,12},{12,16},{16,20},{20,24},{24,28},{28,0},{1,5},{5... | collective-permute-start | bytes 491528 | tf_op jit(solution)/shard_map/ppermute | solution.py:322
  12.6 6.6 %collective-permute-start.6 = (f32[160,256]{1,0:T(8,128)S(1)}, f32[160,256]{1,0:T(8,128)S(1)}, u32[]{:S(2)}, u32[]{:S(2)}) collective-permute-start(f32[160,256]{1,0:T(8,128)S(1)} %get-tuple-element.147), channel_id=1, source_target_pairs={{0,4},{4,8},{8,12},{12,16},{16,20},{20,24},{24,28},{28,0},{1,5},{5... | collective-permute-start | bytes 491528 | tf_op jit(solution)/shard_map/ppermute | solution.py:322
  13.6 7.6 %collective-permute-start.7 = (f32[96,256]{1,0:T(8,128)S(1)}, f32[96,256]{1,0:T(8,128)S(1)}, u32[]{:S(2)}, u32[]{:S(2)}) collective-permute-start(f32[96,256]{1,0:T(8,128)S(1)} %get-tuple-element.150), channel_id=1, source_target_pairs={{0,4},{4,8},{8,12},{12,16},{16,20},{20,24},{24,28},{28,0},{1,5},{5... | collective-permute-start | bytes 294920 | tf_op jit(solution)/shard_map/ppermute | solution.py:322
  15.4 8.2 %collective-permute-start.8 = (f32[96,256]{1,0:T(8,128)S(1)}, f32[96,256]{1,0:T(8,128)S(1)}, u32[]{:S(2)}, u32[]{:S(2)}) collective-permute-start(f32[96,256]{1,0:T(8,128)S(1)} %get-tuple-element.160), channel_id=1, source_target_pairs={{0,1},{1,2},{2,3},{3,0},{4,5},{5,6},{6,7},{7,4},{8,9},{9,10},{10,1... | collective-permute-start | bytes 294920 | tf_op jit(solution)/shard_map/ppermute | solution.py:322
  17.4 9.0 %collective-permute-start.9 = (f32[160,256]{1,0:T(8,128)S(1)}, f32[160,256]{1,0:T(8,128)S(1)}, u32[]{:S(2)}, u32[]{:S(2)}) collective-permute-start(f32[160,256]{1,0:T(8,128)S(1)} %get-tuple-element.165), channel_id=1, source_target_pairs={{0,1},{1,2},{2,3},{3,0},{4,5},{5,6},{6,7},{7,4},{8,9},{9,10},{10,1... | collective-permute-start | bytes 491528 | tf_op jit(solution)/shard_map/ppermute | solution.py:322
  19.5 10.4 %collective-permute-start.10 = (f32[160,256]{1,0:T(8,128)S(1)}, f32[160,256]{1,0:T(8,128)S(1)}, u32[]{:S(2)}, u32[]{:S(2)}) collective-permute-start(f32[160,256]{1,0:T(8,128)S(1)} %get-tuple-element.168), channel_id=1, source_target_pairs={{0,1},{1,2},{2,3},{3,0},{4,5},{5,6},{6,7},{7,4},{8,9},{9,10},{10,1... | collective-permute-start | bytes 491528 | tf_op jit(solution)/shard_map/ppermute | solution.py:322
  21.5 10.5 %collective-permute-start.11 = (f32[96,256]{1,0:T(8,128)S(1)}, f32[96,256]{1,0:T(8,128)S(1)}, u32[]{:S(2)}, u32[]{:S(2)}) collective-permute-start(f32[96,256]{1,0:T(8,128)S(1)} %get-tuple-element.171), channel_id=1, source_target_pairs={{0,1},{1,2},{2,3},{3,0},{4,5},{5,6},{6,7},{7,4},{8,9},{9,10},{10,1... | collective-permute-start | bytes 294920 | tf_op jit(solution)/shard_map/ppermute | solution.py:322
  24.0 9.7 %collective-permute-start.13 = (f32[96,256]{1,0:T(8,128)S(1)}, f32[96,256]{1,0:T(8,128)S(1)}, u32[]{:S(2)}, u32[]{:S(2)}) collective-permute-start(f32[96,256]{1,0:T(8,128)S(1)} %get-tuple-element.184), channel_id=1, source_target_pairs={{0,4},{4,8},{8,12},{12,16},{16,20},{20,24},{24,28},{28,0},{1,5},{5... | collective-permute-start | bytes 294920 | tf_op jit(solution)/shard_map/ppermute | solution.py:322
  26.8 7.3 %collective-permute-start.14 = (f32[160,256]{1,0:T(8,128)S(1)}, f32[160,256]{1,0:T(8,128)S(1)}, u32[]{:S(2)}, u32[]{:S(2)}) collective-permute-start(f32[160,256]{1,0:T(8,128)S(1)} %get-tuple-element.187), channel_id=1, source_target_pairs={{0,4},{4,8},{8,12},{12,16},{16,20},{20,24},{24,28},{28,0},{1,5},{5... | collective-permute-start | bytes 491528 | tf_op jit(solution)/shard_map/ppermute | solution.py:322
  30.3 5.7 %collective-permute-start.15 = (f32[160,256]{1,0:T(8,128)S(1)}, f32[160,256]{1,0:T(8,128)S(1)}, u32[]{:S(2)}, u32[]{:S(2)}) collective-permute-start(f32[160,256]{1,0:T(8,128)S(1)} %get-tuple-element.190), channel_id=1, source_target_pairs={{0,4},{4,8},{8,12},{12,16},{16,20},{20,24},{24,28},{28,0},{1,5},{5... | collective-permute-start | bytes 491528 | tf_op jit(solution)/shard_map/ppermute | solution.py:322
  32.4 5.0 %collective-permute-start.12 = (f32[96,256]{1,0:T(8,128)S(1)}, f32[96,256]{1,0:T(8,128)S(1)}, u32[]{:S(2)}, u32[]{:S(2)}) collective-permute-start(f32[96,256]{1,0:T(8,128)S(1)} %get-tuple-element.183), channel_id=1, source_target_pairs={{0,4},{4,8},{8,12},{12,16},{16,20},{20,24},{24,28},{28,0},{1,5},{5... | collective-permute-start | bytes 294920 | tf_op jit(solution)/shard_map/ppermute | solution.py:322

commit v9 on v7

--- a/solution.py
+++ b/solution.py
@@ -124,8 +124,8 @@
     pairs = [(coords_hbm, coords), (counts_hbm, counts), (x_hbm.at[0], x_ref), (u_hbm, u_ref)]
     pairs += [(c_hbm.at[at], c_ref.at[at]) for at in (head, tail)]
     copies = [pltpu.make_async_copy(s, d, sems.at[i]) for i, (s, d) in enumerate(pairs)]
-    for copy in copies:
-        copy.start()
+    for i in (3, 0, 1, 2, 4, 5):
+        copies[i].start()
     turn[...] = jnp.zeros_like(turn)
     for copy in copies[:3]:
         copy.wait()

time: 38.2 us -> 38.3 us (level)
  no operation moved by 1% of the time
where the time goes in v9:
time: 38.3 us; the launch traced here: 38.1 us
  starting transfers between devices  15.1 us (39%)
  Pallas kernels  12.2 us (32%)
  waiting for transfers between devices  9.97 us (26%)
  between operations  0.9 us (2%)
    ppermute x16, starting transfers between devices, shifted(): return lax.ppermute(chunk, axis, [(i, (i + 1) % n) for i in range(n)])  15.1 us
    pallas_call x24, Pallas kernels, call(): pl.pallas_call(body, out_shape=outs, in_specs=in_specs, out_specs=out_spe...  12.2 us
    ppermute x16, waiting for transfers between devices, shifted(): return lax.ppermute(chunk, axis, [(i, (i + 1) % n) for i in range(n)])  9.97 us
  transfers between devices with their start and end apart: 16, of which 9 were waited for; matrix products, arithmetic and copies ran while one was open for 0% of the time, Pallas kernels for 24%

profile of v9, /device:TPU:0, one launch (start us, length us, event | category | flops | bytes accessed | tf_op | source)
XLA Modules:
  0.0 38.1 jit_solution(12792015075132521655)
XLA Ops:
  0.7 1.8 %first_chunk.1 = (f32[512,256]{1,0:T(8,128)S(1)}, f32[512,256]{1,0:T(8,128)S(1)}, bf16[512,256]{1,0:T(8,128)(2,1)S(1)}, bf16[512,512]{1,0:T(8,128)(2,1)S(1)}, f3...) custom-call(f32[512,256]{1,0:T(8,128)} %u_hbm.1, ...), custom_call_target="tpu_custom_call" | custom-call | flops 10000000 | bytes 1 | tf_op jit(solution)/shard_map/first_chunk/pallas_call | solution.py:24
  2.4 0.5 %collective-permute-start = (f32[96,256]{1,0:T(8,128)S(1)}, f32[96,256]{1,0:T(8,128)S(1)}, u32[]{:S(2)}, u32[]{:S(2)}) collective-permute-start(f32[96,256]{1,0:T(8,128)S(1)} %get-tuple-element.114), channel_id=1, source_target_pairs={{0,4},{4,8},{8,12},{12,16},{16,20},{20,24},{24,28},{28,0},{1,5},{5... | collective-permute-start | bytes 294920 | tf_op jit(solution)/shard_map/ppermute | solution.py:310
  2.9 0.5 %other_chunks.1 = (f32[8,128]{1,0:T(8,128)S(1)}, bf16[416,512]{1,0:T(8,128)(2,1)S(1)}, bf16[416,256]{1,0:T(8,128)(2,1)S(1)}, f32[160,256]{1,0:T(8,128)S(1)}, f32...) custom-call(bf16[512,256]{1,0:T(8,128)(2,1)S(1)} %get-tuple-element.101.refs_0_.refs_1_, ...), custom_call_target="tpu_custom_call", output_to_operand_aliasing={{0}: (4, {})} | custom-call | flops 10000000 | bytes 1 | tf_op jit(solution)/shard_map/other_chunks/pallas_call | solution.py:24
  3.5 2.7 %collective-permute-start.1 = (f32[160,256]{1,0:T(8,128)S(1)}, f32[160,256]{1,0:T(8,128)S(1)}, u32[]{:S(2)}, u32[]{:S(2)}) collective-permute-start(f32[160,256]{1,0:T(8,128)S(1)} %get-tuple-element.119), channel_id=1, source_target_pairs={{0,4},{4,8},{8,12},{12,16},{16,20},{20,24},{24,28},{28,0},{1,5},{5... | collective-permute-start | bytes 491528 | tf_op jit(solution)/shard_map/ppermute | solution.py:310
  6.1 0.1 collective-permute-start.2
  6.2 1.5 %collective-permute-start.3 = (f32[96,256]{1,0:T(8,128)S(1)}, f32[96,256]{1,0:T(8,128)S(1)}, u32[]{:S(2)}, u32[]{:S(2)}) collective-permute-start(f32[96,256]{1,0:T(8,128)S(1)} %get-tuple-element.125), channel_id=1, source_target_pairs={{0,4},{4,8},{8,12},{12,16},{16,20},{20,24},{24,28},{28,0},{1,5},{5... | collective-permute-start | bytes 294920 | tf_op jit(solution)/shard_map/ppermute | solution.py:310
  7.7 1.0 %lay_out_tiles.1 = (f32[8,128]{1,0:T(8,128)S(1)}, bf16[512,512]{1,0:T(8,128)(2,1)S(1)}, bf16[512,512]{1,0:T(8,128)(2,1)S(1)}, bf16[512,512]{1,0:T(8,128)(2,1)S(1...) custom-call(bf16[5,8,128,128]{3,2,1,0:T(8,128)(2,1)S(1)} %copy-done,, ...), custom_call_target="tpu_custom_call", output_to_operand_aliasing={{0}: (3, {})} | custom-call | flops 10000000 | bytes 1 | tf_op jit(solution)/shard_map/lay_out_tiles/pallas_call | solution.py:24
  8.7 0.4 %rows_step.4 = (f32[8,128]{1,0:T(8,128)S(1)}, f32[512,256]{1,0:T(8,128)S(1)}, bf16[512,256]{1,0:T(8,128)(2,1)S(1)}) custom-call(f32[512,256]{1,0:T(8,128)S(1)} %get-tuple-element.100.refs_0_, bf16[512,256]{1,0:T(8,128)(2,1)S(1)} %get-tuple-element.101.refs_0_.refs_1_, ...), custom_call_target="tpu_custom_call", output_to_operand_aliasing={{0}: (6, {}), {1}: (0, {}), {2}: (1, {})} | custom-call | flops 10000000 | bytes 1 | tf_op jit(solution)/shard_map/rows_step/pallas_call | solution.py:24
  9.2 0.3 columns_step.15
  9.5 0.1 collective-permute-start.4
  9.6 0.2 collective-permute-done.1.refs_1_
  9.9 0.4 columns_step.16
  10.3 1.3 %collective-permute-start.5 = (f32[160,256]{1,0:T(8,128)S(1)}, f32[160,256]{1,0:T(8,128)S(1)}, u32[]{:S(2)}, u32[]{:S(2)}) collective-permute-start(f32[160,256]{1,0:T(8,128)S(1)} %get-tuple-element.140), channel_id=1, source_target_pairs={{0,4},{4,8},{8,12},{12,16},{16,20},{20,24},{24,28},{28,0},{1,5},{5... | collective-permute-start | bytes 491528 | tf_op jit(solution)/shard_map/ppermute | solution.py:310
  11.6 0.2 collective-permute-done.2.refs_1_
  11.8 0.4 columns_step.17
  12.2 0.6 %collective-permute-done.3.refs_1_ = f32[96,256]{1,0:T(8,128)S(1)} collective-permute-done((f32[96,256]{1,0:T(8,128)S(1)}, f32[96,256]{1,0:T(8,128)S(1)}, u32[]{:S(2)}, u32[]{:S(2)}) %collective-permute-start.3) | collective-permute-done | bytes 98336 | tf_op jit(solution)/shard_map/ppermute | solution.py:310
  12.8 0.3 columns_step.18
  13.2 0.8 %collective-permute-start.7 = (f32[96,256]{1,0:T(8,128)S(1)}, f32[96,256]{1,0:T(8,128)S(1)}, u32[]{:S(2)}, u32[]{:S(2)}) collective-permute-start(f32[96,256]{1,0:T(8,128)S(1)} %get-tuple-element.146), channel_id=1, source_target_pairs={{0,4},{4,8},{8,12},{12,16},{16,20},{20,24},{24,28},{28,0},{1,5},{5... | collective-permute-start | bytes 294920 | tf_op jit(solution)/shard_map/ppermute | solution.py:310
  13.9 0.5 %rows_step.5 = (f32[8,128]{1,0:T(8,128)S(1)}, f32[512,256]{1,0:T(8,128)S(1)}, bf16[512,256]{1,0:T(8,128)(2,1)S(1)}) custom-call(f32[512,256]{1,0:T(8,128)S(1)} %get-tuple-element.112.refs_0_, bf16[512,256]{1,0:T(8,128)(2,1)S(1)} %get-tuple-element.113.refs_0_.refs_1_, ...), custom_call_target="tpu_custom_call", output_to_operand_aliasing={{0}: (10, {}), {1}: (0, {}), {2}: (1, {})} | custom-call | flops 10000000 | bytes 1 | tf_op jit(solution)/shard_map/rows_step/pallas_call | solution.py:24
  14.4 0.1 collective-permute-done.4.refs_1_
  14.5 0.3 columns_step.19
  14.9 1.6 %collective-permute-start.8 = (f32[96,256]{1,0:T(8,128)S(1)}, f32[96,256]{1,0:T(8,128)S(1)}, u32[]{:S(2)}, u32[]{:S(2)}) collective-permute-start(f32[96,256]{1,0:T(8,128)S(1)} %get-tuple-element.156), channel_id=1, source_target_pairs={{0,1},{1,2},{2,3},{3,0},{4,5},{5,6},{6,7},{7,4},{8,9},{9,10},{10,1... | collective-permute-start | bytes 294920 | tf_op jit(solution)/shard_map/ppermute | solution.py:310
  16.5 0.4 columns_step.20
  16.9 1.8 %collective-permute-start.9 = (f32[160,256]{1,0:T(8,128)S(1)}, f32[160,256]{1,0:T(8,128)S(1)}, u32[]{:S(2)}, u32[]{:S(2)}) collective-permute-start(f32[160,256]{1,0:T(8,128)S(1)} %get-tuple-element.161), channel_id=1, source_target_pairs={{0,1},{1,2},{2,3},{3,0},{4,5},{5,6},{6,7},{7,4},{8,9},{9,10},{10,1... | collective-permute-start | bytes 491528 | tf_op jit(solution)/shard_map/ppermute | solution.py:310
  18.7 0.4 columns_step.21
  19.1 1.6 %collective-permute-start.10 = (f32[160,256]{1,0:T(8,128)S(1)}, f32[160,256]{1,0:T(8,128)S(1)}, u32[]{:S(2)}, u32[]{:S(2)}) collective-permute-start(f32[160,256]{1,0:T(8,128)S(1)} %get-tuple-element.164), channel_id=1, source_target_pairs={{0,1},{1,2},{2,3},{3,0},{4,5},{5,6},{6,7},{7,4},{8,9},{9,10},{10,1... | collective-permute-start | bytes 491528 | tf_op jit(solution)/shard_map/ppermute | solution.py:310
  20.7 0.3 columns_step.22
  21.1 1.6 %collective-permute-start.11 = (f32[96,256]{1,0:T(8,128)S(1)}, f32[96,256]{1,0:T(8,128)S(1)}, u32[]{:S(2)}, u32[]{:S(2)}) collective-permute-start(f32[96,256]{1,0:T(8,128)S(1)} %get-tuple-element.167), channel_id=1, source_target_pairs={{0,1},{1,2},{2,3},{3,0},{4,5},{5,6},{6,7},{7,4},{8,9},{9,10},{10,1... | collective-permute-start | bytes 294920 | tf_op jit(solution)/shard_map/ppermute | solution.py:310
  22.7 0.5 %rows_step.6 = (f32[8,128]{1,0:T(8,128)S(1)}, f32[512,256]{1,0:T(8,128)S(1)}, bf16[512,256]{1,0:T(8,128)(2,1)S(1)}) custom-call(f32[512,256]{1,0:T(8,128)S(1)} %get-tuple-element.133.refs_0_, bf16[512,256]{1,0:T(8,128)(2,1)S(1)} %get-tuple-element.134.refs_0_.refs_1_, ...), custom_call_target="tpu_custom_call", output_to_operand_aliasing={{0}: (10, {}), {1}: (0, {}), {2}: (1, {})} | custom-call | flops 10000000 | bytes 1 | tf_op jit(solution)/shard_map/rows_step/pallas_call | solution.py:24
  23.2 0.3 columns_step.23
  23.5 0.1 collective-permute-start.13
  23.6 2.3 %collective-permute-done.9.refs_1_ = f32[160,256]{1,0:T(8,128)S(1)} collective-permute-done((f32[160,256]{1,0:T(8,128)S(1)}, f32[160,256]{1,0:T(8,128)S(1)}, u32[]{:S(2)}, u32[]{:S(2)}) %collective-permute-start.9) | collective-permute-done | bytes 163872 | tf_op jit(solution)/shard_map/ppermute | solution.py:310
  25.9 0.4 columns_step.24
  26.2 0.2 collective-permute-start.14
  26.5 2.9 %collective-permute-done.10.refs_1_ = f32[160,256]{1,0:T(8,128)S(1)} collective-permute-done((f32[160,256]{1,0:T(8,128)S(1)}, f32[160,256]{1,0:T(8,128)S(1)}, u32[]{:S(2)}, u32[]{:S(2)}) %collective-permute-start.10) | collective-permute-done | bytes 163872 | tf_op jit(solution)/shard_map/ppermute | solution.py:310
  29.4 0.4 columns_step.25
  29.8 0.2 collective-permute-start.15
  30.0 1.5 %collective-permute-done.11.refs_1_ = f32[96,256]{1,0:T(8,128)S(1)} collective-permute-done((f32[96,256]{1,0:T(8,128)S(1)}, f32[96,256]{1,0:T(8,128)S(1)}, u32[]{:S(2)}, u32[]{:S(2)}) %collective-permute-start.11) | collective-permute-done | bytes 98336 | tf_op jit(solution)/shard_map/ppermute | solution.py:310
  31.5 0.3 columns_step.26
  31.8 0.8 %collective-permute-start.12 = (f32[96,256]{1,0:T(8,128)S(1)}, f32[96,256]{1,0:T(8,128)S(1)}, u32[]{:S(2)}, u32[]{:S(2)}) collective-permute-start(f32[96,256]{1,0:T(8,128)S(1)} %get-tuple-element.179), channel_id=1, source_target_pairs={{0,4},{4,8},{8,12},{12,16},{16,20},{20,24},{24,28},{28,0},{1,5},{5... | collective-permute-start | bytes 294920 | tf_op jit(solution)/shard_map/ppermute | solution.py:310
  32.7 0.5 %rows_step.7 = (f32[8,128]{1,0:T(8,128)S(1)}, f32[512,256]{1,0:T(8,128)S(1)}, bf16[512,256]{1,0:T(8,128)(2,1)S(1)}) custom-call(f32[512,256]{1,0:T(8,128)S(1)} %get-tuple-element.154.refs_0_, bf16[512,256]{1,0:T(8,128)(2,1)S(1)} %get-tuple-element.155.refs_0_.refs_1_, ...), custom_call_target="tpu_custom_call", output_to_operand_aliasing={{0}: (10, {}), {1}: (0, {}), {2}: (1, {})} | custom-call | flops 10000000 | bytes 1 | tf_op jit(solution)/shard_map/rows_step/pallas_call | solution.py:24
  33.1 0.3 columns_step.27
  33.5 0.4 columns_step.28
  33.9 1.6 %collective-permute-done.15.refs_1_ = f32[160,256]{1,0:T(8,128)S(1)} collective-permute-done((f32[160,256]{1,0:T(8,128)S(1)}, f32[160,256]{1,0:T(8,128)S(1)}, u32[]{:S(2)}, u32[]{:S(2)}) %collective-permute-start.15) | collective-permute-done | bytes 163872 | tf_op jit(solution)/shard_map/ppermute | solution.py:310
  35.4 0.4 columns_step.29
  35.8 0.4 %rows_gradient.1 = (f32[8,128]{1,0:T(8,128)S(1)}, f32[512,256]{1,0:T(8,128)S(1)}) custom-call(bf16[96,512]{1,0:T(8,128)(2,1)S(1)} %get-tuple-element.182.refs_0_, bf16[160,512]{1,0:T(8,128)(2,1)S(1)} %get-tuple-element.185.refs_1_, bf16[160,512]{1,0:T(8,128)(2,1)S(1)} %get-tuple-element.188.refs_2_, ...), custom_call_target="tpu_custom_call", output_to_operand_aliasing={{0}: (6, {})} | custom-call | flops 10000000 | bytes 1 | tf_op jit(solution)/shard_map/rows_gradient/pallas_call | solution.py:24
  36.2 0.6 %collective-permute-done.12.c_ref = f32[96,256]{1,0:T(8,128)S(1)} collective-permute-done((f32[96,256]{1,0:T(8,128)S(1)}, f32[96,256]{1,0:T(8,128)S(1)}, u32[]{:S(2)}, u32[]{:S(2)}) %collective-permute-start.12) | collective-permute-done | bytes 98336 | tf_op jit(solution)/shard_map/ppermute | solution.py:310
  36.8 1.3 %last_columns_and_rows.1 = (f32[512,256]{1,0:T(8,128)}, f32[512,256]{1,0:T(8,128)}) custom-call(f32[512,256]{1,0:T(8,128)S(1)} %get-tuple-element.175.u_ref, bf16[512,256]{1,0:T(8,128)(2,1)S(1)} %get-tuple-element.176.refs_0_.row_half, bf16[512,512]{1,0:T(8,128)(2,1)S(1)} %get-tuple-element.177.refs_2_.dense, f32[8,512]{1,0:T(8,128)S(1)} %get-tuple-element.178.refs_3_.live, ...), custom_call_target="tpu_custom_call" | custom-call | flops 10000000 | bytes 1 | tf_op jit(solution)/shard_map/last_columns_and_rows/pallas_call | solution.py:24
  (14 shorter events, 0.1 us)
Async XLA Ops:
  0.6 7.1 %copy-start = (bf16[5,8,128,128]{3,2,1,0:T(8,128)(2,1)S(1)}, bf16[5,8,128,128]{3,2,1,0:T(8,128)(2,1)}, u32[]{:S(2)}) copy-start(bf16[5,8,128,128]{3,2,1,0:T(8,128)(2,1)} %x_ref.1) | copy-start | bytes 3932164
  0.6 7.1 %copy-start.1 = (s32[5,8,2]{1,2,0:T(2,128)S(1)}, s32[5,8,2]{1,2,0:T(2,128)}, u32[]{:S(2)}) copy-start(s32[5,8,2]{1,2,0:T(2,128)} %param.8) | copy-start | bytes 964
  0.7 7.1 %copy-start.2 = (s32[5,1]{0,1:T(1,128)S(1)}, s32[5,1]{0,1:T(1,128)}, u32[]{:S(2)}) copy-start(s32[5,1]{0,1:T(1,128)} %param.9) | copy-start | bytes 64
  2.4 6.7 %collective-permute-start = (f32[96,256]{1,0:T(8,128)S(1)}, f32[96,256]{1,0:T(8,128)S(1)}, u32[]{:S(2)}, u32[]{:S(2)}) collective-permute-start(f32[96,256]{1,0:T(8,128)S(1)} %get-tuple-element.114), channel_id=1, source_target_pairs={{0,4},{4,8},{8,12},{12,16},{16,20},{20,24},{24,28},{28,0},{1,5},{5... | collective-permute-start | bytes 294920 | tf_op jit(solution)/shard_map/ppermute | solution.py:310
  3.5 6.4 %collective-permute-start.1 = (f32[160,256]{1,0:T(8,128)S(1)}, f32[160,256]{1,0:T(8,128)S(1)}, u32[]{:S(2)}, u32[]{:S(2)}) collective-permute-start(f32[160,256]{1,0:T(8,128)S(1)} %get-tuple-element.119), channel_id=1, source_target_pairs={{0,4},{4,8},{8,12},{12,16},{16,20},{20,24},{24,28},{28,0},{1,5},{5... | collective-permute-start | bytes 491528 | tf_op jit(solution)/shard_map/ppermute | solution.py:310
  6.1 5.6 %collective-permute-start.2 = (f32[160,256]{1,0:T(8,128)S(1)}, f32[160,256]{1,0:T(8,128)S(1)}, u32[]{:S(2)}, u32[]{:S(2)}) collective-permute-start(f32[160,256]{1,0:T(8,128)S(1)} %get-tuple-element.122), channel_id=1, source_target_pairs={{0,4},{4,8},{8,12},{12,16},{16,20},{20,24},{24,28},{28,0},{1,5},{5... | collective-permute-start | bytes 491528 | tf_op jit(solution)/shard_map/ppermute | solution.py:310
  6.2 6.6 %collective-permute-start.3 = (f32[96,256]{1,0:T(8,128)S(1)}, f32[96,256]{1,0:T(8,128)S(1)}, u32[]{:S(2)}, u32[]{:S(2)}) collective-permute-start(f32[96,256]{1,0:T(8,128)S(1)} %get-tuple-element.125), channel_id=1, source_target_pairs={{0,4},{4,8},{8,12},{12,16},{16,20},{20,24},{24,28},{28,0},{1,5},{5... | collective-permute-start | bytes 294920 | tf_op jit(solution)/shard_map/ppermute | solution.py:310
  9.5 5.0 %collective-permute-start.4 = (f32[96,256]{1,0:T(8,128)S(1)}, f32[96,256]{1,0:T(8,128)S(1)}, u32[]{:S(2)}, u32[]{:S(2)}) collective-permute-start(f32[96,256]{1,0:T(8,128)S(1)} %get-tuple-element.135), channel_id=1, source_target_pairs={{0,4},{4,8},{8,12},{12,16},{16,20},{20,24},{24,28},{28,0},{1,5},{5... | collective-permute-start | bytes 294920 | tf_op jit(solution)/shard_map/ppermute | solution.py:310
  10.3 6.2 %collective-permute-start.5 = (f32[160,256]{1,0:T(8,128)S(1)}, f32[160,256]{1,0:T(8,128)S(1)}, u32[]{:S(2)}, u32[]{:S(2)}) collective-permute-start(f32[160,256]{1,0:T(8,128)S(1)} %get-tuple-element.140), channel_id=1, source_target_pairs={{0,4},{4,8},{8,12},{12,16},{16,20},{20,24},{24,28},{28,0},{1,5},{5... | collective-permute-start | bytes 491528 | tf_op jit(solution)/shard_map/ppermute | solution.py:310
  12.1 6.6 %collective-permute-start.6 = (f32[160,256]{1,0:T(8,128)S(1)}, f32[160,256]{1,0:T(8,128)S(1)}, u32[]{:S(2)}, u32[]{:S(2)}) collective-permute-start(f32[160,256]{1,0:T(8,128)S(1)} %get-tuple-element.143), channel_id=1, source_target_pairs={{0,4},{4,8},{8,12},{12,16},{16,20},{20,24},{24,28},{28,0},{1,5},{5... | collective-permute-start | bytes 491528 | tf_op jit(solution)/shard_map/ppermute | solution.py:310
  13.2 7.6 %collective-permute-start.7 = (f32[96,256]{1,0:T(8,128)S(1)}, f32[96,256]{1,0:T(8,128)S(1)}, u32[]{:S(2)}, u32[]{:S(2)}) collective-permute-start(f32[96,256]{1,0:T(8,128)S(1)} %get-tuple-element.146), channel_id=1, source_target_pairs={{0,4},{4,8},{8,12},{12,16},{16,20},{20,24},{24,28},{28,0},{1,5},{5... | collective-permute-start | bytes 294920 | tf_op jit(solution)/shard_map/ppermute | solution.py:310
  14.9 8.3 %collective-permute-start.8 = (f32[96,256]{1,0:T(8,128)S(1)}, f32[96,256]{1,0:T(8,128)S(1)}, u32[]{:S(2)}, u32[]{:S(2)}) collective-permute-start(f32[96,256]{1,0:T(8,128)S(1)} %get-tuple-element.156), channel_id=1, source_target_pairs={{0,1},{1,2},{2,3},{3,0},{4,5},{5,6},{6,7},{7,4},{8,9},{9,10},{10,1... | collective-permute-start | bytes 294920 | tf_op jit(solution)/shard_map/ppermute | solution.py:310
  16.9 9.0 %collective-permute-start.9 = (f32[160,256]{1,0:T(8,128)S(1)}, f32[160,256]{1,0:T(8,128)S(1)}, u32[]{:S(2)}, u32[]{:S(2)}) collective-permute-start(f32[160,256]{1,0:T(8,128)S(1)} %get-tuple-element.161), channel_id=1, source_target_pairs={{0,1},{1,2},{2,3},{3,0},{4,5},{5,6},{6,7},{7,4},{8,9},{9,10},{10,1... | collective-permute-start | bytes 491528 | tf_op jit(solution)/shard_map/ppermute | solution.py:310
  19.1 10.3 %collective-permute-start.10 = (f32[160,256]{1,0:T(8,128)S(1)}, f32[160,256]{1,0:T(8,128)S(1)}, u32[]{:S(2)}, u32[]{:S(2)}) collective-permute-start(f32[160,256]{1,0:T(8,128)S(1)} %get-tuple-element.164), channel_id=1, source_target_pairs={{0,1},{1,2},{2,3},{3,0},{4,5},{5,6},{6,7},{7,4},{8,9},{9,10},{10,1... | collective-permute-start | bytes 491528 | tf_op jit(solution)/shard_map/ppermute | solution.py:310
  21.1 10.4 %collective-permute-start.11 = (f32[96,256]{1,0:T(8,128)S(1)}, f32[96,256]{1,0:T(8,128)S(1)}, u32[]{:S(2)}, u32[]{:S(2)}) collective-permute-start(f32[96,256]{1,0:T(8,128)S(1)} %get-tuple-element.167), channel_id=1, source_target_pairs={{0,1},{1,2},{2,3},{3,0},{4,5},{5,6},{6,7},{7,4},{8,9},{9,10},{10,1... | collective-permute-start | bytes 294920 | tf_op jit(solution)/shard_map/ppermute | solution.py:310
  23.5 9.6 %collective-permute-start.13 = (f32[96,256]{1,0:T(8,128)S(1)}, f32[96,256]{1,0:T(8,128)S(1)}, u32[]{:S(2)}, u32[]{:S(2)}) collective-permute-start(f32[96,256]{1,0:T(8,128)S(1)} %get-tuple-element.180), channel_id=1, source_target_pairs={{0,4},{4,8},{8,12},{12,16},{16,20},{20,24},{24,28},{28,0},{1,5},{5... | collective-permute-start | bytes 294920 | tf_op jit(solution)/shard_map/ppermute | solution.py:310
  26.2 7.3 %collective-permute-start.14 = (f32[160,256]{1,0:T(8,128)S(1)}, f32[160,256]{1,0:T(8,128)S(1)}, u32[]{:S(2)}, u32[]{:S(2)}) collective-permute-start(f32[160,256]{1,0:T(8,128)S(1)} %get-tuple-element.183), channel_id=1, source_target_pairs={{0,4},{4,8},{8,12},{12,16},{16,20},{20,24},{24,28},{28,0},{1,5},{5... | collective-permute-start | bytes 491528 | tf_op jit(solution)/shard_map/ppermute | solution.py:310
  29.8 5.7 %collective-permute-start.15 = (f32[160,256]{1,0:T(8,128)S(1)}, f32[160,256]{1,0:T(8,128)S(1)}, u32[]{:S(2)}, u32[]{:S(2)}) collective-permute-start(f32[160,256]{1,0:T(8,128)S(1)} %get-tuple-element.186), channel_id=1, source_target_pairs={{0,4},{4,8},{8,12},{12,16},{16,20},{20,24},{24,28},{28,0},{1,5},{5... | collective-permute-start | bytes 491528 | tf_op jit(solution)/shard_map/ppermute | solution.py:310
  31.8 5.0 %collective-permute-start.12 = (f32[96,256]{1,0:T(8,128)S(1)}, f32[96,256]{1,0:T(8,128)S(1)}, u32[]{:S(2)}, u32[]{:S(2)}) collective-permute-start(f32[96,256]{1,0:T(8,128)S(1)} %get-tuple-element.179), channel_id=1, source_target_pairs={{0,4},{4,8},{8,12},{12,16},{16,20},{20,24},{24,28},{28,0},{1,5},{5... | collective-permute-start | bytes 294920 | tf_op jit(solution)/shard_map/ppermute | solution.py:310

commit v10 on v7

--- a/solution.py
+++ b/solution.py
@@ -9,9 +9,10 @@
 
 LEARN_RATE = 0.03
 DECAY_RATE = 0.1
-EDGES = (0, 3, 8, 13, 16)
-CHUNKS = len(EDGES) - 1
-WEIGHTS = (10**9, 10**7, 6 * 10**8, 2 * 10**9)
+EARLY = (0, 3, 8, 13, 16)
+LATER = (0, 3, 8, 11, 14, 16)
+EARLY_WEIGHTS = (1e9, 1e7, 6e8, 2e9)
+LATER_WEIGHTS = (3e8, 1e8, 3e8, 6e8, 6e8)
 SUBLANES = 8
 
 VMEM = pl.BlockSpec(memory_space=pltpu.VMEM)
@@ -65,12 +66,11 @@
     return slice(h * width, (h + 1) * width)
 
 
-def chunk_span(h, cols):
-    return slice(cols * EDGES[h] // 16, cols * EDGES[h + 1] // 16)
-
-
-def chunk_width(h, cols):
-    at = chunk_span(h, cols)
+def spans(edges, cols):
+    return [slice(cols * i // 16, cols * j // 16) for i, j in zip(edges, edges[1:])]
+
+
+def size(at):
     return at.stop - at.start
 
 
@@ -142,7 +142,7 @@
 
 def first(u, c, values, coords, counts):
     rows, cols = u.shape[0], c.shape[0]
-    part = (chunk_width(0, cols), c.shape[1])
+    part = (size(spans(EARLY, cols)[0]), c.shape[1])
     bf16 = jnp.bfloat16
     outs = [like(u), like(c), like(u, dtype=bf16), like(u, (cols, rows), bf16)]
     outs += [like(u, (SUBLANES, rows)), like(u, (SUBLANES, 128))]
@@ -170,20 +170,20 @@
     residue[...], col_half[...], new = columns_step(
         start, tile, row_half[...], c_ref[rest], dense[rest], live
     )
-    for h, c_out in enumerate(c_outs, 1):
-        at = chunk_span(h, cols)
+    for at, c_out in zip(spans(EARLY, cols)[1:], c_outs):
         c_out[...] = new[at.start - start : at.stop - start]
 
 
 def others(line, tile, row_half, c, laid):
     cols, rank = c.shape
-    rest = cols - chunk_width(0, cols)
+    chunks = spans(EARLY, cols)[1:]
+    rest = cols - chunks[0].start
     outs = [like(row_half, (rest, row_half.shape[0])), like(row_half, (rest, rank))]
     return line.call(
         functools.partial(other_kernel, tile),
         "other_chunks",
         (row_half, c, *laid),
-        outs + [like(c, (chunk_width(h, cols), rank)) for h in range(1, CHUNKS)],
+        outs + [like(c, (size(at), rank)) for at in chunks],
     )
 
 
@@ -210,20 +210,30 @@
     return list(zip(out[:later], out[later:]))
 
 
-def columns_kernel(h, tile, row_half, c_ref, dense, live, c_out, residue, col_half):
-    at = chunk_span(h, dense.shape[0])
+def columns_kernel(at, cuts, tile, row_half, dense, live, *refs):
+    *cs, c_out, residue, col_half = refs
+    parts = [c[cut] for c, cut in zip(cs, cuts)]
+    cols = parts[0] if len(parts) == 1 else jnp.concatenate(parts, axis=0)
     residue[...], col_half[...], c_out[...] = columns_step(
-        at.start, tile, row_half[...], c_ref[...], dense[at], live
-    )
-
-
-def columns(line, h, tile, row_half, c, laid):
+        at.start, tile, row_half[...], cols, dense[at], live
+    )
+
+
+def columns(line, at, weight, tile, row_half, arrived, laid):
+    cs, cuts = [], []
+    for there, c in arrived:
+        start, stop = max(at.start, there.start), min(at.stop, there.stop)
+        if start < stop:
+            cs.append(c)
+            cuts.append(slice(start - there.start, stop - there.start))
+    rows, rank = row_half.shape
+    part, bf16 = (size(at), rank), jnp.bfloat16
     return line.call(
-        functools.partial(columns_kernel, h, tile),
+        functools.partial(columns_kernel, at, cuts, tile),
         "columns_step",
-        (row_half, c, *laid),
-        [like(c), like(row_half, (c.shape[0], row_half.shape[0])), like(c, dtype=jnp.bfloat16)],
-        flops=WEIGHTS[h],
+        (row_half, *laid, *cs),
+        [like(cs[0], part), like(row_half, (size(at), rows)), like(row_half, part, bf16)],
+        flops=int(weight),
     )
 
 
@@ -252,9 +262,9 @@
 
 
 def last_kernel(tile, u_ref, row_half, dense, live, c_ref, acc, _, *refs):
-    n = CHUNKS - 1
+    n = len(LATER) - 2
     done, (u_hbm, c_hbm, u_new, c_new, sems) = refs[:n], refs[n:]
-    cols = c_hbm.shape[0]
+    chunks = spans(LATER, c_hbm.shape[0])
     copies = []
 
     def copy(source, target, at):
@@ -263,8 +273,8 @@
         copies[-1].start()
 
     for h, c in enumerate(done):
-        copy(c, c_hbm, chunk_span(h, cols).start)
-    at = chunk_span(n, cols)
+        copy(c, c_hbm, chunks[h].start)
+    at = chunks[n]
     residue, col_half, new_cols = columns_step(
         at.start, tile, row_half[...], c_ref[...], dense[at], live
     )
@@ -280,9 +290,13 @@
 
 
 def final(line, tile, u, row_half, cs, laid):
-    n = CHUNKS - 1
     cols, rank = laid[0].shape[0], u.shape[1]
-    steps = [columns(line, h, tile, row_half, cs[h], laid) for h in range(n)]
+    *before, _ = spans(LATER, cols)
+    n = len(before)
+    steps = [
+        columns(line, at, weight, tile, row_half, cs[h : h + 1], laid)
+        for h, (at, weight) in enumerate(zip(before, LATER_WEIGHTS))
+    ]
     done, residues, halves = zip(*steps)
     (acc,) = line.call(
         gradient_kernel,
@@ -293,14 +307,14 @@
     return call(
         functools.partial(last_kernel, tile),
         "last_columns_and_rows",
-        (u, row_half, *laid, cs[n], acc, line.turn, *done),
+        (u, row_half, *laid, cs[n][1], acc, line.turn, *done),
         [VMEM] * (7 + n),
         [like(u), like(u, (cols, rank))],
         [HBM, HBM],
         scratch=[
             pltpu.VMEM(u.shape, u.dtype),
-            pltpu.VMEM(cs[n].shape, u.dtype),
-            pltpu.SemaphoreType.DMA((CHUNKS + u.shape[0] // tile,)),
+            pltpu.VMEM(cs[n][1].shape, u.dtype),
+            pltpu.SemaphoreType.DMA((n + 1 + u.shape[0] // tile,)),
         ],
     )
 
@@ -325,12 +339,16 @@
     laid = layout(line, tile_values, coords, counts, *sizes)
     u, row_half = rows(line, u, row_half, (residue, residues), (half, halves))
 
+    cs = list(zip(spans(EARLY, sizes[1]), cs))
     for stratum in range(1, strata - 1):
         axis = "group" if stratum == 2 else "blk"
+        edges, weights = (EARLY, EARLY_WEIGHTS) if stratum < 2 else (LATER, LATER_WEIGHTS)
         arrived, cs, residues, halves = cs, [], [], []
-        for h in range(CHUNKS):
-            done, residue, half = columns(line, h, tile, row_half, arrived[h], laid[stratum - 1])
-            cs.append(shifted(done, axis))
+        for at, weight in zip(spans(edges, sizes[1]), weights):
+            done, residue, half = columns(
+                line, at, weight, tile, row_half, arrived, laid[stratum - 1]
+            )
+            cs.append((at, shifted(done, axis)))
             residues.append(residue)
             halves.append(half)
         u, row_half = rows(line, u, row_half, residues, halves)

time: 38.2 us -> 37.8 us (0.990)
  waiting for transfers between devices: 9.93 us -> 4.53 us
  starting transfers between devices: 15.1 us -> 19 us
  Pallas kernels: 12 us -> 13.1 us
    ppermute x16 -> x18, waiting for transfers between devices: 9.93 us -> 4.53 us  [shifted(): return lax.ppermute(chunk, axis, [(i, (i + 1) % n) for i in range(n)])]
    ppermute x16 -> x18, starting transfers between devices: 15.1 us -> 19 us  [shifted(): return lax.ppermute(chunk, axis, [(i, (i + 1) % n) for i in range(n)])]
    pallas_call x24 -> x27, Pallas kernels: 12 us -> 13.1 us  [call(): pl.pallas_call(body, out_shape=outs, in_specs=in_specs, out_specs=out_spe...]
  transfers between devices with their start and end apart: 16 -> 18, of which waited for: 9 -> 10; matrix products, arithmetic and copies ran while one was open for 0% -> 0% of each run, Pallas kernels for 24% -> 27%
where the time goes in v10:
time: 37.8 us; the launch traced here: 37.6 us
  starting transfers between devices  19 us (50%)
  Pallas kernels  13.1 us (35%)
  waiting for transfers between devices  4.53 us (12%)
  between operations  0.93 us (2%)
    ppermute x18, starting transfers between devices, shifted(): return lax.ppermute(chunk, axis, [(i, (i + 1) % n) for i in range(n)])  19 us
    pallas_call x27, Pallas kernels, call(): pl.pallas_call(body, out_shape=outs, in_specs=in_specs, out_specs=out_spe...  13.1 us
    ppermute x18, waiting for transfers between devices, shifted(): return lax.ppermute(chunk, axis, [(i, (i + 1) % n) for i in range(n)])  4.53 us
  transfers between devices with their start and end apart: 18, of which 10 were waited for; matrix products, arithmetic and copies ran while one was open for 0% of the time, Pallas kernels for 27%

profile of v10, /device:TPU:0, one launch (start us, length us, event | category | flops | bytes accessed | tf_op | source)
XLA Modules:
  0.0 37.6 jit_solution(13598317642070021660)
XLA Ops:
  0.7 1.7 %first_chunk.1 = (f32[512,256]{1,0:T(8,128)S(1)}, f32[512,256]{1,0:T(8,128)S(1)}, bf16[512,256]{1,0:T(8,128)(2,1)S(1)}, bf16[512,512]{1,0:T(8,128)(2,1)S(1)}, f3...) custom-call(f32[512,256]{1,0:T(8,128)} %u_hbm.1, ...), custom_call_target="tpu_custom_call" | custom-call | flops 10000000 | bytes 1 | tf_op jit(solution)/shard_map/first_chunk/pallas_call | solution.py:25
  2.3 0.5 %collective-permute-start = (f32[96,256]{1,0:T(8,128)S(1)}, f32[96,256]{1,0:T(8,128)S(1)}, u32[]{:S(2)}, u32[]{:S(2)}) collective-permute-start(f32[96,256]{1,0:T(8,128)S(1)} %get-tuple-element.128), channel_id=1, source_target_pairs={{0,4},{4,8},{8,12},{12,16},{16,20},{20,24},{24,28},{28,0},{1,5},{5... | collective-permute-start | bytes 294920 | tf_op jit(solution)/shard_map/ppermute | solution.py:324
  2.8 0.5 %other_chunks.1 = (f32[8,128]{1,0:T(8,128)S(1)}, bf16[416,512]{1,0:T(8,128)(2,1)S(1)}, bf16[416,256]{1,0:T(8,128)(2,1)S(1)}, f32[160,256]{1,0:T(8,128)S(1)}, f32...) custom-call(bf16[512,256]{1,0:T(8,128)(2,1)S(1)} %get-tuple-element.113.refs_0_.refs_1_, ...), custom_call_target="tpu_custom_call", output_to_operand_aliasing={{0}: (4, {})} | custom-call | flops 10000000 | bytes 1 | tf_op jit(solution)/shard_map/other_chunks/pallas_call | solution.py:25
  3.4 2.7 %collective-permute-start.1 = (f32[160,256]{1,0:T(8,128)S(1)}, f32[160,256]{1,0:T(8,128)S(1)}, u32[]{:S(2)}, u32[]{:S(2)}) collective-permute-start(f32[160,256]{1,0:T(8,128)S(1)} %get-tuple-element.131), channel_id=1, source_target_pairs={{0,4},{4,8},{8,12},{12,16},{16,20},{20,24},{24,28},{28,0},{1,5},{5... | collective-permute-start | bytes 491528 | tf_op jit(solution)/shard_map/ppermute | solution.py:324
  6.1 1.5 %collective-permute-start.3 = (f32[96,256]{1,0:T(8,128)S(1)}, f32[96,256]{1,0:T(8,128)S(1)}, u32[]{:S(2)}, u32[]{:S(2)}) collective-permute-start(f32[96,256]{1,0:T(8,128)S(1)} %get-tuple-element.137), channel_id=1, source_target_pairs={{0,4},{4,8},{8,12},{12,16},{16,20},{20,24},{24,28},{28,0},{1,5},{5... | collective-permute-start | bytes 294920 | tf_op jit(solution)/shard_map/ppermute | solution.py:324
  7.6 1.0 %lay_out_tiles.1 = (f32[8,128]{1,0:T(8,128)S(1)}, bf16[512,512]{1,0:T(8,128)(2,1)S(1)}, bf16[512,512]{1,0:T(8,128)(2,1)S(1)}, bf16[512,512]{1,0:T(8,128)(2,1)S(1...) custom-call(bf16[5,8,128,128]{3,2,1,0:T(8,128)(2,1)S(1)} %copy-done,, ...), custom_call_target="tpu_custom_call", output_to_operand_aliasing={{0}: (3, {})} | custom-call | flops 10000000 | bytes 1 | tf_op jit(solution)/shard_map/lay_out_tiles/pallas_call | solution.py:25
  8.6 0.4 %rows_step.4 = (f32[8,128]{1,0:T(8,128)S(1)}, f32[512,256]{1,0:T(8,128)S(1)}, bf16[512,256]{1,0:T(8,128)(2,1)S(1)}) custom-call(f32[512,256]{1,0:T(8,128)S(1)} %get-tuple-element.112.refs_0_, bf16[512,256]{1,0:T(8,128)(2,1)S(1)} %get-tuple-element.113.refs_0_.refs_1_, ...), custom_call_target="tpu_custom_call", output_to_operand_aliasing={{0}: (6, {}), {1}: (0, {}), {2}: (1, {})} | custom-call | flops 10000000 | bytes 1 | tf_op jit(solution)/shard_map/rows_step/pallas_call | solution.py:25
  9.0 0.3 columns_step.18
  9.5 0.2 collective-permute-done.1.refs_3_
  9.8 0.4 columns_step.19
  10.1 1.4 %collective-permute-start.5 = (f32[160,256]{1,0:T(8,128)S(1)}, f32[160,256]{1,0:T(8,128)S(1)}, u32[]{:S(2)}, u32[]{:S(2)}) collective-permute-start(f32[160,256]{1,0:T(8,128)S(1)} %get-tuple-element.152), channel_id=1, source_target_pairs={{0,4},{4,8},{8,12},{12,16},{16,20},{20,24},{24,28},{28,0},{1,5},{5... | collective-permute-start | bytes 491528 | tf_op jit(solution)/shard_map/ppermute | solution.py:324
  11.6 0.4 columns_step.20
  12.1 0.6 %collective-permute-done.3.refs_3_ = f32[96,256]{1,0:T(8,128)S(1)} collective-permute-done((f32[96,256]{1,0:T(8,128)S(1)}, f32[96,256]{1,0:T(8,128)S(1)}, u32[]{:S(2)}, u32[]{:S(2)}) %collective-permute-start.3) | collective-permute-done | bytes 98336 | tf_op jit(solution)/shard_map/ppermute | solution.py:324
  12.7 0.3 columns_step.21
  13.1 0.8 %collective-permute-start.7 = (f32[96,256]{1,0:T(8,128)S(1)}, f32[96,256]{1,0:T(8,128)S(1)}, u32[]{:S(2)}, u32[]{:S(2)}) collective-permute-start(f32[96,256]{1,0:T(8,128)S(1)} %get-tuple-element.158), channel_id=1, source_target_pairs={{0,4},{4,8},{8,12},{12,16},{16,20},{20,24},{24,28},{28,0},{1,5},{5... | collective-permute-start | bytes 294920 | tf_op jit(solution)/shard_map/ppermute | solution.py:324
  13.8 0.5 %rows_step.5 = (f32[8,128]{1,0:T(8,128)S(1)}, f32[512,256]{1,0:T(8,128)S(1)}, bf16[512,256]{1,0:T(8,128)(2,1)S(1)}) custom-call(f32[512,256]{1,0:T(8,128)S(1)} %get-tuple-element.124.refs_0_, bf16[512,256]{1,0:T(8,128)(2,1)S(1)} %get-tuple-element.125.refs_0_.refs_1_, ...), custom_call_target="tpu_custom_call", output_to_operand_aliasing={{0}: (10, {}), {1}: (0, {}), {2}: (1, {})} | custom-call | flops 10000000 | bytes 1 | tf_op jit(solution)/shard_map/rows_step/pallas_call | solution.py:25
  14.4 0.3 columns_step.22
  14.7 1.6 %collective-permute-start.8 = (f32[96,256]{1,0:T(8,128)S(1)}, f32[96,256]{1,0:T(8,128)S(1)}, u32[]{:S(2)}, u32[]{:S(2)}) collective-permute-start(f32[96,256]{1,0:T(8,128)S(1)} %get-tuple-element.173), channel_id=1, source_target_pairs={{0,1},{1,2},{2,3},{3,0},{4,5},{5,6},{6,7},{7,4},{8,9},{9,10},{10,1... | collective-permute-start | bytes 294920 | tf_op jit(solution)/shard_map/ppermute | solution.py:324
  16.4 0.4 columns_step.23
  16.7 1.8 %collective-permute-start.9 = (f32[160,256]{1,0:T(8,128)S(1)}, f32[160,256]{1,0:T(8,128)S(1)}, u32[]{:S(2)}, u32[]{:S(2)}) collective-permute-start(f32[160,256]{1,0:T(8,128)S(1)} %get-tuple-element.176), channel_id=1, source_target_pairs={{0,1},{1,2},{2,3},{3,0},{4,5},{5,6},{6,7},{7,4},{8,9},{9,10},{10,1... | collective-permute-start | bytes 491528 | tf_op jit(solution)/shard_map/ppermute | solution.py:324
  18.6 0.3 columns_step.24
  18.9 1.6 %collective-permute-start.10 = (f32[96,256]{1,0:T(8,128)S(1)}, f32[96,256]{1,0:T(8,128)S(1)}, u32[]{:S(2)}, u32[]{:S(2)}) collective-permute-start(f32[96,256]{1,0:T(8,128)S(1)} %get-tuple-element.179), channel_id=1, source_target_pairs={{0,1},{1,2},{2,3},{3,0},{4,5},{5,6},{6,7},{7,4},{8,9},{9,10},{10,1... | collective-permute-start | bytes 294920 | tf_op jit(solution)/shard_map/ppermute | solution.py:324
  20.6 0.3 columns_step.25
  20.9 1.6 %collective-permute-start.11 = (f32[96,256]{1,0:T(8,128)S(1)}, f32[96,256]{1,0:T(8,128)S(1)}, u32[]{:S(2)}, u32[]{:S(2)}) collective-permute-start(f32[96,256]{1,0:T(8,128)S(1)} %get-tuple-element.182), channel_id=1, source_target_pairs={{0,1},{1,2},{2,3},{3,0},{4,5},{5,6},{6,7},{7,4},{8,9},{9,10},{10,1... | collective-permute-start | bytes 294920 | tf_op jit(solution)/shard_map/ppermute | solution.py:324
  22.6 0.3 columns_step.26
  22.9 1.4 %collective-permute-start.12 = (f32[64,256]{1,0:T(8,128)S(1)}, f32[64,256]{1,0:T(8,128)S(1)}, u32[]{:S(2)}, u32[]{:S(2)}) collective-permute-start(f32[64,256]{1,0:T(8,128)S(1)} %get-tuple-element.185), channel_id=1, source_target_pairs={{0,1},{1,2},{2,3},{3,0},{4,5},{5,6},{6,7},{7,4},{8,9},{9,10},{10,1... | collective-permute-start | bytes 196616 | tf_op jit(solution)/shard_map/ppermute | solution.py:324
  24.3 0.5 %rows_step.6 = (f32[8,128]{1,0:T(8,128)S(1)}, f32[512,256]{1,0:T(8,128)S(1)}, bf16[512,256]{1,0:T(8,128)(2,1)S(1)}) custom-call(f32[512,256]{1,0:T(8,128)S(1)} %get-tuple-element.145.refs_0_, bf16[512,256]{1,0:T(8,128)(2,1)S(1)} %get-tuple-element.146.refs_0_.refs_1_, ...), custom_call_target="tpu_custom_call", output_to_operand_aliasing={{0}: (12, {}), {1}: (0, {}), {2}: (1, {})} | custom-call | flops 10000000 | bytes 1 | tf_op jit(solution)/shard_map/rows_step/pallas_call | solution.py:25
  24.8 0.3 columns_step.27
  25.2 0.5 %collective-permute-done.9.refs_3_ = f32[160,256]{1,0:T(8,128)S(1)} collective-permute-done((f32[160,256]{1,0:T(8,128)S(1)}, f32[160,256]{1,0:T(8,128)S(1)}, u32[]{:S(2)}, u32[]{:S(2)}) %collective-permute-start.9) | collective-permute-done | bytes 163872 | tf_op jit(solution)/shard_map/ppermute | solution.py:324
  25.7 0.4 columns_step.28
  26.1 0.7 %collective-permute-start.15 = (f32[160,256]{1,0:T(8,128)S(1)}, f32[160,256]{1,0:T(8,128)S(1)}, u32[]{:S(2)}, u32[]{:S(2)}) collective-permute-start(f32[160,256]{1,0:T(8,128)S(1)} %get-tuple-element.202), channel_id=1, source_target_pairs={{0,4},{4,8},{8,12},{12,16},{16,20},{20,24},{24,28},{28,0},{1,5},{5... | collective-permute-start | bytes 491528 | tf_op jit(solution)/shard_map/ppermute | solution.py:324
  26.8 1.1 %collective-permute-done.10.refs_3_ = f32[96,256]{1,0:T(8,128)S(1)} collective-permute-done((f32[96,256]{1,0:T(8,128)S(1)}, f32[96,256]{1,0:T(8,128)S(1)}, u32[]{:S(2)}, u32[]{:S(2)}) %collective-permute-start.10) | collective-permute-done | bytes 98336 | tf_op jit(solution)/shard_map/ppermute | solution.py:324
  27.8 0.3 columns_step.29
  28.2 0.8 %collective-permute-start.16 = (f32[96,256]{1,0:T(8,128)S(1)}, f32[96,256]{1,0:T(8,128)S(1)}, u32[]{:S(2)}, u32[]{:S(2)}) collective-permute-start(f32[96,256]{1,0:T(8,128)S(1)} %get-tuple-element.205), channel_id=1, source_target_pairs={{0,4},{4,8},{8,12},{12,16},{16,20},{20,24},{24,28},{28,0},{1,5},{5... | collective-permute-start | bytes 294920 | tf_op jit(solution)/shard_map/ppermute | solution.py:324
  29.0 0.9 %collective-permute-done.11.refs_3_ = f32[96,256]{1,0:T(8,128)S(1)} collective-permute-done((f32[96,256]{1,0:T(8,128)S(1)}, f32[96,256]{1,0:T(8,128)S(1)}, u32[]{:S(2)}, u32[]{:S(2)}) %collective-permute-start.11) | collective-permute-done | bytes 98336 | tf_op jit(solution)/shard_map/ppermute | solution.py:324
  30.0 0.3 columns_step.30
  30.3 0.8 %collective-permute-start.17 = (f32[96,256]{1,0:T(8,128)S(1)}, f32[96,256]{1,0:T(8,128)S(1)}, u32[]{:S(2)}, u32[]{:S(2)}) collective-permute-start(f32[96,256]{1,0:T(8,128)S(1)} %get-tuple-element.208), channel_id=1, source_target_pairs={{0,4},{4,8},{8,12},{12,16},{16,20},{20,24},{24,28},{28,0},{1,5},{5... | collective-permute-start | bytes 294920 | tf_op jit(solution)/shard_map/ppermute | solution.py:324
  31.1 0.3 collective-permute-done.12.refs_3_
  31.4 0.3 columns_step.31
  31.7 1.5 %collective-permute-start.13 = (f32[64,256]{1,0:T(8,128)S(1)}, f32[64,256]{1,0:T(8,128)S(1)}, u32[]{:S(2)}, u32[]{:S(2)}) collective-permute-start(f32[64,256]{1,0:T(8,128)S(1)} %get-tuple-element.198), channel_id=1, source_target_pairs={{0,4},{4,8},{8,12},{12,16},{16,20},{20,24},{24,28},{28,0},{1,5},{5... | collective-permute-start | bytes 196616 | tf_op jit(solution)/shard_map/ppermute | solution.py:324
  33.2 0.5 %rows_step.7 = (f32[8,128]{1,0:T(8,128)S(1)}, f32[512,256]{1,0:T(8,128)S(1)}, bf16[512,256]{1,0:T(8,128)(2,1)S(1)}) custom-call(f32[512,256]{1,0:T(8,128)S(1)} %get-tuple-element.169.refs_0_, bf16[512,256]{1,0:T(8,128)(2,1)S(1)} %get-tuple-element.170.refs_0_.refs_1_, ...), custom_call_target="tpu_custom_call", output_to_operand_aliasing={{0}: (12, {}), {1}: (0, {}), {2}: (1, {})} | custom-call | flops 10000000 | bytes 1 | tf_op jit(solution)/shard_map/rows_step/pallas_call | solution.py:25
  33.8 0.3 columns_step.32
  34.1 0.4 columns_step.33
  34.5 0.3 columns_step.34
  34.9 0.4 %collective-permute-done.17.refs_3_ = f32[96,256]{1,0:T(8,128)S(1)} collective-permute-done((f32[96,256]{1,0:T(8,128)S(1)}, f32[96,256]{1,0:T(8,128)S(1)}, u32[]{:S(2)}, u32[]{:S(2)}) %collective-permute-start.17) | collective-permute-done | bytes 98336 | tf_op jit(solution)/shard_map/ppermute | solution.py:324
  35.3 0.3 columns_step.35
  35.6 0.5 %rows_gradient.1 = (f32[8,128]{1,0:T(8,128)S(1)}, f32[512,256]{1,0:T(8,128)S(1)}) custom-call(bf16[96,512]{1,0:T(8,128)(2,1)S(1)} %get-tuple-element.201.refs_0_, bf16[160,512]{1,0:T(8,128)(2,1)S(1)} %get-tuple-element.204.refs_1_, bf16[96,512]{1,0:T(8,128)(2,1)S(1)} %get-tuple-element.207.refs_2_, ...), custom_call_target="tpu_custom_call", output_to_operand_aliasing={{0}: (8, {})} | custom-call | flops 10000000 | bytes 1 | tf_op jit(solution)/shard_map/rows_gradient/pallas_call | solution.py:25
  36.3 1.3 %last_columns_and_rows.1 = (f32[512,256]{1,0:T(8,128)}, f32[512,256]{1,0:T(8,128)}) custom-call(f32[512,256]{1,0:T(8,128)S(1)} %get-tuple-element.194.u_ref, bf16[512,256]{1,0:T(8,128)(2,1)S(1)} %get-tuple-element.195.refs_0_.row_half, bf16[512,512]{1,0:T(8,128)(2,1)S(1)} %get-tuple-element.196.refs_1_.dense, f32[8,512]{1,0:T(8,128)S(1)} %get-tuple-element.197.refs_2_.live, ...), custom_call_target="tpu_custom_call" | custom-call | flops 10000000 | bytes 1 | tf_op jit(solution)/shard_map/last_columns_and_rows/pallas_call | solution.py:25
  (21 shorter events, 0.8 us)
Async XLA Ops:
  0.6 7.0 %copy-start = (bf16[5,8,128,128]{3,2,1,0:T(8,128)(2,1)S(1)}, bf16[5,8,128,128]{3,2,1,0:T(8,128)(2,1)}, u32[]{:S(2)}) copy-start(bf16[5,8,128,128]{3,2,1,0:T(8,128)(2,1)} %x_ref.1) | copy-start | bytes 3932164
  0.6 7.0 %copy-start.1 = (s32[5,8,2]{1,2,0:T(2,128)S(1)}, s32[5,8,2]{1,2,0:T(2,128)}, u32[]{:S(2)}) copy-start(s32[5,8,2]{1,2,0:T(2,128)} %param.8) | copy-start | bytes 964
  0.7 7.0 %copy-start.2 = (s32[5,1]{0,1:T(1,128)S(1)}, s32[5,1]{0,1:T(1,128)}, u32[]{:S(2)}) copy-start(s32[5,1]{0,1:T(1,128)} %param.9) | copy-start | bytes 64
  2.3 6.7 %collective-permute-start = (f32[96,256]{1,0:T(8,128)S(1)}, f32[96,256]{1,0:T(8,128)S(1)}, u32[]{:S(2)}, u32[]{:S(2)}) collective-permute-start(f32[96,256]{1,0:T(8,128)S(1)} %get-tuple-element.128), channel_id=1, source_target_pairs={{0,4},{4,8},{8,12},{12,16},{16,20},{20,24},{24,28},{28,0},{1,5},{5... | collective-permute-start | bytes 294920 | tf_op jit(solution)/shard_map/ppermute | solution.py:324
  3.4 6.4 %collective-permute-start.1 = (f32[160,256]{1,0:T(8,128)S(1)}, f32[160,256]{1,0:T(8,128)S(1)}, u32[]{:S(2)}, u32[]{:S(2)}) collective-permute-start(f32[160,256]{1,0:T(8,128)S(1)} %get-tuple-element.131), channel_id=1, source_target_pairs={{0,4},{4,8},{8,12},{12,16},{16,20},{20,24},{24,28},{28,0},{1,5},{5... | collective-permute-start | bytes 491528 | tf_op jit(solution)/shard_map/ppermute | solution.py:324
  6.0 5.6 %collective-permute-start.2 = (f32[160,256]{1,0:T(8,128)S(1)}, f32[160,256]{1,0:T(8,128)S(1)}, u32[]{:S(2)}, u32[]{:S(2)}) collective-permute-start(f32[160,256]{1,0:T(8,128)S(1)} %get-tuple-element.134), channel_id=1, source_target_pairs={{0,4},{4,8},{8,12},{12,16},{16,20},{20,24},{24,28},{28,0},{1,5},{5... | collective-permute-start | bytes 491528 | tf_op jit(solution)/shard_map/ppermute | solution.py:324
  6.1 6.6 %collective-permute-start.3 = (f32[96,256]{1,0:T(8,128)S(1)}, f32[96,256]{1,0:T(8,128)S(1)}, u32[]{:S(2)}, u32[]{:S(2)}) collective-permute-start(f32[96,256]{1,0:T(8,128)S(1)} %get-tuple-element.137), channel_id=1, source_target_pairs={{0,4},{4,8},{8,12},{12,16},{16,20},{20,24},{24,28},{28,0},{1,5},{5... | collective-permute-start | bytes 294920 | tf_op jit(solution)/shard_map/ppermute | solution.py:324
  9.4 5.0 %collective-permute-start.4 = (f32[96,256]{1,0:T(8,128)S(1)}, f32[96,256]{1,0:T(8,128)S(1)}, u32[]{:S(2)}, u32[]{:S(2)}) collective-permute-start(f32[96,256]{1,0:T(8,128)S(1)} %get-tuple-element.149), channel_id=1, source_target_pairs={{0,4},{4,8},{8,12},{12,16},{16,20},{20,24},{24,28},{28,0},{1,5},{5... | collective-permute-start | bytes 294920 | tf_op jit(solution)/shard_map/ppermute | solution.py:324
  10.1 6.2 %collective-permute-start.5 = (f32[160,256]{1,0:T(8,128)S(1)}, f32[160,256]{1,0:T(8,128)S(1)}, u32[]{:S(2)}, u32[]{:S(2)}) collective-permute-start(f32[160,256]{1,0:T(8,128)S(1)} %get-tuple-element.152), channel_id=1, source_target_pairs={{0,4},{4,8},{8,12},{12,16},{16,20},{20,24},{24,28},{28,0},{1,5},{5... | collective-permute-start | bytes 491528 | tf_op jit(solution)/shard_map/ppermute | solution.py:324
  12.0 6.6 %collective-permute-start.6 = (f32[160,256]{1,0:T(8,128)S(1)}, f32[160,256]{1,0:T(8,128)S(1)}, u32[]{:S(2)}, u32[]{:S(2)}) collective-permute-start(f32[160,256]{1,0:T(8,128)S(1)} %get-tuple-element.155), channel_id=1, source_target_pairs={{0,4},{4,8},{8,12},{12,16},{16,20},{20,24},{24,28},{28,0},{1,5},{5... | collective-permute-start | bytes 491528 | tf_op jit(solution)/shard_map/ppermute | solution.py:324
  13.1 7.5 %collective-permute-start.7 = (f32[96,256]{1,0:T(8,128)S(1)}, f32[96,256]{1,0:T(8,128)S(1)}, u32[]{:S(2)}, u32[]{:S(2)}) collective-permute-start(f32[96,256]{1,0:T(8,128)S(1)} %get-tuple-element.158), channel_id=1, source_target_pairs={{0,4},{4,8},{8,12},{12,16},{16,20},{20,24},{24,28},{28,0},{1,5},{5... | collective-permute-start | bytes 294920 | tf_op jit(solution)/shard_map/ppermute | solution.py:324
  14.7 10.1 %collective-permute-start.8 = (f32[96,256]{1,0:T(8,128)S(1)}, f32[96,256]{1,0:T(8,128)S(1)}, u32[]{:S(2)}, u32[]{:S(2)}) collective-permute-start(f32[96,256]{1,0:T(8,128)S(1)} %get-tuple-element.173), channel_id=1, source_target_pairs={{0,1},{1,2},{2,3},{3,0},{4,5},{5,6},{6,7},{7,4},{8,9},{9,10},{10,1... | collective-permute-start | bytes 294920 | tf_op jit(solution)/shard_map/ppermute | solution.py:324
  16.7 9.0 %collective-permute-start.9 = (f32[160,256]{1,0:T(8,128)S(1)}, f32[160,256]{1,0:T(8,128)S(1)}, u32[]{:S(2)}, u32[]{:S(2)}) collective-permute-start(f32[160,256]{1,0:T(8,128)S(1)} %get-tuple-element.176), channel_id=1, source_target_pairs={{0,1},{1,2},{2,3},{3,0},{4,5},{5,6},{6,7},{7,4},{8,9},{9,10},{10,1... | collective-permute-start | bytes 491528 | tf_op jit(solution)/shard_map/ppermute | solution.py:324
  18.9 8.9 %collective-permute-start.10 = (f32[96,256]{1,0:T(8,128)S(1)}, f32[96,256]{1,0:T(8,128)S(1)}, u32[]{:S(2)}, u32[]{:S(2)}) collective-permute-start(f32[96,256]{1,0:T(8,128)S(1)} %get-tuple-element.179), channel_id=1, source_target_pairs={{0,1},{1,2},{2,3},{3,0},{4,5},{5,6},{6,7},{7,4},{8,9},{9,10},{10,1... | collective-permute-start | bytes 294920 | tf_op jit(solution)/shard_map/ppermute | solution.py:324
  20.9 9.0 %collective-permute-start.11 = (f32[96,256]{1,0:T(8,128)S(1)}, f32[96,256]{1,0:T(8,128)S(1)}, u32[]{:S(2)}, u32[]{:S(2)}) collective-permute-start(f32[96,256]{1,0:T(8,128)S(1)} %get-tuple-element.182), channel_id=1, source_target_pairs={{0,1},{1,2},{2,3},{3,0},{4,5},{5,6},{6,7},{7,4},{8,9},{9,10},{10,1... | collective-permute-start | bytes 294920 | tf_op jit(solution)/shard_map/ppermute | solution.py:324
  22.9 8.4 %collective-permute-start.12 = (f32[64,256]{1,0:T(8,128)S(1)}, f32[64,256]{1,0:T(8,128)S(1)}, u32[]{:S(2)}, u32[]{:S(2)}) collective-permute-start(f32[64,256]{1,0:T(8,128)S(1)} %get-tuple-element.185), channel_id=1, source_target_pairs={{0,1},{1,2},{2,3},{3,0},{4,5},{5,6},{6,7},{7,4},{8,9},{9,10},{10,1... | collective-permute-start | bytes 196616 | tf_op jit(solution)/shard_map/ppermute | solution.py:324
  25.2 8.6 %collective-permute-start.14 = (f32[96,256]{1,0:T(8,128)S(1)}, f32[96,256]{1,0:T(8,128)S(1)}, u32[]{:S(2)}, u32[]{:S(2)}) collective-permute-start(f32[96,256]{1,0:T(8,128)S(1)} %get-tuple-element.199), channel_id=1, source_target_pairs={{0,4},{4,8},{8,12},{12,16},{16,20},{20,24},{24,28},{28,0},{1,5},{5... | collective-permute-start | bytes 294920 | tf_op jit(solution)/shard_map/ppermute | solution.py:324
  26.1 8.0 %collective-permute-start.15 = (f32[160,256]{1,0:T(8,128)S(1)}, f32[160,256]{1,0:T(8,128)S(1)}, u32[]{:S(2)}, u32[]{:S(2)}) collective-permute-start(f32[160,256]{1,0:T(8,128)S(1)} %get-tuple-element.202), channel_id=1, source_target_pairs={{0,4},{4,8},{8,12},{12,16},{16,20},{20,24},{24,28},{28,0},{1,5},{5... | collective-permute-start | bytes 491528 | tf_op jit(solution)/shard_map/ppermute | solution.py:324
  28.2 6.3 %collective-permute-start.16 = (f32[96,256]{1,0:T(8,128)S(1)}, f32[96,256]{1,0:T(8,128)S(1)}, u32[]{:S(2)}, u32[]{:S(2)}) collective-permute-start(f32[96,256]{1,0:T(8,128)S(1)} %get-tuple-element.205), channel_id=1, source_target_pairs={{0,4},{4,8},{8,12},{12,16},{16,20},{20,24},{24,28},{28,0},{1,5},{5... | collective-permute-start | bytes 294920 | tf_op jit(solution)/shard_map/ppermute | solution.py:324
  30.3 5.0 %collective-permute-start.17 = (f32[96,256]{1,0:T(8,128)S(1)}, f32[96,256]{1,0:T(8,128)S(1)}, u32[]{:S(2)}, u32[]{:S(2)}) collective-permute-start(f32[96,256]{1,0:T(8,128)S(1)} %get-tuple-element.208), channel_id=1, source_target_pairs={{0,4},{4,8},{8,12},{12,16},{16,20},{20,24},{24,28},{28,0},{1,5},{5... | collective-permute-start | bytes 294920 | tf_op jit(solution)/shard_map/ppermute | solution.py:324
  31.7 4.6 %collective-permute-start.13 = (f32[64,256]{1,0:T(8,128)S(1)}, f32[64,256]{1,0:T(8,128)S(1)}, u32[]{:S(2)}, u32[]{:S(2)}) collective-permute-start(f32[64,256]{1,0:T(8,128)S(1)} %get-tuple-element.198), channel_id=1, source_target_pairs={{0,4},{4,8},{8,12},{12,16},{16,20},{20,24},{24,28},{28,0},{1,5},{5... | collective-permute-start | bytes 196616 | tf_op jit(solution)/shard_map/ppermute | solution.py:324

commit v11 on v10

--- a/solution.py
+++ b/solution.py
@@ -10,7 +10,7 @@
 LEARN_RATE = 0.03
 DECAY_RATE = 0.1
 EARLY = (0, 3, 8, 13, 16)
-LATER = (0, 3, 8, 11, 14, 16)
+LATER = (0, 3, 6, 11, 14, 16)
 EARLY_WEIGHTS = (1e9, 1e7, 6e8, 2e9)
 LATER_WEIGHTS = (3e8, 1e8, 3e8, 6e8, 6e8)
 SUBLANES = 8

time: 37.8 us -> 43.2 us (1.14)
  waiting for transfers between devices: 4.53 us -> 12.5 us
  starting transfers between devices: 19 us -> 16.4 us
    ppermute x18, waiting for transfers between devices: 4.53 us -> 12.5 us  [shifted(): return lax.ppermute(chunk, axis, [(i, (i + 1) % n) for i in range(n)])]
    ppermute x18, starting transfers between devices: 19 us -> 16.4 us  [shifted(): return lax.ppermute(chunk, axis, [(i, (i + 1) % n) for i in range(n)])]
  transfers between devices with their start and end apart: 18 -> 18, of which waited for: 10 -> 10; matrix products, arithmetic and copies ran while one was open for 0% -> 0% of each run, Pallas kernels for 27% -> 24%
where the time goes in v11:
time: 43.2 us; the launch traced here: 43.1 us
  starting transfers between devices  16.4 us (38%)
  Pallas kernels  13.2 us (31%)
  waiting for transfers between devices  12.5 us (29%)
  between operations  0.94 us (2%)
    ppermute x18, starting transfers between devices, shifted(): return lax.ppermute(chunk, axis, [(i, (i + 1) % n) for i in range(n)])  16.4 us
    pallas_call x27, Pallas kernels, call(): pl.pallas_call(body, out_shape=outs, in_specs=in_specs, out_specs=out_spe...  13.2 us
    ppermute x18, waiting for transfers between devices, shifted(): return lax.ppermute(chunk, axis, [(i, (i + 1) % n) for i in range(n)])  12.5 us
  transfers between devices with their start and end apart: 18, of which 10 were waited for; matrix products, arithmetic and copies ran while one was open for 0% of the time, Pallas kernels for 24%

profile of v11, /device:TPU:0, one launch (start us, length us, event | category | flops | bytes accessed | tf_op | source)
XLA Modules:
  0.0 43.1 jit_solution(4706052475441503929)
XLA Ops:
  0.7 1.7 %first_chunk.1 = (f32[512,256]{1,0:T(8,128)S(1)}, f32[512,256]{1,0:T(8,128)S(1)}, bf16[512,256]{1,0:T(8,128)(2,1)S(1)}, bf16[512,512]{1,0:T(8,128)(2,1)S(1)}, f3...) custom-call(f32[512,256]{1,0:T(8,128)} %u_hbm.1, ...), custom_call_target="tpu_custom_call" | custom-call | flops 10000000 | bytes 1 | tf_op jit(solution)/shard_map/first_chunk/pallas_call | solution.py:25
  2.3 0.5 %collective-permute-start = (f32[96,256]{1,0:T(8,128)S(1)}, f32[96,256]{1,0:T(8,128)S(1)}, u32[]{:S(2)}, u32[]{:S(2)}) collective-permute-start(f32[96,256]{1,0:T(8,128)S(1)} %get-tuple-element.128), channel_id=1, source_target_pairs={{0,4},{4,8},{8,12},{12,16},{16,20},{20,24},{24,28},{28,0},{1,5},{5... | collective-permute-start | bytes 294920 | tf_op jit(solution)/shard_map/ppermute | solution.py:324
  2.8 0.5 %other_chunks.1 = (f32[8,128]{1,0:T(8,128)S(1)}, bf16[416,512]{1,0:T(8,128)(2,1)S(1)}, bf16[416,256]{1,0:T(8,128)(2,1)S(1)}, f32[160,256]{1,0:T(8,128)S(1)}, f32...) custom-call(bf16[512,256]{1,0:T(8,128)(2,1)S(1)} %get-tuple-element.113.refs_0_.refs_1_, ...), custom_call_target="tpu_custom_call", output_to_operand_aliasing={{0}: (4, {})} | custom-call | flops 10000000 | bytes 1 | tf_op jit(solution)/shard_map/other_chunks/pallas_call | solution.py:25
  3.4 2.7 %collective-permute-start.1 = (f32[160,256]{1,0:T(8,128)S(1)}, f32[160,256]{1,0:T(8,128)S(1)}, u32[]{:S(2)}, u32[]{:S(2)}) collective-permute-start(f32[160,256]{1,0:T(8,128)S(1)} %get-tuple-element.131), channel_id=1, source_target_pairs={{0,4},{4,8},{8,12},{12,16},{16,20},{20,24},{24,28},{28,0},{1,5},{5... | collective-permute-start | bytes 491528 | tf_op jit(solution)/shard_map/ppermute | solution.py:324
  6.1 1.5 %collective-permute-start.3 = (f32[96,256]{1,0:T(8,128)S(1)}, f32[96,256]{1,0:T(8,128)S(1)}, u32[]{:S(2)}, u32[]{:S(2)}) collective-permute-start(f32[96,256]{1,0:T(8,128)S(1)} %get-tuple-element.137), channel_id=1, source_target_pairs={{0,4},{4,8},{8,12},{12,16},{16,20},{20,24},{24,28},{28,0},{1,5},{5... | collective-permute-start | bytes 294920 | tf_op jit(solution)/shard_map/ppermute | solution.py:324
  7.6 1.0 %lay_out_tiles.1 = (f32[8,128]{1,0:T(8,128)S(1)}, bf16[512,512]{1,0:T(8,128)(2,1)S(1)}, bf16[512,512]{1,0:T(8,128)(2,1)S(1)}, bf16[512,512]{1,0:T(8,128)(2,1)S(1...) custom-call(bf16[5,8,128,128]{3,2,1,0:T(8,128)(2,1)S(1)} %copy-done,, ...), custom_call_target="tpu_custom_call", output_to_operand_aliasing={{0}: (3, {})} | custom-call | flops 10000000 | bytes 1 | tf_op jit(solution)/shard_map/lay_out_tiles/pallas_call | solution.py:25
  8.6 0.4 rows_step.4
  9.0 0.3 columns_step.18
  9.5 0.2 collective-permute-done.1.refs_3_
  9.8 0.4 columns_step.19
  10.1 1.4 %collective-permute-start.5 = (f32[160,256]{1,0:T(8,128)S(1)}, f32[160,256]{1,0:T(8,128)S(1)}, u32[]{:S(2)}, u32[]{:S(2)}) collective-permute-start(f32[160,256]{1,0:T(8,128)S(1)} %get-tuple-element.152), channel_id=1, source_target_pairs={{0,4},{4,8},{8,12},{12,16},{16,20},{20,24},{24,28},{28,0},{1,5},{5... | collective-permute-start | bytes 491528 | tf_op jit(solution)/shard_map/ppermute | solution.py:324
  11.5 0.2 collective-permute-done.2.refs_3_
  11.6 0.4 columns_step.20
  12.1 0.6 %collective-permute-done.3.refs_3_ = f32[96,256]{1,0:T(8,128)S(1)} collective-permute-done((f32[96,256]{1,0:T(8,128)S(1)}, f32[96,256]{1,0:T(8,128)S(1)}, u32[]{:S(2)}, u32[]{:S(2)}) %collective-permute-start.3) | collective-permute-done | bytes 98336 | tf_op jit(solution)/shard_map/ppermute | solution.py:324
  12.7 0.3 columns_step.21
  13.0 0.8 %collective-permute-start.7 = (f32[96,256]{1,0:T(8,128)S(1)}, f32[96,256]{1,0:T(8,128)S(1)}, u32[]{:S(2)}, u32[]{:S(2)}) collective-permute-start(f32[96,256]{1,0:T(8,128)S(1)} %get-tuple-element.158), channel_id=1, source_target_pairs={{0,4},{4,8},{8,12},{12,16},{16,20},{20,24},{24,28},{28,0},{1,5},{5... | collective-permute-start | bytes 294920 | tf_op jit(solution)/shard_map/ppermute | solution.py:324
  13.8 0.5 %rows_step.5 = (f32[8,128]{1,0:T(8,128)S(1)}, f32[512,256]{1,0:T(8,128)S(1)}, bf16[512,256]{1,0:T(8,128)(2,1)S(1)}) custom-call(f32[512,256]{1,0:T(8,128)S(1)} %get-tuple-element.124.refs_0_, bf16[512,256]{1,0:T(8,128)(2,1)S(1)} %get-tuple-element.125.refs_0_.refs_1_, ...), custom_call_target="tpu_custom_call", output_to_operand_aliasing={{0}: (10, {}), {1}: (0, {}), {2}: (1, {})} | custom-call | flops 10000000 | bytes 1 | tf_op jit(solution)/shard_map/rows_step/pallas_call | solution.py:25
  14.4 0.3 columns_step.22
  14.7 1.4 %collective-permute-done.5.refs_3_ = f32[160,256]{1,0:T(8,128)S(1)} collective-permute-done((f32[160,256]{1,0:T(8,128)S(1)}, f32[160,256]{1,0:T(8,128)S(1)}, u32[]{:S(2)}, u32[]{:S(2)}) %collective-permute-start.5) | collective-permute-done | bytes 163872 | tf_op jit(solution)/shard_map/ppermute | solution.py:324
  16.1 0.3 columns_step.23
  16.5 1.4 %collective-permute-done.6.refs_4_.refs_3_ = f32[160,256]{1,0:T(8,128)S(1)} collective-permute-done((f32[160,256]{1,0:T(8,128)S(1)}, f32[160,256]{1,0:T(8,128)S(1)}, u32[]{:S(2)}, u32[]{:S(2)}) %collective-permute-start.6) | collective-permute-done | bytes 163872 | tf_op jit(solution)/shard_map/ppermute | solution.py:324
  17.9 0.4 columns_step.24
  18.3 2.1 %collective-permute-start.10 = (f32[160,256]{1,0:T(8,128)S(1)}, f32[160,256]{1,0:T(8,128)S(1)}, u32[]{:S(2)}, u32[]{:S(2)}) collective-permute-start(f32[160,256]{1,0:T(8,128)S(1)} %get-tuple-element.179), channel_id=1, source_target_pairs={{0,1},{1,2},{2,3},{3,0},{4,5},{5,6},{6,7},{7,4},{8,9},{9,10},{10,1... | collective-permute-start | bytes 491528 | tf_op jit(solution)/shard_map/ppermute | solution.py:324
  20.3 1.6 %collective-permute-start.8 = (f32[96,256]{1,0:T(8,128)S(1)}, f32[96,256]{1,0:T(8,128)S(1)}, u32[]{:S(2)}, u32[]{:S(2)}) collective-permute-start(f32[96,256]{1,0:T(8,128)S(1)} %get-tuple-element.173), channel_id=1, source_target_pairs={{0,1},{1,2},{2,3},{3,0},{4,5},{5,6},{6,7},{7,4},{8,9},{9,10},{10,1... | collective-permute-start | bytes 294920 | tf_op jit(solution)/shard_map/ppermute | solution.py:324
  21.9 1.6 %collective-permute-start.9 = (f32[96,256]{1,0:T(8,128)S(1)}, f32[96,256]{1,0:T(8,128)S(1)}, u32[]{:S(2)}, u32[]{:S(2)}) collective-permute-start(f32[96,256]{1,0:T(8,128)S(1)} %get-tuple-element.176), channel_id=1, source_target_pairs={{0,1},{1,2},{2,3},{3,0},{4,5},{5,6},{6,7},{7,4},{8,9},{9,10},{10,1... | collective-permute-start | bytes 294920 | tf_op jit(solution)/shard_map/ppermute | solution.py:324
  23.5 0.3 columns_step.25
  24.0 0.3 columns_step.26
  24.3 0.5 %rows_step.6 = (f32[8,128]{1,0:T(8,128)S(1)}, f32[512,256]{1,0:T(8,128)S(1)}, bf16[512,256]{1,0:T(8,128)(2,1)S(1)}) custom-call(f32[512,256]{1,0:T(8,128)S(1)} %get-tuple-element.145.refs_0_, bf16[512,256]{1,0:T(8,128)(2,1)S(1)} %get-tuple-element.146.refs_0_.refs_1_, ...), custom_call_target="tpu_custom_call", output_to_operand_aliasing={{0}: (12, {}), {1}: (0, {}), {2}: (1, {})} | custom-call | flops 10000000 | bytes 1 | tf_op jit(solution)/shard_map/rows_step/pallas_call | solution.py:25
  24.9 3.9 %collective-permute-done.8.refs_3_ = f32[96,256]{1,0:T(8,128)S(1)} collective-permute-done((f32[96,256]{1,0:T(8,128)S(1)}, f32[96,256]{1,0:T(8,128)S(1)}, u32[]{:S(2)}, u32[]{:S(2)}) %collective-permute-start.8) | collective-permute-done | bytes 98336 | tf_op jit(solution)/shard_map/ppermute | solution.py:324
  28.8 0.3 columns_step.27
  29.2 0.7 %collective-permute-done.9.refs_3_ = f32[96,256]{1,0:T(8,128)S(1)} collective-permute-done((f32[96,256]{1,0:T(8,128)S(1)}, f32[96,256]{1,0:T(8,128)S(1)}, u32[]{:S(2)}, u32[]{:S(2)}) %collective-permute-start.9) | collective-permute-done | bytes 98336 | tf_op jit(solution)/shard_map/ppermute | solution.py:324
  29.9 0.3 columns_step.28
  30.2 0.4 columns_step.29
  30.7 1.9 %collective-permute-start.14 = (f32[96,256]{1,0:T(8,128)S(1)}, f32[96,256]{1,0:T(8,128)S(1)}, u32[]{:S(2)}, u32[]{:S(2)}) collective-permute-start(f32[96,256]{1,0:T(8,128)S(1)} %get-tuple-element.199), channel_id=1, source_target_pairs={{0,4},{4,8},{8,12},{12,16},{16,20},{20,24},{24,28},{28,0},{1,5},{5... | collective-permute-start | bytes 294920 | tf_op jit(solution)/shard_map/ppermute | solution.py:324
  32.6 0.1 collective-permute-start.15
  32.8 0.3 columns_step.30
  33.1 1.1 %collective-permute-start.17 = (f32[96,256]{1,0:T(8,128)S(1)}, f32[96,256]{1,0:T(8,128)S(1)}, u32[]{:S(2)}, u32[]{:S(2)}) collective-permute-start(f32[96,256]{1,0:T(8,128)S(1)} %get-tuple-element.208), channel_id=1, source_target_pairs={{0,4},{4,8},{8,12},{12,16},{16,20},{20,24},{24,28},{28,0},{1,5},{5... | collective-permute-start | bytes 294920 | tf_op jit(solution)/shard_map/ppermute | solution.py:324
  34.2 2.6 %collective-permute-done.12.refs_3_ = f32[64,256]{1,0:T(8,128)S(1)} collective-permute-done((f32[64,256]{1,0:T(8,128)S(1)}, f32[64,256]{1,0:T(8,128)S(1)}, u32[]{:S(2)}, u32[]{:S(2)}) %collective-permute-start.12) | collective-permute-done | bytes 65568 | tf_op jit(solution)/shard_map/ppermute | solution.py:324
  36.8 0.3 columns_step.31
  37.1 0.8 %collective-permute-start.13 = (f32[64,256]{1,0:T(8,128)S(1)}, f32[64,256]{1,0:T(8,128)S(1)}, u32[]{:S(2)}, u32[]{:S(2)}) collective-permute-start(f32[64,256]{1,0:T(8,128)S(1)} %get-tuple-element.198), channel_id=1, source_target_pairs={{0,4},{4,8},{8,12},{12,16},{16,20},{20,24},{24,28},{28,0},{1,5},{5... | collective-permute-start | bytes 196616 | tf_op jit(solution)/shard_map/ppermute | solution.py:324
  37.9 0.5 %rows_step.7 = (f32[8,128]{1,0:T(8,128)S(1)}, f32[512,256]{1,0:T(8,128)S(1)}, bf16[512,256]{1,0:T(8,128)(2,1)S(1)}) custom-call(f32[512,256]{1,0:T(8,128)S(1)} %get-tuple-element.169.refs_0_, bf16[512,256]{1,0:T(8,128)(2,1)S(1)} %get-tuple-element.170.refs_0_.refs_1_, ...), custom_call_target="tpu_custom_call", output_to_operand_aliasing={{0}: (12, {}), {1}: (0, {}), {2}: (1, {})} | custom-call | flops 10000000 | bytes 1 | tf_op jit(solution)/shard_map/rows_step/pallas_call | solution.py:25
  38.5 0.3 columns_step.32
  38.9 0.3 columns_step.33
  39.2 0.4 columns_step.34
  39.6 0.3 columns_step.35
  40.0 0.5 %rows_gradient.1 = (f32[8,128]{1,0:T(8,128)S(1)}, f32[512,256]{1,0:T(8,128)S(1)}) custom-call(bf16[96,512]{1,0:T(8,128)(2,1)S(1)} %get-tuple-element.201.refs_0_, bf16[96,512]{1,0:T(8,128)(2,1)S(1)} %get-tuple-element.204.refs_1_, bf16[160,512]{1,0:T(8,128)(2,1)S(1)} %get-tuple-element.207.refs_2_, ...), custom_call_target="tpu_custom_call", output_to_operand_aliasing={{0}: (8, {})} | custom-call | flops 10000000 | bytes 1 | tf_op jit(solution)/shard_map/rows_gradient/pallas_call | solution.py:25
  40.4 1.3 %collective-permute-done.13.c_ref = f32[64,256]{1,0:T(8,128)S(1)} collective-permute-done((f32[64,256]{1,0:T(8,128)S(1)}, f32[64,256]{1,0:T(8,128)S(1)}, u32[]{:S(2)}, u32[]{:S(2)}) %collective-permute-start.13) | collective-permute-done | bytes 65568 | tf_op jit(solution)/shard_map/ppermute | solution.py:324
  41.8 1.3 %last_columns_and_rows.1 = (f32[512,256]{1,0:T(8,128)}, f32[512,256]{1,0:T(8,128)}) custom-call(f32[512,256]{1,0:T(8,128)S(1)} %get-tuple-element.194.u_ref, bf16[512,256]{1,0:T(8,128)(2,1)S(1)} %get-tuple-element.195.refs_0_.row_half, bf16[512,512]{1,0:T(8,128)(2,1)S(1)} %get-tuple-element.196.refs_1_.dense, f32[8,512]{1,0:T(8,128)S(1)} %get-tuple-element.197.refs_2_.live, ...), custom_call_target="tpu_custom_call" | custom-call | flops 10000000 | bytes 1 | tf_op jit(solution)/shard_map/last_columns_and_rows/pallas_call | solution.py:25
  (21 shorter events, 0.6 us)
Async XLA Ops:
  0.6 7.0 %copy-start = (bf16[5,8,128,128]{3,2,1,0:T(8,128)(2,1)S(1)}, bf16[5,8,128,128]{3,2,1,0:T(8,128)(2,1)}, u32[]{:S(2)}) copy-start(bf16[5,8,128,128]{3,2,1,0:T(8,128)(2,1)} %x_ref.1) | copy-start | bytes 3932164
  0.6 7.0 %copy-start.1 = (s32[5,8,2]{1,2,0:T(2,128)S(1)}, s32[5,8,2]{1,2,0:T(2,128)}, u32[]{:S(2)}) copy-start(s32[5,8,2]{1,2,0:T(2,128)} %param.8) | copy-start | bytes 964
  0.7 7.0 %copy-start.2 = (s32[5,1]{0,1:T(1,128)S(1)}, s32[5,1]{0,1:T(1,128)}, u32[]{:S(2)}) copy-start(s32[5,1]{0,1:T(1,128)} %param.9) | copy-start | bytes 64
  2.3 6.7 %collective-permute-start = (f32[96,256]{1,0:T(8,128)S(1)}, f32[96,256]{1,0:T(8,128)S(1)}, u32[]{:S(2)}, u32[]{:S(2)}) collective-permute-start(f32[96,256]{1,0:T(8,128)S(1)} %get-tuple-element.128), channel_id=1, source_target_pairs={{0,4},{4,8},{8,12},{12,16},{16,20},{20,24},{24,28},{28,0},{1,5},{5... | collective-permute-start | bytes 294920 | tf_op jit(solution)/shard_map/ppermute | solution.py:324
  3.4 6.4 %collective-permute-start.1 = (f32[160,256]{1,0:T(8,128)S(1)}, f32[160,256]{1,0:T(8,128)S(1)}, u32[]{:S(2)}, u32[]{:S(2)}) collective-permute-start(f32[160,256]{1,0:T(8,128)S(1)} %get-tuple-element.131), channel_id=1, source_target_pairs={{0,4},{4,8},{8,12},{12,16},{16,20},{20,24},{24,28},{28,0},{1,5},{5... | collective-permute-start | bytes 491528 | tf_op jit(solution)/shard_map/ppermute | solution.py:324
  6.0 5.6 %collective-permute-start.2 = (f32[160,256]{1,0:T(8,128)S(1)}, f32[160,256]{1,0:T(8,128)S(1)}, u32[]{:S(2)}, u32[]{:S(2)}) collective-permute-start(f32[160,256]{1,0:T(8,128)S(1)} %get-tuple-element.134), channel_id=1, source_target_pairs={{0,4},{4,8},{8,12},{12,16},{16,20},{20,24},{24,28},{28,0},{1,5},{5... | collective-permute-start | bytes 491528 | tf_op jit(solution)/shard_map/ppermute | solution.py:324
  6.1 6.6 %collective-permute-start.3 = (f32[96,256]{1,0:T(8,128)S(1)}, f32[96,256]{1,0:T(8,128)S(1)}, u32[]{:S(2)}, u32[]{:S(2)}) collective-permute-start(f32[96,256]{1,0:T(8,128)S(1)} %get-tuple-element.137), channel_id=1, source_target_pairs={{0,4},{4,8},{8,12},{12,16},{16,20},{20,24},{24,28},{28,0},{1,5},{5... | collective-permute-start | bytes 294920 | tf_op jit(solution)/shard_map/ppermute | solution.py:324
  9.4 5.0 %collective-permute-start.4 = (f32[96,256]{1,0:T(8,128)S(1)}, f32[96,256]{1,0:T(8,128)S(1)}, u32[]{:S(2)}, u32[]{:S(2)}) collective-permute-start(f32[96,256]{1,0:T(8,128)S(1)} %get-tuple-element.149), channel_id=1, source_target_pairs={{0,4},{4,8},{8,12},{12,16},{16,20},{20,24},{24,28},{28,0},{1,5},{5... | collective-permute-start | bytes 294920 | tf_op jit(solution)/shard_map/ppermute | solution.py:324
  10.1 6.0 %collective-permute-start.5 = (f32[160,256]{1,0:T(8,128)S(1)}, f32[160,256]{1,0:T(8,128)S(1)}, u32[]{:S(2)}, u32[]{:S(2)}) collective-permute-start(f32[160,256]{1,0:T(8,128)S(1)} %get-tuple-element.152), channel_id=1, source_target_pairs={{0,4},{4,8},{8,12},{12,16},{16,20},{20,24},{24,28},{28,0},{1,5},{5... | collective-permute-start | bytes 491528 | tf_op jit(solution)/shard_map/ppermute | solution.py:324
  12.0 5.9 %collective-permute-start.6 = (f32[160,256]{1,0:T(8,128)S(1)}, f32[160,256]{1,0:T(8,128)S(1)}, u32[]{:S(2)}, u32[]{:S(2)}) collective-permute-start(f32[160,256]{1,0:T(8,128)S(1)} %get-tuple-element.155), channel_id=1, source_target_pairs={{0,4},{4,8},{8,12},{12,16},{16,20},{20,24},{24,28},{28,0},{1,5},{5... | collective-permute-start | bytes 491528 | tf_op jit(solution)/shard_map/ppermute | solution.py:324
  13.0 10.5 %collective-permute-start.7 = (f32[96,256]{1,0:T(8,128)S(1)}, f32[96,256]{1,0:T(8,128)S(1)}, u32[]{:S(2)}, u32[]{:S(2)}) collective-permute-start(f32[96,256]{1,0:T(8,128)S(1)} %get-tuple-element.158), channel_id=1, source_target_pairs={{0,4},{4,8},{8,12},{12,16},{16,20},{20,24},{24,28},{28,0},{1,5},{5... | collective-permute-start | bytes 294920 | tf_op jit(solution)/shard_map/ppermute | solution.py:324
  18.3 11.9 %collective-permute-start.10 = (f32[160,256]{1,0:T(8,128)S(1)}, f32[160,256]{1,0:T(8,128)S(1)}, u32[]{:S(2)}, u32[]{:S(2)}) collective-permute-start(f32[160,256]{1,0:T(8,128)S(1)} %get-tuple-element.179), channel_id=1, source_target_pairs={{0,1},{1,2},{2,3},{3,0},{4,5},{5,6},{6,7},{7,4},{8,9},{9,10},{10,1... | collective-permute-start | bytes 491528 | tf_op jit(solution)/shard_map/ppermute | solution.py:324
  20.3 8.5 %collective-permute-start.8 = (f32[96,256]{1,0:T(8,128)S(1)}, f32[96,256]{1,0:T(8,128)S(1)}, u32[]{:S(2)}, u32[]{:S(2)}) collective-permute-start(f32[96,256]{1,0:T(8,128)S(1)} %get-tuple-element.173), channel_id=1, source_target_pairs={{0,1},{1,2},{2,3},{3,0},{4,5},{5,6},{6,7},{7,4},{8,9},{9,10},{10,1... | collective-permute-start | bytes 294920 | tf_op jit(solution)/shard_map/ppermute | solution.py:324
  21.9 7.9 %collective-permute-start.9 = (f32[96,256]{1,0:T(8,128)S(1)}, f32[96,256]{1,0:T(8,128)S(1)}, u32[]{:S(2)}, u32[]{:S(2)}) collective-permute-start(f32[96,256]{1,0:T(8,128)S(1)} %get-tuple-element.176), channel_id=1, source_target_pairs={{0,1},{1,2},{2,3},{3,0},{4,5},{5,6},{6,7},{7,4},{8,9},{9,10},{10,1... | collective-permute-start | bytes 294920 | tf_op jit(solution)/shard_map/ppermute | solution.py:324
  23.9 8.9 %collective-permute-start.11 = (f32[96,256]{1,0:T(8,128)S(1)}, f32[96,256]{1,0:T(8,128)S(1)}, u32[]{:S(2)}, u32[]{:S(2)}) collective-permute-start(f32[96,256]{1,0:T(8,128)S(1)} %get-tuple-element.182), channel_id=1, source_target_pairs={{0,1},{1,2},{2,3},{3,0},{4,5},{5,6},{6,7},{7,4},{8,9},{9,10},{10,1... | collective-permute-start | bytes 294920 | tf_op jit(solution)/shard_map/ppermute | solution.py:324
  30.6 8.6 %collective-permute-start.16 = (f32[160,256]{1,0:T(8,128)S(1)}, f32[160,256]{1,0:T(8,128)S(1)}, u32[]{:S(2)}, u32[]{:S(2)}) collective-permute-start(f32[160,256]{1,0:T(8,128)S(1)} %get-tuple-element.205), channel_id=1, source_target_pairs={{0,4},{4,8},{8,12},{12,16},{16,20},{20,24},{24,28},{28,0},{1,5},{5... | collective-permute-start | bytes 491528 | tf_op jit(solution)/shard_map/ppermute | solution.py:324
  30.7 6.1 %collective-permute-start.12 = (f32[64,256]{1,0:T(8,128)S(1)}, f32[64,256]{1,0:T(8,128)S(1)}, u32[]{:S(2)}, u32[]{:S(2)}) collective-permute-start(f32[64,256]{1,0:T(8,128)S(1)} %get-tuple-element.185), channel_id=1, source_target_pairs={{0,1},{1,2},{2,3},{3,0},{4,5},{5,6},{6,7},{7,4},{8,9},{9,10},{10,1... | collective-permute-start | bytes 196616 | tf_op jit(solution)/shard_map/ppermute | solution.py:324
  30.7 7.8 %collective-permute-start.14 = (f32[96,256]{1,0:T(8,128)S(1)}, f32[96,256]{1,0:T(8,128)S(1)}, u32[]{:S(2)}, u32[]{:S(2)}) collective-permute-start(f32[96,256]{1,0:T(8,128)S(1)} %get-tuple-element.199), channel_id=1, source_target_pairs={{0,4},{4,8},{8,12},{12,16},{16,20},{20,24},{24,28},{28,0},{1,5},{5... | collective-permute-start | bytes 294920 | tf_op jit(solution)/shard_map/ppermute | solution.py:324
  32.6 6.2 %collective-permute-start.15 = (f32[96,256]{1,0:T(8,128)S(1)}, f32[96,256]{1,0:T(8,128)S(1)}, u32[]{:S(2)}, u32[]{:S(2)}) collective-permute-start(f32[96,256]{1,0:T(8,128)S(1)} %get-tuple-element.202), channel_id=1, source_target_pairs={{0,4},{4,8},{8,12},{12,16},{16,20},{20,24},{24,28},{28,0},{1,5},{5... | collective-permute-start | bytes 294920 | tf_op jit(solution)/shard_map/ppermute | solution.py:324
  33.1 6.5 %collective-permute-start.17 = (f32[96,256]{1,0:T(8,128)S(1)}, f32[96,256]{1,0:T(8,128)S(1)}, u32[]{:S(2)}, u32[]{:S(2)}) collective-permute-start(f32[96,256]{1,0:T(8,128)S(1)} %get-tuple-element.208), channel_id=1, source_target_pairs={{0,4},{4,8},{8,12},{12,16},{16,20},{20,24},{24,28},{28,0},{1,5},{5... | collective-permute-start | bytes 294920 | tf_op jit(solution)/shard_map/ppermute | solution.py:324
  37.1 4.6 %collective-permute-start.13 = (f32[64,256]{1,0:T(8,128)S(1)}, f32[64,256]{1,0:T(8,128)S(1)}, u32[]{:S(2)}, u32[]{:S(2)}) collective-permute-start(f32[64,256]{1,0:T(8,128)S(1)} %get-tuple-element.198), channel_id=1, source_target_pairs={{0,4},{4,8},{8,12},{12,16},{16,20},{20,24},{24,28},{28,0},{1,5},{5... | collective-permute-start | bytes 196616 | tf_op jit(solution)/shard_map/ppermute | solution.py:324

commit v12 on v11

--- a/solution.py
+++ b/solution.py
@@ -10,7 +10,7 @@
 LEARN_RATE = 0.03
 DECAY_RATE = 0.1
 EARLY = (0, 3, 8, 13, 16)
-LATER = (0, 3, 6, 11, 14, 16)
+LATER = (0, 3, 7, 11, 14, 16)
 EARLY_WEIGHTS = (1e9, 1e7, 6e8, 2e9)
 LATER_WEIGHTS = (3e8, 1e8, 3e8, 6e8, 6e8)
 SUBLANES = 8

time: 43.2 us -> 37.8 us (0.87)
  waiting for transfers between devices: 12.5 us -> 4.51 us
  starting transfers between devices: 16.4 us -> 19 us
    ppermute x18, waiting for transfers between devices: 12.5 us -> 4.51 us  [shifted(): return lax.ppermute(chunk, axis, [(i, (i + 1) % n) for i in range(n)])]
    ppermute x18, starting transfers between devices: 16.4 us -> 19 us  [shifted(): return lax.ppermute(chunk, axis, [(i, (i + 1) % n) for i in range(n)])]
  transfers between devices with their start and end apart: 18 -> 18, of which waited for: 10 -> 9; matrix products, arithmetic and copies ran while one was open for 0% -> 0% of each run, Pallas kernels for 24% -> 27%
where the time goes in v12:
time: 37.8 us; the launch traced here: 37.6 us
  starting transfers between devices  19 us (50%)
  Pallas kernels  13.2 us (35%)
  waiting for transfers between devices  4.51 us (12%)
  between operations  0.94 us (2%)
    ppermute x18, starting transfers between devices, shifted(): return lax.ppermute(chunk, axis, [(i, (i + 1) % n) for i in range(n)])  19 us
    pallas_call x27, Pallas kernels, call(): pl.pallas_call(body, out_shape=outs, in_specs=in_specs, out_specs=out_spe...  13.2 us
    ppermute x18, waiting for transfers between devices, shifted(): return lax.ppermute(chunk, axis, [(i, (i + 1) % n) for i in range(n)])  4.51 us
  transfers between devices with their start and end apart: 18, of which 9 were waited for; matrix products, arithmetic and copies ran while one was open for 0% of the time, Pallas kernels for 27%

profile of v12, /device:TPU:0, one launch (start us, length us, event | category | flops | bytes accessed | tf_op | source)
XLA Modules:
  0.0 37.6 jit_solution(5587976588039450296)
XLA Ops:
  0.7 1.7 %first_chunk.1 = (f32[512,256]{1,0:T(8,128)S(1)}, f32[512,256]{1,0:T(8,128)S(1)}, bf16[512,256]{1,0:T(8,128)(2,1)S(1)}, bf16[512,512]{1,0:T(8,128)(2,1)S(1)}, f3...) custom-call(f32[512,256]{1,0:T(8,128)} %u_hbm.1, ...), custom_call_target="tpu_custom_call" | custom-call | flops 10000000 | bytes 1 | tf_op jit(solution)/shard_map/first_chunk/pallas_call | solution.py:25
  2.3 0.5 %collective-permute-start = (f32[96,256]{1,0:T(8,128)S(1)}, f32[96,256]{1,0:T(8,128)S(1)}, u32[]{:S(2)}, u32[]{:S(2)}) collective-permute-start(f32[96,256]{1,0:T(8,128)S(1)} %get-tuple-element.128), channel_id=1, source_target_pairs={{0,4},{4,8},{8,12},{12,16},{16,20},{20,24},{24,28},{28,0},{1,5},{5... | collective-permute-start | bytes 294920 | tf_op jit(solution)/shard_map/ppermute | solution.py:324
  2.8 0.5 %other_chunks.1 = (f32[8,128]{1,0:T(8,128)S(1)}, bf16[416,512]{1,0:T(8,128)(2,1)S(1)}, bf16[416,256]{1,0:T(8,128)(2,1)S(1)}, f32[160,256]{1,0:T(8,128)S(1)}, f32...) custom-call(bf16[512,256]{1,0:T(8,128)(2,1)S(1)} %get-tuple-element.113.refs_0_.refs_1_, ...), custom_call_target="tpu_custom_call", output_to_operand_aliasing={{0}: (4, {})} | custom-call | flops 10000000 | bytes 1 | tf_op jit(solution)/shard_map/other_chunks/pallas_call | solution.py:25
  3.4 2.7 %collective-permute-start.1 = (f32[160,256]{1,0:T(8,128)S(1)}, f32[160,256]{1,0:T(8,128)S(1)}, u32[]{:S(2)}, u32[]{:S(2)}) collective-permute-start(f32[160,256]{1,0:T(8,128)S(1)} %get-tuple-element.131), channel_id=1, source_target_pairs={{0,4},{4,8},{8,12},{12,16},{16,20},{20,24},{24,28},{28,0},{1,5},{5... | collective-permute-start | bytes 491528 | tf_op jit(solution)/shard_map/ppermute | solution.py:324
  6.1 1.5 %collective-permute-start.3 = (f32[96,256]{1,0:T(8,128)S(1)}, f32[96,256]{1,0:T(8,128)S(1)}, u32[]{:S(2)}, u32[]{:S(2)}) collective-permute-start(f32[96,256]{1,0:T(8,128)S(1)} %get-tuple-element.137), channel_id=1, source_target_pairs={{0,4},{4,8},{8,12},{12,16},{16,20},{20,24},{24,28},{28,0},{1,5},{5... | collective-permute-start | bytes 294920 | tf_op jit(solution)/shard_map/ppermute | solution.py:324
  7.6 1.0 %lay_out_tiles.1 = (f32[8,128]{1,0:T(8,128)S(1)}, bf16[512,512]{1,0:T(8,128)(2,1)S(1)}, bf16[512,512]{1,0:T(8,128)(2,1)S(1)}, bf16[512,512]{1,0:T(8,128)(2,1)S(1...) custom-call(bf16[5,8,128,128]{3,2,1,0:T(8,128)(2,1)S(1)} %copy-done,, ...), custom_call_target="tpu_custom_call", output_to_operand_aliasing={{0}: (3, {})} | custom-call | flops 10000000 | bytes 1 | tf_op jit(solution)/shard_map/lay_out_tiles/pallas_call | solution.py:25
  8.6 0.4 %rows_step.4 = (f32[8,128]{1,0:T(8,128)S(1)}, f32[512,256]{1,0:T(8,128)S(1)}, bf16[512,256]{1,0:T(8,128)(2,1)S(1)}) custom-call(f32[512,256]{1,0:T(8,128)S(1)} %get-tuple-element.112.refs_0_, bf16[512,256]{1,0:T(8,128)(2,1)S(1)} %get-tuple-element.113.refs_0_.refs_1_, ...), custom_call_target="tpu_custom_call", output_to_operand_aliasing={{0}: (6, {}), {1}: (0, {}), {2}: (1, {})} | custom-call | flops 10000000 | bytes 1 | tf_op jit(solution)/shard_map/rows_step/pallas_call | solution.py:25
  9.0 0.3 columns_step.18
  9.5 0.2 collective-permute-done.1.refs_3_
  9.8 0.4 columns_step.19
  10.1 1.4 %collective-permute-start.5 = (f32[160,256]{1,0:T(8,128)S(1)}, f32[160,256]{1,0:T(8,128)S(1)}, u32[]{:S(2)}, u32[]{:S(2)}) collective-permute-start(f32[160,256]{1,0:T(8,128)S(1)} %get-tuple-element.152), channel_id=1, source_target_pairs={{0,4},{4,8},{8,12},{12,16},{16,20},{20,24},{24,28},{28,0},{1,5},{5... | collective-permute-start | bytes 491528 | tf_op jit(solution)/shard_map/ppermute | solution.py:324
  11.6 0.4 columns_step.20
  12.1 0.6 %collective-permute-done.3.refs_3_ = f32[96,256]{1,0:T(8,128)S(1)} collective-permute-done((f32[96,256]{1,0:T(8,128)S(1)}, f32[96,256]{1,0:T(8,128)S(1)}, u32[]{:S(2)}, u32[]{:S(2)}) %collective-permute-start.3) | collective-permute-done | bytes 98336 | tf_op jit(solution)/shard_map/ppermute | solution.py:324
  12.7 0.3 columns_step.21
  13.0 0.8 %collective-permute-start.7 = (f32[96,256]{1,0:T(8,128)S(1)}, f32[96,256]{1,0:T(8,128)S(1)}, u32[]{:S(2)}, u32[]{:S(2)}) collective-permute-start(f32[96,256]{1,0:T(8,128)S(1)} %get-tuple-element.158), channel_id=1, source_target_pairs={{0,4},{4,8},{8,12},{12,16},{16,20},{20,24},{24,28},{28,0},{1,5},{5... | collective-permute-start | bytes 294920 | tf_op jit(solution)/shard_map/ppermute | solution.py:324
  13.8 0.5 %rows_step.5 = (f32[8,128]{1,0:T(8,128)S(1)}, f32[512,256]{1,0:T(8,128)S(1)}, bf16[512,256]{1,0:T(8,128)(2,1)S(1)}) custom-call(f32[512,256]{1,0:T(8,128)S(1)} %get-tuple-element.124.refs_0_, bf16[512,256]{1,0:T(8,128)(2,1)S(1)} %get-tuple-element.125.refs_0_.refs_1_, ...), custom_call_target="tpu_custom_call", output_to_operand_aliasing={{0}: (10, {}), {1}: (0, {}), {2}: (1, {})} | custom-call | flops 10000000 | bytes 1 | tf_op jit(solution)/shard_map/rows_step/pallas_call | solution.py:25
  14.4 0.3 columns_step.22
  14.7 1.6 %collective-permute-start.8 = (f32[96,256]{1,0:T(8,128)S(1)}, f32[96,256]{1,0:T(8,128)S(1)}, u32[]{:S(2)}, u32[]{:S(2)}) collective-permute-start(f32[96,256]{1,0:T(8,128)S(1)} %get-tuple-element.173), channel_id=1, source_target_pairs={{0,1},{1,2},{2,3},{3,0},{4,5},{5,6},{6,7},{7,4},{8,9},{9,10},{10,1... | collective-permute-start | bytes 294920 | tf_op jit(solution)/shard_map/ppermute | solution.py:324
  16.4 0.4 columns_step.23
  16.7 1.8 %collective-permute-start.9 = (f32[128,256]{1,0:T(8,128)S(1)}, f32[128,256]{1,0:T(8,128)S(1)}, u32[]{:S(2)}, u32[]{:S(2)}) collective-permute-start(f32[128,256]{1,0:T(8,128)S(1)} %get-tuple-element.176), channel_id=1, source_target_pairs={{0,1},{1,2},{2,3},{3,0},{4,5},{5,6},{6,7},{7,4},{8,9},{9,10},{10,1... | collective-permute-start | bytes 393224 | tf_op jit(solution)/shard_map/ppermute | solution.py:324
  18.6 0.4 columns_step.24
  19.0 1.6 %collective-permute-start.10 = (f32[128,256]{1,0:T(8,128)S(1)}, f32[128,256]{1,0:T(8,128)S(1)}, u32[]{:S(2)}, u32[]{:S(2)}) collective-permute-start(f32[128,256]{1,0:T(8,128)S(1)} %get-tuple-element.179), channel_id=1, source_target_pairs={{0,1},{1,2},{2,3},{3,0},{4,5},{5,6},{6,7},{7,4},{8,9},{9,10},{10,1... | collective-permute-start | bytes 393224 | tf_op jit(solution)/shard_map/ppermute | solution.py:324
  20.6 0.3 columns_step.25
  20.9 1.6 %collective-permute-start.11 = (f32[96,256]{1,0:T(8,128)S(1)}, f32[96,256]{1,0:T(8,128)S(1)}, u32[]{:S(2)}, u32[]{:S(2)}) collective-permute-start(f32[96,256]{1,0:T(8,128)S(1)} %get-tuple-element.182), channel_id=1, source_target_pairs={{0,1},{1,2},{2,3},{3,0},{4,5},{5,6},{6,7},{7,4},{8,9},{9,10},{10,1... | collective-permute-start | bytes 294920 | tf_op jit(solution)/shard_map/ppermute | solution.py:324
  22.6 0.3 columns_step.26
  22.9 1.4 %collective-permute-start.12 = (f32[64,256]{1,0:T(8,128)S(1)}, f32[64,256]{1,0:T(8,128)S(1)}, u32[]{:S(2)}, u32[]{:S(2)}) collective-permute-start(f32[64,256]{1,0:T(8,128)S(1)} %get-tuple-element.185), channel_id=1, source_target_pairs={{0,1},{1,2},{2,3},{3,0},{4,5},{5,6},{6,7},{7,4},{8,9},{9,10},{10,1... | collective-permute-start | bytes 196616 | tf_op jit(solution)/shard_map/ppermute | solution.py:324
  24.3 0.5 %rows_step.6 = (f32[8,128]{1,0:T(8,128)S(1)}, f32[512,256]{1,0:T(8,128)S(1)}, bf16[512,256]{1,0:T(8,128)(2,1)S(1)}) custom-call(f32[512,256]{1,0:T(8,128)S(1)} %get-tuple-element.145.refs_0_, bf16[512,256]{1,0:T(8,128)(2,1)S(1)} %get-tuple-element.146.refs_0_.refs_1_, ...), custom_call_target="tpu_custom_call", output_to_operand_aliasing={{0}: (12, {}), {1}: (0, {}), {2}: (1, {})} | custom-call | flops 10000000 | bytes 1 | tf_op jit(solution)/shard_map/rows_step/pallas_call | solution.py:25
  24.9 0.3 columns_step.27
  25.3 0.4 columns_step.28
  25.7 1.1 %collective-permute-start.15 = (f32[128,256]{1,0:T(8,128)S(1)}, f32[128,256]{1,0:T(8,128)S(1)}, u32[]{:S(2)}, u32[]{:S(2)}) collective-permute-start(f32[128,256]{1,0:T(8,128)S(1)} %get-tuple-element.202), channel_id=1, source_target_pairs={{0,4},{4,8},{8,12},{12,16},{16,20},{20,24},{24,28},{28,0},{1,5},{5... | collective-permute-start | bytes 393224 | tf_op jit(solution)/shard_map/ppermute | solution.py:324
  26.8 1.1 %collective-permute-done.10.refs_3_ = f32[128,256]{1,0:T(8,128)S(1)} collective-permute-done((f32[128,256]{1,0:T(8,128)S(1)}, f32[128,256]{1,0:T(8,128)S(1)}, u32[]{:S(2)}, u32[]{:S(2)}) %collective-permute-start.10) | collective-permute-done | bytes 131104 | tf_op jit(solution)/shard_map/ppermute | solution.py:324
  27.8 0.4 columns_step.29
  28.2 0.2 collective-permute-start.16
  28.4 1.5 %collective-permute-done.11.refs_3_ = f32[96,256]{1,0:T(8,128)S(1)} collective-permute-done((f32[96,256]{1,0:T(8,128)S(1)}, f32[96,256]{1,0:T(8,128)S(1)}, u32[]{:S(2)}, u32[]{:S(2)}) %collective-permute-start.11) | collective-permute-done | bytes 98336 | tf_op jit(solution)/shard_map/ppermute | solution.py:324
  29.9 0.3 columns_step.30
  30.3 0.8 %collective-permute-start.17 = (f32[96,256]{1,0:T(8,128)S(1)}, f32[96,256]{1,0:T(8,128)S(1)}, u32[]{:S(2)}, u32[]{:S(2)}) collective-permute-start(f32[96,256]{1,0:T(8,128)S(1)} %get-tuple-element.208), channel_id=1, source_target_pairs={{0,4},{4,8},{8,12},{12,16},{16,20},{20,24},{24,28},{28,0},{1,5},{5... | collective-permute-start | bytes 294920 | tf_op jit(solution)/shard_map/ppermute | solution.py:324
  31.1 0.2 collective-permute-done.12.refs_3_
  31.3 0.3 columns_step.31
  31.7 1.5 %collective-permute-start.13 = (f32[64,256]{1,0:T(8,128)S(1)}, f32[64,256]{1,0:T(8,128)S(1)}, u32[]{:S(2)}, u32[]{:S(2)}) collective-permute-start(f32[64,256]{1,0:T(8,128)S(1)} %get-tuple-element.198), channel_id=1, source_target_pairs={{0,4},{4,8},{8,12},{12,16},{16,20},{20,24},{24,28},{28,0},{1,5},{5... | collective-permute-start | bytes 196616 | tf_op jit(solution)/shard_map/ppermute | solution.py:324
  33.2 0.5 %rows_step.7 = (f32[8,128]{1,0:T(8,128)S(1)}, f32[512,256]{1,0:T(8,128)S(1)}, bf16[512,256]{1,0:T(8,128)(2,1)S(1)}) custom-call(f32[512,256]{1,0:T(8,128)S(1)} %get-tuple-element.169.refs_0_, bf16[512,256]{1,0:T(8,128)(2,1)S(1)} %get-tuple-element.170.refs_0_.refs_1_, ...), custom_call_target="tpu_custom_call", output_to_operand_aliasing={{0}: (12, {}), {1}: (0, {}), {2}: (1, {})} | custom-call | flops 10000000 | bytes 1 | tf_op jit(solution)/shard_map/rows_step/pallas_call | solution.py:25
  33.8 0.3 columns_step.32
  34.1 0.4 columns_step.33
  34.5 0.4 columns_step.34
  34.9 0.4 %collective-permute-done.17.refs_3_ = f32[96,256]{1,0:T(8,128)S(1)} collective-permute-done((f32[96,256]{1,0:T(8,128)S(1)}, f32[96,256]{1,0:T(8,128)S(1)}, u32[]{:S(2)}, u32[]{:S(2)}) %collective-permute-start.17) | collective-permute-done | bytes 98336 | tf_op jit(solution)/shard_map/ppermute | solution.py:324
  35.3 0.3 columns_step.35
  35.6 0.5 %rows_gradient.1 = (f32[8,128]{1,0:T(8,128)S(1)}, f32[512,256]{1,0:T(8,128)S(1)}) custom-call(bf16[96,512]{1,0:T(8,128)(2,1)S(1)} %get-tuple-element.201.refs_0_, bf16[128,512]{1,0:T(8,128)(2,1)S(1)} %get-tuple-element.204.refs_1_, bf16[128,512]{1,0:T(8,128)(2,1)S(1)} %get-tuple-element.207.refs_2_, ...), custom_call_target="tpu_custom_call", output_to_operand_aliasing={{0}: (8, {})} | custom-call | flops 10000000 | bytes 1 | tf_op jit(solution)/shard_map/rows_gradient/pallas_call | solution.py:25
  36.1 0.2 collective-permute-done.13.c_ref
  36.3 1.3 %last_columns_and_rows.1 = (f32[512,256]{1,0:T(8,128)}, f32[512,256]{1,0:T(8,128)}) custom-call(f32[512,256]{1,0:T(8,128)S(1)} %get-tuple-element.194.u_ref, bf16[512,256]{1,0:T(8,128)(2,1)S(1)} %get-tuple-element.195.refs_0_.row_half, bf16[512,512]{1,0:T(8,128)(2,1)S(1)} %get-tuple-element.196.refs_1_.dense, f32[8,512]{1,0:T(8,128)S(1)} %get-tuple-element.197.refs_2_.live, ...), custom_call_target="tpu_custom_call" | custom-call | flops 10000000 | bytes 1 | tf_op jit(solution)/shard_map/last_columns_and_rows/pallas_call | solution.py:25
  (21 shorter events, 0.6 us)
Async XLA Ops:
  0.6 7.0 %copy-start = (bf16[5,8,128,128]{3,2,1,0:T(8,128)(2,1)S(1)}, bf16[5,8,128,128]{3,2,1,0:T(8,128)(2,1)}, u32[]{:S(2)}) copy-start(bf16[5,8,128,128]{3,2,1,0:T(8,128)(2,1)} %x_ref.1) | copy-start | bytes 3932164
  0.6 7.0 %copy-start.1 = (s32[5,8,2]{1,2,0:T(2,128)S(1)}, s32[5,8,2]{1,2,0:T(2,128)}, u32[]{:S(2)}) copy-start(s32[5,8,2]{1,2,0:T(2,128)} %param.8) | copy-start | bytes 964
  0.7 7.0 %copy-start.2 = (s32[5,1]{0,1:T(1,128)S(1)}, s32[5,1]{0,1:T(1,128)}, u32[]{:S(2)}) copy-start(s32[5,1]{0,1:T(1,128)} %param.9) | copy-start | bytes 64
  2.3 6.7 %collective-permute-start = (f32[96,256]{1,0:T(8,128)S(1)}, f32[96,256]{1,0:T(8,128)S(1)}, u32[]{:S(2)}, u32[]{:S(2)}) collective-permute-start(f32[96,256]{1,0:T(8,128)S(1)} %get-tuple-element.128), channel_id=1, source_target_pairs={{0,4},{4,8},{8,12},{12,16},{16,20},{20,24},{24,28},{28,0},{1,5},{5... | collective-permute-start | bytes 294920 | tf_op jit(solution)/shard_map/ppermute | solution.py:324
  3.4 6.4 %collective-permute-start.1 = (f32[160,256]{1,0:T(8,128)S(1)}, f32[160,256]{1,0:T(8,128)S(1)}, u32[]{:S(2)}, u32[]{:S(2)}) collective-permute-start(f32[160,256]{1,0:T(8,128)S(1)} %get-tuple-element.131), channel_id=1, source_target_pairs={{0,4},{4,8},{8,12},{12,16},{16,20},{20,24},{24,28},{28,0},{1,5},{5... | collective-permute-start | bytes 491528 | tf_op jit(solution)/shard_map/ppermute | solution.py:324
  6.0 5.6 %collective-permute-start.2 = (f32[160,256]{1,0:T(8,128)S(1)}, f32[160,256]{1,0:T(8,128)S(1)}, u32[]{:S(2)}, u32[]{:S(2)}) collective-permute-start(f32[160,256]{1,0:T(8,128)S(1)} %get-tuple-element.134), channel_id=1, source_target_pairs={{0,4},{4,8},{8,12},{12,16},{16,20},{20,24},{24,28},{28,0},{1,5},{5... | collective-permute-start | bytes 491528 | tf_op jit(solution)/shard_map/ppermute | solution.py:324
  6.1 6.6 %collective-permute-start.3 = (f32[96,256]{1,0:T(8,128)S(1)}, f32[96,256]{1,0:T(8,128)S(1)}, u32[]{:S(2)}, u32[]{:S(2)}) collective-permute-start(f32[96,256]{1,0:T(8,128)S(1)} %get-tuple-element.137), channel_id=1, source_target_pairs={{0,4},{4,8},{8,12},{12,16},{16,20},{20,24},{24,28},{28,0},{1,5},{5... | collective-permute-start | bytes 294920 | tf_op jit(solution)/shard_map/ppermute | solution.py:324
  9.4 5.0 %collective-permute-start.4 = (f32[96,256]{1,0:T(8,128)S(1)}, f32[96,256]{1,0:T(8,128)S(1)}, u32[]{:S(2)}, u32[]{:S(2)}) collective-permute-start(f32[96,256]{1,0:T(8,128)S(1)} %get-tuple-element.149), channel_id=1, source_target_pairs={{0,4},{4,8},{8,12},{12,16},{16,20},{20,24},{24,28},{28,0},{1,5},{5... | collective-permute-start | bytes 294920 | tf_op jit(solution)/shard_map/ppermute | solution.py:324
  10.1 6.2 %collective-permute-start.5 = (f32[160,256]{1,0:T(8,128)S(1)}, f32[160,256]{1,0:T(8,128)S(1)}, u32[]{:S(2)}, u32[]{:S(2)}) collective-permute-start(f32[160,256]{1,0:T(8,128)S(1)} %get-tuple-element.152), channel_id=1, source_target_pairs={{0,4},{4,8},{8,12},{12,16},{16,20},{20,24},{24,28},{28,0},{1,5},{5... | collective-permute-start | bytes 491528 | tf_op jit(solution)/shard_map/ppermute | solution.py:324
  12.0 6.6 %collective-permute-start.6 = (f32[160,256]{1,0:T(8,128)S(1)}, f32[160,256]{1,0:T(8,128)S(1)}, u32[]{:S(2)}, u32[]{:S(2)}) collective-permute-start(f32[160,256]{1,0:T(8,128)S(1)} %get-tuple-element.155), channel_id=1, source_target_pairs={{0,4},{4,8},{8,12},{12,16},{16,20},{20,24},{24,28},{28,0},{1,5},{5... | collective-permute-start | bytes 491528 | tf_op jit(solution)/shard_map/ppermute | solution.py:324
  13.0 7.5 %collective-permute-start.7 = (f32[96,256]{1,0:T(8,128)S(1)}, f32[96,256]{1,0:T(8,128)S(1)}, u32[]{:S(2)}, u32[]{:S(2)}) collective-permute-start(f32[96,256]{1,0:T(8,128)S(1)} %get-tuple-element.158), channel_id=1, source_target_pairs={{0,4},{4,8},{8,12},{12,16},{16,20},{20,24},{24,28},{28,0},{1,5},{5... | collective-permute-start | bytes 294920 | tf_op jit(solution)/shard_map/ppermute | solution.py:324
  14.7 10.1 %collective-permute-start.8 = (f32[96,256]{1,0:T(8,128)S(1)}, f32[96,256]{1,0:T(8,128)S(1)}, u32[]{:S(2)}, u32[]{:S(2)}) collective-permute-start(f32[96,256]{1,0:T(8,128)S(1)} %get-tuple-element.173), channel_id=1, source_target_pairs={{0,1},{1,2},{2,3},{3,0},{4,5},{5,6},{6,7},{7,4},{8,9},{9,10},{10,1... | collective-permute-start | bytes 294920 | tf_op jit(solution)/shard_map/ppermute | solution.py:324
  16.7 8.5 %collective-permute-start.9 = (f32[128,256]{1,0:T(8,128)S(1)}, f32[128,256]{1,0:T(8,128)S(1)}, u32[]{:S(2)}, u32[]{:S(2)}) collective-permute-start(f32[128,256]{1,0:T(8,128)S(1)} %get-tuple-element.176), channel_id=1, source_target_pairs={{0,1},{1,2},{2,3},{3,0},{4,5},{5,6},{6,7},{7,4},{8,9},{9,10},{10,1... | collective-permute-start | bytes 393224 | tf_op jit(solution)/shard_map/ppermute | solution.py:324
  19.0 8.9 %collective-permute-start.10 = (f32[128,256]{1,0:T(8,128)S(1)}, f32[128,256]{1,0:T(8,128)S(1)}, u32[]{:S(2)}, u32[]{:S(2)}) collective-permute-start(f32[128,256]{1,0:T(8,128)S(1)} %get-tuple-element.179), channel_id=1, source_target_pairs={{0,1},{1,2},{2,3},{3,0},{4,5},{5,6},{6,7},{7,4},{8,9},{9,10},{10,1... | collective-permute-start | bytes 393224 | tf_op jit(solution)/shard_map/ppermute | solution.py:324
  20.9 9.0 %collective-permute-start.11 = (f32[96,256]{1,0:T(8,128)S(1)}, f32[96,256]{1,0:T(8,128)S(1)}, u32[]{:S(2)}, u32[]{:S(2)}) collective-permute-start(f32[96,256]{1,0:T(8,128)S(1)} %get-tuple-element.182), channel_id=1, source_target_pairs={{0,1},{1,2},{2,3},{3,0},{4,5},{5,6},{6,7},{7,4},{8,9},{9,10},{10,1... | collective-permute-start | bytes 294920 | tf_op jit(solution)/shard_map/ppermute | solution.py:324
  22.9 8.4 %collective-permute-start.12 = (f32[64,256]{1,0:T(8,128)S(1)}, f32[64,256]{1,0:T(8,128)S(1)}, u32[]{:S(2)}, u32[]{:S(2)}) collective-permute-start(f32[64,256]{1,0:T(8,128)S(1)} %get-tuple-element.185), channel_id=1, source_target_pairs={{0,1},{1,2},{2,3},{3,0},{4,5},{5,6},{6,7},{7,4},{8,9},{9,10},{10,1... | collective-permute-start | bytes 196616 | tf_op jit(solution)/shard_map/ppermute | solution.py:324
  25.2 8.5 %collective-permute-start.14 = (f32[96,256]{1,0:T(8,128)S(1)}, f32[96,256]{1,0:T(8,128)S(1)}, u32[]{:S(2)}, u32[]{:S(2)}) collective-permute-start(f32[96,256]{1,0:T(8,128)S(1)} %get-tuple-element.199), channel_id=1, source_target_pairs={{0,4},{4,8},{8,12},{12,16},{16,20},{20,24},{24,28},{28,0},{1,5},{5... | collective-permute-start | bytes 294920 | tf_op jit(solution)/shard_map/ppermute | solution.py:324
  25.7 8.5 %collective-permute-start.15 = (f32[128,256]{1,0:T(8,128)S(1)}, f32[128,256]{1,0:T(8,128)S(1)}, u32[]{:S(2)}, u32[]{:S(2)}) collective-permute-start(f32[128,256]{1,0:T(8,128)S(1)} %get-tuple-element.202), channel_id=1, source_target_pairs={{0,4},{4,8},{8,12},{12,16},{16,20},{20,24},{24,28},{28,0},{1,5},{5... | collective-permute-start | bytes 393224 | tf_op jit(solution)/shard_map/ppermute | solution.py:324
  28.2 6.3 %collective-permute-start.16 = (f32[128,256]{1,0:T(8,128)S(1)}, f32[128,256]{1,0:T(8,128)S(1)}, u32[]{:S(2)}, u32[]{:S(2)}) collective-permute-start(f32[128,256]{1,0:T(8,128)S(1)} %get-tuple-element.205), channel_id=1, source_target_pairs={{0,4},{4,8},{8,12},{12,16},{16,20},{20,24},{24,28},{28,0},{1,5},{5... | collective-permute-start | bytes 393224 | tf_op jit(solution)/shard_map/ppermute | solution.py:324
  30.3 5.0 %collective-permute-start.17 = (f32[96,256]{1,0:T(8,128)S(1)}, f32[96,256]{1,0:T(8,128)S(1)}, u32[]{:S(2)}, u32[]{:S(2)}) collective-permute-start(f32[96,256]{1,0:T(8,128)S(1)} %get-tuple-element.208), channel_id=1, source_target_pairs={{0,4},{4,8},{8,12},{12,16},{16,20},{20,24},{24,28},{28,0},{1,5},{5... | collective-permute-start | bytes 294920 | tf_op jit(solution)/shard_map/ppermute | solution.py:324
  31.7 4.6 %collective-permute-start.13 = (f32[64,256]{1,0:T(8,128)S(1)}, f32[64,256]{1,0:T(8,128)S(1)}, u32[]{:S(2)}, u32[]{:S(2)}) collective-permute-start(f32[64,256]{1,0:T(8,128)S(1)} %get-tuple-element.198), channel_id=1, source_target_pairs={{0,4},{4,8},{8,12},{12,16},{16,20},{20,24},{24,28},{28,0},{1,5},{5... | collective-permute-start | bytes 196616 | tf_op jit(solution)/shard_map/ppermute | solution.py:324
